TPU v7x, 32 devices: a whole 2x2x4 slice. The times are simulated.
32 devices in a mesh: parts: 2 (over y), dp: 4 (over z), seq: 4 (over x, core).
Axes of the slice: x: 2, y: 2, z: 4, core: 2. Of those that a mesh axis runs over, the one named last changes fastest.
Arguments:
- queries: bfloat16 [8, 4, 128, 32, 128], P(('parts', 'dp'), None, 'seq'), parts along dimension 0, may hold values from -6 to 6
- key_rows: bfloat16 [8, 4, 128, 32, 128], P(('parts', 'dp'), None, 'seq'), parts along dimension 0, may hold values from -6 to 6
- value_rows: bfloat16 [8, 4, 128, 32, 128], P(('parts', 'dp'), None, 'seq'), parts along dimension 0, may hold values from -6 to 6
- out_grad: bfloat16 [8, 4, 128, 32, 128], P(('parts', 'dp'), None, 'seq'), parts along dimension 0, may hold values from -6 to 6
- norm_gains: float32 [2, 32, 128], P(None, 'seq'), may hold values from 0.1 to 1.9
- clip_units: int32 [8, 4], P('parts'), parts along dimension 0, may hold values from 0 to 3, as said below
Outputs:
- gain_grads: float32 [4, 32, 128], P('parts', 'seq', 'dp'), parts along dimension 0
There are 2 independent parts, one for each index of `parts`. A program takes and returns all parts, laid end to end along the dimension named above; an argument that names none is the same for every part. Nothing has to cross between parts.
Inputs may be any that keep to these rules, and one draw needn't show every extreme that they name: `clip_units`: row g describes group g's 4 slots: entry j is the number of token blocks of the clip that begins at slot j, and 0 where no clip begins. The clips of a row are consecutive and fill all 4 slots; each spans 1 to 3 slots, and some row holds a clip of 3 slots.
All inputs are finite; a program needn't handle non-finite values.
Results may differ from a plain program's by a relative error of at most 0.0065.
Values may be sent and summed in bfloat16 or wider, within the bound.
No kernel may reach another device: no remote copies, remote signals or barrier semaphores. Data moves between devices by JAX's collectives and lax.ppermute only.
A program may use at most 64 MiB of HBM per device.

v0:
```python
import jax
import jax.numpy as jnp
from jax import lax
from jax.sharding import PartitionSpec as P

MAXCLIP = 3


def unit_plan(clip_table):
    positions = jnp.arange(clip_table.shape[0], dtype=jnp.int32)
    earlier = (positions[None, :] <= positions[:, None]) & (clip_table[None, :] > 0)
    unit_starts = jnp.max(jnp.where(earlier, positions[None, :], 0), axis=1)
    unit_sizes = jnp.sum(
        jnp.where(positions[None, :] == unit_starts[:, None], clip_table[None, :], 0), axis=1
    )
    unit_sizes = jnp.where(positions < unit_starts + unit_sizes, unit_sizes, 0)
    return (unit_starts, unit_sizes)


def normalize(values):
    widened = values.astype(jnp.float32)
    return widened * lax.rsqrt(jnp.mean(widened * widened, axis=-1, keepdims=True) + 1e-06)


def clip_terms(query_unit, key_clip, value_clip, grad_unit, gains):
    score_scale = query_unit.shape[-1] ** (-0.5)
    query_hat = normalize(query_unit)
    key_hat = normalize(key_clip)
    query_norm = (query_hat * gains[0]).astype(jnp.bfloat16)
    key_norm = (key_hat * gains[1]).astype(jnp.bfloat16)
    scores = (
        jnp.einsum("qhd,khd->hqk", query_norm, key_norm, preferred_element_type=jnp.float32)
        * score_scale
    )
    expo = jnp.exp(scores)
    prob = expo / jnp.sum(expo, axis=-1, keepdims=True)
    prob_low = prob.astype(jnp.bfloat16)
    attn_out = jnp.einsum("hqk,khd->qhd", prob_low, value_clip, preferred_element_type=jnp.float32)
    delta = jnp.einsum("qhd,qhd->hq", grad_unit.astype(jnp.float32), attn_out)
    dprob = jnp.einsum("qhd,khd->hqk", grad_unit, value_clip, preferred_element_type=jnp.float32)
    dscore = (prob * (dprob - delta[:, :, None])).astype(jnp.bfloat16)
    dq_norm = (
        jnp.einsum("hqk,khd->qhd", dscore, key_norm, preferred_element_type=jnp.float32)
        * score_scale
    )
    dk_norm = (
        jnp.einsum("hqk,qhd->khd", dscore, query_norm, preferred_element_type=jnp.float32)
        * score_scale
    )
    return jnp.stack([jnp.sum(dq_norm * query_hat, axis=0), jnp.sum(dk_norm * key_hat, axis=0)])


def slot_term(pieces, slot_index, clip_start, clip_size, gains):
    query_all, key_all, value_all, grad_all = pieces
    unit_rows = query_all.shape[1]
    head_count = query_all.shape[2]
    head_size = query_all.shape[3]

    def branch_for(unit_count):

        def run(slot_at, start_at):
            query_unit = lax.dynamic_slice_in_dim(query_all, slot_at, 1, 0)[0]
            grad_unit = lax.dynamic_slice_in_dim(grad_all, slot_at, 1, 0)[0]
            key_clip = lax.dynamic_slice_in_dim(key_all, start_at, unit_count, 0).reshape(
                unit_count * unit_rows, head_count, head_size
            )
            value_clip = lax.dynamic_slice_in_dim(value_all, start_at, unit_count, 0).reshape(
                unit_count * unit_rows, head_count, head_size
            )
            return clip_terms(query_unit, key_clip, value_clip, grad_unit, gains)

        return run

    def empty_branch(slot_at, start_at):
        return jnp.zeros((2, head_count, head_size), jnp.float32)

    branches = [empty_branch] + [branch_for(unit_count) for unit_count in range(1, MAXCLIP + 1)]
    return lax.switch(clip_size, branches, slot_index, clip_start)


def piece_terms(pieces, clip_table, gains):
    unit_starts, unit_sizes = unit_plan(clip_table)
    head_count = pieces[0].shape[2]
    head_size = pieces[0].shape[3]

    def advance(slot_index, running):
        return running + slot_term(
            pieces, slot_index, unit_starts[slot_index], unit_sizes[slot_index], gains
        )

    return lax.fori_loop(
        0, clip_table.shape[0], advance, jnp.zeros((2, head_count, head_size), jnp.float32)
    )


def body(queries, key_rows, value_rows, out_grad, norm_gains, clip_units):
    group = lax.axis_index("dp")
    local = (queries[0], key_rows[0], value_rows[0], out_grad[0])
    own_table = lax.dynamic_index_in_dim(clip_units, group, 0, keepdims=False)
    gathered = (
        lax.all_to_all(local[0], "seq", split_axis=2, concat_axis=1, tiled=True),
        lax.all_to_all(local[1], "seq", split_axis=2, concat_axis=1, tiled=True),
        lax.all_to_all(local[2], "seq", split_axis=2, concat_axis=1, tiled=True),
        lax.all_to_all(local[3], "seq", split_axis=2, concat_axis=1, tiled=True),
    )
    totals = piece_terms(gathered, own_table, norm_gains)
    return lax.psum_scatter(totals, "dp", scatter_dimension=2, tiled=True)


def solution(mesh):
    return jax.shard_map(
        body,
        mesh=mesh,
        in_specs=(
            P(("parts", "dp"), None, "seq", None, None),
            P(("parts", "dp"), None, "seq", None, None),
            P(("parts", "dp"), None, "seq", None, None),
            P(("parts", "dp"), None, "seq", None, None),
            P(None, "seq", None),
            P("parts", None),
        ),
        out_specs=P("parts", "seq", "dp"),
        check_vma=False,
    )
```

profile of v0, /device:TPU:0, one launch (start us, length us, event | category | flops | bytes accessed | tf_op | source)
XLA Modules:
  0.0 198.9 jit_solution(18232070362199689832)
XLA Ops:
  6.5 2.7 %copy.157 = bf16[1,4,32,32,128]{4,2,1,3,0:T(8,128)(2,1)} copy(bf16[1,4,32,32,128]{4,3,2,1,0:T(8,128)(2,1)} %param.12) | data formatting | bytes 2097152 | tf_op args[0]
  9.2 4.3 %all-to-all-start.1 = ((bf16[4,32,32,128]{3,1,0,2:T(8,128)(2,1)}), bf16[4,32,32,128]{3,1,0,2:T(8,128)(2,1)S(1)}, u32[]{:S(2)}, u32[]{:S(2)}) async-start(bf16[4,32,32,128]{3,1,0,2:T(8,128)(2,1)} %bitcast.226), calls=%async_computation.1 | async-start | bytes 2097152 | tf_op jit(solution)/shard_map/all_to_all | solution.py:101
  13.5 1.4 copy.158
  14.9 13.1 %all-to-all-done.1 = bf16[4,32,32,128]{3,1,0,2:T(8,128)(2,1)S(1)} async-done(((bf16[4,32,32,128]{3,1,0,2:T(8,128)(2,1)}), bf16[4,32,32,128]{3,1,0,2:T(8,128)(2,1)S(1)}, u32[]{:S(2)}, u32[]{:S(2)}) %all-to-all-start.1) | async-done | bytes 1048608 | tf_op jit(solution)/shard_map/all_to_all | solution.py:101
  28.0 3.5 %all-to-all-start = ((bf16[4,32,32,128]{3,1,0,2:T(8,128)(2,1)}), bf16[4,32,32,128]{3,1,0,2:T(8,128)(2,1)S(1)}, u32[]{:S(2)}, u32[]{:S(2)}) async-start(bf16[4,32,32,128]{3,1,0,2:T(8,128)(2,1)} %bitcast.227), calls=%async_computation | async-start | bytes 2097152 | tf_op jit(solution)/shard_map/all_to_all | solution.py:102
  31.5 1.4 copy.155
  33.0 13.0 %all-to-all-done = bf16[4,32,32,128]{3,1,0,2:T(8,128)(2,1)S(1)} async-done(((bf16[4,32,32,128]{3,1,0,2:T(8,128)(2,1)}), bf16[4,32,32,128]{3,1,0,2:T(8,128)(2,1)S(1)}, u32[]{:S(2)}, u32[]{:S(2)}) %all-to-all-start) | async-done | bytes 1048608 | tf_op jit(solution)/shard_map/all_to_all | solution.py:102
  46.0 3.5 %all-to-all-start.3 = ((bf16[4,32,32,128]{3,1,0,2:T(8,128)(2,1)}), bf16[4,32,32,128]{3,1,0,2:T(8,128)(2,1)S(1)}, u32[]{:S(2)}, u32[]{:S(2)}) async-start(bf16[4,32,32,128]{3,1,0,2:T(8,128)(2,1)} %bitcast.241), calls=%async_computation.3 | async-start | bytes 2097152 | tf_op jit(solution)/shard_map/all_to_all | solution.py:103
  49.5 2.6 %copy.156 = bf16[1,4,32,32,128]{4,2,1,3,0:T(8,128)(2,1)} copy(bf16[1,4,32,32,128]{4,3,2,1,0:T(8,128)(2,1)} %param.15) | data formatting | bytes 2097152 | tf_op args[3]
  52.1 11.8 %all-to-all-done.3 = bf16[4,32,32,128]{3,1,0,2:T(8,128)(2,1)S(1)} async-done(((bf16[4,32,32,128]{3,1,0,2:T(8,128)(2,1)}), bf16[4,32,32,128]{3,1,0,2:T(8,128)(2,1)S(1)}, u32[]{:S(2)}, u32[]{:S(2)}) %all-to-all-start.3) | async-done | bytes 1048608 | tf_op jit(solution)/shard_map/all_to_all | solution.py:103
  63.9 4.3 %all-to-all-start.2 = ((bf16[4,32,32,128]{3,1,0,2:T(8,128)(2,1)}), bf16[4,32,32,128]{3,1,0,2:T(8,128)(2,1)}, u32[]{:S(2)}, u32[]{:S(2)}) async-start(bf16[4,32,32,128]{3,1,0,2:T(8,128)(2,1)} %bitcast.240), calls=%async_computation.2 | async-start | bytes 2097152 | tf_op jit(solution)/shard_map/all_to_all | solution.py:104
  68.6 1.1 copy.103
  70.4 1.2 copy.107
  71.6 11.1 %all-to-all-done.2 = bf16[4,32,32,128]{3,1,0,2:T(8,128)(2,1)} async-done(((bf16[4,32,32,128]{3,1,0,2:T(8,128)(2,1)}), bf16[4,32,32,128]{3,1,0,2:T(8,128)(2,1)}, u32[]{:S(2)}, u32[]{:S(2)}) %all-to-all-start.2) | async-done | bytes 1048608 | tf_op jit(solution)/shard_map/all_to_all | solution.py:104
  82.7 2.3 %copy.105 = bf16[4,4,32,8,128]{4,2,1,3,0:T(8,128)(2,1)} copy(bf16[4,4,32,8,128]{4,2,0,3,1:T(8,128)(2,1)} %bitcast.65) | data formatting | bytes 2097152 | tf_op jit(solution)/shard_map/all_to_all | solution.py:104
  85.1 70.5 %while.14 = (s32[]{:T(128)}, f32[2,8,128]{2,1,0:T(8,128)S(1)}, s32[4]{0:T(128)S(1)}, s32[4]{0:T(128)S(1)}, bf16[4,128,8,128]{3,2,1,0:T(8,128)(2,1)S(1)}, /*index...) while((s32[]{:T(128)}, f32[2,8,128]{2,1,0:T(8,128)S(1)}, ...), condition=%wide.region_22.23_spmd.clone, body=%wide.region_2.22_spmd.clone.sunk | while | flops 513679744 | bytes 31408504 | solution.py:91
  86.3 13.5 %conditional.3 = (f32[2,8,128]{2,1,0:T(8,128)S(1)}) conditional(s32[]{:T(128)} %bitcast.229, () %tuple.62, (s32[4]{0:T(128)S(1)}, s32[]{:T(128)}, bf16[4,128,8,128]{3,2,1,0:T(8,128)(2,1)S(1)}, f32[2,8,128]{2,1,0:T(8,128)S(1)}, bf16[4,128,8,128]{3,1,2,0:T(8,128)(2,1)}, /*index=5*/bf16[4,128,8,128]{3,1,2,0:T(8,128)(2,1)}, ...), branch_computations={%region_3.3_spmd, %region_4.9_spmd, %region_10.15_spmd, %region_16... | conditional | flops 513675648 | bytes 31383704 | solution.py:78
  89.1 1.2 fusion.16
  91.9 2.3 %fusion.118 = (bf16[8,128,128]{1,2,0:T(8,128)(2,1)S(1)}, f32[8,128,128]{1,2,0:T(8,128)}) fusion(f32[8,128]{1,0:T(8,128)S(1)} %get-tuple-element.353, f32[128,8]{0,1:T(8,128)S(1)} %get-tuple-element.357, bf16[4,128,8,128]{3,1,2,0:T(8,128)(2,1)S(1)} %copy.96, s32[]{:T(128)S(6)} %select_n.35, f32[8,128]{1,0:T(8,128)S(1)} %get-tuple-element.352, ...), kind=kOutput, calls=%fused_computation.147 | convolution fusion | flops 34997376 | bytes 1327112 | tf_op jit(solution)/shard_map/while/body/eval_jaxpr/cond/branch_1_fun/div | solution.py:36
  94.2 1.2 fusion.8
  95.4 1.5 fusion.7
  96.9 1.3 fusion.10
  98.3 1.5 fusion.9
  101.1 13.5 %conditional.3 = (f32[2,8,128]{2,1,0:T(8,128)S(1)}) conditional(s32[]{:T(128)} %bitcast.229, () %tuple.62, (s32[4]{0:T(128)S(1)}, s32[]{:T(128)}, bf16[4,128,8,128]{3,2,1,0:T(8,128)(2,1)S(1)}, f32[2,8,128]{2,1,0:T(8,128)S(1)}, bf16[4,128,8,128]{3,1,2,0:T(8,128)(2,1)}, /*index=5*/bf16[4,128,8,128]{3,1,2,0:T(8,128)(2,1)}, ...), branch_computations={%region_3.3_spmd, %region_4.9_spmd, %region_10.15_spmd, %region_16... | conditional | flops 513675648 | bytes 31383704 | solution.py:78
  103.8 1.2 fusion.16
  106.7 2.3 %fusion.118 = (bf16[8,128,128]{1,2,0:T(8,128)(2,1)S(1)}, f32[8,128,128]{1,2,0:T(8,128)}) fusion(f32[8,128]{1,0:T(8,128)S(1)} %get-tuple-element.353, f32[128,8]{0,1:T(8,128)S(1)} %get-tuple-element.357, bf16[4,128,8,128]{3,1,2,0:T(8,128)(2,1)S(1)} %copy.96, s32[]{:T(128)S(6)} %select_n.35, f32[8,128]{1,0:T(8,128)S(1)} %get-tuple-element.352, ...), kind=kOutput, calls=%fused_computation.147 | convolution fusion | flops 34997376 | bytes 1327112 | tf_op jit(solution)/shard_map/while/body/eval_jaxpr/cond/branch_1_fun/div | solution.py:36
  109.0 1.2 fusion.8
  110.2 1.5 fusion.7
  111.7 1.4 fusion.10
  113.1 1.5 fusion.9
  115.8 19.2 %conditional.3 = (f32[2,8,128]{2,1,0:T(8,128)S(1)}) conditional(s32[]{:T(128)} %bitcast.229, () %tuple.62, (s32[4]{0:T(128)S(1)}, s32[]{:T(128)}, bf16[4,128,8,128]{3,2,1,0:T(8,128)(2,1)S(1)}, f32[2,8,128]{2,1,0:T(8,128)S(1)}, bf16[4,128,8,128]{3,1,2,0:T(8,128)(2,1)}, /*index=5*/bf16[4,128,8,128]{3,1,2,0:T(8,128)(2,1)}, ...), branch_computations={%region_3.3_spmd, %region_4.9_spmd, %region_10.15_spmd, %region_16... | conditional | flops 513675648 | bytes 31383704 | solution.py:78
  118.6 1.1 constant_dynamic-slice_fusion
  119.7 1.2 fusion.86
  123.9 1.4 dynamic-slice_convert_fusion
  125.4 3.0 %reshape.102 = f32[256,8,128]{0,2,1:T(8,128)} reshape(f32[2,128,8,128]{1,0,3,2:T(2,128)} %dynamic-slice_convert_fusion) | data formatting | bytes 2097152 | tf_op jit(solution)/shard_map/while/body/eval_jaxpr/cond/branch_2_fun/convert_element_type | solution.py:21
  128.4 1.9 fusion.89
  130.7 1.3 fusion.77
  132.1 1.6 fusion.78
  133.7 1.3 fusion.82
  136.3 19.2 %conditional.3 = (f32[2,8,128]{2,1,0:T(8,128)S(1)}) conditional(s32[]{:T(128)} %bitcast.229, () %tuple.62, (s32[4]{0:T(128)S(1)}, s32[]{:T(128)}, bf16[4,128,8,128]{3,2,1,0:T(8,128)(2,1)S(1)}, f32[2,8,128]{2,1,0:T(8,128)S(1)}, bf16[4,128,8,128]{3,1,2,0:T(8,128)(2,1)}, /*index=5*/bf16[4,128,8,128]{3,1,2,0:T(8,128)(2,1)}, ...), branch_computations={%region_3.3_spmd, %region_4.9_spmd, %region_10.15_spmd, %region_16... | conditional | flops 513675648 | bytes 31383704 | solution.py:78
  140.2 1.2 fusion.86
  144.4 1.4 dynamic-slice_convert_fusion
  145.9 3.0 %reshape.102 = f32[256,8,128]{0,2,1:T(8,128)} reshape(f32[2,128,8,128]{1,0,3,2:T(2,128)} %dynamic-slice_convert_fusion) | data formatting | bytes 2097152 | tf_op jit(solution)/shard_map/while/body/eval_jaxpr/cond/branch_2_fun/convert_element_type | solution.py:21
  148.9 1.9 fusion.89
  151.2 1.4 fusion.77
  152.6 1.6 fusion.78
  154.2 1.3 fusion.82
  156.5 34.1 %reduce-scatter.4.cloned.1.call-done = f32[32,16]{1,0:T(8,128)} async-done(((f32[128,16]{1,0:T(8,128)}), f32[32,16]{1,0:T(8,128)}) %reduce-scatter.4.cloned.1.call-update) | async-done | bytes 2064
  (72 shorter events, 19.7 us)
Async XLA Ops:
  9.2 4.3 %copy-start.3 = (bf16[1,4,32,32,128]{4,3,2,1,0:T(8,128)(2,1)S(1)}, bf16[1,4,32,32,128]{4,3,2,1,0:T(8,128)(2,1)}, u32[]{:S(2)}) copy-start(bf16[1,4,32,32,128]{4,3,2,1,0:T(8,128)(2,1)} %param.13) | copy-start | bytes 3145732
  9.2 18.8 %all-to-all-start.1 = ((bf16[4,32,32,128]{3,1,0,2:T(8,128)(2,1)}), bf16[4,32,32,128]{3,1,0,2:T(8,128)(2,1)S(1)}, u32[]{:S(2)}, u32[]{:S(2)}) async-start(bf16[4,32,32,128]{3,1,0,2:T(8,128)(2,1)} %bitcast.226), calls=%async_computation.1 | async-start | bytes 2097152 | tf_op jit(solution)/shard_map/all_to_all | solution.py:101
  14.9 16.6 %copy-start.4 = (bf16[1,4,32,32,128]{4,3,2,1,0:T(8,128)(2,1)S(1)}, bf16[1,4,32,32,128]{4,3,2,1,0:T(8,128)(2,1)}, u32[]{:S(2)}) copy-start(bf16[1,4,32,32,128]{4,3,2,1,0:T(8,128)(2,1)} %param.14) | copy-start | bytes 3145732
  28.0 18.0 %all-to-all-start = ((bf16[4,32,32,128]{3,1,0,2:T(8,128)(2,1)}), bf16[4,32,32,128]{3,1,0,2:T(8,128)(2,1)S(1)}, u32[]{:S(2)}, u32[]{:S(2)}) async-start(bf16[4,32,32,128]{3,1,0,2:T(8,128)(2,1)} %bitcast.227), calls=%async_computation | async-start | bytes 2097152 | tf_op jit(solution)/shard_map/all_to_all | solution.py:102
  46.0 18.0 %all-to-all-start.3 = ((bf16[4,32,32,128]{3,1,0,2:T(8,128)(2,1)}), bf16[4,32,32,128]{3,1,0,2:T(8,128)(2,1)S(1)}, u32[]{:S(2)}, u32[]{:S(2)}) async-start(bf16[4,32,32,128]{3,1,0,2:T(8,128)(2,1)} %bitcast.241), calls=%async_computation.3 | async-start | bytes 2097152 | tf_op jit(solution)/shard_map/all_to_all | solution.py:103
  52.1 16.1 %copy-start.5 = (s32[4,4]{1,0:T(4,128)S(1)}, s32[4,4]{1,0:T(4,128)}, u32[]{:S(2)}) copy-start(s32[4,4]{1,0:T(4,128)} %param.17) | copy-start | bytes 196
  63.9 18.8 %all-to-all-start.2 = ((bf16[4,32,32,128]{3,1,0,2:T(8,128)(2,1)}), bf16[4,32,32,128]{3,1,0,2:T(8,128)(2,1)}, u32[]{:S(2)}, u32[]{:S(2)}) async-start(bf16[4,32,32,128]{3,1,0,2:T(8,128)(2,1)} %bitcast.240), calls=%async_computation.2 | async-start | bytes 2097152 | tf_op jit(solution)/shard_map/all_to_all | solution.py:104
  68.2 122.4 %reduce-scatter.4.cloned.1.call-start = ((), (), s32[]{:S(2)}) async-start(), calls=%async_computation.5 | async-start | bytes 81920
  71.6 13.5 %copy-start.2 = (f32[2,8,128]{2,1,0:T(8,128)S(1)}, f32[2,8,128]{2,1,0:T(8,128)}, u32[]{:S(2)}) copy-start(f32[2,8,128]{2,1,0:T(8,128)} %param.16) | copy-start | bytes 24580
  130.7 1.4 copy-start.1
  151.2 1.4 copy-start.1
Sparse Core Ops, SparseCore 0:
  156.6 33.9 reduce-scatter.3
where the time goes:
time: 201 us; the launch traced here: 199 us
  waiting for transfers between devices  83.1 us (41%)
  local copies, waits for them, and re-layouts  32.4 us (16%)
  matrix products  28.9 us (14%)
  starting transfers between devices  15.7 us (8%)
  other arithmetic  14 us (7%)
  between operations  13.5 us (7%)
  loops' own time  11.4 us (6%)
    unnamed x2, waiting for transfers between devices  34.1 us
    all_to_all x1, waiting for transfers between devices, body(): lax.all_to_all(local[0], 'seq', split_axis=2, concat_axis=1, tiled=True)  13.1 us
    all_to_all x1, waiting for transfers between devices, body(): lax.all_to_all(local[1], 'seq', split_axis=2, concat_axis=1, tiled=True)  13 us
    all_to_all x1, waiting for transfers between devices, body(): lax.all_to_all(local[2], 'seq', split_axis=2, concat_axis=1, tiled=True)  11.8 us
    all_to_all x1, waiting for transfers between devices, body(): lax.all_to_all(local[3], 'seq', split_axis=2, concat_axis=1, tiled=True)  11.1 us
    unnamed x16, local copies, waits for them, and re-layouts  10.5 us
    another operation x4, loops' own time, slot_term(): return lax.switch(clip_size, branches, slot_index, clip_start)  8.83 us
    div x4, matrix products, clip_terms(): prob = expo / jnp.sum(expo, axis=-1, keepdims=True)  8.4 us
  transfers between devices with their start and end apart: 5, of which 5 were waited for; matrix products, arithmetic and copies ran while one was open for 4% of the time, Pallas kernels for 0%

commit v1 on v0

v1 whole, which is shorter than its diff:
```python
import functools
import math

import jax
import jax.numpy as jnp
from jax import lax
from jax.experimental import pallas as pl
from jax.experimental.pallas import tpu as pltpu
from jax.sharding import PartitionSpec as P

MAXCLIP = 3
TILE = 8
EPS = 1e-06
VMEM_LIMIT = 48 * 1024 * 1024


def head_chunks(heads):
    sizes = {8: (2, 2, 2, 2)}.get(heads)
    if sizes is None:
        sizes = (1,) * heads if heads <= 2 else (heads - heads // 2, heads // 2)
    bounds, start = [], 0
    for size in sizes:
        bounds.append((start, start + size))
        start += size
    return bounds


def pack_kernel(plan, heads, *refs):
    arrays = refs[:4]
    outs = refs[4 : 4 + sum(len(chunks) for _, chunks in plan)]
    raw, wide, sems = refs[4 + len(outs) :]
    me = lax.axis_index("seq")
    slots, rows = raw.shape[2], raw.shape[3]
    spans = max(1, heads // TILE)

    def copy(index, array, span, first):
        return pltpu.make_async_copy(
            arrays[array].at[0, :, :, pl.ds(first + span * TILE, TILE), :],
            raw.at[index, array * spans + span],
            sems.at[index, array * spans + span],
        )

    firsts, offsets = [], []
    for flip, _ in plan:
        head = jnp.bitwise_xor(me, flip) * heads
        firsts.append(pl.multiple_of((head // TILE) * TILE, TILE))
        offsets.append(0 if heads % TILE == 0 else lax.rem(head, TILE))
    for index in range(len(plan)):
        for array in range(4):
            for span in range(spans):
                copy(index, array, span, firsts[index]).start()
    place = 0
    for index, (_, chunks) in enumerate(plan):
        for array in range(4):
            for span in range(spans):
                copy(index, array, span, firsts[index]).wait()
                for slot in range(slots):
                    wide[slot] = (
                        raw[index, array * spans + span, slot]
                        .astype(jnp.float32)
                        .reshape(rows * TILE, wide.shape[-1])
                    )
                    for number, (low, high) in enumerate(chunks):
                        for head in range(max(low, span * TILE), min(high, (span + 1) * TILE)):
                            outs[place + number][head - low, array, slot * rows : (slot + 1) * rows, :] = wide[
                                slot, pl.ds(offsets[index] + head - span * TILE, rows, stride=TILE), :
                            ].astype(jnp.bfloat16)
        place += len(chunks)


def pack(arrays, plan, heads):
    _, slots, rows, _, size = arrays[0].shape
    spans = max(1, heads // TILE)
    shapes = [
        jax.ShapeDtypeStruct((high - low, 4, slots * rows, size), jnp.bfloat16)
        for _, chunks in plan
        for low, high in chunks
    ]
    count = len(plan)
    moved = count * 4 * spans * slots * rows * TILE * size * 2
    return pl.pallas_call(
        functools.partial(pack_kernel, plan, heads),
        out_shape=shapes,
        in_specs=[pl.BlockSpec(memory_space=pl.ANY)] * 4,
        out_specs=[pl.BlockSpec(memory_space=pltpu.VMEM)] * len(shapes),
        scratch_shapes=[
            pltpu.VMEM((count, 4 * spans, slots, rows, TILE, size), jnp.bfloat16),
            pltpu.VMEM((slots, rows * TILE, size), jnp.float32),
            pltpu.SemaphoreType.DMA((count, 4 * spans)),
        ],
        compiler_params=pltpu.CompilerParams(vmem_limit_bytes=VMEM_LIMIT),
        cost_estimate=pl.CostEstimate(flops=moved, bytes_accessed=2 * moved, transcendentals=0),
        name="pack",
    )(*arrays)


def contract_last(left, right):
    return lax.dot_general(left, right, (((1,), (1,)), ((), ())), preferred_element_type=jnp.float32)


def attention_chunk(low, units, gains, pieces, held, total):
    query, key, value, grad = held
    group = lax.axis_index("dp")
    count, _, tokens, size = pieces[0].shape
    slots = units.shape[1]
    rows = tokens // slots
    unit = rows * len(pieces)
    for head in range(count):
        for array, kept in ((0, query), (1, key)):
            gain = gains[array, low + head : low + head + 1, :]
            for source, piece in enumerate(pieces):
                wide = piece[head, array].astype(jnp.float32)
                normed = wide * lax.rsqrt(jnp.mean(wide * wide, axis=-1, keepdims=True) + EPS)
                normed = (normed * gain).astype(jnp.bfloat16)
                for slot in range(slots):
                    kept[head, slot * unit + source * rows : slot * unit + (source + 1) * rows, :] = normed[
                        slot * rows : (slot + 1) * rows
                    ]
        for array, kept in ((2, value), (3, grad)):
            for source, piece in enumerate(pieces):
                for slot in range(slots):
                    kept[head, slot * unit + source * rows : slot * unit + (source + 1) * rows, :] = piece[
                        head, array, slot * rows : (slot + 1) * rows, :
                    ]
    total[...] = jnp.zeros_like(total)
    factor = size ** (-0.5) * math.log2(math.e)

    def clip(slot, span):
        length = span * unit
        start = pl.multiple_of(slot * unit, unit)
        for head in range(count):
            q = query[head, pl.ds(start, length), :]
            k = key[head, pl.ds(start, length), :]
            expo = jnp.exp2(contract_last(k, q) * factor)
            dprob = contract_last(value[head, pl.ds(start, length), :], grad[head, pl.ds(start, length), :])
            prob = expo * (1.0 / jnp.sum(expo, axis=0, keepdims=True))
            delta = jnp.sum(prob * dprob, axis=0, keepdims=True)
            dscore = (prob * (dprob - delta)).astype(jnp.bfloat16)
            mixed = jnp.dot(dscore, q, preferred_element_type=jnp.float32)
            total[head : head + 1, :] += jnp.sum(mixed * k.astype(jnp.float32), axis=0, keepdims=True)

    def at_slot(slot, carry):
        span_here = units[group, slot]
        for span in range(1, min(MAXCLIP, slots) + 1):

            @pl.when(jnp.logical_and(span_here == span, slot + span <= slots))
            def _():
                clip(slot, span)

        return carry

    lax.fori_loop(0, slots, at_slot, 0)


def chunk_kernel(low, sources, units, gains, *refs):
    pieces, out, held = refs[:sources], refs[sources], refs[sources + 1 :]
    attention_chunk(low, units, gains, pieces, held, out)


def last_kernel(low, sources, earlier, peers, units, gains, *refs):
    pieces = refs[:sources]
    before = refs[sources : sources + earlier]
    outs = refs[sources + earlier : sources + earlier + len(peers)]
    held, total = refs[sources + earlier + len(peers) : -1], refs[-1]
    attention_chunk(low, units, gains, pieces, held, total)
    group = lax.axis_index("dp")
    size = total.shape[-1]
    width = outs[0].shape[-1]
    scaled = jnp.concatenate([ref[...] for ref in before] + [total[...]], axis=0) * (size ** (-0.5))
    for side in range(2):
        grads = scaled / gains[side]
        for out, flip in zip(outs, peers):
            shift = lax.rem(size - jnp.bitwise_xor(group, flip) * width, size)
            out[side] = pltpu.roll(grads, shift, 1)[:, :width]


def attend(low, units, gains, pieces, earlier=None, peers=None):
    count, _, tokens, size = pieces[0].shape
    all_tokens = tokens * len(pieces)
    held = [pltpu.VMEM((count, all_tokens, size), jnp.bfloat16)] * 4
    if earlier is None:
        kernel = functools.partial(chunk_kernel, low, len(pieces))
        shapes = jax.ShapeDtypeStruct((count, size), jnp.float32)
        earlier = []
        outs = pl.BlockSpec(memory_space=pltpu.VMEM)
    else:
        kernel = functools.partial(last_kernel, low, len(pieces), len(earlier), peers)
        heads = gains.shape[1]
        shapes = [jax.ShapeDtypeStruct((2, heads, size // len(peers)), jnp.float32)] * len(peers)
        held.append(pltpu.VMEM((count, size), jnp.float32))
        outs = [pl.BlockSpec(memory_space=pltpu.VMEM)] * len(peers)
    pairs = count * all_tokens * all_tokens // 2
    return pl.pallas_call(
        kernel,
        out_shape=shapes,
        in_specs=[pl.BlockSpec(memory_space=pltpu.SMEM)]
        + [pl.BlockSpec(memory_space=pltpu.VMEM)] * (1 + len(pieces) + len(earlier)),
        out_specs=outs,
        scratch_shapes=held,
        compiler_params=pltpu.CompilerParams(vmem_limit_bytes=VMEM_LIMIT),
        cost_estimate=pl.CostEstimate(
            flops=6 * pairs * size, bytes_accessed=len(pieces) * count * 4 * tokens * size * 2, transcendentals=pairs
        ),
        name="attend",
    )(units, gains, *pieces, *earlier)


def body(sequence, groups, queries, key_rows, value_rows, out_grad, norm_gains, clip_units):
    arrays = (queries, key_rows, value_rows, out_grad)
    heads = norm_gains.shape[1]
    chunks = head_chunks(heads)
    far = list(range(2, sequence)) or [1]
    near = [flip for flip in range(1, sequence) if flip not in far]

    def send(block, flip):
        return lax.ppermute(block, "seq", [(s, s ^ flip) for s in range(sequence)])

    held = [{} for _ in chunks]
    first = pack(arrays, [(flip, chunks[:1]) for flip in far], heads)
    for flip, block in zip(far, first):
        held[0][flip] = send(block, flip)
    plan = [(flip, chunks[1:]) for flip in far] + [(flip, chunks) for flip in near] + [(0, chunks)]
    blocks = iter(pack(arrays, plan, heads))
    for flip, wanted in plan:
        for bounds in wanted:
            block = next(blocks)
            held[chunks.index(bounds)][flip] = send(block, flip) if flip else block
    sums = []
    for number, (low, _) in enumerate(chunks[:-1]):
        pieces = [held[number][flip] for flip in range(sequence)]
        sums.append(attend(low, clip_units, norm_gains, pieces))
    pieces = [held[-1][flip] for flip in range(sequence)]
    parts = attend(chunks[-1][0], clip_units, norm_gains, pieces, sums, list(range(groups)))
    result = parts[0]
    for flip in range(1, groups):
        result = result + lax.ppermute(parts[flip], "dp", [(g, g ^ flip) for g in range(groups)])
    return result


def solution(mesh):
    return jax.shard_map(
        functools.partial(body, mesh.shape["seq"], mesh.shape["dp"]),
        mesh=mesh,
        in_specs=(
            P(("parts", "dp"), None, "seq", None, None),
            P(("parts", "dp"), None, "seq", None, None),
            P(("parts", "dp"), None, "seq", None, None),
            P(("parts", "dp"), None, "seq", None, None),
            P(None, "seq", None),
            P("parts", None),
        ),
        out_specs=P("parts", "seq", "dp"),
        check_vma=False,
    )
```

time: 201 us -> 66.3 us (0.33)
  waiting for transfers between devices: 83.1 us -> 34.6 us
  local copies, waits for them, and re-layouts: 32.4 us -> 2.47 us
  matrix products: 28.9 us -> 0 us
  Pallas kernels: 0 us -> 14.5 us
  between operations: 13.5 us -> 0.09 us
  other arithmetic: 14 us -> 0.6 us
  loops' own time: 11.4 us -> 0 us
    all_to_all x4 -> x0, waiting for transfers between devices: 49 us -> none  [the longest x1 13.1 us: body(): lax.all_to_all(local[0], 'seq', split_axis=2, concat_axis=1, tiled=True)]
    ppermute x0 -> x15, waiting for transfers between devices: none -> 34.6 us  [the longest x12 29.4 us: send(): return lax.ppermute(block, 'seq', [(s, s ^ flip) for s in range(sequence)])]
    unnamed x2 -> x0, waiting for transfers between devices: 34.1 us -> none
    dot_general x14 -> x0, matrix products: 18 us -> none  [the longest x4 5.89 us: clip_terms(): jnp.einsum('hqk,qhd->khd', dscore, query_norm, preferred_element_type=jnp...]
    all_to_all x4 -> x0, starting transfers between devices: 15.6 us -> none  [the longest x1 4.34 us: body(): lax.all_to_all(local[0], 'seq', split_axis=2, concat_axis=1, tiled=True)]
    pallas_call x0 -> x6, Pallas kernels: none -> 14.5 us  [the longest x4 10.7 us: attend(): pl.pallas_call(kernel, out_shape=shapes, in_specs=[pl.BlockSpec(memory_sp...]
    ppermute x0 -> x15, starting transfers between devices: none -> 13.9 us  [the longest x12 9.5 us: send(): return lax.ppermute(block, 'seq', [(s, s ^ flip) for s in range(sequence)])]
    another operation x5 -> x0, loops' own time: 11.4 us -> none  [the longest x4 8.83 us: slot_term(): return lax.switch(clip_size, branches, slot_index, clip_start)]
  transfers between devices with their start and end apart: 5 -> 15, of which waited for: 5 -> 9; matrix products, arithmetic and copies ran while one was open for 4% -> 0% of each run, Pallas kernels for 0% -> 13%
where the time goes in v1:
time: 66.3 us; the launch traced here: 66.1 us
  waiting for transfers between devices  34.6 us (52%)
  Pallas kernels  14.5 us (22%)
  starting transfers between devices  13.9 us (21%)
  local copies, waits for them, and re-layouts  2.47 us (4%)
    ppermute x12, waiting for transfers between devices, send(): return lax.ppermute(block, 'seq', [(s, s ^ flip) for s in range(sequence)])  29.4 us
    pallas_call x4, Pallas kernels, attend(): pl.pallas_call(kernel, out_shape=shapes, in_specs=[pl.BlockSpec(memory_sp...  10.7 us
    ppermute x12, starting transfers between devices, send(): return lax.ppermute(block, 'seq', [(s, s ^ flip) for s in range(sequence)])  9.5 us
    ppermute x3, waiting for transfers between devices, body(): lax.ppermute(parts[flip], 'dp', [(g, g ^ flip) for g in range(groups)])  5.23 us
    ppermute x3, starting transfers between devices, body(): lax.ppermute(parts[flip], 'dp', [(g, g ^ flip) for g in range(groups)])  4.4 us
    pallas_call x2, Pallas kernels, pack(): pl.pallas_call(functools.partial(pack_kernel, plan, heads), out_shape=sha...  3.75 us
    unnamed x12, local copies, waits for them, and re-layouts  2.47 us
  transfers between devices with their start and end apart: 15, of which 9 were waited for; matrix products, arithmetic and copies ran while one was open for 0% of the time, Pallas kernels for 13%

profile of v1, /device:TPU:0, one launch (start us, length us, event | category | flops | bytes accessed | tf_op | source)
XLA Modules:
  0.0 66.1 jit_solution(13794529546622176885)
XLA Ops:
  0.0 0.0 copy-start
  0.0 1.2 %copy-done = bf16[1,4,32,32,128]{4,3,2,1,0:T(8,128)(2,1)S(1)} copy-done((bf16[1,4,32,32,128]{4,3,2,1,0:T(8,128)(2,1)S(1)}, bf16[1,4,32,32,128]{4,3,2,1,0:T(8,128)(2,1)}, u32[]{:S(2)}) %copy-start) | copy-done | bytes 1048600
  1.2 0.0 copy-start.1
  1.2 1.2 %copy-done.1 = bf16[1,4,32,32,128]{4,3,2,1,0:T(8,128)(2,1)S(1)} copy-done((bf16[1,4,32,32,128]{4,3,2,1,0:T(8,128)(2,1)S(1)}, bf16[1,4,32,32,128]{4,3,2,1,0:T(8,128)(2,1)}, u32[]{:S(2)}) %copy-start.1) | copy-done | bytes 1048600
  2.5 0.0 copy-start.2
  2.5 0.0 copy-start.3
  2.5 2.9 %pack.2 = (bf16[2,4,128,128]{3,2,1,0:T(8,128)(2,1)S(1)}, bf16[2,4,128,128]{3,2,1,0:T(8,128)(2,1)S(1)}, bf16[2,4,128,128]{3,2,1,0:T(8,128)(2,1)S(1)}, bf16[2,4,12...) custom-call(bf16[1,4,32,32,128]{4,3,2,1,0:T(8,128)(2,1)S(1)} %copy-d, ...), custom_call_target="tpu_custom_call" | custom-call | flops 4194304 | bytes 8388608 | tf_op jit(solution)/shard_map/pack/pallas_call | solution.py:81
  5.3 3.0 %collective-permute-start.10 = (bf16[2,4,128,128]{3,2,1,0:T(8,128)(2,1)S(1)}, bf16[2,4,128,128]{3,2,1,0:T(8,128)(2,1)S(1)}, u32[]{:S(2)}, u32[]{:S(2)}) collective-permute-start(bf16[2,4,128,128]{3,2,1,0:T(8,128)(2,1)S(1)} %get-tuple-element.39), channel_id=1, source_target_pairs={{0,2},{1,3},{2,0},{3,1},{4,6},{5,7},{6,4},{7,5},{8,10},{9,11},{10,... | collective-permute-start | bytes 786440 | tf_op jit(solution)/shard_map/ppermute | solution.py:216
  8.3 0.0 collective-permute-start.11
  8.3 0.2 collective-permute-start.9
  8.5 0.3 collective-permute-start.6
  8.8 1.6 %collective-permute-start.7 = (bf16[2,4,128,128]{3,2,1,0:T(8,128)(2,1)S(1)}, bf16[2,4,128,128]{3,2,1,0:T(8,128)(2,1)S(1)}, u32[]{:S(2)}, u32[]{:S(2)}) collective-permute-start(bf16[2,4,128,128]{3,2,1,0:T(8,128)(2,1)S(1)} %get-tuple-element.35), channel_id=1, source_target_pairs={{0,2},{1,3},{2,0},{3,1},{4,6},{5,7},{6,4},{7,5},{8,10},{9,11},{10,... | collective-permute-start | bytes 786440 | tf_op jit(solution)/shard_map/ppermute | solution.py:216
  10.5 5.0 %collective-permute-done.10.refs_2_ = bf16[2,4,128,128]{3,2,1,0:T(8,128)(2,1)S(1)} collective-permute-done((bf16[2,4,128,128]{3,2,1,0:T(8,128)(2,1)S(1)}, bf16[2,4,128,128]{3,2,1,0:T(8,128)(2,1)S(1)}, u32[]{:S(2)}, u32[]{:S(2)}) %collective-permute-start.10) | collective-permute-done | bytes 262176 | tf_op jit(solution)/shard_map/ppermute | solution.py:216
  15.5 0.0 collective-permute-start.8
  15.5 5.2 %collective-permute-done.11.refs_3_ = bf16[2,4,128,128]{3,2,1,0:T(8,128)(2,1)S(1)} collective-permute-done((bf16[2,4,128,128]{3,2,1,0:T(8,128)(2,1)S(1)}, bf16[2,4,128,128]{3,2,1,0:T(8,128)(2,1)S(1)}, u32[]{:S(2)}, u32[]{:S(2)}) %collective-permute-start.11) | collective-permute-done | bytes 262176 | tf_op jit(solution)/shard_map/ppermute | solution.py:216
  20.6 0.2 collective-permute-start.3
  20.9 0.0 copy-done.2
  20.9 0.0 copy-done.3
  20.9 0.9 %pack.3 = (bf16[2,4,128,128]{3,2,1,0:T(8,128)(2,1)S(1)}, bf16[2,4,128,128]{3,2,1,0:T(8,128)(2,1)S(1)}) custom-call(bf16[1,4,32,32,128]{4,3,2,1,0:T(8,128)(2,1)S(1)} %copy-done, bf16[1,4,32,32,128]{4,3,2,1,0:T(8,128)(2,1)S(1)} %copy-done.1, bf16[1,4,32,32,128]{4,3,2,1,0:T(8,128)(2,1)S(1)} %copy-done.2, bf16[1,4,32,32,128]{4,3,2,1,0:T(8,128)(2,1)S(1)} %copy-done.3), custom_call_target="tpu_custom_call" | custom-call | flops 2097152 | bytes 4194304 | tf_op jit(solution)/shard_map/pack/pallas_call | solution.py:81
  21.8 0.0 copy-start.4
  21.8 0.0 collective-permute-done.9.refs_1_
  21.8 2.1 %collective-permute-start.4 = (bf16[2,4,128,128]{3,2,1,0:T(8,128)(2,1)S(1)}, bf16[2,4,128,128]{3,2,1,0:T(8,128)(2,1)S(1)}, u32[]{:S(2)}, u32[]{:S(2)}) collective-permute-start(bf16[2,4,128,128]{3,2,1,0:T(8,128)(2,1)S(1)} %get-tuple-element.31), channel_id=1, source_target_pairs={{0,2},{1,3},{2,0},{3,1},{4,6},{5,7},{6,4},{7,5},{8,10},{9,11},{10,... | collective-permute-start | bytes 786440 | tf_op jit(solution)/shard_map/ppermute | solution.py:216
  24.0 0.0 collective-permute-done.6.refs_1_
  24.0 0.0 collective-permute-start.5
  24.0 2.7 %collective-permute-done.7.refs_2_ = bf16[2,4,128,128]{3,2,1,0:T(8,128)(2,1)S(1)} collective-permute-done((bf16[2,4,128,128]{3,2,1,0:T(8,128)(2,1)S(1)}, bf16[2,4,128,128]{3,2,1,0:T(8,128)(2,1)S(1)}, u32[]{:S(2)}, u32[]{:S(2)}) %collective-permute-start.7) | collective-permute-done | bytes 262176 | tf_op jit(solution)/shard_map/ppermute | solution.py:216
  26.7 0.0 collective-permute-start
  26.7 5.2 %collective-permute-done.8.refs_3_ = bf16[2,4,128,128]{3,2,1,0:T(8,128)(2,1)S(1)} collective-permute-done((bf16[2,4,128,128]{3,2,1,0:T(8,128)(2,1)S(1)}, bf16[2,4,128,128]{3,2,1,0:T(8,128)(2,1)S(1)}, u32[]{:S(2)}, u32[]{:S(2)}) %collective-permute-start.8) | collective-permute-done | bytes 262176 | tf_op jit(solution)/shard_map/ppermute | solution.py:216
  31.9 0.2 collective-permute-start.1
  32.1 0.0 collective-permute-done.3.refs_1_
  32.1 1.8 %collective-permute-start.2 = (bf16[2,4,128,128]{3,2,1,0:T(8,128)(2,1)S(1)}, bf16[2,4,128,128]{3,2,1,0:T(8,128)(2,1)S(1)}, u32[]{:S(2)}, u32[]{:S(2)}) collective-permute-start(bf16[2,4,128,128]{3,2,1,0:T(8,128)(2,1)S(1)} %get-tuple-element.28), channel_id=1, source_target_pairs={{0,3},{1,2},{2,1},{3,0},{4,7},{5,6},{6,5},{7,4},{8,11},{9,10},{10,... | collective-permute-start | bytes 786440 | tf_op jit(solution)/shard_map/ppermute | solution.py:216
  33.9 0.0 copy-done.4
  33.9 0.0 copy-done.5
  33.9 2.8 %attend.6.refs_6_ = f32[2,128]{1,0:T(2,128)S(1)} custom-call(s32[4,4]{1,0:T(4,128)S(1)} %copy-done.5, f32[2,8,128]{2,1,0:T(8,128)S(1)} %copy-done.4, bf16[2,4,128,128]{3,2,1,0:T(8,128)(2,1)S(1)} %get-tuple-element.37.refs_0_, bf16[2,4,128,128]{3,2,1,0:T(8,128)(2,1)S(1)} %collective-permute-done.9.refs_1_, ...), custom_call_target="tpu_custom_call" | custom-call | flops 201326592 | bytes 1048576 | tf_op jit(solution)/shard_map/attend/pallas_call | solution.py:193
  36.7 2.6 %attend.5.refs_5_ = f32[2,128]{1,0:T(2,128)S(1)} custom-call(s32[4,4]{1,0:T(4,128)S(1)} %copy-done.5, f32[2,8,128]{2,1,0:T(8,128)S(1)} %copy-done.4, bf16[2,4,128,128]{3,2,1,0:T(8,128)(2,1)S(1)} %get-tuple-element.33.refs_0_, bf16[2,4,128,128]{3,2,1,0:T(8,128)(2,1)S(1)} %collective-permute-done.6.refs_1_, ...), custom_call_target="tpu_custom_call" | custom-call | flops 201326592 | bytes 1048576 | tf_op jit(solution)/shard_map/attend/pallas_call | solution.py:193
  39.3 0.0 collective-permute-done.4.refs_2_
  39.3 3.8 %collective-permute-done.5.refs_3_ = bf16[2,4,128,128]{3,2,1,0:T(8,128)(2,1)S(1)} collective-permute-done((bf16[2,4,128,128]{3,2,1,0:T(8,128)(2,1)S(1)}, bf16[2,4,128,128]{3,2,1,0:T(8,128)(2,1)S(1)}, u32[]{:S(2)}, u32[]{:S(2)}) %collective-permute-start.5) | collective-permute-done | bytes 262176 | tf_op jit(solution)/shard_map/ppermute | solution.py:216
  43.1 2.6 %attend.4.refs_4_ = f32[2,128]{1,0:T(2,128)S(1)} custom-call(s32[4,4]{1,0:T(4,128)S(1)} %copy-done.5, f32[2,8,128]{2,1,0:T(8,128)S(1)} %copy-done.4, bf16[2,4,128,128]{3,2,1,0:T(8,128)(2,1)S(1)} %get-tuple-element.29.refs_0_, bf16[2,4,128,128]{3,2,1,0:T(8,128)(2,1)S(1)} %collective-permute-done.3.refs_1_, ...), custom_call_target="tpu_custom_call" | custom-call | flops 201326592 | bytes 1048576 | tf_op jit(solution)/shard_map/attend/pallas_call | solution.py:193
  45.7 0.0 collective-permute-done.refs_1_
  45.8 3.4 %collective-permute-done.1.refs_2_ = bf16[2,4,128,128]{3,2,1,0:T(8,128)(2,1)S(1)} collective-permute-done((bf16[2,4,128,128]{3,2,1,0:T(8,128)(2,1)S(1)}, bf16[2,4,128,128]{3,2,1,0:T(8,128)(2,1)S(1)}, u32[]{:S(2)}, u32[]{:S(2)}) %collective-permute-start.1) | collective-permute-done | bytes 262176 | tf_op jit(solution)/shard_map/ppermute | solution.py:216
  49.2 4.0 %collective-permute-done.2.refs_3_ = bf16[2,4,128,128]{3,2,1,0:T(8,128)(2,1)S(1)} collective-permute-done((bf16[2,4,128,128]{3,2,1,0:T(8,128)(2,1)S(1)}, bf16[2,4,128,128]{3,2,1,0:T(8,128)(2,1)S(1)}, u32[]{:S(2)}, u32[]{:S(2)}) %collective-permute-start.2) | collective-permute-done | bytes 262176 | tf_op jit(solution)/shard_map/ppermute | solution.py:216
  53.2 2.7 %attend.7 = (f32[2,8,32]{2,1,0:T(8,128)S(1)}, f32[2,8,32]{2,1,0:T(8,128)S(1)}, f32[2,8,32]{2,1,0:T(8,128)S(1)}, f32[2,8,32]{2,1,0:T(8,128)S(1)}) custom-call(s32[4,4]{1,0:T(4,128)S(1)} %copy-done.5, f32[2,8,128]{2,1,0:T(8,128)S(1)} %copy-done.4, bf16[2,4,128,128]{3,2,1,0:T(8,128)(2,1)S(1)} %get-tuple-element.25.refs_0_, ...), custom_call_target="tpu_custom_call" | custom-call | flops 201326592 | bytes 1048576 | tf_op jit(solution)/shard_map/attend/pallas_call | solution.py:193
  55.9 1.6 %collective-permute-start.12 = (f32[2,8,32]{2,1,0:T(8,128)S(1)}, f32[2,8,32]{2,1,0:T(8,128)S(1)}, u32[]{:S(2)}, u32[]{:S(2)}) collective-permute-start(f32[2,8,32]{2,1,0:T(8,128)S(1)} %get-tuple-element.42), channel_id=1, source_target_pairs={{0,4},{4,0},{8,12},{12,8},{1,5},{5,1},{9,13},{13,9},{2,6},{6,2},{1... | collective-permute-start | bytes 6152 | tf_op jit(solution)/shard_map/ppermute | solution.py:236
  57.5 2.6 %collective-permute-start.13 = (f32[2,8,32]{2,1,0:T(8,128)S(1)}, f32[2,8,32]{2,1,0:T(8,128)S(1)}, u32[]{:S(2)}, u32[]{:S(2)}) collective-permute-start(f32[2,8,32]{2,1,0:T(8,128)S(1)} %get-tuple-element.43), channel_id=1, source_target_pairs={{0,8},{4,12},{8,0},{12,4},{1,9},{5,13},{9,1},{13,5},{2,10},{6,14},... | collective-permute-start | bytes 6152 | tf_op jit(solution)/shard_map/ppermute | solution.py:236
  60.1 0.2 collective-permute-start.14
  60.3 0.0 collective-permute-done.12
  60.3 1.7 %collective-permute-done.13 = f32[2,8,32]{2,1,0:T(8,128)S(1)} collective-permute-done((f32[2,8,32]{2,1,0:T(8,128)S(1)}, f32[2,8,32]{2,1,0:T(8,128)S(1)}, u32[]{:S(2)}, u32[]{:S(2)}) %collective-permute-start.13) | collective-permute-done | bytes 2080 | tf_op jit(solution)/shard_map/ppermute | solution.py:236
  62.0 3.5 %collective-permute-done.14 = f32[2,8,32]{2,1,0:T(8,128)S(1)} collective-permute-done((f32[2,8,32]{2,1,0:T(8,128)S(1)}, f32[2,8,32]{2,1,0:T(8,128)S(1)}, u32[]{:S(2)}, u32[]{:S(2)}) %collective-permute-start.14) | collective-permute-done | bytes 2080 | tf_op jit(solution)/shard_map/ppermute | solution.py:236
  65.5 0.6 add_add_fusion
  (1 shorter events, 0.0 us)
Async XLA Ops:
  0.0 1.2 %copy-start = (bf16[1,4,32,32,128]{4,3,2,1,0:T(8,128)(2,1)S(1)}, bf16[1,4,32,32,128]{4,3,2,1,0:T(8,128)(2,1)}, u32[]{:S(2)}) copy-start(bf16[1,4,32,32,128]{4,3,2,1,0:T(8,128)(2,1)} %refs_0_.3) | copy-start | bytes 3145732
  1.2 1.2 %copy-start.1 = (bf16[1,4,32,32,128]{4,3,2,1,0:T(8,128)(2,1)S(1)}, bf16[1,4,32,32,128]{4,3,2,1,0:T(8,128)(2,1)}, u32[]{:S(2)}) copy-start(bf16[1,4,32,32,128]{4,3,2,1,0:T(8,128)(2,1)} %refs_1_.3) | copy-start | bytes 3145732
  2.5 18.4 %copy-start.2 = (bf16[1,4,32,32,128]{4,3,2,1,0:T(8,128)(2,1)S(1)}, bf16[1,4,32,32,128]{4,3,2,1,0:T(8,128)(2,1)}, u32[]{:S(2)}) copy-start(bf16[1,4,32,32,128]{4,3,2,1,0:T(8,128)(2,1)} %refs_2_.3) | copy-start | bytes 3145732
  2.5 18.4 %copy-start.3 = (bf16[1,4,32,32,128]{4,3,2,1,0:T(8,128)(2,1)S(1)}, bf16[1,4,32,32,128]{4,3,2,1,0:T(8,128)(2,1)}, u32[]{:S(2)}) copy-start(bf16[1,4,32,32,128]{4,3,2,1,0:T(8,128)(2,1)} %refs_3_.3) | copy-start | bytes 3145732
  5.3 10.1 %collective-permute-start.10 = (bf16[2,4,128,128]{3,2,1,0:T(8,128)(2,1)S(1)}, bf16[2,4,128,128]{3,2,1,0:T(8,128)(2,1)S(1)}, u32[]{:S(2)}, u32[]{:S(2)}) collective-permute-start(bf16[2,4,128,128]{3,2,1,0:T(8,128)(2,1)S(1)} %get-tuple-element.39), channel_id=1, source_target_pairs={{0,2},{1,3},{2,0},{3,1},{4,6},{5,7},{6,4},{7,5},{8,10},{9,11},{10,... | collective-permute-start | bytes 786440 | tf_op jit(solution)/shard_map/ppermute | solution.py:216
  8.3 12.3 %collective-permute-start.11 = (bf16[2,4,128,128]{3,2,1,0:T(8,128)(2,1)S(1)}, bf16[2,4,128,128]{3,2,1,0:T(8,128)(2,1)S(1)}, u32[]{:S(2)}, u32[]{:S(2)}) collective-permute-start(bf16[2,4,128,128]{3,2,1,0:T(8,128)(2,1)S(1)} %get-tuple-element.40), channel_id=1, source_target_pairs={{0,3},{1,2},{2,1},{3,0},{4,7},{5,6},{6,5},{7,4},{8,11},{9,10},{10,... | collective-permute-start | bytes 786440 | tf_op jit(solution)/shard_map/ppermute | solution.py:216
  8.3 13.5 %collective-permute-start.9 = (bf16[2,4,128,128]{3,2,1,0:T(8,128)(2,1)S(1)}, bf16[2,4,128,128]{3,2,1,0:T(8,128)(2,1)S(1)}, u32[]{:S(2)}, u32[]{:S(2)}) collective-permute-start(bf16[2,4,128,128]{3,2,1,0:T(8,128)(2,1)S(1)} %get-tuple-element.38), channel_id=1, source_target_pairs={{0,1},{1,0},{2,3},{3,2},{4,5},{5,4},{6,7},{7,6},{8,9},{9,8},{10,11... | collective-permute-start | bytes 786440 | tf_op jit(solution)/shard_map/ppermute | solution.py:216
  8.5 15.4 %collective-permute-start.6 = (bf16[2,4,128,128]{3,2,1,0:T(8,128)(2,1)S(1)}, bf16[2,4,128,128]{3,2,1,0:T(8,128)(2,1)S(1)}, u32[]{:S(2)}, u32[]{:S(2)}) collective-permute-start(bf16[2,4,128,128]{3,2,1,0:T(8,128)(2,1)S(1)} %get-tuple-element.34), channel_id=1, source_target_pairs={{0,1},{1,0},{2,3},{3,2},{4,5},{5,4},{6,7},{7,6},{8,9},{9,8},{10,11... | collective-permute-start | bytes 786440 | tf_op jit(solution)/shard_map/ppermute | solution.py:216
  8.8 17.9 %collective-permute-start.7 = (bf16[2,4,128,128]{3,2,1,0:T(8,128)(2,1)S(1)}, bf16[2,4,128,128]{3,2,1,0:T(8,128)(2,1)S(1)}, u32[]{:S(2)}, u32[]{:S(2)}) collective-permute-start(bf16[2,4,128,128]{3,2,1,0:T(8,128)(2,1)S(1)} %get-tuple-element.35), channel_id=1, source_target_pairs={{0,2},{1,3},{2,0},{3,1},{4,6},{5,7},{6,4},{7,5},{8,10},{9,11},{10,... | collective-permute-start | bytes 786440 | tf_op jit(solution)/shard_map/ppermute | solution.py:216
  15.5 16.4 %collective-permute-start.8 = (bf16[2,4,128,128]{3,2,1,0:T(8,128)(2,1)S(1)}, bf16[2,4,128,128]{3,2,1,0:T(8,128)(2,1)S(1)}, u32[]{:S(2)}, u32[]{:S(2)}) collective-permute-start(bf16[2,4,128,128]{3,2,1,0:T(8,128)(2,1)S(1)} %get-tuple-element.36), channel_id=1, source_target_pairs={{0,3},{1,2},{2,1},{3,0},{4,7},{5,6},{6,5},{7,4},{8,11},{9,10},{10,... | collective-permute-start | bytes 786440 | tf_op jit(solution)/shard_map/ppermute | solution.py:216
  20.6 11.4 %collective-permute-start.3 = (bf16[2,4,128,128]{3,2,1,0:T(8,128)(2,1)S(1)}, bf16[2,4,128,128]{3,2,1,0:T(8,128)(2,1)S(1)}, u32[]{:S(2)}, u32[]{:S(2)}) collective-permute-start(bf16[2,4,128,128]{3,2,1,0:T(8,128)(2,1)S(1)} %get-tuple-element.30), channel_id=1, source_target_pairs={{0,1},{1,0},{2,3},{3,2},{4,5},{5,4},{6,7},{7,6},{8,9},{9,8},{10,11... | collective-permute-start | bytes 786440 | tf_op jit(solution)/shard_map/ppermute | solution.py:216
  21.8 12.1 %copy-start.4 = (f32[2,8,128]{2,1,0:T(8,128)S(1)}, f32[2,8,128]{2,1,0:T(8,128)}, u32[]{:S(2)}) copy-start(f32[2,8,128]{2,1,0:T(8,128)} %gains.7) | copy-start | bytes 24580
  21.8 17.5 %collective-permute-start.4 = (bf16[2,4,128,128]{3,2,1,0:T(8,128)(2,1)S(1)}, bf16[2,4,128,128]{3,2,1,0:T(8,128)(2,1)S(1)}, u32[]{:S(2)}, u32[]{:S(2)}) collective-permute-start(bf16[2,4,128,128]{3,2,1,0:T(8,128)(2,1)S(1)} %get-tuple-element.31), channel_id=1, source_target_pairs={{0,2},{1,3},{2,0},{3,1},{4,6},{5,7},{6,4},{7,5},{8,10},{9,11},{10,... | collective-permute-start | bytes 786440 | tf_op jit(solution)/shard_map/ppermute | solution.py:216
  24.0 19.2 %collective-permute-start.5 = (bf16[2,4,128,128]{3,2,1,0:T(8,128)(2,1)S(1)}, bf16[2,4,128,128]{3,2,1,0:T(8,128)(2,1)S(1)}, u32[]{:S(2)}, u32[]{:S(2)}) collective-permute-start(bf16[2,4,128,128]{3,2,1,0:T(8,128)(2,1)S(1)} %get-tuple-element.32), channel_id=1, source_target_pairs={{0,3},{1,2},{2,1},{3,0},{4,7},{5,6},{6,5},{7,4},{8,11},{9,10},{10,... | collective-permute-start | bytes 786440 | tf_op jit(solution)/shard_map/ppermute | solution.py:216
  26.7 19.1 %collective-permute-start = (bf16[2,4,128,128]{3,2,1,0:T(8,128)(2,1)S(1)}, bf16[2,4,128,128]{3,2,1,0:T(8,128)(2,1)S(1)}, u32[]{:S(2)}, u32[]{:S(2)}) collective-permute-start(bf16[2,4,128,128]{3,2,1,0:T(8,128)(2,1)S(1)} %get-tuple-element.26), channel_id=1, source_target_pairs={{0,1},{1,0},{2,3},{3,2},{4,5},{5,4},{6,7},{7,6},{8,9},{9,8},{10,11... | collective-permute-start | bytes 786440 | tf_op jit(solution)/shard_map/ppermute | solution.py:216
  31.9 2.0 %copy-start.5 = (s32[4,4]{1,0:T(4,128)S(1)}, s32[4,4]{1,0:T(4,128)}, u32[]{:S(2)}) copy-start(s32[4,4]{1,0:T(4,128)} %units.7) | copy-start | bytes 196
  31.9 17.3 %collective-permute-start.1 = (bf16[2,4,128,128]{3,2,1,0:T(8,128)(2,1)S(1)}, bf16[2,4,128,128]{3,2,1,0:T(8,128)(2,1)S(1)}, u32[]{:S(2)}, u32[]{:S(2)}) collective-permute-start(bf16[2,4,128,128]{3,2,1,0:T(8,128)(2,1)S(1)} %get-tuple-element.27), channel_id=1, source_target_pairs={{0,2},{1,3},{2,0},{3,1},{4,6},{5,7},{6,4},{7,5},{8,10},{9,11},{10,... | collective-permute-start | bytes 786440 | tf_op jit(solution)/shard_map/ppermute | solution.py:216
  32.1 21.1 %collective-permute-start.2 = (bf16[2,4,128,128]{3,2,1,0:T(8,128)(2,1)S(1)}, bf16[2,4,128,128]{3,2,1,0:T(8,128)(2,1)S(1)}, u32[]{:S(2)}, u32[]{:S(2)}) collective-permute-start(bf16[2,4,128,128]{3,2,1,0:T(8,128)(2,1)S(1)} %get-tuple-element.28), channel_id=1, source_target_pairs={{0,3},{1,2},{2,1},{3,0},{4,7},{5,6},{6,5},{7,4},{8,11},{9,10},{10,... | collective-permute-start | bytes 786440 | tf_op jit(solution)/shard_map/ppermute | solution.py:216
  55.9 4.4 %collective-permute-start.12 = (f32[2,8,32]{2,1,0:T(8,128)S(1)}, f32[2,8,32]{2,1,0:T(8,128)S(1)}, u32[]{:S(2)}, u32[]{:S(2)}) collective-permute-start(f32[2,8,32]{2,1,0:T(8,128)S(1)} %get-tuple-element.42), channel_id=1, source_target_pairs={{0,4},{4,0},{8,12},{12,8},{1,5},{5,1},{9,13},{13,9},{2,6},{6,2},{1... | collective-permute-start | bytes 6152 | tf_op jit(solution)/shard_map/ppermute | solution.py:236
  57.5 4.5 %collective-permute-start.13 = (f32[2,8,32]{2,1,0:T(8,128)S(1)}, f32[2,8,32]{2,1,0:T(8,128)S(1)}, u32[]{:S(2)}, u32[]{:S(2)}) collective-permute-start(f32[2,8,32]{2,1,0:T(8,128)S(1)} %get-tuple-element.43), channel_id=1, source_target_pairs={{0,8},{4,12},{8,0},{12,4},{1,9},{5,13},{9,1},{13,5},{2,10},{6,14},... | collective-permute-start | bytes 6152 | tf_op jit(solution)/shard_map/ppermute | solution.py:236
  60.1 5.4 %collective-permute-start.14 = (f32[2,8,32]{2,1,0:T(8,128)S(1)}, f32[2,8,32]{2,1,0:T(8,128)S(1)}, u32[]{:S(2)}, u32[]{:S(2)}) collective-permute-start(f32[2,8,32]{2,1,0:T(8,128)S(1)} %get-tuple-element.44), channel_id=1, source_target_pairs={{0,12},{4,8},{8,4},{12,0},{1,13},{5,9},{9,5},{13,1},{2,14},{6,10},... | collective-permute-start | bytes 6152 | tf_op jit(solution)/shard_map/ppermute | solution.py:236

commit v2 on v1

--- a/solution.py
+++ b/solution.py
@@ -12,10 +12,11 @@
 TILE = 8
 EPS = 1e-06
 VMEM_LIMIT = 48 * 1024 * 1024
+PACK_VMEM_LIMIT = 60 * 1024 * 1024
 
 
 def head_chunks(heads):
-    sizes = {8: (2, 2, 2, 2)}.get(heads)
+    sizes = {8: (2, 3, 2, 1)}.get(heads)
     if sizes is None:
         sizes = (1,) * heads if heads <= 2 else (heads - heads // 2, heads // 2)
     bounds, start = [], 0
@@ -25,10 +26,10 @@
     return bounds
 
 
-def pack_kernel(plan, heads, *refs):
+def pack_kernel(plan, heads, after, *refs):
     arrays = refs[:4]
-    outs = refs[4 : 4 + sum(len(chunks) for _, chunks in plan)]
-    raw, wide, sems = refs[4 + len(outs) :]
+    outs = refs[4 + after : 4 + after + sum(len(chunks) for _, chunks in plan)]
+    raw, wide, sems = refs[4 + after + len(outs) :]
     me = lax.axis_index("seq")
     slots, rows = raw.shape[2], raw.shape[3]
     spans = max(1, heads // TILE)
@@ -68,7 +69,7 @@
         place += len(chunks)
 
 
-def pack(arrays, plan, heads):
+def pack(arrays, plan, heads, after=()):
     _, slots, rows, _, size = arrays[0].shape
     spans = max(1, heads // TILE)
     shapes = [
@@ -79,19 +80,19 @@
     count = len(plan)
     moved = count * 4 * spans * slots * rows * TILE * size * 2
     return pl.pallas_call(
-        functools.partial(pack_kernel, plan, heads),
+        functools.partial(pack_kernel, plan, heads, len(after)),
         out_shape=shapes,
-        in_specs=[pl.BlockSpec(memory_space=pl.ANY)] * 4,
+        in_specs=[pl.BlockSpec(memory_space=pltpu.HBM)] * 4 + [pl.BlockSpec(memory_space=pl.ANY)] * len(after),
         out_specs=[pl.BlockSpec(memory_space=pltpu.VMEM)] * len(shapes),
         scratch_shapes=[
             pltpu.VMEM((count, 4 * spans, slots, rows, TILE, size), jnp.bfloat16),
             pltpu.VMEM((slots, rows * TILE, size), jnp.float32),
             pltpu.SemaphoreType.DMA((count, 4 * spans)),
         ],
-        compiler_params=pltpu.CompilerParams(vmem_limit_bytes=VMEM_LIMIT),
+        compiler_params=pltpu.CompilerParams(vmem_limit_bytes=PACK_VMEM_LIMIT),
         cost_estimate=pl.CostEstimate(flops=moved, bytes_accessed=2 * moved, transcendentals=0),
         name="pack",
-    )(*arrays)
+    )(*arrays, *after)
 
 
 def contract_last(left, right):
@@ -220,7 +221,7 @@
     for flip, block in zip(far, first):
         held[0][flip] = send(block, flip)
     plan = [(flip, chunks[1:]) for flip in far] + [(flip, chunks) for flip in near] + [(0, chunks)]
-    blocks = iter(pack(arrays, plan, heads))
+    blocks = iter(pack(arrays, plan, heads, first[:1]))
     for flip, wanted in plan:
         for bounds in wanted:
             block = next(blocks)

time: 66.3 us -> 70.5 us (1.063)
  Pallas kernels: 14.5 us -> 18.4 us
  starting transfers between devices: 13.9 us -> 16.6 us
  local copies, waits for them, and re-layouts: 2.47 us -> 0.96 us
  waiting for transfers between devices: 34.6 us -> 33.1 us
    pallas_call x2, Pallas kernels: 3.75 us -> 6.91 us  [pack(): pl.pallas_call(functools.partial(pack_kernel, plan, heads, len(after)), o...]
    ppermute x12, starting transfers between devices: 9.5 us -> 11.4 us  [send(): return lax.ppermute(block, 'seq', [(s, s ^ flip) for s in range(sequence)])]
    ppermute x3, waiting for transfers between devices: 5.23 us -> 3.47 us  [body(): lax.ppermute(parts[flip], 'dp', [(g, g ^ flip) for g in range(groups)])]
    unnamed x12, local copies, waits for them, and re-layouts: 2.47 us -> 0.96 us
    ppermute x3, starting transfers between devices: 4.4 us -> 5.22 us  [body(): lax.ppermute(parts[flip], 'dp', [(g, g ^ flip) for g in range(groups)])]
    pallas_call x4, Pallas kernels: 10.7 us -> 11.5 us  [attend(): pl.pallas_call(kernel, out_shape=shapes, in_specs=[pl.BlockSpec(memory_sp...]
  transfers between devices with their start and end apart: 15 -> 15, of which waited for: 9 -> 6; matrix products, arithmetic and copies ran while one was open for 0% -> 0% of each run, Pallas kernels for 13% -> 20%
where the time goes in v2:
time: 70.5 us; the launch traced here: 69.8 us
  waiting for transfers between devices  33.1 us (47%)
  Pallas kernels  18.4 us (26%)
  starting transfers between devices  16.6 us (24%)
  local copies, waits for them, and re-layouts  0.96 us (1%)
    ppermute x12, waiting for transfers between devices, send(): return lax.ppermute(block, 'seq', [(s, s ^ flip) for s in range(sequence)])  29.6 us
    pallas_call x4, Pallas kernels, attend(): pl.pallas_call(kernel, out_shape=shapes, in_specs=[pl.BlockSpec(memory_sp...  11.5 us
    ppermute x12, starting transfers between devices, send(): return lax.ppermute(block, 'seq', [(s, s ^ flip) for s in range(sequence)])  11.4 us
    pallas_call x2, Pallas kernels, pack(): pl.pallas_call(functools.partial(pack_kernel, plan, heads, len(after)), o...  6.91 us
    ppermute x3, starting transfers between devices, body(): lax.ppermute(parts[flip], 'dp', [(g, g ^ flip) for g in range(groups)])  5.22 us
    ppermute x3, waiting for transfers between devices, body(): lax.ppermute(parts[flip], 'dp', [(g, g ^ flip) for g in range(groups)])  3.47 us
  transfers between devices with their start and end apart: 15, of which 6 were waited for; matrix products, arithmetic and copies ran while one was open for 0% of the time, Pallas kernels for 20%

profile of v2, /device:TPU:0, one launch (start us, length us, event | category | flops | bytes accessed | tf_op | source)
XLA Modules:
  0.0 69.8 jit_solution(4617693708214186435)
XLA Ops:
  0.0 2.4 %pack.2 = (bf16[2,4,128,128]{3,2,1,0:T(8,128)(2,1)}, bf16[2,4,128,128]{3,2,1,0:T(8,128)(2,1)}) custom-call(bf16[1,4,32,32,128]{4,3,2,1,0:T(8,128)(2,1)} %refs_0_.3, bf16[1,4,32,32,128]{4,3,2,1,0:T(8,128)(2,1)} %refs_1_.3, bf16[1,4,32,32,128]{4,3,2,1,0:T(8,128)(2,1)} %refs_2_.3, bf16[1,4,32,32,128]{4,3,2,1,0:T(8,128)(2,1)} %refs_3_.3), custom_call_target="tpu_custom_call" | custom-call | flops 2097152 | bytes 4194304 | tf_op jit(solution)/shard_map/pack/pallas_call | solution.py:82
  2.4 2.4 %collective-permute-start.5 = (bf16[2,4,128,128]{3,2,1,0:T(8,128)(2,1)}, bf16[2,4,128,128]{3,2,1,0:T(8,128)(2,1)S(1)}, u32[]{:S(2)}, u32[]{:S(2)}) collective-permute-start(bf16[2,4,128,128]{3,2,1,0:T(8,128)(2,1)} %get-tuple-element.32), channel_id=1, source_target_pairs={{0,3},{1,2},{2,1},{3,0},{4,7},{5,6},{6,5},{7,4},{8,11},{9,10},{10,... | collective-permute-start | bytes 786440 | tf_op jit(solution)/shard_map/ppermute | solution.py:217
  4.9 0.6 collective-permute-start.4
  5.5 4.5 %pack.3 = (bf16[3,4,128,128]{3,2,1,0:T(8,128)(2,1)}, bf16[2,4,128,128]{3,2,1,0:T(8,128)(2,1)}, bf16[1,4,128,128]{3,2,1,0:T(8,128)(2,1)}, bf16[3,4,128,128]{3,2,1...) custom-call(bf16[1,4,32,32,128]{4,3,2,1,0:T(8,128)(2,1)} %refs_0_.3,, ...), custom_call_target="tpu_custom_call" | custom-call | flops 4194304 | bytes 8388608 | tf_op jit(solution)/shard_map/pack/pallas_call | solution.py:82
  10.0 0.1 collective-permute-start.3
  10.1 0.5 collective-permute-start.9
  10.6 0.0 copy-start.3
  10.6 0.1 collective-permute-start.6
  10.7 1.2 %collective-permute-done.5.refs_3_ = bf16[2,4,128,128]{3,2,1,0:T(8,128)(2,1)S(1)} collective-permute-done((bf16[2,4,128,128]{3,2,1,0:T(8,128)(2,1)}, bf16[2,4,128,128]{3,2,1,0:T(8,128)(2,1)S(1)}, u32[]{:S(2)}, u32[]{:S(2)}) %collective-permute-start.5) | collective-permute-done | bytes 262176 | tf_op jit(solution)/shard_map/ppermute | solution.py:217
  11.9 2.3 %collective-permute-start.7 = (bf16[3,4,128,128]{3,2,1,0:T(8,128)(2,1)}, bf16[3,4,128,128]{3,2,1,0:T(8,128)(2,1)S(1)}, u32[]{:S(2)}, u32[]{:S(2)}) collective-permute-start(bf16[3,4,128,128]{3,2,1,0:T(8,128)(2,1)} %get-tuple-element.35), channel_id=1, source_target_pairs={{0,2},{1,3},{2,0},{3,1},{4,6},{5,7},{6,4},{7,5},{8,10},{9,11},{10,... | collective-permute-start | bytes 1179656 | tf_op jit(solution)/shard_map/ppermute | solution.py:217
  14.3 4.2 %collective-permute-done.4.refs_2_ = bf16[2,4,128,128]{3,2,1,0:T(8,128)(2,1)S(1)} collective-permute-done((bf16[2,4,128,128]{3,2,1,0:T(8,128)(2,1)}, bf16[2,4,128,128]{3,2,1,0:T(8,128)(2,1)S(1)}, u32[]{:S(2)}, u32[]{:S(2)}) %collective-permute-start.4) | collective-permute-done | bytes 262176 | tf_op jit(solution)/shard_map/ppermute | solution.py:217
  18.4 1.2 %collective-permute-start.8 = (bf16[3,4,128,128]{3,2,1,0:T(8,128)(2,1)}, bf16[3,4,128,128]{3,2,1,0:T(8,128)(2,1)S(1)}, u32[]{:S(2)}, u32[]{:S(2)}) collective-permute-start(bf16[3,4,128,128]{3,2,1,0:T(8,128)(2,1)} %get-tuple-element.36), channel_id=1, source_target_pairs={{0,3},{1,2},{2,1},{3,0},{4,7},{5,6},{6,5},{7,4},{8,11},{9,10},{10,... | collective-permute-start | bytes 1179656 | tf_op jit(solution)/shard_map/ppermute | solution.py:217
  19.6 0.0 collective-permute-done.3.refs_1_
  19.6 0.3 collective-permute-start.10
  19.9 0.0 collective-permute-done.9.refs_1_
  19.9 1.5 %collective-permute-start.11 = (bf16[2,4,128,128]{3,2,1,0:T(8,128)(2,1)}, bf16[2,4,128,128]{3,2,1,0:T(8,128)(2,1)S(1)}, u32[]{:S(2)}, u32[]{:S(2)}) collective-permute-start(bf16[2,4,128,128]{3,2,1,0:T(8,128)(2,1)} %get-tuple-element.40), channel_id=1, source_target_pairs={{0,3},{1,2},{2,1},{3,0},{4,7},{5,6},{6,5},{7,4},{8,11},{9,10},{10,... | collective-permute-start | bytes 786440 | tf_op jit(solution)/shard_map/ppermute | solution.py:217
  21.4 19.5 %collective-permute-done.10.refs_2_ = bf16[2,4,128,128]{3,2,1,0:T(8,128)(2,1)S(1)} collective-permute-done((bf16[2,4,128,128]{3,2,1,0:T(8,128)(2,1)}, bf16[2,4,128,128]{3,2,1,0:T(8,128)(2,1)S(1)}, u32[]{:S(2)}, u32[]{:S(2)}) %collective-permute-start.10) | collective-permute-done | bytes 262176 | tf_op jit(solution)/shard_map/ppermute | solution.py:217
  40.9 0.0 collective-permute-start
  40.9 4.7 %collective-permute-done.11.refs_3_ = bf16[2,4,128,128]{3,2,1,0:T(8,128)(2,1)S(1)} collective-permute-done((bf16[2,4,128,128]{3,2,1,0:T(8,128)(2,1)}, bf16[2,4,128,128]{3,2,1,0:T(8,128)(2,1)S(1)}, u32[]{:S(2)}, u32[]{:S(2)}) %collective-permute-start.11) | collective-permute-done | bytes 262176 | tf_op jit(solution)/shard_map/ppermute | solution.py:217
  45.6 0.0 copy-start.5
  45.6 2.4 %collective-permute-start.1 = (bf16[1,4,128,128]{3,2,1,0:T(8,128)(2,1)}, bf16[1,4,128,128]{3,2,1,0:T(8,128)(2,1)S(1)}, u32[]{:S(2)}, u32[]{:S(2)}) collective-permute-start(bf16[1,4,128,128]{3,2,1,0:T(8,128)(2,1)} %get-tuple-element.28), channel_id=1, source_target_pairs={{0,2},{1,3},{2,0},{3,1},{4,6},{5,7},{6,4},{7,5},{8,10},{9,11},{10,... | collective-permute-start | bytes 393224 | tf_op jit(solution)/shard_map/ppermute | solution.py:217
  48.0 0.0 collective-permute-done.6.refs_1_
  48.0 0.0 collective-permute-start.2
  48.0 0.0 copy-done.3
  48.0 0.0 copy-done.5
  48.0 0.0 copy-start.2
  48.0 0.9 %copy-done.2 = bf16[2,4,128,128]{3,2,1,0:T(8,128)(2,1)S(1)} copy-done((bf16[2,4,128,128]{3,2,1,0:T(8,128)(2,1)S(1)}, bf16[2,4,128,128]{3,2,1,0:T(8,128)(2,1)}, u32[]{:S(2)}) %copy-start.2) | copy-done | bytes 262168
  48.9 2.9 %attend.4.refs_4_ = f32[2,128]{1,0:T(2,128)S(1)} custom-call(s32[4,4]{1,0:T(4,128)S(1)} %copy-done.5, f32[2,8,128]{2,1,0:T(8,128)S(1)} %copy-done.3, bf16[2,4,128,128]{3,2,1,0:T(8,128)(2,1)S(1)} %copy-done.2, bf16[2,4,128,128]{3,2,1,0:T(8,128)(2,1)S(1)} %collective-permute-done.3.refs_1_, bf16[2,4,128,128]{3,2,1,0:T(8,128)(2,1)S(1)} %collective-permute-done.4.refs_2_, ...), custom_call_target="tpu_custom_call" | custom-call | flops 201326592 | bytes 1048576 | tf_op jit(solution)/shard_map/attend/pallas_call | solution.py:194
  51.8 0.0 copy-done.1
  51.8 0.0 copy-start
  51.8 2.9 %attend.6.refs_6_ = f32[2,128]{1,0:T(2,128)S(1)} custom-call(s32[4,4]{1,0:T(4,128)S(1)} %copy-done.5, f32[2,8,128]{2,1,0:T(8,128)S(1)} %copy-done.3, bf16[2,4,128,128]{3,2,1,0:T(8,128)(2,1)S(1)} %copy-done.1, bf16[2,4,128,128]{3,2,1,0:T(8,128)(2,1)S(1)} %collective-permute-done.9.refs_1_, bf16[2,4,128,128]{3,2,1,0:T(8,128)(2,1)S(1)} %collective-permute-done.10.refs_2_, ...), custom_call_target="tpu_custom_call" | custom-call | flops 201326592 | bytes 1048576 | tf_op jit(solution)/shard_map/attend/pallas_call | solution.py:194
  54.7 0.0 collective-permute-done.7.refs_2_
  54.7 0.0 collective-permute-done.8.refs_3_
  54.7 0.0 copy-done
  54.7 0.0 copy-start.4
  54.7 3.6 %attend.5.refs_5_ = f32[3,128]{1,0:T(4,128)S(1)} custom-call(s32[4,4]{1,0:T(4,128)S(1)} %copy-done.5, f32[2,8,128]{2,1,0:T(8,128)S(1)} %copy-done.3, bf16[3,4,128,128]{3,2,1,0:T(8,128)(2,1)S(1)} %copy-done, bf16[3,4,128,128]{3,2,1,0:T(8,128)(2,1)S(1)} %collective-permute-done.6.refs_1_, bf16[3,4,128,128]{3,2,1,0:T(8,128)(2,1)S(1)} %collective-permute-done.7.refs_2_, ...), custom_call_target="tpu_custom_call" | custom-call | flops 301989888 | bytes 1572864 | tf_op jit(solution)/shard_map/attend/pallas_call | solution.py:194
  58.4 0.0 collective-permute-done.refs_1_
  58.4 0.0 collective-permute-done.1.refs_2_
  58.4 0.0 collective-permute-done.2.refs_3_
  58.4 0.0 copy-done.4
  58.4 2.2 %attend.7 = (f32[2,8,32]{2,1,0:T(8,128)S(1)}, f32[2,8,32]{2,1,0:T(8,128)S(1)}, f32[2,8,32]{2,1,0:T(8,128)S(1)}, f32[2,8,32]{2,1,0:T(8,128)S(1)}) custom-call(s32[4,4]{1,0:T(4,128)S(1)} %copy-done.5, f32[2,8,128]{2,1,0:T(8,128)S(1)} %copy-done.3, bf16[1,4,128,128]{3,2,1,0:T(8,128)(2,1)S(1)} %copy-done.4, ...), custom_call_target="tpu_custom_call" | custom-call | flops 100663296 | bytes 524288 | tf_op jit(solution)/shard_map/attend/pallas_call | solution.py:194
  60.5 2.8 %collective-permute-start.12 = (f32[2,8,32]{2,1,0:T(8,128)S(1)}, f32[2,8,32]{2,1,0:T(8,128)S(1)}, u32[]{:S(2)}, u32[]{:S(2)}) collective-permute-start(f32[2,8,32]{2,1,0:T(8,128)S(1)} %get-tuple-element.42), channel_id=1, source_target_pairs={{0,4},{4,0},{8,12},{12,8},{1,5},{5,1},{9,13},{13,9},{2,6},{6,2},{1... | collective-permute-start | bytes 6152 | tf_op jit(solution)/shard_map/ppermute | solution.py:237
  63.3 0.5 collective-permute-start.13
  63.8 2.0 %collective-permute-start.14 = (f32[2,8,32]{2,1,0:T(8,128)S(1)}, f32[2,8,32]{2,1,0:T(8,128)S(1)}, u32[]{:S(2)}, u32[]{:S(2)}) collective-permute-start(f32[2,8,32]{2,1,0:T(8,128)S(1)} %get-tuple-element.44), channel_id=1, source_target_pairs={{0,12},{4,8},{8,4},{12,0},{1,13},{5,9},{9,5},{13,1},{2,14},{6,10},... | collective-permute-start | bytes 6152 | tf_op jit(solution)/shard_map/ppermute | solution.py:237
  65.8 0.0 collective-permute-done.12
  65.8 2.1 %collective-permute-done.13 = f32[2,8,32]{2,1,0:T(8,128)S(1)} collective-permute-done((f32[2,8,32]{2,1,0:T(8,128)S(1)}, f32[2,8,32]{2,1,0:T(8,128)S(1)}, u32[]{:S(2)}, u32[]{:S(2)}) %collective-permute-start.13) | collective-permute-done | bytes 2080 | tf_op jit(solution)/shard_map/ppermute | solution.py:237
  67.9 1.4 %collective-permute-done.14 = f32[2,8,32]{2,1,0:T(8,128)S(1)} collective-permute-done((f32[2,8,32]{2,1,0:T(8,128)S(1)}, f32[2,8,32]{2,1,0:T(8,128)S(1)}, u32[]{:S(2)}, u32[]{:S(2)}) %collective-permute-start.14) | collective-permute-done | bytes 2080 | tf_op jit(solution)/shard_map/ppermute | solution.py:237
  69.2 0.6 add_add_fusion
  (1 shorter events, 0.0 us)
Async XLA Ops:
  2.4 9.5 %collective-permute-start.5 = (bf16[2,4,128,128]{3,2,1,0:T(8,128)(2,1)}, bf16[2,4,128,128]{3,2,1,0:T(8,128)(2,1)S(1)}, u32[]{:S(2)}, u32[]{:S(2)}) collective-permute-start(bf16[2,4,128,128]{3,2,1,0:T(8,128)(2,1)} %get-tuple-element.32), channel_id=1, source_target_pairs={{0,3},{1,2},{2,1},{3,0},{4,7},{5,6},{6,5},{7,4},{8,11},{9,10},{10,... | collective-permute-start | bytes 786440 | tf_op jit(solution)/shard_map/ppermute | solution.py:217
  4.9 13.5 %collective-permute-start.4 = (bf16[2,4,128,128]{3,2,1,0:T(8,128)(2,1)}, bf16[2,4,128,128]{3,2,1,0:T(8,128)(2,1)S(1)}, u32[]{:S(2)}, u32[]{:S(2)}) collective-permute-start(bf16[2,4,128,128]{3,2,1,0:T(8,128)(2,1)} %get-tuple-element.25.refs_4_), channel_id=1, source_target_pairs={{0,2},{1,3},{2,0},{3,1},{4,6},{5,7},{6,4},{7,5},{8,10},{9,11},{10,... | collective-permute-start | bytes 786440 | tf_op jit(solution)/shard_map/ppermute | solution.py:217
  10.0 9.6 %collective-permute-start.3 = (bf16[2,4,128,128]{3,2,1,0:T(8,128)(2,1)}, bf16[2,4,128,128]{3,2,1,0:T(8,128)(2,1)S(1)}, u32[]{:S(2)}, u32[]{:S(2)}) collective-permute-start(bf16[2,4,128,128]{3,2,1,0:T(8,128)(2,1)} %get-tuple-element.31), channel_id=1, source_target_pairs={{0,1},{1,0},{2,3},{3,2},{4,5},{5,4},{6,7},{7,6},{8,9},{9,8},{10,11... | collective-permute-start | bytes 786440 | tf_op jit(solution)/shard_map/ppermute | solution.py:217
  10.1 9.8 %collective-permute-start.9 = (bf16[2,4,128,128]{3,2,1,0:T(8,128)(2,1)}, bf16[2,4,128,128]{3,2,1,0:T(8,128)(2,1)S(1)}, u32[]{:S(2)}, u32[]{:S(2)}) collective-permute-start(bf16[2,4,128,128]{3,2,1,0:T(8,128)(2,1)} %get-tuple-element.38), channel_id=1, source_target_pairs={{0,1},{1,0},{2,3},{3,2},{4,5},{5,4},{6,7},{7,6},{8,9},{9,8},{10,11... | collective-permute-start | bytes 786440 | tf_op jit(solution)/shard_map/ppermute | solution.py:217
  10.6 37.4 %copy-start.3 = (f32[2,8,128]{2,1,0:T(8,128)S(1)}, f32[2,8,128]{2,1,0:T(8,128)}, u32[]{:S(2)}) copy-start(f32[2,8,128]{2,1,0:T(8,128)} %gains.7) | copy-start | bytes 24580
  10.6 37.4 %collective-permute-start.6 = (bf16[3,4,128,128]{3,2,1,0:T(8,128)(2,1)}, bf16[3,4,128,128]{3,2,1,0:T(8,128)(2,1)S(1)}, u32[]{:S(2)}, u32[]{:S(2)}) collective-permute-start(bf16[3,4,128,128]{3,2,1,0:T(8,128)(2,1)} %get-tuple-element.34), channel_id=1, source_target_pairs={{0,1},{1,0},{2,3},{3,2},{4,5},{5,4},{6,7},{7,6},{8,9},{9,8},{10,11... | collective-permute-start | bytes 1179656 | tf_op jit(solution)/shard_map/ppermute | solution.py:217
  11.9 42.8 %collective-permute-start.7 = (bf16[3,4,128,128]{3,2,1,0:T(8,128)(2,1)}, bf16[3,4,128,128]{3,2,1,0:T(8,128)(2,1)S(1)}, u32[]{:S(2)}, u32[]{:S(2)}) collective-permute-start(bf16[3,4,128,128]{3,2,1,0:T(8,128)(2,1)} %get-tuple-element.35), channel_id=1, source_target_pairs={{0,2},{1,3},{2,0},{3,1},{4,6},{5,7},{6,4},{7,5},{8,10},{9,11},{10,... | collective-permute-start | bytes 1179656 | tf_op jit(solution)/shard_map/ppermute | solution.py:217
  18.4 36.3 %collective-permute-start.8 = (bf16[3,4,128,128]{3,2,1,0:T(8,128)(2,1)}, bf16[3,4,128,128]{3,2,1,0:T(8,128)(2,1)S(1)}, u32[]{:S(2)}, u32[]{:S(2)}) collective-permute-start(bf16[3,4,128,128]{3,2,1,0:T(8,128)(2,1)} %get-tuple-element.36), channel_id=1, source_target_pairs={{0,3},{1,2},{2,1},{3,0},{4,7},{5,6},{6,5},{7,4},{8,11},{9,10},{10,... | collective-permute-start | bytes 1179656 | tf_op jit(solution)/shard_map/ppermute | solution.py:217
  19.6 21.3 %collective-permute-start.10 = (bf16[2,4,128,128]{3,2,1,0:T(8,128)(2,1)}, bf16[2,4,128,128]{3,2,1,0:T(8,128)(2,1)S(1)}, u32[]{:S(2)}, u32[]{:S(2)}) collective-permute-start(bf16[2,4,128,128]{3,2,1,0:T(8,128)(2,1)} %get-tuple-element.39), channel_id=1, source_target_pairs={{0,2},{1,3},{2,0},{3,1},{4,6},{5,7},{6,4},{7,5},{8,10},{9,11},{10,... | collective-permute-start | bytes 786440 | tf_op jit(solution)/shard_map/ppermute | solution.py:217
  19.9 25.7 %collective-permute-start.11 = (bf16[2,4,128,128]{3,2,1,0:T(8,128)(2,1)}, bf16[2,4,128,128]{3,2,1,0:T(8,128)(2,1)S(1)}, u32[]{:S(2)}, u32[]{:S(2)}) collective-permute-start(bf16[2,4,128,128]{3,2,1,0:T(8,128)(2,1)} %get-tuple-element.40), channel_id=1, source_target_pairs={{0,3},{1,2},{2,1},{3,0},{4,7},{5,6},{6,5},{7,4},{8,11},{9,10},{10,... | collective-permute-start | bytes 786440 | tf_op jit(solution)/shard_map/ppermute | solution.py:217
  40.9 17.5 %collective-permute-start = (bf16[1,4,128,128]{3,2,1,0:T(8,128)(2,1)}, bf16[1,4,128,128]{3,2,1,0:T(8,128)(2,1)S(1)}, u32[]{:S(2)}, u32[]{:S(2)}) collective-permute-start(bf16[1,4,128,128]{3,2,1,0:T(8,128)(2,1)} %get-tuple-element.27), channel_id=1, source_target_pairs={{0,1},{1,0},{2,3},{3,2},{4,5},{5,4},{6,7},{7,6},{8,9},{9,8},{10,11... | collective-permute-start | bytes 393224 | tf_op jit(solution)/shard_map/ppermute | solution.py:217
  45.6 2.4 %copy-start.5 = (s32[4,4]{1,0:T(4,128)S(1)}, s32[4,4]{1,0:T(4,128)}, u32[]{:S(2)}) copy-start(s32[4,4]{1,0:T(4,128)} %units.7) | copy-start | bytes 196
  45.6 12.8 %collective-permute-start.1 = (bf16[1,4,128,128]{3,2,1,0:T(8,128)(2,1)}, bf16[1,4,128,128]{3,2,1,0:T(8,128)(2,1)S(1)}, u32[]{:S(2)}, u32[]{:S(2)}) collective-permute-start(bf16[1,4,128,128]{3,2,1,0:T(8,128)(2,1)} %get-tuple-element.28), channel_id=1, source_target_pairs={{0,2},{1,3},{2,0},{3,1},{4,6},{5,7},{6,4},{7,5},{8,10},{9,11},{10,... | collective-permute-start | bytes 393224 | tf_op jit(solution)/shard_map/ppermute | solution.py:217
  48.0 10.4 %collective-permute-start.2 = (bf16[1,4,128,128]{3,2,1,0:T(8,128)(2,1)}, bf16[1,4,128,128]{3,2,1,0:T(8,128)(2,1)S(1)}, u32[]{:S(2)}, u32[]{:S(2)}) collective-permute-start(bf16[1,4,128,128]{3,2,1,0:T(8,128)(2,1)} %get-tuple-element.29), channel_id=1, source_target_pairs={{0,3},{1,2},{2,1},{3,0},{4,7},{5,6},{6,5},{7,4},{8,11},{9,10},{10,... | collective-permute-start | bytes 393224 | tf_op jit(solution)/shard_map/ppermute | solution.py:217
  48.0 1.0 %copy-start.2 = (bf16[2,4,128,128]{3,2,1,0:T(8,128)(2,1)S(1)}, bf16[2,4,128,128]{3,2,1,0:T(8,128)(2,1)}, u32[]{:S(2)}) copy-start(bf16[2,4,128,128]{3,2,1,0:T(8,128)(2,1)} %get-tuple-element.30.refs_0_) | copy-start | bytes 786436
  48.9 2.9 %copy-start.1 = (bf16[2,4,128,128]{3,2,1,0:T(8,128)(2,1)S(1)}, bf16[2,4,128,128]{3,2,1,0:T(8,128)(2,1)}, u32[]{:S(2)}) copy-start(bf16[2,4,128,128]{3,2,1,0:T(8,128)(2,1)} %get-tuple-element.37.refs_0_) | copy-start | bytes 786436
  51.8 2.9 %copy-start = (bf16[3,4,128,128]{3,2,1,0:T(8,128)(2,1)S(1)}, bf16[3,4,128,128]{3,2,1,0:T(8,128)(2,1)}, u32[]{:S(2)}) copy-start(bf16[3,4,128,128]{3,2,1,0:T(8,128)(2,1)} %get-tuple-element.33.refs_0_) | copy-start | bytes 1179652
  54.7 3.7 %copy-start.4 = (bf16[1,4,128,128]{3,2,1,0:T(8,128)(2,1)S(1)}, bf16[1,4,128,128]{3,2,1,0:T(8,128)(2,1)}, u32[]{:S(2)}) copy-start(bf16[1,4,128,128]{3,2,1,0:T(8,128)(2,1)} %get-tuple-element.26.refs_0_) | copy-start | bytes 393220
  60.5 5.2 %collective-permute-start.12 = (f32[2,8,32]{2,1,0:T(8,128)S(1)}, f32[2,8,32]{2,1,0:T(8,128)S(1)}, u32[]{:S(2)}, u32[]{:S(2)}) collective-permute-start(f32[2,8,32]{2,1,0:T(8,128)S(1)} %get-tuple-element.42), channel_id=1, source_target_pairs={{0,4},{4,0},{8,12},{12,8},{1,5},{5,1},{9,13},{13,9},{2,6},{6,2},{1... | collective-permute-start | bytes 6152 | tf_op jit(solution)/shard_map/ppermute | solution.py:237
  63.3 4.5 %collective-permute-start.13 = (f32[2,8,32]{2,1,0:T(8,128)S(1)}, f32[2,8,32]{2,1,0:T(8,128)S(1)}, u32[]{:S(2)}, u32[]{:S(2)}) collective-permute-start(f32[2,8,32]{2,1,0:T(8,128)S(1)} %get-tuple-element.43), channel_id=1, source_target_pairs={{0,8},{4,12},{8,0},{12,4},{1,9},{5,13},{9,1},{13,5},{2,10},{6,14},... | collective-permute-start | bytes 6152 | tf_op jit(solution)/shard_map/ppermute | solution.py:237
  63.8 5.4 %collective-permute-start.14 = (f32[2,8,32]{2,1,0:T(8,128)S(1)}, f32[2,8,32]{2,1,0:T(8,128)S(1)}, u32[]{:S(2)}, u32[]{:S(2)}) collective-permute-start(f32[2,8,32]{2,1,0:T(8,128)S(1)} %get-tuple-element.44), channel_id=1, source_target_pairs={{0,12},{4,8},{8,4},{12,0},{1,13},{5,9},{9,5},{13,1},{2,14},{6,10},... | collective-permute-start | bytes 6152 | tf_op jit(solution)/shard_map/ppermute | solution.py:237

commit v3 on v2

--- a/solution.py
+++ b/solution.py
@@ -16,7 +16,7 @@
 
 
 def head_chunks(heads):
-    sizes = {8: (2, 3, 2, 1)}.get(heads)
+    sizes = {8: (3, 2, 2, 1)}.get(heads)
     if sizes is None:
         sizes = (1,) * heads if heads <= 2 else (heads - heads // 2, heads // 2)
     bounds, start = [], 0
@@ -29,7 +29,8 @@
 def pack_kernel(plan, heads, after, *refs):
     arrays = refs[:4]
     outs = refs[4 + after : 4 + after + sum(len(chunks) for _, chunks in plan)]
-    raw, wide, sems = refs[4 + after + len(outs) :]
+    token, raw, wide, sems = refs[4 + after + len(outs) :]
+    token[...] = jnp.zeros_like(token)
     me = lax.axis_index("seq")
     slots, rows = raw.shape[2], raw.shape[3]
     spans = max(1, heads // TILE)
@@ -76,7 +77,7 @@
         jax.ShapeDtypeStruct((high - low, 4, slots * rows, size), jnp.bfloat16)
         for _, chunks in plan
         for low, high in chunks
-    ]
+    ] + [jax.ShapeDtypeStruct((TILE, size), jnp.float32)]
     count = len(plan)
     moved = count * 4 * spans * slots * rows * TILE * size * 2
     return pl.pallas_call(
@@ -99,71 +100,108 @@
     return lax.dot_general(left, right, (((1,), (1,)), ((), ())), preferred_element_type=jnp.float32)
 
 
-def attention_chunk(low, units, gains, pieces, held, total):
+def layouts(slots):
+    found = []
+
+    def extend(start, clips):
+        if start == slots:
+            found.append(tuple(clips))
+        for span in range(1, min(MAXCLIP, slots - start) + 1):
+            extend(start + span, clips + [(start, span)])
+
+    extend(0, [])
+    return found
+
+
+def normalized(block, gain):
+    wide = block.astype(jnp.float32)
+    wide = wide * lax.rsqrt(jnp.mean(wide * wide, axis=-1, keepdims=True) + EPS)
+    return (wide * gain).astype(jnp.bfloat16)
+
+
+def prepare_kernel(low, after, gains, *refs):
+    pieces, out = refs[after:-1], refs[-1]
+    heads, _, tokens, _ = pieces[0].shape
+    slots = out.shape[2]
+    rows = tokens // slots
+
+    for head in range(heads):
+        for array in range(4):
+            for source, piece in enumerate(pieces):
+                block = piece[head, array]
+                if array < 2:
+                    block = normalized(block, gains[array, low + head : low + head + 1, :])
+                for slot in range(slots):
+                    out[head, array, slot, source * rows : (source + 1) * rows, :] = block[
+                        slot * rows : (slot + 1) * rows
+                    ]
+
+
+def prepare(low, gains, pieces, slots, after):
+    heads, _, tokens, size = pieces[0].shape
+    moved = len(pieces) * heads * 4 * tokens * size * 2
+    return pl.pallas_call(
+        functools.partial(prepare_kernel, low, len(after)),
+        out_shape=jax.ShapeDtypeStruct((heads, 4, slots, len(pieces) * tokens // slots, size), jnp.bfloat16),
+        in_specs=[pl.BlockSpec(memory_space=pltpu.VMEM)] * (1 + len(after) + len(pieces)),
+        out_specs=pl.BlockSpec(memory_space=pltpu.VMEM),
+        compiler_params=pltpu.CompilerParams(vmem_limit_bytes=VMEM_LIMIT),
+        cost_estimate=pl.CostEstimate(flops=1, bytes_accessed=1, transcendentals=0),
+        name="prepare",
+    )(gains, *after, *pieces)
+
+
+def attention_chunk(low, count, units, gains, close, pieces, held, total):
     query, key, value, grad = held
     group = lax.axis_index("dp")
-    count, _, tokens, size = pieces[0].shape
-    slots = units.shape[1]
+    _, _, tokens, size = pieces[0].shape
+    slots, near = close.shape[2:4]
     rows = tokens // slots
-    unit = rows * len(pieces)
+    unit = near + rows * len(pieces)
     for head in range(count):
-        for array, kept in ((0, query), (1, key)):
-            gain = gains[array, low + head : low + head + 1, :]
+        for array, kept in enumerate(held):
+            for slot in range(slots):
+                kept[head, slot * unit : slot * unit + near, :] = close[head, array, slot]
             for source, piece in enumerate(pieces):
-                wide = piece[head, array].astype(jnp.float32)
-                normed = wide * lax.rsqrt(jnp.mean(wide * wide, axis=-1, keepdims=True) + EPS)
-                normed = (normed * gain).astype(jnp.bfloat16)
+                block = piece[head, array]
+                if array < 2:
+                    block = normalized(block, gains[array, low + head : low + head + 1, :])
                 for slot in range(slots):
-                    kept[head, slot * unit + source * rows : slot * unit + (source + 1) * rows, :] = normed[
-                        slot * rows : (slot + 1) * rows
-                    ]
-        for array, kept in ((2, value), (3, grad)):
-            for source, piece in enumerate(pieces):
-                for slot in range(slots):
-                    kept[head, slot * unit + source * rows : slot * unit + (source + 1) * rows, :] = piece[
-                        head, array, slot * rows : (slot + 1) * rows, :
-                    ]
-    total[...] = jnp.zeros_like(total)
+                    start = slot * unit + near + source * rows
+                    kept[head, start : start + rows, :] = block[slot * rows : (slot + 1) * rows]
     factor = size ** (-0.5) * math.log2(math.e)
 
-    def clip(slot, span):
-        length = span * unit
-        start = pl.multiple_of(slot * unit, unit)
-        for head in range(count):
-            q = query[head, pl.ds(start, length), :]
-            k = key[head, pl.ds(start, length), :]
-            expo = jnp.exp2(contract_last(k, q) * factor)
-            dprob = contract_last(value[head, pl.ds(start, length), :], grad[head, pl.ds(start, length), :])
-            prob = expo * (1.0 / jnp.sum(expo, axis=0, keepdims=True))
-            delta = jnp.sum(prob * dprob, axis=0, keepdims=True)
-            dscore = (prob * (dprob - delta)).astype(jnp.bfloat16)
-            mixed = jnp.dot(dscore, q, preferred_element_type=jnp.float32)
-            total[head : head + 1, :] += jnp.sum(mixed * k.astype(jnp.float32), axis=0, keepdims=True)
-
-    def at_slot(slot, carry):
-        span_here = units[group, slot]
-        for span in range(1, min(MAXCLIP, slots) + 1):
-
-            @pl.when(jnp.logical_and(span_here == span, slot + span <= slots))
-            def _():
-                clip(slot, span)
-
-        return carry
-
-    lax.fori_loop(0, slots, at_slot, 0)
-
-
-def chunk_kernel(low, sources, units, gains, *refs):
-    pieces, out, held = refs[:sources], refs[sources], refs[sources + 1 :]
-    attention_chunk(low, units, gains, pieces, held, out)
-
-
-def last_kernel(low, sources, earlier, peers, units, gains, *refs):
+    def clip(head, slot, span):
+        where = slice(slot * unit, (slot + span) * unit)
+        q, k = query[head, where, :], key[head, where, :]
+        expo = jnp.exp2(contract_last(k, q) * factor)
+        dprob = contract_last(value[head, where, :], grad[head, where, :])
+        prob = expo * (1.0 / jnp.sum(expo, axis=0, keepdims=True))
+        delta = jnp.sum(prob * dprob, axis=0, keepdims=True)
+        dscore = (prob * (dprob - delta)).astype(jnp.bfloat16)
+        mixed = jnp.dot(dscore, q, preferred_element_type=jnp.float32)
+        return jnp.sum(mixed * k.astype(jnp.float32), axis=0, keepdims=True)
+
+    begins = sum(jnp.where(units[group, slot] > 0, 1 << slot, 0) for slot in range(slots))
+    for layout in layouts(slots):
+
+        @pl.when(begins == sum(1 << slot for slot, _ in layout))
+        def _():
+            for head in range(count):
+                total[head : head + 1, :] = sum(clip(head, slot, span) for slot, span in layout)
+
+
+def chunk_kernel(low, units, gains, close, *refs):
+    pieces, out, held = refs[:-5], refs[-5], refs[-4:]
+    attention_chunk(low, out.shape[0], units, gains, close, pieces, held, out)
+
+
+def last_kernel(low, sources, earlier, peers, units, gains, close, *refs):
     pieces = refs[:sources]
     before = refs[sources : sources + earlier]
     outs = refs[sources + earlier : sources + earlier + len(peers)]
     held, total = refs[sources + earlier + len(peers) : -1], refs[-1]
-    attention_chunk(low, units, gains, pieces, held, total)
+    attention_chunk(low, total.shape[0], units, gains, close, pieces, held, total)
     group = lax.axis_index("dp")
     size = total.shape[-1]
     width = outs[0].shape[-1]
@@ -175,12 +213,12 @@
             out[side] = pltpu.roll(grads, shift, 1)[:, :width]
 
 
-def attend(low, units, gains, pieces, earlier=None, peers=None):
-    count, _, tokens, size = pieces[0].shape
-    all_tokens = tokens * len(pieces)
+def attend(low, count, units, gains, close, pieces, earlier=None, peers=None):
+    _, _, tokens, size = pieces[0].shape
+    all_tokens = close.shape[2] * close.shape[3] + tokens * len(pieces)
     held = [pltpu.VMEM((count, all_tokens, size), jnp.bfloat16)] * 4
     if earlier is None:
-        kernel = functools.partial(chunk_kernel, low, len(pieces))
+        kernel = functools.partial(chunk_kernel, low)
         shapes = jax.ShapeDtypeStruct((count, size), jnp.float32)
         earlier = []
         outs = pl.BlockSpec(memory_space=pltpu.VMEM)
@@ -195,7 +233,7 @@
         kernel,
         out_shape=shapes,
         in_specs=[pl.BlockSpec(memory_space=pltpu.SMEM)]
-        + [pl.BlockSpec(memory_space=pltpu.VMEM)] * (1 + len(pieces) + len(earlier)),
+        + [pl.BlockSpec(memory_space=pltpu.VMEM)] * (2 + len(pieces) + len(earlier)),
         out_specs=outs,
         scratch_shapes=held,
         compiler_params=pltpu.CompilerParams(vmem_limit_bytes=VMEM_LIMIT),
@@ -203,7 +241,23 @@
             flops=6 * pairs * size, bytes_accessed=len(pieces) * count * 4 * tokens * size * 2, transcendentals=pairs
         ),
         name="attend",
-    )(units, gains, *pieces, *earlier)
+    )(units, gains, close, *pieces, *earlier)
+
+
+def seen_kernel(*refs):
+    refs[-1][...] = jnp.zeros_like(refs[-1])
+
+
+def seen(blocks):
+    return pl.pallas_call(
+        seen_kernel,
+        out_shape=jax.ShapeDtypeStruct((TILE, blocks[0].shape[-1]), jnp.float32),
+        in_specs=[pl.BlockSpec(memory_space=pl.ANY)] * len(blocks),
+        out_specs=pl.BlockSpec(memory_space=pltpu.VMEM),
+        compiler_params=pltpu.CompilerParams(vmem_limit_bytes=1024 * 1024),
+        cost_estimate=pl.CostEstimate(flops=1, bytes_accessed=1024 * 1024, transcendentals=0),
+        name="seen",
+    )(*blocks)
 
 
 def body(sequence, groups, queries, key_rows, value_rows, out_grad, norm_gains, clip_units):
@@ -216,22 +270,31 @@
     def send(block, flip):
         return lax.ppermute(block, "seq", [(s, s ^ flip) for s in range(sequence)])
 
-    held = [{} for _ in chunks]
-    first = pack(arrays, [(flip, chunks[:1]) for flip in far], heads)
-    for flip, block in zip(far, first):
-        held[0][flip] = send(block, flip)
-    plan = [(flip, chunks[1:]) for flip in far] + [(flip, chunks) for flip in near] + [(0, chunks)]
-    blocks = iter(pack(arrays, plan, heads, first[:1]))
-    for flip, wanted in plan:
-        for bounds in wanted:
-            block = next(blocks)
-            held[chunks.index(bounds)][flip] = send(block, flip) if flip else block
-    sums = []
-    for number, (low, _) in enumerate(chunks[:-1]):
-        pieces = [held[number][flip] for flip in range(sequence)]
-        sums.append(attend(low, clip_units, norm_gains, pieces))
-    pieces = [held[-1][flip] for flip in range(sequence)]
-    parts = attend(chunks[-1][0], clip_units, norm_gains, pieces, sums, list(range(groups)))
+    slots = clip_units.shape[1]
+    close = near + [0]
+
+    def pack_and_send(number, after):
+        plan = [(flip, [chunks[number]]) for flip in far]
+        if number == 1:
+            plan += [(flip, chunks) for flip in close]
+        *blocks, token = pack(arrays, plan, heads, after)
+        received.append([send(block, flip) for flip, block in zip(far, blocks)])
+        return blocks[len(far) :], token
+
+    received, sums = [], []
+    _, token = pack_and_send(0, [])
+    rest, _ = pack_and_send(1, [token])
+    for number, (low, high) in enumerate(chunks):
+        if 0 < number < len(chunks) - 1:
+            pack_and_send(number + 1, sums[number - 1 :])
+        pieces = [
+            send(block, flip) if flip else block for flip, block in zip(close, rest[number :: len(chunks)])
+        ]
+        after = [seen(received[0])] if number == 0 else []
+        prepared = prepare(low, norm_gains, pieces, slots, after)
+        if number + 1 < len(chunks):
+            sums.append(attend(low, high - low, clip_units, norm_gains, prepared, received[number]))
+    parts = attend(low, high - low, clip_units, norm_gains, prepared, received[-1], sums, list(range(groups)))
     result = parts[0]
     for flip in range(1, groups):
         result = result + lax.ppermute(parts[flip], "dp", [(g, g ^ flip) for g in range(groups)])

time: 70.5 us -> 62.4 us (0.89)
  waiting for transfers between devices: 33.1 us -> 22.6 us
  Pallas kernels: 18.4 us -> 21.6 us
  starting transfers between devices: 16.6 us -> 14.1 us
  local copies, waits for them, and re-layouts: 0.96 us -> 3.18 us
    ppermute x12, waiting for transfers between devices: 29.6 us -> 18.7 us  [send(): return lax.ppermute(block, 'seq', [(s, s ^ flip) for s in range(sequence)])]
    pallas_call x2 -> x4, Pallas kernels: 6.91 us -> 11.5 us  [pack(): pl.pallas_call(functools.partial(pack_kernel, plan, heads, len(after)), o...]
    pallas_call x4, Pallas kernels: 11.5 us -> 9.12 us  [attend(): pl.pallas_call(kernel, out_shape=shapes, in_specs=[pl.BlockSpec(memory_sp...]
    unnamed x12 -> x22, local copies, waits for them, and re-layouts: 0.96 us -> 3.18 us
    ppermute x12, starting transfers between devices: 11.4 us -> 9.42 us  [send(): return lax.ppermute(block, 'seq', [(s, s ^ flip) for s in range(sequence)])]
    pallas_call x0 -> x5, Pallas kernels: none -> 0.9 us  [the longest x4 0.9 us: prepare(): pl.pallas_call(functools.partial(prepare_kernel, low, len(after)), out_sh...]
  transfers between devices with their start and end apart: 15 -> 15, of which waited for: 6 -> 7; matrix products, arithmetic and copies ran while one was open for 0% -> 0% of each run, Pallas kernels for 20% -> 28%
where the time goes in v3:
time: 62.4 us; the launch traced here: 62.1 us
  waiting for transfers between devices  22.6 us (36%)
  Pallas kernels  21.6 us (35%)
  starting transfers between devices  14.1 us (23%)
  local copies, waits for them, and re-layouts  3.18 us (5%)
    ppermute x12, waiting for transfers between devices, send(): return lax.ppermute(block, 'seq', [(s, s ^ flip) for s in range(sequence)])  18.7 us
    pallas_call x4, Pallas kernels, pack(): pl.pallas_call(functools.partial(pack_kernel, plan, heads, len(after)), o...  11.5 us
    ppermute x12, starting transfers between devices, send(): return lax.ppermute(block, 'seq', [(s, s ^ flip) for s in range(sequence)])  9.42 us
    pallas_call x4, Pallas kernels, attend(): pl.pallas_call(kernel, out_shape=shapes, in_specs=[pl.BlockSpec(memory_sp...  9.12 us
    ppermute x3, starting transfers between devices, body(): lax.ppermute(parts[flip], 'dp', [(g, g ^ flip) for g in range(groups)])  4.65 us
    ppermute x3, waiting for transfers between devices, body(): lax.ppermute(parts[flip], 'dp', [(g, g ^ flip) for g in range(groups)])  3.91 us
    unnamed x22, local copies, waits for them, and re-layouts  3.18 us
  transfers between devices with their start and end apart: 15, of which 7 were waited for; matrix products, arithmetic and copies ran while one was open for 0% of the time, Pallas kernels for 28%

profile of v3, /device:TPU:0, one launch (start us, length us, event | category | flops | bytes accessed | tf_op | source)
XLA Modules:
  0.0 62.1 jit_solution(10252742838324124276)
XLA Ops:
  0.0 2.5 %pack.4 = (bf16[3,4,128,128]{3,2,1,0:T(8,128)(2,1)}, bf16[3,4,128,128]{3,2,1,0:T(8,128)(2,1)}, f32[8,128]{1,0:T(8,128)}) custom-call(bf16[1,4,32,32,128]{4,3,2,1,0:T(8,128)(2,1)} %refs_0_.7, bf16[1,4,32,32,128]{4,3,2,1,0:T(8,128)(2,1)} %refs_1_.7, bf16[1,4,32,32,128]{4,3,2,1,0:T(8,128)(2,1)} %refs_2_.7, bf16[1,4,32,32,128]{4,3,2,1,0:T(8,128)(2,1)} %refs_3_.7), custom_call_target="tpu_custom_call" | custom-call | flops 2097152 | bytes 4194304 | tf_op jit(solution)/shard_map/pack/pallas_call | solution.py:83
  2.5 3.0 %collective-permute-start.6 = (bf16[3,4,128,128]{3,2,1,0:T(8,128)(2,1)}, bf16[3,4,128,128]{3,2,1,0:T(8,128)(2,1)S(1)}, u32[]{:S(2)}, u32[]{:S(2)}) collective-permute-start(bf16[3,4,128,128]{3,2,1,0:T(8,128)(2,1)} %get-tuple-element.35), channel_id=1, source_target_pairs={{0,2},{1,3},{2,0},{3,1},{4,6},{5,7},{6,4},{7,5},{8,10},{9,11},{10,... | collective-permute-start | bytes 1179656 | tf_op jit(solution)/shard_map/ppermute | solution.py:271
  5.5 0.0 collective-permute-start.7
  5.5 4.1 %pack.5 = (bf16[2,4,128,128]{3,2,1,0:T(8,128)(2,1)}, bf16[2,4,128,128]{3,2,1,0:T(8,128)(2,1)}, bf16[3,4,128,128]{3,2,1,0:T(8,128)(2,1)}, bf16[2,4,128,128]{3,2,1...) custom-call(bf16[1,4,32,32,128]{4,3,2,1,0:T(8,128)(2,1)} %refs_0_.7,, ...), custom_call_target="tpu_custom_call" | custom-call | flops 4194304 | bytes 8388608 | tf_op jit(solution)/shard_map/pack/pallas_call | solution.py:83
  9.7 0.3 collective-permute-start.8
  9.9 0.3 collective-permute-start.1
  10.2 1.7 %collective-permute-start.2 = (bf16[2,4,128,128]{3,2,1,0:T(8,128)(2,1)}, bf16[2,4,128,128]{3,2,1,0:T(8,128)(2,1)S(1)}, u32[]{:S(2)}, u32[]{:S(2)}) collective-permute-start(bf16[2,4,128,128]{3,2,1,0:T(8,128)(2,1)} %get-tuple-element.31), channel_id=1, source_target_pairs={{0,2},{1,3},{2,0},{3,1},{4,6},{5,7},{6,4},{7,5},{8,10},{9,11},{10,... | collective-permute-start | bytes 786440 | tf_op jit(solution)/shard_map/ppermute | solution.py:271
  11.9 3.8 %collective-permute-done.6.refs_0_ = bf16[3,4,128,128]{3,2,1,0:T(8,128)(2,1)S(1)} collective-permute-done((bf16[3,4,128,128]{3,2,1,0:T(8,128)(2,1)}, bf16[3,4,128,128]{3,2,1,0:T(8,128)(2,1)S(1)}, u32[]{:S(2)}, u32[]{:S(2)}) %collective-permute-start.6) | collective-permute-done | bytes 393248 | tf_op jit(solution)/shard_map/ppermute | solution.py:271
  15.7 0.0 collective-permute-start.3
  15.7 8.1 %collective-permute-done.7.refs_1_ = bf16[3,4,128,128]{3,2,1,0:T(8,128)(2,1)S(1)} collective-permute-done((bf16[3,4,128,128]{3,2,1,0:T(8,128)(2,1)}, bf16[3,4,128,128]{3,2,1,0:T(8,128)(2,1)S(1)}, u32[]{:S(2)}, u32[]{:S(2)}) %collective-permute-start.7) | collective-permute-done | bytes 393248 | tf_op jit(solution)/shard_map/ppermute | solution.py:271
  23.8 0.1 collective-permute-start.9
  24.0 0.0 collective-permute-done.8.refs_1_
  24.0 0.5 copy-done
  24.5 0.3 copy-done.1
  24.8 0.3 prepare.6.close
  25.1 0.4 copy-done.5
  25.5 3.0 %attend.5.refs_4_.refs_2_ = f32[3,128]{1,0:T(4,128)S(1)} custom-call(s32[4,4]{1,0:T(4,128)S(1)} %copy-done.5, f32[2,8,128]{2,1,0:T(8,128)S(1)} %copy-done, bf16[3,4,4,64,128]{4,3,2,1,0:T(8,128)(2,1)S(1)} %prepare.6.close, bf16[3,4,128,128]{3,2,1,0:T(8,128)(2,1)S(1)} %collective-permute-done.6.refs_0_, bf16[3,4,128,128]{3,2,1,0:T(8,128)(2,1)S(1)} %collective-permute-done.7.refs_1_), custom_call_target="tpu_custom_call" | custom-call | flops 301989888 | bytes 786432 | tf_op jit(solution)/shard_map/attend/pallas_call | solution.py:232
  28.5 0.6 copy-done.6
  29.1 2.5 %pack.7 = (bf16[2,4,128,128]{3,2,1,0:T(8,128)(2,1)}, bf16[2,4,128,128]{3,2,1,0:T(8,128)(2,1)}, f32[8,128]{1,0:T(8,128)}) custom-call(bf16[1,4,32,32,128]{4,3,2,1,0:T(8,128)(2,1)} %refs_0_.7, bf16[1,4,32,32,128]{4,3,2,1,0:T(8,128)(2,1)} %refs_1_.7, bf16[1,4,32,32,128]{4,3,2,1,0:T(8,128)(2,1)} %refs_2_.7, bf16[1,4,32,32,128]{4,3,2,1,0:T(8,128)(2,1)} %refs_3_.7, ...), custom_call_target="tpu_custom_call" | custom-call | flops 2097152 | bytes 4194304 | tf_op jit(solution)/shard_map/pack/pallas_call | solution.py:83
  31.6 1.3 %collective-permute-start.10 = (bf16[2,4,128,128]{3,2,1,0:T(8,128)(2,1)}, bf16[2,4,128,128]{3,2,1,0:T(8,128)(2,1)S(1)}, u32[]{:S(2)}, u32[]{:S(2)}) collective-permute-start(bf16[2,4,128,128]{3,2,1,0:T(8,128)(2,1)} %get-tuple-element.41), channel_id=1, source_target_pairs={{0,2},{1,3},{2,0},{3,1},{4,6},{5,7},{6,4},{7,5},{8,10},{9,11},{10,... | collective-permute-start | bytes 786440 | tf_op jit(solution)/shard_map/ppermute | solution.py:271
  32.9 0.0 collective-permute-done.1.refs_0_
  32.9 0.7 %collective-permute-start.11 = (bf16[2,4,128,128]{3,2,1,0:T(8,128)(2,1)}, bf16[2,4,128,128]{3,2,1,0:T(8,128)(2,1)S(1)}, u32[]{:S(2)}, u32[]{:S(2)}) collective-permute-start(bf16[2,4,128,128]{3,2,1,0:T(8,128)(2,1)} %get-tuple-element.42), channel_id=1, source_target_pairs={{0,3},{1,2},{2,1},{3,0},{4,7},{5,6},{6,5},{7,4},{8,11},{9,10},{10,... | collective-permute-start | bytes 786440 | tf_op jit(solution)/shard_map/ppermute | solution.py:271
  33.6 0.0 collective-permute-done.2.refs_0_
  33.6 0.2 collective-permute-start
  33.8 0.2 prepare.5.close
  34.0 0.0 collective-permute-done.3.refs_1_
  34.1 2.2 %attend.4.refs_4_.refs_3_ = f32[2,128]{1,0:T(2,128)S(1)} custom-call(s32[4,4]{1,0:T(4,128)S(1)} %copy-done.5, f32[2,8,128]{2,1,0:T(8,128)S(1)} %copy-done, bf16[2,4,4,64,128]{4,3,2,1,0:T(8,128)(2,1)S(1)} %prepare.5.close, bf16[2,4,128,128]{3,2,1,0:T(8,128)(2,1)S(1)} %collective-permute-done.2.refs_0_, bf16[2,4,128,128]{3,2,1,0:T(8,128)(2,1)S(1)} %collective-permute-done.3.refs_1_), custom_call_target="tpu_custom_call" | custom-call | flops 201326592 | bytes 524288 | tf_op jit(solution)/shard_map/attend/pallas_call | solution.py:232
  36.2 0.5 copy-done.8
  36.8 2.4 %pack.6 = (bf16[1,4,128,128]{3,2,1,0:T(8,128)(2,1)}, bf16[1,4,128,128]{3,2,1,0:T(8,128)(2,1)}, f32[8,128]{1,0:T(8,128)}) custom-call(bf16[1,4,32,32,128]{4,3,2,1,0:T(8,128)(2,1)} %refs_0_.7, bf16[1,4,32,32,128]{4,3,2,1,0:T(8,128)(2,1)} %refs_1_.7, bf16[1,4,32,32,128]{4,3,2,1,0:T(8,128)(2,1)} %refs_2_.7, bf16[1,4,32,32,128]{4,3,2,1,0:T(8,128)(2,1)} %refs_3_.7, ...), custom_call_target="tpu_custom_call" | custom-call | flops 2097152 | bytes 4194304 | tf_op jit(solution)/shard_map/pack/pallas_call | solution.py:83
  39.2 1.5 %collective-permute-start.4 = (bf16[1,4,128,128]{3,2,1,0:T(8,128)(2,1)}, bf16[1,4,128,128]{3,2,1,0:T(8,128)(2,1)S(1)}, u32[]{:S(2)}, u32[]{:S(2)}) collective-permute-start(bf16[1,4,128,128]{3,2,1,0:T(8,128)(2,1)} %get-tuple-element.33), channel_id=1, source_target_pairs={{0,2},{1,3},{2,0},{3,1},{4,6},{5,7},{6,4},{7,5},{8,10},{9,11},{10,... | collective-permute-start | bytes 393224 | tf_op jit(solution)/shard_map/ppermute | solution.py:271
  40.7 0.0 collective-permute-done.refs_0_
  40.7 0.3 collective-permute-start.5
  41.0 0.2 prepare.4.close
  41.1 0.0 collective-permute-done.9.refs_0_
  41.1 0.8 %copy-done.2 = bf16[2,4,128,128]{3,2,1,0:T(8,128)(2,1)S(1)} copy-done((bf16[2,4,128,128]{3,2,1,0:T(8,128)(2,1)S(1)}, bf16[2,4,128,128]{3,2,1,0:T(8,128)(2,1)}, u32[]{:S(2)}) %copy-start.2) | copy-done | bytes 262168
  41.9 0.2 prepare.7.close
  42.2 0.0 collective-permute-done.10.refs_0_
  42.2 3.6 %collective-permute-done.11.refs_1_ = bf16[2,4,128,128]{3,2,1,0:T(8,128)(2,1)S(1)} collective-permute-done((bf16[2,4,128,128]{3,2,1,0:T(8,128)(2,1)}, bf16[2,4,128,128]{3,2,1,0:T(8,128)(2,1)S(1)}, u32[]{:S(2)}, u32[]{:S(2)}) %collective-permute-start.11) | collective-permute-done | bytes 262176 | tf_op jit(solution)/shard_map/ppermute | solution.py:271
  45.7 2.4 %attend.6.refs_4_ = f32[2,128]{1,0:T(2,128)S(1)} custom-call(s32[4,4]{1,0:T(4,128)S(1)} %copy-done.5, f32[2,8,128]{2,1,0:T(8,128)S(1)} %copy-done, bf16[2,4,4,64,128]{4,3,2,1,0:T(8,128)(2,1)S(1)} %prepare.7.close, bf16[2,4,128,128]{3,2,1,0:T(8,128)(2,1)S(1)} %collective-permute-done.10.refs_0_, bf16[2,4,128,128]{3,2,1,0:T(8,128)(2,1)S(1)} %collective-permute-done.11.refs_1_), custom_call_target="tpu_custom_call" | custom-call | flops 201326592 | bytes 524288 | tf_op jit(solution)/shard_map/attend/pallas_call | solution.py:232
  48.1 1.3 %collective-permute-done.4.refs_0_ = bf16[1,4,128,128]{3,2,1,0:T(8,128)(2,1)S(1)} collective-permute-done((bf16[1,4,128,128]{3,2,1,0:T(8,128)(2,1)}, bf16[1,4,128,128]{3,2,1,0:T(8,128)(2,1)S(1)}, u32[]{:S(2)}, u32[]{:S(2)}) %collective-permute-start.4) | collective-permute-done | bytes 131104 | tf_op jit(solution)/shard_map/ppermute | solution.py:271
  49.4 1.9 %collective-permute-done.5.refs_1_ = bf16[1,4,128,128]{3,2,1,0:T(8,128)(2,1)S(1)} collective-permute-done((bf16[1,4,128,128]{3,2,1,0:T(8,128)(2,1)}, bf16[1,4,128,128]{3,2,1,0:T(8,128)(2,1)S(1)}, u32[]{:S(2)}, u32[]{:S(2)}) %collective-permute-start.5) | collective-permute-done | bytes 131104 | tf_op jit(solution)/shard_map/ppermute | solution.py:271
  51.4 1.6 %attend.7 = (f32[2,8,32]{2,1,0:T(8,128)S(1)}, f32[2,8,32]{2,1,0:T(8,128)S(1)}, f32[2,8,32]{2,1,0:T(8,128)S(1)}, f32[2,8,32]{2,1,0:T(8,128)S(1)}) custom-call(s32[4,4]{1,0:T(4,128)S(1)} %copy-done.5, f32[2,8,128]{2,1,0:T(8,128)S(1)} %copy-done, bf16[1,4,4,64,128]{4,3,2,1,0:T(8,128)(2,1)S(1)} %prepare.4.close, ...), custom_call_target="tpu_custom_call" | custom-call | flops 100663296 | bytes 262144 | tf_op jit(solution)/shard_map/attend/pallas_call | solution.py:232
  53.0 4.0 %collective-permute-start.14 = (f32[2,8,32]{2,1,0:T(8,128)S(1)}, f32[2,8,32]{2,1,0:T(8,128)S(1)}, u32[]{:S(2)}, u32[]{:S(2)}) collective-permute-start(f32[2,8,32]{2,1,0:T(8,128)S(1)} %get-tuple-element.46), channel_id=1, source_target_pairs={{0,12},{4,8},{8,4},{12,0},{1,13},{5,9},{9,5},{13,1},{2,14},{6,10},... | collective-permute-start | bytes 6152 | tf_op jit(solution)/shard_map/ppermute | solution.py:300
  57.0 0.6 %collective-permute-start.12 = (f32[2,8,32]{2,1,0:T(8,128)S(1)}, f32[2,8,32]{2,1,0:T(8,128)S(1)}, u32[]{:S(2)}, u32[]{:S(2)}) collective-permute-start(f32[2,8,32]{2,1,0:T(8,128)S(1)} %get-tuple-element.44), channel_id=1, source_target_pairs={{0,4},{4,0},{8,12},{12,8},{1,5},{5,1},{9,13},{13,9},{2,6},{6,2},{1... | collective-permute-start | bytes 6152 | tf_op jit(solution)/shard_map/ppermute | solution.py:300
  57.6 1.0 %collective-permute-done.14 = f32[2,8,32]{2,1,0:T(8,128)S(1)} collective-permute-done((f32[2,8,32]{2,1,0:T(8,128)S(1)}, f32[2,8,32]{2,1,0:T(8,128)S(1)}, u32[]{:S(2)}, u32[]{:S(2)}) %collective-permute-start.14) | collective-permute-done | bytes 2080 | tf_op jit(solution)/shard_map/ppermute | solution.py:300
  58.6 2.9 %collective-permute-done.13 = f32[2,8,32]{2,1,0:T(8,128)S(1)} collective-permute-done((f32[2,8,32]{2,1,0:T(8,128)S(1)}, f32[2,8,32]{2,1,0:T(8,128)S(1)}, u32[]{:S(2)}, u32[]{:S(2)}) %collective-permute-start.13) | collective-permute-done | bytes 2080 | tf_op jit(solution)/shard_map/ppermute | solution.py:300
  61.5 0.0 collective-permute-done.12
  61.5 0.6 add_add_fusion
  (18 shorter events, 0.0 us)
Async XLA Ops:
  2.5 13.2 %collective-permute-start.6 = (bf16[3,4,128,128]{3,2,1,0:T(8,128)(2,1)}, bf16[3,4,128,128]{3,2,1,0:T(8,128)(2,1)S(1)}, u32[]{:S(2)}, u32[]{:S(2)}) collective-permute-start(bf16[3,4,128,128]{3,2,1,0:T(8,128)(2,1)} %get-tuple-element.35), channel_id=1, source_target_pairs={{0,2},{1,3},{2,0},{3,1},{4,6},{5,7},{6,4},{7,5},{8,10},{9,11},{10,... | collective-permute-start | bytes 1179656 | tf_op jit(solution)/shard_map/ppermute | solution.py:271
  5.5 18.3 %collective-permute-start.7 = (bf16[3,4,128,128]{3,2,1,0:T(8,128)(2,1)}, bf16[3,4,128,128]{3,2,1,0:T(8,128)(2,1)S(1)}, u32[]{:S(2)}, u32[]{:S(2)}) collective-permute-start(bf16[3,4,128,128]{3,2,1,0:T(8,128)(2,1)} %get-tuple-element.36), channel_id=1, source_target_pairs={{0,3},{1,2},{2,1},{3,0},{4,7},{5,6},{6,5},{7,4},{8,11},{9,10},{10,... | collective-permute-start | bytes 1179656 | tf_op jit(solution)/shard_map/ppermute | solution.py:271
  9.7 14.3 %collective-permute-start.8 = (bf16[3,4,128,128]{3,2,1,0:T(8,128)(2,1)}, bf16[3,4,128,128]{3,2,1,0:T(8,128)(2,1)S(1)}, u32[]{:S(2)}, u32[]{:S(2)}) collective-permute-start(bf16[3,4,128,128]{3,2,1,0:T(8,128)(2,1)} %get-tuple-element.37), channel_id=1, source_target_pairs={{0,1},{1,0},{2,3},{3,2},{4,5},{5,4},{6,7},{7,6},{8,9},{9,8},{10,11... | collective-permute-start | bytes 1179656 | tf_op jit(solution)/shard_map/ppermute | solution.py:271
  9.9 23.0 %collective-permute-start.1 = (bf16[2,4,128,128]{3,2,1,0:T(8,128)(2,1)}, bf16[2,4,128,128]{3,2,1,0:T(8,128)(2,1)S(1)}, u32[]{:S(2)}, u32[]{:S(2)}) collective-permute-start(bf16[2,4,128,128]{3,2,1,0:T(8,128)(2,1)} %get-tuple-element.29), channel_id=1, source_target_pairs={{0,1},{1,0},{2,3},{3,2},{4,5},{5,4},{6,7},{7,6},{8,9},{9,8},{10,11... | collective-permute-start | bytes 786440 | tf_op jit(solution)/shard_map/ppermute | solution.py:271
  10.2 23.3 %collective-permute-start.2 = (bf16[2,4,128,128]{3,2,1,0:T(8,128)(2,1)}, bf16[2,4,128,128]{3,2,1,0:T(8,128)(2,1)S(1)}, u32[]{:S(2)}, u32[]{:S(2)}) collective-permute-start(bf16[2,4,128,128]{3,2,1,0:T(8,128)(2,1)} %get-tuple-element.31), channel_id=1, source_target_pairs={{0,2},{1,3},{2,0},{3,1},{4,6},{5,7},{6,4},{7,5},{8,10},{9,11},{10,... | collective-permute-start | bytes 786440 | tf_op jit(solution)/shard_map/ppermute | solution.py:271
  15.7 18.3 %collective-permute-start.3 = (bf16[2,4,128,128]{3,2,1,0:T(8,128)(2,1)}, bf16[2,4,128,128]{3,2,1,0:T(8,128)(2,1)S(1)}, u32[]{:S(2)}, u32[]{:S(2)}) collective-permute-start(bf16[2,4,128,128]{3,2,1,0:T(8,128)(2,1)} %get-tuple-element.32), channel_id=1, source_target_pairs={{0,3},{1,2},{2,1},{3,0},{4,7},{5,6},{6,5},{7,4},{8,11},{9,10},{10,... | collective-permute-start | bytes 786440 | tf_op jit(solution)/shard_map/ppermute | solution.py:271
  23.8 0.7 %copy-start = (f32[2,8,128]{2,1,0:T(8,128)S(1)}, f32[2,8,128]{2,1,0:T(8,128)}, u32[]{:S(2)}) copy-start(f32[2,8,128]{2,1,0:T(8,128)} %gains.15) | copy-start | bytes 24580
  23.8 1.0 %copy-start.1 = (bf16[3,4,128,128]{3,2,1,0:T(8,128)(2,1)S(1)}, bf16[3,4,128,128]{3,2,1,0:T(8,128)(2,1)}, u32[]{:S(2)}) copy-start(bf16[3,4,128,128]{3,2,1,0:T(8,128)(2,1)} %get-tuple-element.38.refs_2_) | copy-start | bytes 1179652
  23.8 17.3 %collective-permute-start.9 = (bf16[2,4,128,128]{3,2,1,0:T(8,128)(2,1)}, bf16[2,4,128,128]{3,2,1,0:T(8,128)(2,1)S(1)}, u32[]{:S(2)}, u32[]{:S(2)}) collective-permute-start(bf16[2,4,128,128]{3,2,1,0:T(8,128)(2,1)} %get-tuple-element.39), channel_id=1, source_target_pairs={{0,1},{1,0},{2,3},{3,2},{4,5},{5,4},{6,7},{7,6},{8,9},{9,8},{10,11... | collective-permute-start | bytes 786440 | tf_op jit(solution)/shard_map/ppermute | solution.py:271
  24.8 0.7 %copy-start.5 = (s32[4,4]{1,0:T(4,128)S(1)}, s32[4,4]{1,0:T(4,128)}, u32[]{:S(2)}) copy-start(s32[4,4]{1,0:T(4,128)} %units.7) | copy-start | bytes 196
  28.5 0.6 copy-start.6
  29.1 4.5 %copy-start.10 = (bf16[1,4,128,128]{3,2,1,0:T(8,128)(2,1)S(1)}, bf16[1,4,128,128]{3,2,1,0:T(8,128)(2,1)}, u32[]{:S(2)}) copy-start(bf16[1,4,128,128]{3,2,1,0:T(8,128)(2,1)} %get-tuple-element.27) | copy-start | bytes 393220
  29.1 4.7 %copy-start.3 = (bf16[2,4,128,128]{3,2,1,0:T(8,128)(2,1)S(1)}, bf16[2,4,128,128]{3,2,1,0:T(8,128)(2,1)}, u32[]{:S(2)}) copy-start(bf16[2,4,128,128]{3,2,1,0:T(8,128)(2,1)} %get-tuple-element.30.refs_1_) | copy-start | bytes 786436
  31.6 10.6 %collective-permute-start.10 = (bf16[2,4,128,128]{3,2,1,0:T(8,128)(2,1)}, bf16[2,4,128,128]{3,2,1,0:T(8,128)(2,1)S(1)}, u32[]{:S(2)}, u32[]{:S(2)}) collective-permute-start(bf16[2,4,128,128]{3,2,1,0:T(8,128)(2,1)} %get-tuple-element.41), channel_id=1, source_target_pairs={{0,2},{1,3},{2,0},{3,1},{4,6},{5,7},{6,4},{7,5},{8,10},{9,11},{10,... | collective-permute-start | bytes 786440 | tf_op jit(solution)/shard_map/ppermute | solution.py:271
  32.9 12.9 %collective-permute-start.11 = (bf16[2,4,128,128]{3,2,1,0:T(8,128)(2,1)}, bf16[2,4,128,128]{3,2,1,0:T(8,128)(2,1)S(1)}, u32[]{:S(2)}, u32[]{:S(2)}) collective-permute-start(bf16[2,4,128,128]{3,2,1,0:T(8,128)(2,1)} %get-tuple-element.42), channel_id=1, source_target_pairs={{0,3},{1,2},{2,1},{3,0},{4,7},{5,6},{6,5},{7,4},{8,11},{9,10},{10,... | collective-permute-start | bytes 786440 | tf_op jit(solution)/shard_map/ppermute | solution.py:271
  33.6 7.1 %collective-permute-start = (bf16[1,4,128,128]{3,2,1,0:T(8,128)(2,1)S(1)}, bf16[1,4,128,128]{3,2,1,0:T(8,128)(2,1)S(1)}, u32[]{:S(2)}, u32[]{:S(2)}) collective-permute-start(bf16[1,4,128,128]{3,2,1,0:T(8,128)(2,1)S(1)} %copy-done.10), channel_id=1, source_target_pairs={{0,1},{1,0},{2,3},{3,2},{4,5},{5,4},{6,7},{7,6},{8,9},{9,8},{10,11... | collective-permute-start | bytes 393224 | tf_op jit(solution)/shard_map/ppermute | solution.py:271
  36.2 0.5 copy-start.8
  36.8 4.2 %copy-start.4 = (bf16[1,4,128,128]{3,2,1,0:T(8,128)(2,1)S(1)}, bf16[1,4,128,128]{3,2,1,0:T(8,128)(2,1)}, u32[]{:S(2)}) copy-start(bf16[1,4,128,128]{3,2,1,0:T(8,128)(2,1)} %get-tuple-element.28.refs_1_) | copy-start | bytes 393220
  39.2 10.2 %collective-permute-start.4 = (bf16[1,4,128,128]{3,2,1,0:T(8,128)(2,1)}, bf16[1,4,128,128]{3,2,1,0:T(8,128)(2,1)S(1)}, u32[]{:S(2)}, u32[]{:S(2)}) collective-permute-start(bf16[1,4,128,128]{3,2,1,0:T(8,128)(2,1)} %get-tuple-element.33), channel_id=1, source_target_pairs={{0,2},{1,3},{2,0},{3,1},{4,6},{5,7},{6,4},{7,5},{8,10},{9,11},{10,... | collective-permute-start | bytes 393224 | tf_op jit(solution)/shard_map/ppermute | solution.py:271
  40.7 10.7 %collective-permute-start.5 = (bf16[1,4,128,128]{3,2,1,0:T(8,128)(2,1)}, bf16[1,4,128,128]{3,2,1,0:T(8,128)(2,1)S(1)}, u32[]{:S(2)}, u32[]{:S(2)}) collective-permute-start(bf16[1,4,128,128]{3,2,1,0:T(8,128)(2,1)} %get-tuple-element.34), channel_id=1, source_target_pairs={{0,3},{1,2},{2,1},{3,0},{4,7},{5,6},{6,5},{7,4},{8,11},{9,10},{10,... | collective-permute-start | bytes 393224 | tf_op jit(solution)/shard_map/ppermute | solution.py:271
  41.0 1.0 %copy-start.2 = (bf16[2,4,128,128]{3,2,1,0:T(8,128)(2,1)S(1)}, bf16[2,4,128,128]{3,2,1,0:T(8,128)(2,1)}, u32[]{:S(2)}) copy-start(bf16[2,4,128,128]{3,2,1,0:T(8,128)(2,1)} %get-tuple-element.40.refs_1_) | copy-start | bytes 786436
  42.1 9.2 %copy-start.7 = (f32[3,128]{1,0:T(4,128)S(1)}, f32[3,128]{1,0:T(4,128)}, u32[]{:S(2)}) copy-start(f32[3,128]{1,0:T(4,128)} %copy-done.6) | copy-start | bytes 4612
  42.2 9.2 %copy-start.9 = (f32[2,128]{1,0:T(2,128)S(1)}, f32[2,128]{1,0:T(2,128)}, u32[]{:S(2)}) copy-start(f32[2,128]{1,0:T(2,128)} %copy-done.8) | copy-start | bytes 3076
  53.0 5.6 %collective-permute-start.14 = (f32[2,8,32]{2,1,0:T(8,128)S(1)}, f32[2,8,32]{2,1,0:T(8,128)S(1)}, u32[]{:S(2)}, u32[]{:S(2)}) collective-permute-start(f32[2,8,32]{2,1,0:T(8,128)S(1)} %get-tuple-element.46), channel_id=1, source_target_pairs={{0,12},{4,8},{8,4},{12,0},{1,13},{5,9},{9,5},{13,1},{2,14},{6,10},... | collective-permute-start | bytes 6152 | tf_op jit(solution)/shard_map/ppermute | solution.py:300
  57.0 4.5 %collective-permute-start.13 = (f32[2,8,32]{2,1,0:T(8,128)S(1)}, f32[2,8,32]{2,1,0:T(8,128)S(1)}, u32[]{:S(2)}, u32[]{:S(2)}) collective-permute-start(f32[2,8,32]{2,1,0:T(8,128)S(1)} %get-tuple-element.45), channel_id=1, source_target_pairs={{0,8},{4,12},{8,0},{12,4},{1,9},{5,13},{9,1},{13,5},{2,10},{6,14},... | collective-permute-start | bytes 6152 | tf_op jit(solution)/shard_map/ppermute | solution.py:300
  57.0 4.5 %collective-permute-start.12 = (f32[2,8,32]{2,1,0:T(8,128)S(1)}, f32[2,8,32]{2,1,0:T(8,128)S(1)}, u32[]{:S(2)}, u32[]{:S(2)}) collective-permute-start(f32[2,8,32]{2,1,0:T(8,128)S(1)} %get-tuple-element.44), channel_id=1, source_target_pairs={{0,4},{4,0},{8,12},{12,8},{1,5},{5,1},{9,13},{13,9},{2,6},{6,2},{1... | collective-permute-start | bytes 6152 | tf_op jit(solution)/shard_map/ppermute | solution.py:300

commit v4 on v3

--- a/solution.py
+++ b/solution.py
@@ -9,6 +9,8 @@
 from jax.sharding import PartitionSpec as P
 
 MAXCLIP = 3
+VALUES = 2
+OTHERS = (0, 1, 3)
 TILE = 8
 EPS = 1e-06
 VMEM_LIMIT = 48 * 1024 * 1024
@@ -16,7 +18,7 @@
 
 
 def head_chunks(heads):
-    sizes = {8: (3, 2, 2, 1)}.get(heads)
+    sizes = {8: (4, 3, 1)}.get(heads)
     if sizes is None:
         sizes = (1,) * heads if heads <= 2 else (heads - heads // 2, heads // 2)
     bounds, start = [], 0
@@ -26,12 +28,76 @@
     return bounds
 
 
+def tile_start(heads, flip):
+    head = jnp.bitwise_xor(lax.axis_index("seq"), flip) * heads
+    offset = 0 if heads % TILE == 0 else lax.rem(head, TILE)
+    return pl.multiple_of((head // TILE) * TILE, TILE), offset
+
+
+def cut_kernel(flips, heads, array, *refs):
+    outs, token, sems = refs[:-2], refs[-2], refs[-1]
+    token[...] = jnp.zeros_like(token)
+    copies = []
+    for index, flip in enumerate(flips):
+        start, _ = tile_start(heads, flip)
+        source = array.at[0, :, :, pl.ds(start, outs[index].shape[2]), :]
+        copies.append(pltpu.make_async_copy(source, outs[index], sems.at[index]))
+        copies[-1].start()
+    for copy in copies:
+        copy.wait()
+
+
+def cut(array, flips, heads):
+    _, slots, rows, _, size = array.shape
+    shape = jax.ShapeDtypeStruct((slots, rows, max(heads, TILE), size), array.dtype)
+    return pl.pallas_call(
+        functools.partial(cut_kernel, flips, heads),
+        out_shape=[shape] * len(flips) + [jax.ShapeDtypeStruct((TILE, size), jnp.float32)],
+        in_specs=[pl.BlockSpec(memory_space=pltpu.HBM)],
+        out_specs=[pl.BlockSpec(memory_space=pltpu.HBM)] * len(flips) + [pl.BlockSpec(memory_space=pltpu.VMEM)],
+        scratch_shapes=[pltpu.SemaphoreType.DMA((len(flips),))],
+        compiler_params=pltpu.CompilerParams(vmem_limit_bytes=PACK_VMEM_LIMIT),
+        name="cut",
+    )(array)
+
+
+def arrange_kernel(*refs):
+    pieces, out, wide = refs[:-2], refs[-2], refs[-1]
+    heads, slots = out.shape[:2]
+    rows, held = pieces[0].shape[1:3]
+    _, offset = tile_start(heads, 0)
+    for source, piece in enumerate(pieces):
+        for slot in range(slots):
+            for span in range(held // TILE):
+                place = (source * slots + slot) % wide.shape[0]
+                block = piece[slot, :, span * TILE : (span + 1) * TILE, :]
+                wide[place] = block.astype(jnp.float32).reshape(rows * TILE, wide.shape[-1])
+                for head in range(span * TILE, min(heads, (span + 1) * TILE)):
+                    out[head, slot, source * rows : (source + 1) * rows, :] = wide[
+                        place, pl.ds(offset + head - span * TILE, rows, stride=TILE), :
+                    ].astype(jnp.bfloat16)
+
+
+def arrange(pieces, heads):
+    slots, rows, held, size = pieces[0].shape
+    moved = len(pieces) * slots * rows * held * size * 2
+    return pl.pallas_call(
+        arrange_kernel,
+        out_shape=jax.ShapeDtypeStruct((heads, slots, len(pieces) * rows, size), jnp.bfloat16),
+        in_specs=[pl.BlockSpec(memory_space=pltpu.VMEM)] * len(pieces),
+        out_specs=pl.BlockSpec(memory_space=pltpu.VMEM),
+        scratch_shapes=[pltpu.VMEM((slots, rows * TILE, size), jnp.float32)],
+        compiler_params=pltpu.CompilerParams(vmem_limit_bytes=VMEM_LIMIT),
+        cost_estimate=pl.CostEstimate(flops=moved, bytes_accessed=2 * moved, transcendentals=0),
+        name="arrange",
+    )(*pieces)
+
+
 def pack_kernel(plan, heads, after, *refs):
     arrays = refs[:4]
-    outs = refs[4 + after : 4 + after + sum(len(chunks) for _, chunks in plan)]
+    outs = refs[4 + after : 4 + after + sum(len(chunks) for _, _, chunks in plan)]
     token, raw, wide, sems = refs[4 + after + len(outs) :]
     token[...] = jnp.zeros_like(token)
-    me = lax.axis_index("seq")
     slots, rows = raw.shape[2], raw.shape[3]
     spans = max(1, heads // TILE)
 
@@ -42,18 +108,14 @@
             sems.at[index, array * spans + span],
         )
 
-    firsts, offsets = [], []
-    for flip, _ in plan:
-        head = jnp.bitwise_xor(me, flip) * heads
-        firsts.append(pl.multiple_of((head // TILE) * TILE, TILE))
-        offsets.append(0 if heads % TILE == 0 else lax.rem(head, TILE))
-    for index in range(len(plan)):
-        for array in range(4):
+    firsts, offsets = zip(*[tile_start(heads, flip) for flip, _, _ in plan])
+    for index, (_, wanted, _) in enumerate(plan):
+        for array in wanted:
             for span in range(spans):
                 copy(index, array, span, firsts[index]).start()
     place = 0
-    for index, (_, chunks) in enumerate(plan):
-        for array in range(4):
+    for index, (_, wanted, chunks) in enumerate(plan):
+        for position, array in enumerate(wanted):
             for span in range(spans):
                 copy(index, array, span, firsts[index]).wait()
                 for slot in range(slots):
@@ -64,7 +126,7 @@
                     )
                     for number, (low, high) in enumerate(chunks):
                         for head in range(max(low, span * TILE), min(high, (span + 1) * TILE)):
-                            outs[place + number][head - low, array, slot * rows : (slot + 1) * rows, :] = wide[
+                            outs[place + number][head - low, position, slot * rows : (slot + 1) * rows, :] = wide[
                                 slot, pl.ds(offsets[index] + head - span * TILE, rows, stride=TILE), :
                             ].astype(jnp.bfloat16)
         place += len(chunks)
@@ -74,8 +136,8 @@
     _, slots, rows, _, size = arrays[0].shape
     spans = max(1, heads // TILE)
     shapes = [
-        jax.ShapeDtypeStruct((high - low, 4, slots * rows, size), jnp.bfloat16)
-        for _, chunks in plan
+        jax.ShapeDtypeStruct((high - low, len(wanted), slots * rows, size), jnp.bfloat16)
+        for _, wanted, chunks in plan
         for low, high in chunks
     ] + [jax.ShapeDtypeStruct((TILE, size), jnp.float32)]
     count = len(plan)
@@ -124,11 +186,10 @@
     heads, _, tokens, _ = pieces[0].shape
     slots = out.shape[2]
     rows = tokens // slots
-
     for head in range(heads):
         for array in range(4):
-            for source, piece in enumerate(pieces):
-                block = piece[head, array]
+            for source, piece in enumerate(pieces[array // 2 :: 2]):
+                block = piece[head, array % 2]
                 if array < 2:
                     block = normalized(block, gains[array, low + head : low + head + 1, :])
                 for slot in range(slots):
@@ -139,10 +200,10 @@
 
 def prepare(low, gains, pieces, slots, after):
     heads, _, tokens, size = pieces[0].shape
-    moved = len(pieces) * heads * 4 * tokens * size * 2
+    moved = len(pieces) * heads * 2 * tokens * size * 2
     return pl.pallas_call(
         functools.partial(prepare_kernel, low, len(after)),
-        out_shape=jax.ShapeDtypeStruct((heads, 4, slots, len(pieces) * tokens // slots, size), jnp.bfloat16),
+        out_shape=jax.ShapeDtypeStruct((heads, 4, slots, len(pieces) // 2 * tokens // slots, size), jnp.bfloat16),
         in_specs=[pl.BlockSpec(memory_space=pltpu.VMEM)] * (1 + len(after) + len(pieces)),
         out_specs=pl.BlockSpec(memory_space=pltpu.VMEM),
         compiler_params=pltpu.CompilerParams(vmem_limit_bytes=VMEM_LIMIT),
@@ -151,7 +212,7 @@
     )(gains, *after, *pieces)
 
 
-def attention_chunk(low, count, units, gains, close, pieces, held, total):
+def attention_chunk(low, count, units, gains, values, close, pieces, held, total):
     query, key, value, grad = held
     group = lax.axis_index("dp")
     _, _, tokens, size = pieces[0].shape
@@ -162,8 +223,12 @@
         for array, kept in enumerate(held):
             for slot in range(slots):
                 kept[head, slot * unit : slot * unit + near, :] = close[head, array, slot]
+                if array == VALUES:
+                    kept[head, slot * unit + near : (slot + 1) * unit, :] = values[low + head, slot]
+            if array == VALUES:
+                continue
             for source, piece in enumerate(pieces):
-                block = piece[head, array]
+                block = piece[head, OTHERS.index(array)]
                 if array < 2:
                     block = normalized(block, gains[array, low + head : low + head + 1, :])
                 for slot in range(slots):
@@ -191,17 +256,17 @@
                 total[head : head + 1, :] = sum(clip(head, slot, span) for slot, span in layout)
 
 
-def chunk_kernel(low, units, gains, close, *refs):
+def chunk_kernel(low, units, gains, values, close, *refs):
     pieces, out, held = refs[:-5], refs[-5], refs[-4:]
-    attention_chunk(low, out.shape[0], units, gains, close, pieces, held, out)
-
-
-def last_kernel(low, sources, earlier, peers, units, gains, close, *refs):
+    attention_chunk(low, out.shape[0], units, gains, values, close, pieces, held, out)
+
+
+def last_kernel(low, sources, earlier, peers, units, gains, values, close, *refs):
     pieces = refs[:sources]
     before = refs[sources : sources + earlier]
     outs = refs[sources + earlier : sources + earlier + len(peers)]
     held, total = refs[sources + earlier + len(peers) : -1], refs[-1]
-    attention_chunk(low, total.shape[0], units, gains, close, pieces, held, total)
+    attention_chunk(low, total.shape[0], units, gains, values, close, pieces, held, total)
     group = lax.axis_index("dp")
     size = total.shape[-1]
     width = outs[0].shape[-1]
@@ -213,7 +278,7 @@
             out[side] = pltpu.roll(grads, shift, 1)[:, :width]
 
 
-def attend(low, count, units, gains, close, pieces, earlier=None, peers=None):
+def attend(low, count, units, gains, values, close, pieces, earlier=None, peers=None):
     _, _, tokens, size = pieces[0].shape
     all_tokens = close.shape[2] * close.shape[3] + tokens * len(pieces)
     held = [pltpu.VMEM((count, all_tokens, size), jnp.bfloat16)] * 4
@@ -233,7 +298,7 @@
         kernel,
         out_shape=shapes,
         in_specs=[pl.BlockSpec(memory_space=pltpu.SMEM)]
-        + [pl.BlockSpec(memory_space=pltpu.VMEM)] * (2 + len(pieces) + len(earlier)),
+        + [pl.BlockSpec(memory_space=pltpu.VMEM)] * (3 + len(pieces) + len(earlier)),
         out_specs=outs,
         scratch_shapes=held,
         compiler_params=pltpu.CompilerParams(vmem_limit_bytes=VMEM_LIMIT),
@@ -241,7 +306,7 @@
             flops=6 * pairs * size, bytes_accessed=len(pieces) * count * 4 * tokens * size * 2, transcendentals=pairs
         ),
         name="attend",
-    )(units, gains, close, *pieces, *earlier)
+    )(units, gains, values, close, *pieces, *earlier)
 
 
 def seen_kernel(*refs):
@@ -273,28 +338,35 @@
     slots = clip_units.shape[1]
     close = near + [0]
 
-    def pack_and_send(number, after):
-        plan = [(flip, [chunks[number]]) for flip in far]
-        if number == 1:
-            plan += [(flip, chunks) for flip in close]
+    def pack_and_send(plan, after):
         *blocks, token = pack(arrays, plan, heads, after)
-        received.append([send(block, flip) for flip, block in zip(far, blocks)])
-        return blocks[len(far) :], token
-
-    received, sums = [], []
-    _, token = pack_and_send(0, [])
-    rest, _ = pack_and_send(1, [token])
-    for number, (low, high) in enumerate(chunks):
-        if 0 < number < len(chunks) - 1:
-            pack_and_send(number + 1, sums[number - 1 :])
-        pieces = [
-            send(block, flip) if flip else block for flip, block in zip(close, rest[number :: len(chunks)])
-        ]
-        after = [seen(received[0])] if number == 0 else []
-        prepared = prepare(low, norm_gains, pieces, slots, after)
-        if number + 1 < len(chunks):
-            sums.append(attend(low, high - low, clip_units, norm_gains, prepared, received[number]))
-    parts = attend(low, high - low, clip_units, norm_gains, prepared, received[-1], sums, list(range(groups)))
+        flips = [flip for flip, _, wanted in plan for _ in wanted]
+        return [send(block, flip) if flip else block for flip, block in zip(flips, blocks)], token
+
+    def far_plan(number):
+        return [(flip, OTHERS, chunks[number : number + 1]) for flip in far]
+
+    *tiles, token = cut(arrays[VALUES], far, heads)
+    tiles = [send(block, flip) for flip, block in zip(far, tiles)]
+    received, token = pack_and_send(far_plan(0), [token])
+    later = far_plan(1) if len(chunks) > 1 else []
+    whole = [(flip, pair, chunks) for flip in close for pair in ((0, 1), (2, 3))]
+    blocks, _ = pack_and_send(later + whole, [token, seen(tiles)])
+    values = arrange(tiles, heads)
+    prepared = [
+        prepare(low, norm_gains, blocks[len(later) + number :: len(chunks)], slots, [] if number else [seen(received)])
+        for number, (low, _) in enumerate(chunks)
+    ]
+    waiting, sums = blocks[: len(later)], []
+    for number, (low, high) in enumerate(chunks[:-1]):
+        sums.append(attend(low, high - low, clip_units, norm_gains, values, prepared[number], received))
+        received = waiting
+        if number + 2 < len(chunks):
+            waiting, _ = pack_and_send(far_plan(number + 2), sums[-1:])
+    low, high = chunks[-1]
+    parts = attend(
+        low, high - low, clip_units, norm_gains, values, prepared[-1], received, sums, list(range(groups))
+    )
     result = parts[0]
     for flip in range(1, groups):
         result = result + lax.ppermute(parts[flip], "dp", [(g, g ^ flip) for g in range(groups)])

time: 62.4 us -> 78.7 us (1.26)
  Pallas kernels: 21.6 us -> 36.6 us
    pallas_call x0 -> x2, Pallas kernels: none -> 17.8 us  [the longest x1 17.6 us: cut(): pl.pallas_call(functools.partial(cut_kernel, flips, heads), out_shape=[sh...]
    pallas_call x4 -> x3, Pallas kernels: 11.5 us -> 8.57 us  [pack(): pl.pallas_call(functools.partial(pack_kernel, plan, heads, len(after)), o...]
    ppermute x12 -> x14, starting transfers between devices: 9.42 us -> 10.2 us  [send(): return lax.ppermute(block, 'seq', [(s, s ^ flip) for s in range(sequence)])]
    pallas_call x4 -> x3, Pallas kernels: 9.12 us -> 9.39 us  [attend(): pl.pallas_call(kernel, out_shape=shapes, in_specs=[pl.BlockSpec(memory_sp...]
    ppermute x12 -> x14, waiting for transfers between devices: 18.7 us -> 18.5 us  [send(): return lax.ppermute(block, 'seq', [(s, s ^ flip) for s in range(sequence)])]
  transfers between devices with their start and end apart: 15 -> 17, of which waited for: 7 -> 7; matrix products, arithmetic and copies ran while one was open for 0% -> 0% of each run, Pallas kernels for 28% -> 22%
where the time goes in v4:
time: 78.7 us; the launch traced here: 78.5 us
  Pallas kernels  36.6 us (47%)
  waiting for transfers between devices  23.1 us (29%)
  starting transfers between devices  14.6 us (19%)
  local copies, waits for them, and re-layouts  3.34 us (4%)
    ppermute x14, waiting for transfers between devices, send(): return lax.ppermute(block, 'seq', [(s, s ^ flip) for s in range(sequence)])  18.5 us
    pallas_call x1, Pallas kernels, cut(): pl.pallas_call(functools.partial(cut_kernel, flips, heads), out_shape=[sh...  17.6 us
    ppermute x14, starting transfers between devices, send(): return lax.ppermute(block, 'seq', [(s, s ^ flip) for s in range(sequence)])  10.2 us
    pallas_call x3, Pallas kernels, attend(): pl.pallas_call(kernel, out_shape=shapes, in_specs=[pl.BlockSpec(memory_sp...  9.39 us
    pallas_call x3, Pallas kernels, pack(): pl.pallas_call(functools.partial(pack_kernel, plan, heads, len(after)), o...  8.57 us
    ppermute x3, waiting for transfers between devices, body(): lax.ppermute(parts[flip], 'dp', [(g, g ^ flip) for g in range(groups)])  4.56 us
    ppermute x3, starting transfers between devices, body(): lax.ppermute(parts[flip], 'dp', [(g, g ^ flip) for g in range(groups)])  4.4 us
    unnamed x22, local copies, waits for them, and re-layouts  3.34 us
  transfers between devices with their start and end apart: 17, of which 7 were waited for; matrix products, arithmetic and copies ran while one was open for 0% of the time, Pallas kernels for 22%

profile of v4, /device:TPU:0, one launch (start us, length us, event | category | flops | bytes accessed | tf_op | source)
XLA Modules:
  0.0 78.5 jit_solution(4291322357218316184)
XLA Ops:
  0.0 17.6 %cut.1 = (bf16[4,32,8,128]{3,2,1,0:T(8,128)(2,1)}, bf16[4,32,8,128]{3,2,1,0:T(8,128)(2,1)}, f32[8,128]{1,0:T(8,128)}) custom-call(bf16[1,4,32,32,128]{4,3,2,1,0:T(8,128)(2,1)} %refs_2_.5), custom_call_target="tpu_custom_call" | custom-call | tf_op jit(solution)/shard_map/cut/pallas_call | solution.py:53
  17.6 3.0 %collective-permute-start = (bf16[4,32,8,128]{3,2,1,0:T(8,128)(2,1)}, bf16[4,32,8,128]{3,2,1,0:T(8,128)(2,1)S(1)}, u32[]{:S(2)}, u32[]{:S(2)}) collective-permute-start(bf16[4,32,8,128]{3,2,1,0:T(8,128)(2,1)} %get-tuple-element.31), channel_id=1, source_target_pairs={{0,2},{1,3},{2,0},{3,1},{4,6},{5,7},{6,4},{7,5},{8,10},{9,11},{10,... | collective-permute-start | bytes 786440 | tf_op jit(solution)/shard_map/ppermute | solution.py:336
  20.6 0.0 collective-permute-start.1
  20.6 2.4 %pack.3 = (bf16[4,3,128,128]{3,2,1,0:T(8,128)(2,1)}, bf16[4,3,128,128]{3,2,1,0:T(8,128)(2,1)}, f32[8,128]{1,0:T(8,128)}) custom-call(bf16[1,4,32,32,128]{4,3,2,1,0:T(8,128)(2,1)} %refs_0_.5, bf16[1,4,32,32,128]{4,3,2,1,0:T(8,128)(2,1)} %refs_1_.5, bf16[1,4,32,32,128]{4,3,2,1,0:T(8,128)(2,1)} %refs_2_.5, bf16[1,4,32,32,128]{4,3,2,1,0:T(8,128)(2,1)} %refs_3_.5, ...), custom_call_target="tpu_custom_call" | custom-call | flops 2097152 | bytes 4194304 | tf_op jit(solution)/shard_map/pack/pallas_call | solution.py:145
  23.0 1.2 %collective-permute-start.4 = (bf16[4,3,128,128]{3,2,1,0:T(8,128)(2,1)}, bf16[4,3,128,128]{3,2,1,0:T(8,128)(2,1)S(1)}, u32[]{:S(2)}, u32[]{:S(2)}) collective-permute-start(bf16[4,3,128,128]{3,2,1,0:T(8,128)(2,1)} %get-tuple-element.39), channel_id=1, source_target_pairs={{0,2},{1,3},{2,0},{3,1},{4,6},{5,7},{6,4},{7,5},{8,10},{9,11},{10,... | collective-permute-start | bytes 1179656 | tf_op jit(solution)/shard_map/ppermute | solution.py:336
  24.2 0.6 collective-permute-start.5
  24.9 3.1 %collective-permute-done.refs_0_ = bf16[4,32,8,128]{3,2,1,0:T(8,128)(2,1)S(1)} collective-permute-done((bf16[4,32,8,128]{3,2,1,0:T(8,128)(2,1)}, bf16[4,32,8,128]{3,2,1,0:T(8,128)(2,1)S(1)}, u32[]{:S(2)}, u32[]{:S(2)}) %collective-permute-start) | collective-permute-done | bytes 262176 | tf_op jit(solution)/shard_map/ppermute | solution.py:336
  27.9 5.3 %collective-permute-done.1.refs_1_ = bf16[4,32,8,128]{3,2,1,0:T(8,128)(2,1)S(1)} collective-permute-done((bf16[4,32,8,128]{3,2,1,0:T(8,128)(2,1)}, bf16[4,32,8,128]{3,2,1,0:T(8,128)(2,1)S(1)}, u32[]{:S(2)}, u32[]{:S(2)}) %collective-permute-start.1) | collective-permute-done | bytes 262176 | tf_op jit(solution)/shard_map/ppermute | solution.py:336
  33.3 0.6 copy-done.10
  33.8 4.0 %pack.4 = (bf16[3,3,128,128]{3,2,1,0:T(8,128)(2,1)}, bf16[3,3,128,128]{3,2,1,0:T(8,128)(2,1)}, bf16[4,2,128,128]{3,2,1,0:T(8,128)(2,1)}, bf16[3,2,128,128]{3,2,1...) custom-call(bf16[1,4,32,32,128]{4,3,2,1,0:T(8,128)(2,1)} %refs_0_.5,, ...), custom_call_target="tpu_custom_call" | custom-call | flops 6291456 | bytes 12582912 | tf_op jit(solution)/shard_map/pack/pallas_call | solution.py:145
  37.9 0.2 collective-permute-start.6
  38.1 0.4 collective-permute-start.7
  38.5 0.1 collective-permute-start.2
  38.6 1.6 %collective-permute-done.2.refs_0_ = bf16[1,2,128,128]{3,2,1,0:T(8,128)(2,1)S(1)} collective-permute-done((bf16[1,2,128,128]{3,2,1,0:T(8,128)(2,1)}, bf16[1,2,128,128]{3,2,1,0:T(8,128)(2,1)S(1)}, u32[]{:S(2)}, u32[]{:S(2)}) %collective-permute-start.2) | collective-permute-done | bytes 65568 | tf_op jit(solution)/shard_map/ppermute | solution.py:336
  40.2 1.9 %collective-permute-start.12 = (bf16[3,3,128,128]{3,2,1,0:T(8,128)(2,1)}, bf16[3,3,128,128]{3,2,1,0:T(8,128)(2,1)S(1)}, u32[]{:S(2)}, u32[]{:S(2)}) collective-permute-start(bf16[3,3,128,128]{3,2,1,0:T(8,128)(2,1)} %get-tuple-element.51), channel_id=1, source_target_pairs={{0,2},{1,3},{2,0},{3,1},{4,6},{5,7},{6,4},{7,5},{8,10},{9,11},{10,... | collective-permute-start | bytes 884744 | tf_op jit(solution)/shard_map/ppermute | solution.py:336
  42.0 0.0 collective-permute-done.4.refs_0_
  42.0 0.0 collective-permute-start.13
  42.0 8.1 %collective-permute-done.5.refs_1_ = bf16[4,3,128,128]{3,2,1,0:T(8,128)(2,1)S(1)} collective-permute-done((bf16[4,3,128,128]{3,2,1,0:T(8,128)(2,1)}, bf16[4,3,128,128]{3,2,1,0:T(8,128)(2,1)S(1)}, u32[]{:S(2)}, u32[]{:S(2)}) %collective-permute-start.5) | collective-permute-done | bytes 393248 | tf_op jit(solution)/shard_map/ppermute | solution.py:336
  50.1 0.1 collective-permute-start.10
  50.2 0.4 collective-permute-start.11
  50.6 0.1 collective-permute-start.3
  50.8 0.2 arrange.1.values
  51.0 0.0 copy-start
  51.0 0.7 copy-done
  51.7 0.3 copy-done.1
  52.0 0.1 copy-done.2
  52.0 0.4 prepare.4.close
  52.4 0.3 copy-done.9
  52.7 4.2 %attend.3.refs_4_.refs_2_ = f32[4,128]{1,0:T(4,128)S(1)} custom-call(s32[4,4]{1,0:T(4,128)S(1)} %copy-done.9, f32[2,8,128]{2,1,0:T(8,128)S(1)} %copy-done, bf16[8,4,64,128]{3,2,1,0:T(8,128)(2,1)S(1)} %arrange.1.values, bf16[4,4,4,64,128]{4,3,2,1,0:T(8,128)(2,1)S(1)} %prepare.4.close, bf16[4,3,128,128]{3,2,1,0:T(8,128)(2,1)S(1)} %collective-permute-done.4.refs_0_, ...), custom_call_target="tpu_custom_call" | custom-call | flops 402653184 | bytes 1048576 | tf_op jit(solution)/shard_map/attend/pallas_call | solution.py:297
  57.0 0.6 copy-done.7
  57.5 2.2 %pack.5 = (bf16[1,3,128,128]{3,2,1,0:T(8,128)(2,1)}, bf16[1,3,128,128]{3,2,1,0:T(8,128)(2,1)}, f32[8,128]{1,0:T(8,128)}) custom-call(bf16[1,4,32,32,128]{4,3,2,1,0:T(8,128)(2,1)} %refs_0_.5, bf16[1,4,32,32,128]{4,3,2,1,0:T(8,128)(2,1)} %refs_1_.5, bf16[1,4,32,32,128]{4,3,2,1,0:T(8,128)(2,1)} %refs_2_.5, bf16[1,4,32,32,128]{4,3,2,1,0:T(8,128)(2,1)} %refs_3_.5, ...), custom_call_target="tpu_custom_call" | custom-call | flops 2097152 | bytes 4194304 | tf_op jit(solution)/shard_map/pack/pallas_call | solution.py:145
  59.7 0.0 collective-permute-done.3.refs_1_
  59.7 2.1 %collective-permute-start.8 = (bf16[1,3,128,128]{3,2,1,0:T(8,128)(2,1)}, bf16[1,3,128,128]{3,2,1,0:T(8,128)(2,1)S(1)}, u32[]{:S(2)}, u32[]{:S(2)}) collective-permute-start(bf16[1,3,128,128]{3,2,1,0:T(8,128)(2,1)} %get-tuple-element.45), channel_id=1, source_target_pairs={{0,2},{1,3},{2,0},{3,1},{4,6},{5,7},{6,4},{7,5},{8,10},{9,11},{10,... | collective-permute-start | bytes 294920 | tf_op jit(solution)/shard_map/ppermute | solution.py:336
  61.9 0.2 prepare.3.close
  62.1 0.0 collective-permute-done.11.refs_1_
  62.1 0.7 copy-done.3
  62.8 0.1 copy-done.4
  62.9 0.3 prepare.5.close
  63.2 0.0 collective-permute-done.13.refs_1_
  63.2 3.5 %attend.4.refs_3_ = f32[3,128]{1,0:T(4,128)S(1)} custom-call(s32[4,4]{1,0:T(4,128)S(1)} %copy-done.9, f32[2,8,128]{2,1,0:T(8,128)S(1)} %copy-done, bf16[8,4,64,128]{3,2,1,0:T(8,128)(2,1)S(1)} %arrange.1.values, bf16[3,4,4,64,128]{4,3,2,1,0:T(8,128)(2,1)S(1)} %prepare.5.close, bf16[3,3,128,128]{3,2,1,0:T(8,128)(2,1)S(1)} %collective-permute-done.12.refs_0_, ...), custom_call_target="tpu_custom_call" | custom-call | flops 301989888 | bytes 786432 | tf_op jit(solution)/shard_map/attend/pallas_call | solution.py:297
  66.7 0.5 collective-permute-done.9.refs_1_
  67.2 1.7 %attend.5 = (f32[2,8,32]{2,1,0:T(8,128)S(1)}, f32[2,8,32]{2,1,0:T(8,128)S(1)}, f32[2,8,32]{2,1,0:T(8,128)S(1)}, f32[2,8,32]{2,1,0:T(8,128)S(1)}) custom-call(s32[4,4]{1,0:T(4,128)S(1)} %copy-done.9, f32[2,8,128]{2,1,0:T(8,128)S(1)} %copy-done, bf16[8,4,64,128]{3,2,1,0:T(8,128)(2,1)S(1)} %arrange.1.values, bf16[1,4,4,64,128]{4,3,2,1,0:T(8,128)(2,1)S(1)} %prepare.3.close, ...), custom_call_target="tpu_custom_call" | custom-call | flops 100663296 | bytes 262144 | tf_op jit(solution)/shard_map/attend/pallas_call | solution.py:297
  68.9 0.8 %collective-permute-start.14 = (f32[2,8,32]{2,1,0:T(8,128)S(1)}, f32[2,8,32]{2,1,0:T(8,128)S(1)}, u32[]{:S(2)}, u32[]{:S(2)}) collective-permute-start(f32[2,8,32]{2,1,0:T(8,128)S(1)} %get-tuple-element.54), channel_id=1, source_target_pairs={{0,4},{4,0},{8,12},{12,8},{1,5},{5,1},{9,13},{13,9},{2,6},{6,2},{1... | collective-permute-start | bytes 6152 | tf_op jit(solution)/shard_map/ppermute | solution.py:372
  69.7 2.7 %collective-permute-start.15 = (f32[2,8,32]{2,1,0:T(8,128)S(1)}, f32[2,8,32]{2,1,0:T(8,128)S(1)}, u32[]{:S(2)}, u32[]{:S(2)}) collective-permute-start(f32[2,8,32]{2,1,0:T(8,128)S(1)} %get-tuple-element.55), channel_id=1, source_target_pairs={{0,8},{4,12},{8,0},{12,4},{1,9},{5,13},{9,1},{13,5},{2,10},{6,14},... | collective-permute-start | bytes 6152 | tf_op jit(solution)/shard_map/ppermute | solution.py:372
  72.4 0.9 %collective-permute-start.16 = (f32[2,8,32]{2,1,0:T(8,128)S(1)}, f32[2,8,32]{2,1,0:T(8,128)S(1)}, u32[]{:S(2)}, u32[]{:S(2)}) collective-permute-start(f32[2,8,32]{2,1,0:T(8,128)S(1)} %get-tuple-element.56), channel_id=1, source_target_pairs={{0,12},{4,8},{8,4},{12,0},{1,13},{5,9},{9,5},{13,1},{2,14},{6,10},... | collective-permute-start | bytes 6152 | tf_op jit(solution)/shard_map/ppermute | solution.py:372
  73.3 1.0 %collective-permute-done.15 = f32[2,8,32]{2,1,0:T(8,128)S(1)} collective-permute-done((f32[2,8,32]{2,1,0:T(8,128)S(1)}, f32[2,8,32]{2,1,0:T(8,128)S(1)}, u32[]{:S(2)}, u32[]{:S(2)}) %collective-permute-start.15) | collective-permute-done | bytes 2080 | tf_op jit(solution)/shard_map/ppermute | solution.py:372
  74.3 3.6 %collective-permute-done.16 = f32[2,8,32]{2,1,0:T(8,128)S(1)} collective-permute-done((f32[2,8,32]{2,1,0:T(8,128)S(1)}, f32[2,8,32]{2,1,0:T(8,128)S(1)}, u32[]{:S(2)}, u32[]{:S(2)}) %collective-permute-start.16) | collective-permute-done | bytes 2080 | tf_op jit(solution)/shard_map/ppermute | solution.py:372
  77.9 0.6 add_add_fusion
  (22 shorter events, 0.0 us)
Async XLA Ops:
  17.6 10.3 %collective-permute-start = (bf16[4,32,8,128]{3,2,1,0:T(8,128)(2,1)}, bf16[4,32,8,128]{3,2,1,0:T(8,128)(2,1)S(1)}, u32[]{:S(2)}, u32[]{:S(2)}) collective-permute-start(bf16[4,32,8,128]{3,2,1,0:T(8,128)(2,1)} %get-tuple-element.31), channel_id=1, source_target_pairs={{0,2},{1,3},{2,0},{3,1},{4,6},{5,7},{6,4},{7,5},{8,10},{9,11},{10,... | collective-permute-start | bytes 786440 | tf_op jit(solution)/shard_map/ppermute | solution.py:336
  20.6 12.6 %collective-permute-start.1 = (bf16[4,32,8,128]{3,2,1,0:T(8,128)(2,1)}, bf16[4,32,8,128]{3,2,1,0:T(8,128)(2,1)S(1)}, u32[]{:S(2)}, u32[]{:S(2)}) collective-permute-start(bf16[4,32,8,128]{3,2,1,0:T(8,128)(2,1)} %get-tuple-element.32), channel_id=1, source_target_pairs={{0,3},{1,2},{2,1},{3,0},{4,7},{5,6},{6,5},{7,4},{8,11},{9,10},{10,... | collective-permute-start | bytes 786440 | tf_op jit(solution)/shard_map/ppermute | solution.py:336
  23.0 19.0 %collective-permute-start.4 = (bf16[4,3,128,128]{3,2,1,0:T(8,128)(2,1)}, bf16[4,3,128,128]{3,2,1,0:T(8,128)(2,1)S(1)}, u32[]{:S(2)}, u32[]{:S(2)}) collective-permute-start(bf16[4,3,128,128]{3,2,1,0:T(8,128)(2,1)} %get-tuple-element.39), channel_id=1, source_target_pairs={{0,2},{1,3},{2,0},{3,1},{4,6},{5,7},{6,4},{7,5},{8,10},{9,11},{10,... | collective-permute-start | bytes 1179656 | tf_op jit(solution)/shard_map/ppermute | solution.py:336
  24.2 25.9 %collective-permute-start.5 = (bf16[4,3,128,128]{3,2,1,0:T(8,128)(2,1)}, bf16[4,3,128,128]{3,2,1,0:T(8,128)(2,1)S(1)}, u32[]{:S(2)}, u32[]{:S(2)}) collective-permute-start(bf16[4,3,128,128]{3,2,1,0:T(8,128)(2,1)} %get-tuple-element.40), channel_id=1, source_target_pairs={{0,3},{1,2},{2,1},{3,0},{4,7},{5,6},{6,5},{7,4},{8,11},{9,10},{10,... | collective-permute-start | bytes 1179656 | tf_op jit(solution)/shard_map/ppermute | solution.py:336
  33.2 0.6 copy-start.10
  37.9 12.4 %collective-permute-start.6 = (bf16[4,2,128,128]{3,2,1,0:T(8,128)(2,1)}, bf16[4,2,128,128]{3,2,1,0:T(8,128)(2,1)S(1)}, u32[]{:S(2)}, u32[]{:S(2)}) collective-permute-start(bf16[4,2,128,128]{3,2,1,0:T(8,128)(2,1)} %get-tuple-element.41), channel_id=1, source_target_pairs={{0,1},{1,0},{2,3},{3,2},{4,5},{5,4},{6,7},{7,6},{8,9},{9,8},{10,11... | collective-permute-start | bytes 786440 | tf_op jit(solution)/shard_map/ppermute | solution.py:336
  38.1 12.5 %collective-permute-start.7 = (bf16[4,2,128,128]{3,2,1,0:T(8,128)(2,1)}, bf16[4,2,128,128]{3,2,1,0:T(8,128)(2,1)S(1)}, u32[]{:S(2)}, u32[]{:S(2)}) collective-permute-start(bf16[4,2,128,128]{3,2,1,0:T(8,128)(2,1)} %get-tuple-element.42), channel_id=1, source_target_pairs={{0,1},{1,0},{2,3},{3,2},{4,5},{5,4},{6,7},{7,6},{8,9},{9,8},{10,11... | collective-permute-start | bytes 786440 | tf_op jit(solution)/shard_map/ppermute | solution.py:336
  38.5 1.7 %collective-permute-start.2 = (bf16[1,2,128,128]{3,2,1,0:T(8,128)(2,1)}, bf16[1,2,128,128]{3,2,1,0:T(8,128)(2,1)S(1)}, u32[]{:S(2)}, u32[]{:S(2)}) collective-permute-start(bf16[1,2,128,128]{3,2,1,0:T(8,128)(2,1)} %get-tuple-element.35), channel_id=1, source_target_pairs={{0,1},{1,0},{2,3},{3,2},{4,5},{5,4},{6,7},{7,6},{8,9},{9,8},{10,11... | collective-permute-start | bytes 196616 | tf_op jit(solution)/shard_map/ppermute | solution.py:336
  40.2 23.1 %collective-permute-start.12 = (bf16[3,3,128,128]{3,2,1,0:T(8,128)(2,1)}, bf16[3,3,128,128]{3,2,1,0:T(8,128)(2,1)S(1)}, u32[]{:S(2)}, u32[]{:S(2)}) collective-permute-start(bf16[3,3,128,128]{3,2,1,0:T(8,128)(2,1)} %get-tuple-element.51), channel_id=1, source_target_pairs={{0,2},{1,3},{2,0},{3,1},{4,6},{5,7},{6,4},{7,5},{8,10},{9,11},{10,... | collective-permute-start | bytes 884744 | tf_op jit(solution)/shard_map/ppermute | solution.py:336
  42.0 21.2 %collective-permute-start.13 = (bf16[3,3,128,128]{3,2,1,0:T(8,128)(2,1)}, bf16[3,3,128,128]{3,2,1,0:T(8,128)(2,1)S(1)}, u32[]{:S(2)}, u32[]{:S(2)}) collective-permute-start(bf16[3,3,128,128]{3,2,1,0:T(8,128)(2,1)} %get-tuple-element.52), channel_id=1, source_target_pairs={{0,3},{1,2},{2,1},{3,0},{4,7},{5,6},{6,5},{7,4},{8,11},{9,10},{10,... | collective-permute-start | bytes 884744 | tf_op jit(solution)/shard_map/ppermute | solution.py:336
  50.1 11.8 %collective-permute-start.10 = (bf16[3,2,128,128]{3,2,1,0:T(8,128)(2,1)}, bf16[3,2,128,128]{3,2,1,0:T(8,128)(2,1)S(1)}, u32[]{:S(2)}, u32[]{:S(2)}) collective-permute-start(bf16[3,2,128,128]{3,2,1,0:T(8,128)(2,1)} %get-tuple-element.47), channel_id=1, source_target_pairs={{0,1},{1,0},{2,3},{3,2},{4,5},{5,4},{6,7},{7,6},{8,9},{9,8},{10,11... | collective-permute-start | bytes 589832 | tf_op jit(solution)/shard_map/ppermute | solution.py:336
  50.2 11.8 %collective-permute-start.11 = (bf16[3,2,128,128]{3,2,1,0:T(8,128)(2,1)}, bf16[3,2,128,128]{3,2,1,0:T(8,128)(2,1)S(1)}, u32[]{:S(2)}, u32[]{:S(2)}) collective-permute-start(bf16[3,2,128,128]{3,2,1,0:T(8,128)(2,1)} %get-tuple-element.48), channel_id=1, source_target_pairs={{0,1},{1,0},{2,3},{3,2},{4,5},{5,4},{6,7},{7,6},{8,9},{9,8},{10,11... | collective-permute-start | bytes 589832 | tf_op jit(solution)/shard_map/ppermute | solution.py:336
  50.6 9.1 %collective-permute-start.3 = (bf16[1,2,128,128]{3,2,1,0:T(8,128)(2,1)}, bf16[1,2,128,128]{3,2,1,0:T(8,128)(2,1)S(1)}, u32[]{:S(2)}, u32[]{:S(2)}) collective-permute-start(bf16[1,2,128,128]{3,2,1,0:T(8,128)(2,1)} %get-tuple-element.36), channel_id=1, source_target_pairs={{0,1},{1,0},{2,3},{3,2},{4,5},{5,4},{6,7},{7,6},{8,9},{9,8},{10,11... | collective-permute-start | bytes 196616 | tf_op jit(solution)/shard_map/ppermute | solution.py:336
  51.0 0.7 copy-start
  51.0 1.0 %copy-start.1 = (bf16[4,2,128,128]{3,2,1,0:T(8,128)(2,1)S(1)}, bf16[4,2,128,128]{3,2,1,0:T(8,128)(2,1)}, u32[]{:S(2)}) copy-start(bf16[4,2,128,128]{3,2,1,0:T(8,128)(2,1)} %get-tuple-element.43.refs_3_) | copy-start | bytes 786436
  51.0 1.0 %copy-start.2 = (bf16[4,2,128,128]{3,2,1,0:T(8,128)(2,1)S(1)}, bf16[4,2,128,128]{3,2,1,0:T(8,128)(2,1)}, u32[]{:S(2)}) copy-start(bf16[4,2,128,128]{3,2,1,0:T(8,128)(2,1)} %get-tuple-element.44.refs_4_) | copy-start | bytes 786436
  52.0 0.7 copy-start.9
  56.9 0.6 copy-start.7
  57.5 4.3 %copy-start.5 = (bf16[1,2,128,128]{3,2,1,0:T(8,128)(2,1)S(1)}, bf16[1,2,128,128]{3,2,1,0:T(8,128)(2,1)}, u32[]{:S(2)}) copy-start(bf16[1,2,128,128]{3,2,1,0:T(8,128)(2,1)} %get-tuple-element.37.refs_2_) | copy-start | bytes 196612
  57.5 4.3 %copy-start.6 = (bf16[1,2,128,128]{3,2,1,0:T(8,128)(2,1)S(1)}, bf16[1,2,128,128]{3,2,1,0:T(8,128)(2,1)}, u32[]{:S(2)}) copy-start(bf16[1,2,128,128]{3,2,1,0:T(8,128)(2,1)} %get-tuple-element.38.refs_3_) | copy-start | bytes 196612
  59.7 7.0 %collective-permute-start.8 = (bf16[1,3,128,128]{3,2,1,0:T(8,128)(2,1)}, bf16[1,3,128,128]{3,2,1,0:T(8,128)(2,1)S(1)}, u32[]{:S(2)}, u32[]{:S(2)}) collective-permute-start(bf16[1,3,128,128]{3,2,1,0:T(8,128)(2,1)} %get-tuple-element.45), channel_id=1, source_target_pairs={{0,2},{1,3},{2,0},{3,1},{4,6},{5,7},{6,4},{7,5},{8,10},{9,11},{10,... | collective-permute-start | bytes 294920 | tf_op jit(solution)/shard_map/ppermute | solution.py:336
  61.9 5.3 %collective-permute-start.9 = (bf16[1,3,128,128]{3,2,1,0:T(8,128)(2,1)}, bf16[1,3,128,128]{3,2,1,0:T(8,128)(2,1)S(1)}, u32[]{:S(2)}, u32[]{:S(2)}) collective-permute-start(bf16[1,3,128,128]{3,2,1,0:T(8,128)(2,1)} %get-tuple-element.46), channel_id=1, source_target_pairs={{0,3},{1,2},{2,1},{3,0},{4,7},{5,6},{6,5},{7,4},{8,11},{9,10},{10,... | collective-permute-start | bytes 294920 | tf_op jit(solution)/shard_map/ppermute | solution.py:336
  61.9 0.9 %copy-start.3 = (bf16[3,2,128,128]{3,2,1,0:T(8,128)(2,1)S(1)}, bf16[3,2,128,128]{3,2,1,0:T(8,128)(2,1)}, u32[]{:S(2)}) copy-start(bf16[3,2,128,128]{3,2,1,0:T(8,128)(2,1)} %get-tuple-element.49.refs_2_) | copy-start | bytes 589828
  61.9 1.0 %copy-start.4 = (bf16[3,2,128,128]{3,2,1,0:T(8,128)(2,1)S(1)}, bf16[3,2,128,128]{3,2,1,0:T(8,128)(2,1)}, u32[]{:S(2)}) copy-start(bf16[3,2,128,128]{3,2,1,0:T(8,128)(2,1)} %get-tuple-element.50.refs_3_) | copy-start | bytes 589828
  63.2 4.0 %copy-start.8 = (f32[4,128]{1,0:T(4,128)S(1)}, f32[4,128]{1,0:T(4,128)}, u32[]{:S(2)}) copy-start(f32[4,128]{1,0:T(4,128)} %copy-done.7) | copy-start | bytes 6148
  68.9 4.4 %collective-permute-start.14 = (f32[2,8,32]{2,1,0:T(8,128)S(1)}, f32[2,8,32]{2,1,0:T(8,128)S(1)}, u32[]{:S(2)}, u32[]{:S(2)}) collective-permute-start(f32[2,8,32]{2,1,0:T(8,128)S(1)} %get-tuple-element.54), channel_id=1, source_target_pairs={{0,4},{4,0},{8,12},{12,8},{1,5},{5,1},{9,13},{13,9},{2,6},{6,2},{1... | collective-permute-start | bytes 6152 | tf_op jit(solution)/shard_map/ppermute | solution.py:372
  69.7 4.5 %collective-permute-start.15 = (f32[2,8,32]{2,1,0:T(8,128)S(1)}, f32[2,8,32]{2,1,0:T(8,128)S(1)}, u32[]{:S(2)}, u32[]{:S(2)}) collective-permute-start(f32[2,8,32]{2,1,0:T(8,128)S(1)} %get-tuple-element.55), channel_id=1, source_target_pairs={{0,8},{4,12},{8,0},{12,4},{1,9},{5,13},{9,1},{13,5},{2,10},{6,14},... | collective-permute-start | bytes 6152 | tf_op jit(solution)/shard_map/ppermute | solution.py:372
  72.4 5.4 %collective-permute-start.16 = (f32[2,8,32]{2,1,0:T(8,128)S(1)}, f32[2,8,32]{2,1,0:T(8,128)S(1)}, u32[]{:S(2)}, u32[]{:S(2)}) collective-permute-start(f32[2,8,32]{2,1,0:T(8,128)S(1)} %get-tuple-element.56), channel_id=1, source_target_pairs={{0,12},{4,8},{8,4},{12,0},{1,13},{5,9},{9,5},{13,1},{2,14},{6,10},... | collective-permute-start | bytes 6152 | tf_op jit(solution)/shard_map/ppermute | solution.py:372

commit v5 on v4

--- a/solution.py
+++ b/solution.py
@@ -14,7 +14,7 @@
 TILE = 8
 EPS = 1e-06
 VMEM_LIMIT = 48 * 1024 * 1024
-PACK_VMEM_LIMIT = 60 * 1024 * 1024
+PACK_VMEM_LIMIT = 53 * 1024 * 1024
 
 
 def head_chunks(heads):
@@ -54,7 +54,7 @@
         functools.partial(cut_kernel, flips, heads),
         out_shape=[shape] * len(flips) + [jax.ShapeDtypeStruct((TILE, size), jnp.float32)],
         in_specs=[pl.BlockSpec(memory_space=pltpu.HBM)],
-        out_specs=[pl.BlockSpec(memory_space=pltpu.HBM)] * len(flips) + [pl.BlockSpec(memory_space=pltpu.VMEM)],
+        out_specs=[pl.BlockSpec(memory_space=pltpu.VMEM)] * (len(flips) + 1),
         scratch_shapes=[pltpu.SemaphoreType.DMA((len(flips),))],
         compiler_params=pltpu.CompilerParams(vmem_limit_bytes=PACK_VMEM_LIMIT),
         name="cut",

time: 78.7 us -> 61.5 us (0.78)
  Pallas kernels: 36.6 us -> 18 us
  waiting for transfers between devices: 23.1 us -> 25.5 us
  local copies, waits for them, and re-layouts: 3.34 us -> 2.08 us
    pallas_call x1, Pallas kernels: 17.6 us -> 1.05 us  [cut(): pl.pallas_call(functools.partial(cut_kernel, flips, heads), out_shape=[sh...]
    ppermute x14, waiting for transfers between devices: 18.5 us -> 20 us  [send(): return lax.ppermute(block, 'seq', [(s, s ^ flip) for s in range(sequence)])]
    unnamed x22 -> x10, local copies, waits for them, and re-layouts: 3.34 us -> 2.08 us
    pallas_call x3, Pallas kernels: 8.57 us -> 7.37 us  [pack(): pl.pallas_call(functools.partial(pack_kernel, plan, heads, len(after)), o...]
    pallas_call x3, Pallas kernels: 9.39 us -> 8.5 us  [attend(): pl.pallas_call(kernel, out_shape=shapes, in_specs=[pl.BlockSpec(memory_sp...]
    ppermute x3, waiting for transfers between devices: 4.56 us -> 5.43 us  [body(): lax.ppermute(parts[flip], 'dp', [(g, g ^ flip) for g in range(groups)])]
  transfers between devices with their start and end apart: 17 -> 17, of which waited for: 7 -> 9; matrix products, arithmetic and copies ran while one was open for 0% -> 0% of each run, Pallas kernels for 22% -> 25%
where the time goes in v5:
time: 61.5 us; the launch traced here: 61.2 us
  waiting for transfers between devices  25.5 us (41%)
  Pallas kernels  18 us (29%)
  starting transfers between devices  14.9 us (24%)
  local copies, waits for them, and re-layouts  2.08 us (3%)
    ppermute x14, waiting for transfers between devices, send(): return lax.ppermute(block, 'seq', [(s, s ^ flip) for s in range(sequence)])  20 us
    ppermute x14, starting transfers between devices, send(): return lax.ppermute(block, 'seq', [(s, s ^ flip) for s in range(sequence)])  10.5 us
    pallas_call x3, Pallas kernels, attend(): pl.pallas_call(kernel, out_shape=shapes, in_specs=[pl.BlockSpec(memory_sp...  8.5 us
    pallas_call x3, Pallas kernels, pack(): pl.pallas_call(functools.partial(pack_kernel, plan, heads, len(after)), o...  7.37 us
    ppermute x3, waiting for transfers between devices, body(): lax.ppermute(parts[flip], 'dp', [(g, g ^ flip) for g in range(groups)])  5.43 us
    ppermute x3, starting transfers between devices, body(): lax.ppermute(parts[flip], 'dp', [(g, g ^ flip) for g in range(groups)])  4.4 us
    unnamed x10, local copies, waits for them, and re-layouts  2.08 us
  transfers between devices with their start and end apart: 17, of which 9 were waited for; matrix products, arithmetic and copies ran while one was open for 0% of the time, Pallas kernels for 25%

profile of v5, /device:TPU:0, one launch (start us, length us, event | category | flops | bytes accessed | tf_op | source)
XLA Modules:
  0.0 61.2 jit_solution(16003638316766863711)
XLA Ops:
  0.0 1.1 %cut.1 = (bf16[4,32,8,128]{3,2,1,0:T(8,128)(2,1)S(1)}, bf16[4,32,8,128]{3,2,1,0:T(8,128)(2,1)S(1)}, f32[8,128]{1,0:T(8,128)S(1)}) custom-call(bf16[1,4,32,32,128]{4,3,2,1,0:T(8,128)(2,1)} %refs_2_.5), custom_call_target="tpu_custom_call" | custom-call | tf_op jit(solution)/shard_map/cut/pallas_call | solution.py:53
  1.1 3.0 %collective-permute-start = (bf16[4,32,8,128]{3,2,1,0:T(8,128)(2,1)S(1)}, bf16[4,32,8,128]{3,2,1,0:T(8,128)(2,1)S(1)}, u32[]{:S(2)}, u32[]{:S(2)}) collective-permute-start(bf16[4,32,8,128]{3,2,1,0:T(8,128)(2,1)S(1)} %get-tuple-element.31), channel_id=1, source_target_pairs={{0,2},{1,3},{2,0},{3,1},{4,6},{5,7},{6,4},{7,5},{8,10},{9,11},{10,... | collective-permute-start | bytes 786440 | tf_op jit(solution)/shard_map/ppermute | solution.py:336
  4.1 0.0 collective-permute-start.1
  4.1 1.5 %pack.3 = (bf16[4,3,128,128]{3,2,1,0:T(8,128)(2,1)S(1)}, bf16[4,3,128,128]{3,2,1,0:T(8,128)(2,1)S(1)}, f32[8,128]{1,0:T(8,128)S(1)}) custom-call(bf16[1,4,32,32,128]{4,3,2,1,0:T(8,128)(2,1)} %refs_0_.5, bf16[1,4,32,32,128]{4,3,2,1,0:T(8,128)(2,1)} %refs_1_.5, bf16[1,4,32,32,128]{4,3,2,1,0:T(8,128)(2,1)} %refs_2_.5, bf16[1,4,32,32,128]{4,3,2,1,0:T(8,128)(2,1)} %refs_3_.5, ...), custom_call_target="tpu_custom_call" | custom-call | flops 2097152 | bytes 4194304 | tf_op jit(solution)/shard_map/pack/pallas_call | solution.py:145
  5.6 1.2 %collective-permute-start.4 = (bf16[4,3,128,128]{3,2,1,0:T(8,128)(2,1)S(1)}, bf16[4,3,128,128]{3,2,1,0:T(8,128)(2,1)S(1)}, u32[]{:S(2)}, u32[]{:S(2)}) collective-permute-start(bf16[4,3,128,128]{3,2,1,0:T(8,128)(2,1)S(1)} %get-tuple-element.39), channel_id=1, source_target_pairs={{0,2},{1,3},{2,0},{3,1},{4,6},{5,7},{6,4},{7,5},{8,10},{9,11},{10,... | collective-permute-start | bytes 1179656 | tf_op jit(solution)/shard_map/ppermute | solution.py:336
  6.9 0.6 %collective-permute-start.5 = (bf16[4,3,128,128]{3,2,1,0:T(8,128)(2,1)S(1)}, bf16[4,3,128,128]{3,2,1,0:T(8,128)(2,1)S(1)}, u32[]{:S(2)}, u32[]{:S(2)}) collective-permute-start(bf16[4,3,128,128]{3,2,1,0:T(8,128)(2,1)S(1)} %get-tuple-element.40), channel_id=1, source_target_pairs={{0,3},{1,2},{2,1},{3,0},{4,7},{5,6},{6,5},{7,4},{8,11},{9,10},{10,... | collective-permute-start | bytes 1179656 | tf_op jit(solution)/shard_map/ppermute | solution.py:336
  7.5 3.7 %collective-permute-done.refs_0_ = bf16[4,32,8,128]{3,2,1,0:T(8,128)(2,1)S(1)} collective-permute-done((bf16[4,32,8,128]{3,2,1,0:T(8,128)(2,1)S(1)}, bf16[4,32,8,128]{3,2,1,0:T(8,128)(2,1)S(1)}, u32[]{:S(2)}, u32[]{:S(2)}) %collective-permute-start) | collective-permute-done | bytes 262176 | tf_op jit(solution)/shard_map/ppermute | solution.py:336
  11.2 5.2 %collective-permute-done.1.refs_1_ = bf16[4,32,8,128]{3,2,1,0:T(8,128)(2,1)S(1)} collective-permute-done((bf16[4,32,8,128]{3,2,1,0:T(8,128)(2,1)S(1)}, bf16[4,32,8,128]{3,2,1,0:T(8,128)(2,1)S(1)}, u32[]{:S(2)}, u32[]{:S(2)}) %collective-permute-start.1) | collective-permute-done | bytes 262176 | tf_op jit(solution)/shard_map/ppermute | solution.py:336
  16.4 3.8 %pack.4 = (bf16[3,3,128,128]{3,2,1,0:T(8,128)(2,1)}, bf16[3,3,128,128]{3,2,1,0:T(8,128)(2,1)}, bf16[4,2,128,128]{3,2,1,0:T(8,128)(2,1)}, bf16[3,2,128,128]{3,2,1...) custom-call(bf16[1,4,32,32,128]{4,3,2,1,0:T(8,128)(2,1)} %refs_0_.5,, ...), custom_call_target="tpu_custom_call" | custom-call | flops 6291456 | bytes 12582912 | tf_op jit(solution)/shard_map/pack/pallas_call | solution.py:145
  20.2 0.3 collective-permute-start.6
  20.5 0.3 collective-permute-start.7
  20.8 0.2 collective-permute-start.2
  21.0 1.2 %collective-permute-done.2.refs_0_ = bf16[1,2,128,128]{3,2,1,0:T(8,128)(2,1)S(1)} collective-permute-done((bf16[1,2,128,128]{3,2,1,0:T(8,128)(2,1)S(1)}, bf16[1,2,128,128]{3,2,1,0:T(8,128)(2,1)S(1)}, u32[]{:S(2)}, u32[]{:S(2)}) %collective-permute-start.2) | collective-permute-done | bytes 65568 | tf_op jit(solution)/shard_map/ppermute | solution.py:336
  22.2 1.9 %collective-permute-start.12 = (bf16[3,3,128,128]{3,2,1,0:T(8,128)(2,1)}, bf16[3,3,128,128]{3,2,1,0:T(8,128)(2,1)S(1)}, u32[]{:S(2)}, u32[]{:S(2)}) collective-permute-start(bf16[3,3,128,128]{3,2,1,0:T(8,128)(2,1)} %get-tuple-element.51), channel_id=1, source_target_pairs={{0,2},{1,3},{2,0},{3,1},{4,6},{5,7},{6,4},{7,5},{8,10},{9,11},{10,... | collective-permute-start | bytes 884744 | tf_op jit(solution)/shard_map/ppermute | solution.py:336
  24.2 1.1 %collective-permute-done.4.refs_0_ = bf16[4,3,128,128]{3,2,1,0:T(8,128)(2,1)S(1)} collective-permute-done((bf16[4,3,128,128]{3,2,1,0:T(8,128)(2,1)S(1)}, bf16[4,3,128,128]{3,2,1,0:T(8,128)(2,1)S(1)}, u32[]{:S(2)}, u32[]{:S(2)}) %collective-permute-start.4) | collective-permute-done | bytes 393248 | tf_op jit(solution)/shard_map/ppermute | solution.py:336
  25.2 0.0 collective-permute-start.13
  25.2 8.0 %collective-permute-done.5.refs_1_ = bf16[4,3,128,128]{3,2,1,0:T(8,128)(2,1)S(1)} collective-permute-done((bf16[4,3,128,128]{3,2,1,0:T(8,128)(2,1)S(1)}, bf16[4,3,128,128]{3,2,1,0:T(8,128)(2,1)S(1)}, u32[]{:S(2)}, u32[]{:S(2)}) %collective-permute-start.5) | collective-permute-done | bytes 393248 | tf_op jit(solution)/shard_map/ppermute | solution.py:336
  33.2 0.2 collective-permute-start.10
  33.5 0.0 collective-permute-done.6.refs_1_
  33.5 0.3 collective-permute-start.11
  33.8 0.2 collective-permute-start.3
  34.0 0.2 arrange.1.values
  34.2 0.0 copy-start
  34.3 0.7 %copy-done = f32[2,8,128]{2,1,0:T(8,128)S(1)} copy-done((f32[2,8,128]{2,1,0:T(8,128)S(1)}, f32[2,8,128]{2,1,0:T(8,128)}, u32[]{:S(2)}) %copy-start) | copy-done | bytes 8216
  34.9 0.3 copy-done.1
  35.2 0.1 copy-done.2
  35.3 0.4 prepare.4.close
  35.7 0.3 copy-done.4
  36.0 3.7 %attend.3.refs_4_.refs_2_ = f32[4,128]{1,0:T(4,128)S(1)} custom-call(s32[4,4]{1,0:T(4,128)S(1)} %copy-done.4, f32[2,8,128]{2,1,0:T(8,128)S(1)} %copy-done, bf16[8,4,64,128]{3,2,1,0:T(8,128)(2,1)S(1)} %arrange.1.values, bf16[4,4,4,64,128]{4,3,2,1,0:T(8,128)(2,1)S(1)} %prepare.4.close, bf16[4,3,128,128]{3,2,1,0:T(8,128)(2,1)S(1)} %collective-permute-done.4.refs_0_, ...), custom_call_target="tpu_custom_call" | custom-call | flops 402653184 | bytes 1048576 | tf_op jit(solution)/shard_map/attend/pallas_call | solution.py:297
  39.7 2.1 %pack.5 = (bf16[1,3,128,128]{3,2,1,0:T(8,128)(2,1)S(1)}, bf16[1,3,128,128]{3,2,1,0:T(8,128)(2,1)S(1)}, f32[8,128]{1,0:T(8,128)}) custom-call(bf16[1,4,32,32,128]{4,3,2,1,0:T(8,128)(2,1)} %refs_0_.5, bf16[1,4,32,32,128]{4,3,2,1,0:T(8,128)(2,1)} %refs_1_.5, bf16[1,4,32,32,128]{4,3,2,1,0:T(8,128)(2,1)} %refs_2_.5, bf16[1,4,32,32,128]{4,3,2,1,0:T(8,128)(2,1)} %refs_3_.5, ...), custom_call_target="tpu_custom_call" | custom-call | flops 2097152 | bytes 4194304 | tf_op jit(solution)/shard_map/pack/pallas_call | solution.py:145
  41.8 0.0 collective-permute-done.3.refs_1_
  41.8 2.1 %collective-permute-start.8 = (bf16[1,3,128,128]{3,2,1,0:T(8,128)(2,1)S(1)}, bf16[1,3,128,128]{3,2,1,0:T(8,128)(2,1)S(1)}, u32[]{:S(2)}, u32[]{:S(2)}) collective-permute-start(bf16[1,3,128,128]{3,2,1,0:T(8,128)(2,1)S(1)} %get-tuple-element.45), channel_id=1, source_target_pairs={{0,2},{1,3},{2,0},{3,1},{4,6},{5,7},{6,4},{7,5},{8,10},{9,11},{10,... | collective-permute-start | bytes 294920 | tf_op jit(solution)/shard_map/ppermute | solution.py:336
  43.9 0.0 collective-permute-done.10.refs_0_
  43.9 0.0 collective-permute-start.9
  43.9 0.2 prepare.3.close
  44.1 0.0 collective-permute-done.11.refs_1_
  44.1 0.8 %copy-done.3 = bf16[3,2,128,128]{3,2,1,0:T(8,128)(2,1)S(1)} copy-done((bf16[3,2,128,128]{3,2,1,0:T(8,128)(2,1)S(1)}, bf16[3,2,128,128]{3,2,1,0:T(8,128)(2,1)}, u32[]{:S(2)}) %copy-start.3) | copy-done | bytes 196632
  44.9 0.3 prepare.5.close
  45.2 0.3 collective-permute-done.13.refs_1_
  45.4 3.1 %attend.4.refs_3_ = f32[3,128]{1,0:T(4,128)S(1)} custom-call(s32[4,4]{1,0:T(4,128)S(1)} %copy-done.4, f32[2,8,128]{2,1,0:T(8,128)S(1)} %copy-done, bf16[8,4,64,128]{3,2,1,0:T(8,128)(2,1)S(1)} %arrange.1.values, bf16[3,4,4,64,128]{4,3,2,1,0:T(8,128)(2,1)S(1)} %prepare.5.close, bf16[3,3,128,128]{3,2,1,0:T(8,128)(2,1)S(1)} %collective-permute-done.12.refs_0_, ...), custom_call_target="tpu_custom_call" | custom-call | flops 301989888 | bytes 786432 | tf_op jit(solution)/shard_map/attend/pallas_call | solution.py:297
  48.6 0.5 collective-permute-done.9.refs_1_
  49.1 1.6 %attend.5 = (f32[2,8,32]{2,1,0:T(8,128)S(1)}, f32[2,8,32]{2,1,0:T(8,128)S(1)}, f32[2,8,32]{2,1,0:T(8,128)S(1)}, f32[2,8,32]{2,1,0:T(8,128)S(1)}) custom-call(s32[4,4]{1,0:T(4,128)S(1)} %copy-done.4, f32[2,8,128]{2,1,0:T(8,128)S(1)} %copy-done, bf16[8,4,64,128]{3,2,1,0:T(8,128)(2,1)S(1)} %arrange.1.values, bf16[1,4,4,64,128]{4,3,2,1,0:T(8,128)(2,1)S(1)} %prepare.3.close, ...), custom_call_target="tpu_custom_call" | custom-call | flops 100663296 | bytes 262144 | tf_op jit(solution)/shard_map/attend/pallas_call | solution.py:297
  50.8 1.6 %collective-permute-start.14 = (f32[2,8,32]{2,1,0:T(8,128)S(1)}, f32[2,8,32]{2,1,0:T(8,128)S(1)}, u32[]{:S(2)}, u32[]{:S(2)}) collective-permute-start(f32[2,8,32]{2,1,0:T(8,128)S(1)} %get-tuple-element.54), channel_id=1, source_target_pairs={{0,4},{4,0},{8,12},{12,8},{1,5},{5,1},{9,13},{13,9},{2,6},{6,2},{1... | collective-permute-start | bytes 6152 | tf_op jit(solution)/shard_map/ppermute | solution.py:372
  52.4 2.7 %collective-permute-start.15 = (f32[2,8,32]{2,1,0:T(8,128)S(1)}, f32[2,8,32]{2,1,0:T(8,128)S(1)}, u32[]{:S(2)}, u32[]{:S(2)}) collective-permute-start(f32[2,8,32]{2,1,0:T(8,128)S(1)} %get-tuple-element.55), channel_id=1, source_target_pairs={{0,8},{4,12},{8,0},{12,4},{1,9},{5,13},{9,1},{13,5},{2,10},{6,14},... | collective-permute-start | bytes 6152 | tf_op jit(solution)/shard_map/ppermute | solution.py:372
  55.1 0.0 collective-permute-start.16
  55.2 1.8 %collective-permute-done.15 = f32[2,8,32]{2,1,0:T(8,128)S(1)} collective-permute-done((f32[2,8,32]{2,1,0:T(8,128)S(1)}, f32[2,8,32]{2,1,0:T(8,128)S(1)}, u32[]{:S(2)}, u32[]{:S(2)}) %collective-permute-start.15) | collective-permute-done | bytes 2080 | tf_op jit(solution)/shard_map/ppermute | solution.py:372
  57.0 3.6 %collective-permute-done.16 = f32[2,8,32]{2,1,0:T(8,128)S(1)} collective-permute-done((f32[2,8,32]{2,1,0:T(8,128)S(1)}, f32[2,8,32]{2,1,0:T(8,128)S(1)}, u32[]{:S(2)}, u32[]{:S(2)}) %collective-permute-start.16) | collective-permute-done | bytes 2080 | tf_op jit(solution)/shard_map/ppermute | solution.py:372
  60.6 0.6 add_add_fusion
  (10 shorter events, 0.0 us)
Async XLA Ops:
  1.1 10.1 %collective-permute-start = (bf16[4,32,8,128]{3,2,1,0:T(8,128)(2,1)S(1)}, bf16[4,32,8,128]{3,2,1,0:T(8,128)(2,1)S(1)}, u32[]{:S(2)}, u32[]{:S(2)}) collective-permute-start(bf16[4,32,8,128]{3,2,1,0:T(8,128)(2,1)S(1)} %get-tuple-element.31), channel_id=1, source_target_pairs={{0,2},{1,3},{2,0},{3,1},{4,6},{5,7},{6,4},{7,5},{8,10},{9,11},{10,... | collective-permute-start | bytes 786440 | tf_op jit(solution)/shard_map/ppermute | solution.py:336
  4.1 12.3 %collective-permute-start.1 = (bf16[4,32,8,128]{3,2,1,0:T(8,128)(2,1)S(1)}, bf16[4,32,8,128]{3,2,1,0:T(8,128)(2,1)S(1)}, u32[]{:S(2)}, u32[]{:S(2)}) collective-permute-start(bf16[4,32,8,128]{3,2,1,0:T(8,128)(2,1)S(1)} %get-tuple-element.32), channel_id=1, source_target_pairs={{0,3},{1,2},{2,1},{3,0},{4,7},{5,6},{6,5},{7,4},{8,11},{9,10},{10,... | collective-permute-start | bytes 786440 | tf_op jit(solution)/shard_map/ppermute | solution.py:336
  5.6 19.6 %collective-permute-start.4 = (bf16[4,3,128,128]{3,2,1,0:T(8,128)(2,1)S(1)}, bf16[4,3,128,128]{3,2,1,0:T(8,128)(2,1)S(1)}, u32[]{:S(2)}, u32[]{:S(2)}) collective-permute-start(bf16[4,3,128,128]{3,2,1,0:T(8,128)(2,1)S(1)} %get-tuple-element.39), channel_id=1, source_target_pairs={{0,2},{1,3},{2,0},{3,1},{4,6},{5,7},{6,4},{7,5},{8,10},{9,11},{10,... | collective-permute-start | bytes 1179656 | tf_op jit(solution)/shard_map/ppermute | solution.py:336
  6.9 26.4 %collective-permute-start.5 = (bf16[4,3,128,128]{3,2,1,0:T(8,128)(2,1)S(1)}, bf16[4,3,128,128]{3,2,1,0:T(8,128)(2,1)S(1)}, u32[]{:S(2)}, u32[]{:S(2)}) collective-permute-start(bf16[4,3,128,128]{3,2,1,0:T(8,128)(2,1)S(1)} %get-tuple-element.40), channel_id=1, source_target_pairs={{0,3},{1,2},{2,1},{3,0},{4,7},{5,6},{6,5},{7,4},{8,11},{9,10},{10,... | collective-permute-start | bytes 1179656 | tf_op jit(solution)/shard_map/ppermute | solution.py:336
  20.2 13.3 %collective-permute-start.6 = (bf16[4,2,128,128]{3,2,1,0:T(8,128)(2,1)}, bf16[4,2,128,128]{3,2,1,0:T(8,128)(2,1)S(1)}, u32[]{:S(2)}, u32[]{:S(2)}) collective-permute-start(bf16[4,2,128,128]{3,2,1,0:T(8,128)(2,1)} %get-tuple-element.41), channel_id=1, source_target_pairs={{0,1},{1,0},{2,3},{3,2},{4,5},{5,4},{6,7},{7,6},{8,9},{9,8},{10,11... | collective-permute-start | bytes 786440 | tf_op jit(solution)/shard_map/ppermute | solution.py:336
  20.5 13.3 %collective-permute-start.7 = (bf16[4,2,128,128]{3,2,1,0:T(8,128)(2,1)}, bf16[4,2,128,128]{3,2,1,0:T(8,128)(2,1)S(1)}, u32[]{:S(2)}, u32[]{:S(2)}) collective-permute-start(bf16[4,2,128,128]{3,2,1,0:T(8,128)(2,1)} %get-tuple-element.42), channel_id=1, source_target_pairs={{0,1},{1,0},{2,3},{3,2},{4,5},{5,4},{6,7},{7,6},{8,9},{9,8},{10,11... | collective-permute-start | bytes 786440 | tf_op jit(solution)/shard_map/ppermute | solution.py:336
  20.8 1.5 %collective-permute-start.2 = (bf16[1,2,128,128]{3,2,1,0:T(8,128)(2,1)S(1)}, bf16[1,2,128,128]{3,2,1,0:T(8,128)(2,1)S(1)}, u32[]{:S(2)}, u32[]{:S(2)}) collective-permute-start(bf16[1,2,128,128]{3,2,1,0:T(8,128)(2,1)S(1)} %get-tuple-element.35), channel_id=1, source_target_pairs={{0,1},{1,0},{2,3},{3,2},{4,5},{5,4},{6,7},{7,6},{8,9},{9,8},{10,11... | collective-permute-start | bytes 196616 | tf_op jit(solution)/shard_map/ppermute | solution.py:336
  22.2 22.9 %collective-permute-start.12 = (bf16[3,3,128,128]{3,2,1,0:T(8,128)(2,1)}, bf16[3,3,128,128]{3,2,1,0:T(8,128)(2,1)S(1)}, u32[]{:S(2)}, u32[]{:S(2)}) collective-permute-start(bf16[3,3,128,128]{3,2,1,0:T(8,128)(2,1)} %get-tuple-element.51), channel_id=1, source_target_pairs={{0,2},{1,3},{2,0},{3,1},{4,6},{5,7},{6,4},{7,5},{8,10},{9,11},{10,... | collective-permute-start | bytes 884744 | tf_op jit(solution)/shard_map/ppermute | solution.py:336
  25.2 20.2 %collective-permute-start.13 = (bf16[3,3,128,128]{3,2,1,0:T(8,128)(2,1)}, bf16[3,3,128,128]{3,2,1,0:T(8,128)(2,1)S(1)}, u32[]{:S(2)}, u32[]{:S(2)}) collective-permute-start(bf16[3,3,128,128]{3,2,1,0:T(8,128)(2,1)} %get-tuple-element.52), channel_id=1, source_target_pairs={{0,3},{1,2},{2,1},{3,0},{4,7},{5,6},{6,5},{7,4},{8,11},{9,10},{10,... | collective-permute-start | bytes 884744 | tf_op jit(solution)/shard_map/ppermute | solution.py:336
  33.2 10.7 %collective-permute-start.10 = (bf16[3,2,128,128]{3,2,1,0:T(8,128)(2,1)S(1)}, bf16[3,2,128,128]{3,2,1,0:T(8,128)(2,1)S(1)}, u32[]{:S(2)}, u32[]{:S(2)}) collective-permute-start(bf16[3,2,128,128]{3,2,1,0:T(8,128)(2,1)S(1)} %get-tuple-element.47), channel_id=1, source_target_pairs={{0,1},{1,0},{2,3},{3,2},{4,5},{5,4},{6,7},{7,6},{8,9},{9,8},{10,11... | collective-permute-start | bytes 589832 | tf_op jit(solution)/shard_map/ppermute | solution.py:336
  33.5 10.6 %collective-permute-start.11 = (bf16[3,2,128,128]{3,2,1,0:T(8,128)(2,1)S(1)}, bf16[3,2,128,128]{3,2,1,0:T(8,128)(2,1)S(1)}, u32[]{:S(2)}, u32[]{:S(2)}) collective-permute-start(bf16[3,2,128,128]{3,2,1,0:T(8,128)(2,1)S(1)} %get-tuple-element.48), channel_id=1, source_target_pairs={{0,1},{1,0},{2,3},{3,2},{4,5},{5,4},{6,7},{7,6},{8,9},{9,8},{10,11... | collective-permute-start | bytes 589832 | tf_op jit(solution)/shard_map/ppermute | solution.py:336
  33.8 8.0 %collective-permute-start.3 = (bf16[1,2,128,128]{3,2,1,0:T(8,128)(2,1)S(1)}, bf16[1,2,128,128]{3,2,1,0:T(8,128)(2,1)S(1)}, u32[]{:S(2)}, u32[]{:S(2)}) collective-permute-start(bf16[1,2,128,128]{3,2,1,0:T(8,128)(2,1)S(1)} %get-tuple-element.36), channel_id=1, source_target_pairs={{0,1},{1,0},{2,3},{3,2},{4,5},{5,4},{6,7},{7,6},{8,9},{9,8},{10,11... | collective-permute-start | bytes 196616 | tf_op jit(solution)/shard_map/ppermute | solution.py:336
  34.2 0.7 %copy-start = (f32[2,8,128]{2,1,0:T(8,128)S(1)}, f32[2,8,128]{2,1,0:T(8,128)}, u32[]{:S(2)}) copy-start(f32[2,8,128]{2,1,0:T(8,128)} %gains.11) | copy-start | bytes 24580
  34.3 1.0 %copy-start.1 = (bf16[4,2,128,128]{3,2,1,0:T(8,128)(2,1)S(1)}, bf16[4,2,128,128]{3,2,1,0:T(8,128)(2,1)}, u32[]{:S(2)}) copy-start(bf16[4,2,128,128]{3,2,1,0:T(8,128)(2,1)} %get-tuple-element.43.refs_3_) | copy-start | bytes 786436
  34.3 1.0 %copy-start.2 = (bf16[4,2,128,128]{3,2,1,0:T(8,128)(2,1)S(1)}, bf16[4,2,128,128]{3,2,1,0:T(8,128)(2,1)}, u32[]{:S(2)}) copy-start(bf16[4,2,128,128]{3,2,1,0:T(8,128)(2,1)} %get-tuple-element.44.refs_4_) | copy-start | bytes 786436
  35.3 0.7 %copy-start.4 = (s32[4,4]{1,0:T(4,128)S(1)}, s32[4,4]{1,0:T(4,128)}, u32[]{:S(2)}) copy-start(s32[4,4]{1,0:T(4,128)} %units.5) | copy-start | bytes 196
  41.8 6.8 %collective-permute-start.8 = (bf16[1,3,128,128]{3,2,1,0:T(8,128)(2,1)S(1)}, bf16[1,3,128,128]{3,2,1,0:T(8,128)(2,1)S(1)}, u32[]{:S(2)}, u32[]{:S(2)}) collective-permute-start(bf16[1,3,128,128]{3,2,1,0:T(8,128)(2,1)S(1)} %get-tuple-element.45), channel_id=1, source_target_pairs={{0,2},{1,3},{2,0},{3,1},{4,6},{5,7},{6,4},{7,5},{8,10},{9,11},{10,... | collective-permute-start | bytes 294920 | tf_op jit(solution)/shard_map/ppermute | solution.py:336
  43.9 5.2 %collective-permute-start.9 = (bf16[1,3,128,128]{3,2,1,0:T(8,128)(2,1)S(1)}, bf16[1,3,128,128]{3,2,1,0:T(8,128)(2,1)S(1)}, u32[]{:S(2)}, u32[]{:S(2)}) collective-permute-start(bf16[1,3,128,128]{3,2,1,0:T(8,128)(2,1)S(1)} %get-tuple-element.46), channel_id=1, source_target_pairs={{0,3},{1,2},{2,1},{3,0},{4,7},{5,6},{6,5},{7,4},{8,11},{9,10},{10,... | collective-permute-start | bytes 294920 | tf_op jit(solution)/shard_map/ppermute | solution.py:336
  43.9 0.9 %copy-start.3 = (bf16[3,2,128,128]{3,2,1,0:T(8,128)(2,1)S(1)}, bf16[3,2,128,128]{3,2,1,0:T(8,128)(2,1)}, u32[]{:S(2)}) copy-start(bf16[3,2,128,128]{3,2,1,0:T(8,128)(2,1)} %get-tuple-element.50.refs_3_) | copy-start | bytes 589828
  50.8 4.4 %collective-permute-start.14 = (f32[2,8,32]{2,1,0:T(8,128)S(1)}, f32[2,8,32]{2,1,0:T(8,128)S(1)}, u32[]{:S(2)}, u32[]{:S(2)}) collective-permute-start(f32[2,8,32]{2,1,0:T(8,128)S(1)} %get-tuple-element.54), channel_id=1, source_target_pairs={{0,4},{4,0},{8,12},{12,8},{1,5},{5,1},{9,13},{13,9},{2,6},{6,2},{1... | collective-permute-start | bytes 6152 | tf_op jit(solution)/shard_map/ppermute | solution.py:372
  52.4 4.5 %collective-permute-start.15 = (f32[2,8,32]{2,1,0:T(8,128)S(1)}, f32[2,8,32]{2,1,0:T(8,128)S(1)}, u32[]{:S(2)}, u32[]{:S(2)}) collective-permute-start(f32[2,8,32]{2,1,0:T(8,128)S(1)} %get-tuple-element.55), channel_id=1, source_target_pairs={{0,8},{4,12},{8,0},{12,4},{1,9},{5,13},{9,1},{13,5},{2,10},{6,14},... | collective-permute-start | bytes 6152 | tf_op jit(solution)/shard_map/ppermute | solution.py:372
  55.1 5.4 %collective-permute-start.16 = (f32[2,8,32]{2,1,0:T(8,128)S(1)}, f32[2,8,32]{2,1,0:T(8,128)S(1)}, u32[]{:S(2)}, u32[]{:S(2)}) collective-permute-start(f32[2,8,32]{2,1,0:T(8,128)S(1)} %get-tuple-element.56), channel_id=1, source_target_pairs={{0,12},{4,8},{8,4},{12,0},{1,13},{5,9},{9,5},{13,1},{2,14},{6,10},... | collective-permute-start | bytes 6152 | tf_op jit(solution)/shard_map/ppermute | solution.py:372

commit v6 on v5

--- a/solution.py
+++ b/solution.py
@@ -368,7 +368,7 @@
         low, high - low, clip_units, norm_gains, values, prepared[-1], received, sums, list(range(groups))
     )
     result = parts[0]
-    for flip in range(1, groups):
+    for flip in reversed(range(1, groups)):
         result = result + lax.ppermute(parts[flip], "dp", [(g, g ^ flip) for g in range(groups)])
     return result
 

time: 61.5 us -> 60 us (0.976)
  waiting for transfers between devices: 25.5 us -> 24 us
    ppermute x3, waiting for transfers between devices: 5.43 us -> 3.87 us  [body(): lax.ppermute(parts[flip], 'dp', [(g, g ^ flip) for g in range(groups)])]
where the time goes in v6:
time: 60 us; the launch traced here: 59.5 us
  waiting for transfers between devices  24 us (40%)
  Pallas kernels  17.7 us (30%)
  starting transfers between devices  14.9 us (25%)
  local copies, waits for them, and re-layouts  2.08 us (3%)
  other arithmetic  0.6 us (1%)
    ppermute x14, waiting for transfers between devices, send(): return lax.ppermute(block, 'seq', [(s, s ^ flip) for s in range(sequence)])  20.2 us
    ppermute x14, starting transfers between devices, send(): return lax.ppermute(block, 'seq', [(s, s ^ flip) for s in range(sequence)])  10.5 us
    pallas_call x3, Pallas kernels, attend(): pl.pallas_call(kernel, out_shape=shapes, in_specs=[pl.BlockSpec(memory_sp...  8.25 us
    pallas_call x3, Pallas kernels, pack(): pl.pallas_call(functools.partial(pack_kernel, plan, heads, len(after)), o...  7.37 us
    ppermute x3, starting transfers between devices, body(): lax.ppermute(parts[flip], 'dp', [(g, g ^ flip) for g in range(groups)])  4.4 us
    ppermute x3, waiting for transfers between devices, body(): lax.ppermute(parts[flip], 'dp', [(g, g ^ flip) for g in range(groups)])  3.87 us
    unnamed x10, local copies, waits for them, and re-layouts  2.08 us
  transfers between devices with their start and end apart: 17, of which 9 were waited for; matrix products, arithmetic and copies ran while one was open for 0% of the time, Pallas kernels for 25%

profile of v6, /device:TPU:0, one launch (start us, length us, event | category | flops | bytes accessed | tf_op | source)
XLA Modules:
  0.0 59.5 jit_solution(14179831990218885506)
XLA Ops:
  0.0 1.1 %cut.1 = (bf16[4,32,8,128]{3,2,1,0:T(8,128)(2,1)S(1)}, bf16[4,32,8,128]{3,2,1,0:T(8,128)(2,1)S(1)}, f32[8,128]{1,0:T(8,128)S(1)}) custom-call(bf16[1,4,32,32,128]{4,3,2,1,0:T(8,128)(2,1)} %refs_2_.5), custom_call_target="tpu_custom_call" | custom-call | tf_op jit(solution)/shard_map/cut/pallas_call | solution.py:53
  1.1 3.0 %collective-permute-start = (bf16[4,32,8,128]{3,2,1,0:T(8,128)(2,1)S(1)}, bf16[4,32,8,128]{3,2,1,0:T(8,128)(2,1)S(1)}, u32[]{:S(2)}, u32[]{:S(2)}) collective-permute-start(bf16[4,32,8,128]{3,2,1,0:T(8,128)(2,1)S(1)} %get-tuple-element.31), channel_id=1, source_target_pairs={{0,2},{1,3},{2,0},{3,1},{4,6},{5,7},{6,4},{7,5},{8,10},{9,11},{10,... | collective-permute-start | bytes 786440 | tf_op jit(solution)/shard_map/ppermute | solution.py:336
  4.1 0.0 collective-permute-start.1
  4.1 1.5 %pack.3 = (bf16[4,3,128,128]{3,2,1,0:T(8,128)(2,1)S(1)}, bf16[4,3,128,128]{3,2,1,0:T(8,128)(2,1)S(1)}, f32[8,128]{1,0:T(8,128)S(1)}) custom-call(bf16[1,4,32,32,128]{4,3,2,1,0:T(8,128)(2,1)} %refs_0_.5, bf16[1,4,32,32,128]{4,3,2,1,0:T(8,128)(2,1)} %refs_1_.5, bf16[1,4,32,32,128]{4,3,2,1,0:T(8,128)(2,1)} %refs_2_.5, bf16[1,4,32,32,128]{4,3,2,1,0:T(8,128)(2,1)} %refs_3_.5, ...), custom_call_target="tpu_custom_call" | custom-call | flops 2097152 | bytes 4194304 | tf_op jit(solution)/shard_map/pack/pallas_call | solution.py:145
  5.6 1.2 %collective-permute-start.4 = (bf16[4,3,128,128]{3,2,1,0:T(8,128)(2,1)S(1)}, bf16[4,3,128,128]{3,2,1,0:T(8,128)(2,1)S(1)}, u32[]{:S(2)}, u32[]{:S(2)}) collective-permute-start(bf16[4,3,128,128]{3,2,1,0:T(8,128)(2,1)S(1)} %get-tuple-element.39), channel_id=1, source_target_pairs={{0,2},{1,3},{2,0},{3,1},{4,6},{5,7},{6,4},{7,5},{8,10},{9,11},{10,... | collective-permute-start | bytes 1179656 | tf_op jit(solution)/shard_map/ppermute | solution.py:336
  6.9 0.6 %collective-permute-start.5 = (bf16[4,3,128,128]{3,2,1,0:T(8,128)(2,1)S(1)}, bf16[4,3,128,128]{3,2,1,0:T(8,128)(2,1)S(1)}, u32[]{:S(2)}, u32[]{:S(2)}) collective-permute-start(bf16[4,3,128,128]{3,2,1,0:T(8,128)(2,1)S(1)} %get-tuple-element.40), channel_id=1, source_target_pairs={{0,3},{1,2},{2,1},{3,0},{4,7},{5,6},{6,5},{7,4},{8,11},{9,10},{10,... | collective-permute-start | bytes 1179656 | tf_op jit(solution)/shard_map/ppermute | solution.py:336
  7.5 3.7 %collective-permute-done.refs_0_ = bf16[4,32,8,128]{3,2,1,0:T(8,128)(2,1)S(1)} collective-permute-done((bf16[4,32,8,128]{3,2,1,0:T(8,128)(2,1)S(1)}, bf16[4,32,8,128]{3,2,1,0:T(8,128)(2,1)S(1)}, u32[]{:S(2)}, u32[]{:S(2)}) %collective-permute-start) | collective-permute-done | bytes 262176 | tf_op jit(solution)/shard_map/ppermute | solution.py:336
  11.2 5.2 %collective-permute-done.1.refs_1_ = bf16[4,32,8,128]{3,2,1,0:T(8,128)(2,1)S(1)} collective-permute-done((bf16[4,32,8,128]{3,2,1,0:T(8,128)(2,1)S(1)}, bf16[4,32,8,128]{3,2,1,0:T(8,128)(2,1)S(1)}, u32[]{:S(2)}, u32[]{:S(2)}) %collective-permute-start.1) | collective-permute-done | bytes 262176 | tf_op jit(solution)/shard_map/ppermute | solution.py:336
  16.4 3.8 %pack.4 = (bf16[3,3,128,128]{3,2,1,0:T(8,128)(2,1)}, bf16[3,3,128,128]{3,2,1,0:T(8,128)(2,1)}, bf16[4,2,128,128]{3,2,1,0:T(8,128)(2,1)}, bf16[3,2,128,128]{3,2,1...) custom-call(bf16[1,4,32,32,128]{4,3,2,1,0:T(8,128)(2,1)} %refs_0_.5,, ...), custom_call_target="tpu_custom_call" | custom-call | flops 6291456 | bytes 12582912 | tf_op jit(solution)/shard_map/pack/pallas_call | solution.py:145
  20.2 0.3 collective-permute-start.6
  20.5 0.3 collective-permute-start.7
  20.8 0.2 collective-permute-start.2
  21.0 1.2 %collective-permute-done.2.refs_0_ = bf16[1,2,128,128]{3,2,1,0:T(8,128)(2,1)S(1)} collective-permute-done((bf16[1,2,128,128]{3,2,1,0:T(8,128)(2,1)S(1)}, bf16[1,2,128,128]{3,2,1,0:T(8,128)(2,1)S(1)}, u32[]{:S(2)}, u32[]{:S(2)}) %collective-permute-start.2) | collective-permute-done | bytes 65568 | tf_op jit(solution)/shard_map/ppermute | solution.py:336
  22.2 1.9 %collective-permute-start.12 = (bf16[3,3,128,128]{3,2,1,0:T(8,128)(2,1)}, bf16[3,3,128,128]{3,2,1,0:T(8,128)(2,1)S(1)}, u32[]{:S(2)}, u32[]{:S(2)}) collective-permute-start(bf16[3,3,128,128]{3,2,1,0:T(8,128)(2,1)} %get-tuple-element.51), channel_id=1, source_target_pairs={{0,2},{1,3},{2,0},{3,1},{4,6},{5,7},{6,4},{7,5},{8,10},{9,11},{10,... | collective-permute-start | bytes 884744 | tf_op jit(solution)/shard_map/ppermute | solution.py:336
  24.2 1.1 %collective-permute-done.4.refs_0_ = bf16[4,3,128,128]{3,2,1,0:T(8,128)(2,1)S(1)} collective-permute-done((bf16[4,3,128,128]{3,2,1,0:T(8,128)(2,1)S(1)}, bf16[4,3,128,128]{3,2,1,0:T(8,128)(2,1)S(1)}, u32[]{:S(2)}, u32[]{:S(2)}) %collective-permute-start.4) | collective-permute-done | bytes 393248 | tf_op jit(solution)/shard_map/ppermute | solution.py:336
  25.2 0.0 collective-permute-start.13
  25.2 8.0 %collective-permute-done.5.refs_1_ = bf16[4,3,128,128]{3,2,1,0:T(8,128)(2,1)S(1)} collective-permute-done((bf16[4,3,128,128]{3,2,1,0:T(8,128)(2,1)S(1)}, bf16[4,3,128,128]{3,2,1,0:T(8,128)(2,1)S(1)}, u32[]{:S(2)}, u32[]{:S(2)}) %collective-permute-start.5) | collective-permute-done | bytes 393248 | tf_op jit(solution)/shard_map/ppermute | solution.py:336
  33.2 0.2 collective-permute-start.10
  33.5 0.0 collective-permute-done.6.refs_1_
  33.5 0.3 collective-permute-start.11
  33.8 0.0 collective-permute-done.7.refs_2_
  33.8 0.2 collective-permute-start.3
  34.0 0.2 arrange.1.values
  34.2 0.0 copy-start
  34.3 0.7 %copy-done = f32[2,8,128]{2,1,0:T(8,128)S(1)} copy-done((f32[2,8,128]{2,1,0:T(8,128)S(1)}, f32[2,8,128]{2,1,0:T(8,128)}, u32[]{:S(2)}) %copy-start) | copy-done | bytes 8216
  34.9 0.3 copy-done.1
  35.2 0.1 copy-done.2
  35.3 0.4 prepare.4.close
  35.7 0.3 copy-done.4
  36.0 3.6 %attend.3.refs_4_.refs_2_ = f32[4,128]{1,0:T(4,128)S(1)} custom-call(s32[4,4]{1,0:T(4,128)S(1)} %copy-done.4, f32[2,8,128]{2,1,0:T(8,128)S(1)} %copy-done, bf16[8,4,64,128]{3,2,1,0:T(8,128)(2,1)S(1)} %arrange.1.values, bf16[4,4,4,64,128]{4,3,2,1,0:T(8,128)(2,1)S(1)} %prepare.4.close, bf16[4,3,128,128]{3,2,1,0:T(8,128)(2,1)S(1)} %collective-permute-done.4.refs_0_, ...), custom_call_target="tpu_custom_call" | custom-call | flops 402653184 | bytes 1048576 | tf_op jit(solution)/shard_map/attend/pallas_call | solution.py:297
  39.6 2.1 %pack.5 = (bf16[1,3,128,128]{3,2,1,0:T(8,128)(2,1)S(1)}, bf16[1,3,128,128]{3,2,1,0:T(8,128)(2,1)S(1)}, f32[8,128]{1,0:T(8,128)}) custom-call(bf16[1,4,32,32,128]{4,3,2,1,0:T(8,128)(2,1)} %refs_0_.5, bf16[1,4,32,32,128]{4,3,2,1,0:T(8,128)(2,1)} %refs_1_.5, bf16[1,4,32,32,128]{4,3,2,1,0:T(8,128)(2,1)} %refs_2_.5, bf16[1,4,32,32,128]{4,3,2,1,0:T(8,128)(2,1)} %refs_3_.5, ...), custom_call_target="tpu_custom_call" | custom-call | flops 2097152 | bytes 4194304 | tf_op jit(solution)/shard_map/pack/pallas_call | solution.py:145
  41.7 0.0 collective-permute-done.3.refs_1_
  41.7 2.1 %collective-permute-start.8 = (bf16[1,3,128,128]{3,2,1,0:T(8,128)(2,1)S(1)}, bf16[1,3,128,128]{3,2,1,0:T(8,128)(2,1)S(1)}, u32[]{:S(2)}, u32[]{:S(2)}) collective-permute-start(bf16[1,3,128,128]{3,2,1,0:T(8,128)(2,1)S(1)} %get-tuple-element.45), channel_id=1, source_target_pairs={{0,2},{1,3},{2,0},{3,1},{4,6},{5,7},{6,4},{7,5},{8,10},{9,11},{10,... | collective-permute-start | bytes 294920 | tf_op jit(solution)/shard_map/ppermute | solution.py:336
  43.8 0.2 prepare.3.close
  44.0 0.8 %copy-done.3 = bf16[3,2,128,128]{3,2,1,0:T(8,128)(2,1)S(1)} copy-done((bf16[3,2,128,128]{3,2,1,0:T(8,128)(2,1)S(1)}, bf16[3,2,128,128]{3,2,1,0:T(8,128)(2,1)}, u32[]{:S(2)}) %copy-start.3) | copy-done | bytes 196632
  44.7 0.3 prepare.5.close
  45.0 0.0 collective-permute-done.12.refs_0_
  45.1 0.5 collective-permute-done.13.refs_1_
  45.5 3.0 %attend.4.refs_3_ = f32[3,128]{1,0:T(4,128)S(1)} custom-call(s32[4,4]{1,0:T(4,128)S(1)} %copy-done.4, f32[2,8,128]{2,1,0:T(8,128)S(1)} %copy-done, bf16[8,4,64,128]{3,2,1,0:T(8,128)(2,1)S(1)} %arrange.1.values, bf16[3,4,4,64,128]{4,3,2,1,0:T(8,128)(2,1)S(1)} %prepare.5.close, bf16[3,3,128,128]{3,2,1,0:T(8,128)(2,1)S(1)} %collective-permute-done.12.refs_0_, ...), custom_call_target="tpu_custom_call" | custom-call | flops 301989888 | bytes 786432 | tf_op jit(solution)/shard_map/attend/pallas_call | solution.py:297
  48.5 0.0 collective-permute-done.8.refs_0_
  48.6 0.5 collective-permute-done.9.refs_1_
  49.0 1.6 %attend.5 = (f32[2,8,32]{2,1,0:T(8,128)S(1)}, f32[2,8,32]{2,1,0:T(8,128)S(1)}, f32[2,8,32]{2,1,0:T(8,128)S(1)}, f32[2,8,32]{2,1,0:T(8,128)S(1)}) custom-call(s32[4,4]{1,0:T(4,128)S(1)} %copy-done.4, f32[2,8,128]{2,1,0:T(8,128)S(1)} %copy-done, bf16[8,4,64,128]{3,2,1,0:T(8,128)(2,1)S(1)} %arrange.1.values, bf16[1,4,4,64,128]{4,3,2,1,0:T(8,128)(2,1)S(1)} %prepare.3.close, ...), custom_call_target="tpu_custom_call" | custom-call | flops 100663296 | bytes 262144 | tf_op jit(solution)/shard_map/attend/pallas_call | solution.py:297
  50.6 3.7 %collective-permute-start.14 = (f32[2,8,32]{2,1,0:T(8,128)S(1)}, f32[2,8,32]{2,1,0:T(8,128)S(1)}, u32[]{:S(2)}, u32[]{:S(2)}) collective-permute-start(f32[2,8,32]{2,1,0:T(8,128)S(1)} %get-tuple-element.54), channel_id=1, source_target_pairs={{0,12},{4,8},{8,4},{12,0},{1,13},{5,9},{9,5},{13,1},{2,14},{6,10},... | collective-permute-start | bytes 6152 | tf_op jit(solution)/shard_map/ppermute | solution.py:372
  54.3 0.7 %collective-permute-start.16 = (f32[2,8,32]{2,1,0:T(8,128)S(1)}, f32[2,8,32]{2,1,0:T(8,128)S(1)}, u32[]{:S(2)}, u32[]{:S(2)}) collective-permute-start(f32[2,8,32]{2,1,0:T(8,128)S(1)} %get-tuple-element.56), channel_id=1, source_target_pairs={{0,4},{4,0},{8,12},{12,8},{1,5},{5,1},{9,13},{13,9},{2,6},{6,2},{1... | collective-permute-start | bytes 6152 | tf_op jit(solution)/shard_map/ppermute | solution.py:372
  55.0 1.1 %collective-permute-done.14 = f32[2,8,32]{2,1,0:T(8,128)S(1)} collective-permute-done((f32[2,8,32]{2,1,0:T(8,128)S(1)}, f32[2,8,32]{2,1,0:T(8,128)S(1)}, u32[]{:S(2)}, u32[]{:S(2)}) %collective-permute-start.14) | collective-permute-done | bytes 2080 | tf_op jit(solution)/shard_map/ppermute | solution.py:372
  56.1 2.8 %collective-permute-done.15 = f32[2,8,32]{2,1,0:T(8,128)S(1)} collective-permute-done((f32[2,8,32]{2,1,0:T(8,128)S(1)}, f32[2,8,32]{2,1,0:T(8,128)S(1)}, u32[]{:S(2)}, u32[]{:S(2)}) %collective-permute-start.15) | collective-permute-done | bytes 2080 | tf_op jit(solution)/shard_map/ppermute | solution.py:372
  58.9 0.0 collective-permute-done.16
  58.9 0.6 %add_add_fusion = f32[2,8,32]{2,1,0:T(8,128)} fusion(f32[2,8,32]{2,1,0:T(8,128)S(1)} %collective-permute-done.16, f32[2,8,32]{2,1,0:T(8,128)S(1)} %collective-permute-done.15, f32[2,8,32]{2,1,0:T(8,128)S(1)} %get-tuple-element.53, f32[2,8,32]{2,1,0:T(8,128)S(1)} %collective-permute-done.14), kind=kLoop, calls=%fused_computation | loop fusion | flops 1536 | bytes 10240 | tf_op jit(solution)/shard_map/add | solution.py:372
  (10 shorter events, 0.0 us)
Async XLA Ops:
  1.1 10.1 %collective-permute-start = (bf16[4,32,8,128]{3,2,1,0:T(8,128)(2,1)S(1)}, bf16[4,32,8,128]{3,2,1,0:T(8,128)(2,1)S(1)}, u32[]{:S(2)}, u32[]{:S(2)}) collective-permute-start(bf16[4,32,8,128]{3,2,1,0:T(8,128)(2,1)S(1)} %get-tuple-element.31), channel_id=1, source_target_pairs={{0,2},{1,3},{2,0},{3,1},{4,6},{5,7},{6,4},{7,5},{8,10},{9,11},{10,... | collective-permute-start | bytes 786440 | tf_op jit(solution)/shard_map/ppermute | solution.py:336
  4.1 12.3 %collective-permute-start.1 = (bf16[4,32,8,128]{3,2,1,0:T(8,128)(2,1)S(1)}, bf16[4,32,8,128]{3,2,1,0:T(8,128)(2,1)S(1)}, u32[]{:S(2)}, u32[]{:S(2)}) collective-permute-start(bf16[4,32,8,128]{3,2,1,0:T(8,128)(2,1)S(1)} %get-tuple-element.32), channel_id=1, source_target_pairs={{0,3},{1,2},{2,1},{3,0},{4,7},{5,6},{6,5},{7,4},{8,11},{9,10},{10,... | collective-permute-start | bytes 786440 | tf_op jit(solution)/shard_map/ppermute | solution.py:336
  5.6 19.6 %collective-permute-start.4 = (bf16[4,3,128,128]{3,2,1,0:T(8,128)(2,1)S(1)}, bf16[4,3,128,128]{3,2,1,0:T(8,128)(2,1)S(1)}, u32[]{:S(2)}, u32[]{:S(2)}) collective-permute-start(bf16[4,3,128,128]{3,2,1,0:T(8,128)(2,1)S(1)} %get-tuple-element.39), channel_id=1, source_target_pairs={{0,2},{1,3},{2,0},{3,1},{4,6},{5,7},{6,4},{7,5},{8,10},{9,11},{10,... | collective-permute-start | bytes 1179656 | tf_op jit(solution)/shard_map/ppermute | solution.py:336
  6.9 26.4 %collective-permute-start.5 = (bf16[4,3,128,128]{3,2,1,0:T(8,128)(2,1)S(1)}, bf16[4,3,128,128]{3,2,1,0:T(8,128)(2,1)S(1)}, u32[]{:S(2)}, u32[]{:S(2)}) collective-permute-start(bf16[4,3,128,128]{3,2,1,0:T(8,128)(2,1)S(1)} %get-tuple-element.40), channel_id=1, source_target_pairs={{0,3},{1,2},{2,1},{3,0},{4,7},{5,6},{6,5},{7,4},{8,11},{9,10},{10,... | collective-permute-start | bytes 1179656 | tf_op jit(solution)/shard_map/ppermute | solution.py:336
  20.2 13.3 %collective-permute-start.6 = (bf16[4,2,128,128]{3,2,1,0:T(8,128)(2,1)}, bf16[4,2,128,128]{3,2,1,0:T(8,128)(2,1)S(1)}, u32[]{:S(2)}, u32[]{:S(2)}) collective-permute-start(bf16[4,2,128,128]{3,2,1,0:T(8,128)(2,1)} %get-tuple-element.41), channel_id=1, source_target_pairs={{0,1},{1,0},{2,3},{3,2},{4,5},{5,4},{6,7},{7,6},{8,9},{9,8},{10,11... | collective-permute-start | bytes 786440 | tf_op jit(solution)/shard_map/ppermute | solution.py:336
  20.5 13.3 %collective-permute-start.7 = (bf16[4,2,128,128]{3,2,1,0:T(8,128)(2,1)}, bf16[4,2,128,128]{3,2,1,0:T(8,128)(2,1)S(1)}, u32[]{:S(2)}, u32[]{:S(2)}) collective-permute-start(bf16[4,2,128,128]{3,2,1,0:T(8,128)(2,1)} %get-tuple-element.42), channel_id=1, source_target_pairs={{0,1},{1,0},{2,3},{3,2},{4,5},{5,4},{6,7},{7,6},{8,9},{9,8},{10,11... | collective-permute-start | bytes 786440 | tf_op jit(solution)/shard_map/ppermute | solution.py:336
  20.8 1.5 %collective-permute-start.2 = (bf16[1,2,128,128]{3,2,1,0:T(8,128)(2,1)S(1)}, bf16[1,2,128,128]{3,2,1,0:T(8,128)(2,1)S(1)}, u32[]{:S(2)}, u32[]{:S(2)}) collective-permute-start(bf16[1,2,128,128]{3,2,1,0:T(8,128)(2,1)S(1)} %get-tuple-element.35), channel_id=1, source_target_pairs={{0,1},{1,0},{2,3},{3,2},{4,5},{5,4},{6,7},{7,6},{8,9},{9,8},{10,11... | collective-permute-start | bytes 196616 | tf_op jit(solution)/shard_map/ppermute | solution.py:336
  22.2 22.8 %collective-permute-start.12 = (bf16[3,3,128,128]{3,2,1,0:T(8,128)(2,1)}, bf16[3,3,128,128]{3,2,1,0:T(8,128)(2,1)S(1)}, u32[]{:S(2)}, u32[]{:S(2)}) collective-permute-start(bf16[3,3,128,128]{3,2,1,0:T(8,128)(2,1)} %get-tuple-element.51), channel_id=1, source_target_pairs={{0,2},{1,3},{2,0},{3,1},{4,6},{5,7},{6,4},{7,5},{8,10},{9,11},{10,... | collective-permute-start | bytes 884744 | tf_op jit(solution)/shard_map/ppermute | solution.py:336
  25.2 20.3 %collective-permute-start.13 = (bf16[3,3,128,128]{3,2,1,0:T(8,128)(2,1)}, bf16[3,3,128,128]{3,2,1,0:T(8,128)(2,1)S(1)}, u32[]{:S(2)}, u32[]{:S(2)}) collective-permute-start(bf16[3,3,128,128]{3,2,1,0:T(8,128)(2,1)} %get-tuple-element.52), channel_id=1, source_target_pairs={{0,3},{1,2},{2,1},{3,0},{4,7},{5,6},{6,5},{7,4},{8,11},{9,10},{10,... | collective-permute-start | bytes 884744 | tf_op jit(solution)/shard_map/ppermute | solution.py:336
  33.2 10.6 %collective-permute-start.10 = (bf16[3,2,128,128]{3,2,1,0:T(8,128)(2,1)S(1)}, bf16[3,2,128,128]{3,2,1,0:T(8,128)(2,1)S(1)}, u32[]{:S(2)}, u32[]{:S(2)}) collective-permute-start(bf16[3,2,128,128]{3,2,1,0:T(8,128)(2,1)S(1)} %get-tuple-element.47), channel_id=1, source_target_pairs={{0,1},{1,0},{2,3},{3,2},{4,5},{5,4},{6,7},{7,6},{8,9},{9,8},{10,11... | collective-permute-start | bytes 589832 | tf_op jit(solution)/shard_map/ppermute | solution.py:336
  33.5 10.5 %collective-permute-start.11 = (bf16[3,2,128,128]{3,2,1,0:T(8,128)(2,1)S(1)}, bf16[3,2,128,128]{3,2,1,0:T(8,128)(2,1)S(1)}, u32[]{:S(2)}, u32[]{:S(2)}) collective-permute-start(bf16[3,2,128,128]{3,2,1,0:T(8,128)(2,1)S(1)} %get-tuple-element.48), channel_id=1, source_target_pairs={{0,1},{1,0},{2,3},{3,2},{4,5},{5,4},{6,7},{7,6},{8,9},{9,8},{10,11... | collective-permute-start | bytes 589832 | tf_op jit(solution)/shard_map/ppermute | solution.py:336
  33.8 7.9 %collective-permute-start.3 = (bf16[1,2,128,128]{3,2,1,0:T(8,128)(2,1)S(1)}, bf16[1,2,128,128]{3,2,1,0:T(8,128)(2,1)S(1)}, u32[]{:S(2)}, u32[]{:S(2)}) collective-permute-start(bf16[1,2,128,128]{3,2,1,0:T(8,128)(2,1)S(1)} %get-tuple-element.36), channel_id=1, source_target_pairs={{0,1},{1,0},{2,3},{3,2},{4,5},{5,4},{6,7},{7,6},{8,9},{9,8},{10,11... | collective-permute-start | bytes 196616 | tf_op jit(solution)/shard_map/ppermute | solution.py:336
  34.2 0.7 %copy-start = (f32[2,8,128]{2,1,0:T(8,128)S(1)}, f32[2,8,128]{2,1,0:T(8,128)}, u32[]{:S(2)}) copy-start(f32[2,8,128]{2,1,0:T(8,128)} %gains.11) | copy-start | bytes 24580
  34.3 1.0 %copy-start.1 = (bf16[4,2,128,128]{3,2,1,0:T(8,128)(2,1)S(1)}, bf16[4,2,128,128]{3,2,1,0:T(8,128)(2,1)}, u32[]{:S(2)}) copy-start(bf16[4,2,128,128]{3,2,1,0:T(8,128)(2,1)} %get-tuple-element.43.refs_3_) | copy-start | bytes 786436
  34.3 1.0 %copy-start.2 = (bf16[4,2,128,128]{3,2,1,0:T(8,128)(2,1)S(1)}, bf16[4,2,128,128]{3,2,1,0:T(8,128)(2,1)}, u32[]{:S(2)}) copy-start(bf16[4,2,128,128]{3,2,1,0:T(8,128)(2,1)} %get-tuple-element.44.refs_4_) | copy-start | bytes 786436
  35.3 0.7 %copy-start.4 = (s32[4,4]{1,0:T(4,128)S(1)}, s32[4,4]{1,0:T(4,128)}, u32[]{:S(2)}) copy-start(s32[4,4]{1,0:T(4,128)} %units.5) | copy-start | bytes 196
  41.7 6.9 %collective-permute-start.8 = (bf16[1,3,128,128]{3,2,1,0:T(8,128)(2,1)S(1)}, bf16[1,3,128,128]{3,2,1,0:T(8,128)(2,1)S(1)}, u32[]{:S(2)}, u32[]{:S(2)}) collective-permute-start(bf16[1,3,128,128]{3,2,1,0:T(8,128)(2,1)S(1)} %get-tuple-element.45), channel_id=1, source_target_pairs={{0,2},{1,3},{2,0},{3,1},{4,6},{5,7},{6,4},{7,5},{8,10},{9,11},{10,... | collective-permute-start | bytes 294920 | tf_op jit(solution)/shard_map/ppermute | solution.py:336
  43.8 5.2 %collective-permute-start.9 = (bf16[1,3,128,128]{3,2,1,0:T(8,128)(2,1)S(1)}, bf16[1,3,128,128]{3,2,1,0:T(8,128)(2,1)S(1)}, u32[]{:S(2)}, u32[]{:S(2)}) collective-permute-start(bf16[1,3,128,128]{3,2,1,0:T(8,128)(2,1)S(1)} %get-tuple-element.46), channel_id=1, source_target_pairs={{0,3},{1,2},{2,1},{3,0},{4,7},{5,6},{6,5},{7,4},{8,11},{9,10},{10,... | collective-permute-start | bytes 294920 | tf_op jit(solution)/shard_map/ppermute | solution.py:336
  43.8 0.9 %copy-start.3 = (bf16[3,2,128,128]{3,2,1,0:T(8,128)(2,1)S(1)}, bf16[3,2,128,128]{3,2,1,0:T(8,128)(2,1)}, u32[]{:S(2)}) copy-start(bf16[3,2,128,128]{3,2,1,0:T(8,128)(2,1)} %get-tuple-element.50.refs_3_) | copy-start | bytes 589828
  50.6 5.5 %collective-permute-start.14 = (f32[2,8,32]{2,1,0:T(8,128)S(1)}, f32[2,8,32]{2,1,0:T(8,128)S(1)}, u32[]{:S(2)}, u32[]{:S(2)}) collective-permute-start(f32[2,8,32]{2,1,0:T(8,128)S(1)} %get-tuple-element.54), channel_id=1, source_target_pairs={{0,12},{4,8},{8,4},{12,0},{1,13},{5,9},{9,5},{13,1},{2,14},{6,10},... | collective-permute-start | bytes 6152 | tf_op jit(solution)/shard_map/ppermute | solution.py:372
  54.3 4.5 %collective-permute-start.15 = (f32[2,8,32]{2,1,0:T(8,128)S(1)}, f32[2,8,32]{2,1,0:T(8,128)S(1)}, u32[]{:S(2)}, u32[]{:S(2)}) collective-permute-start(f32[2,8,32]{2,1,0:T(8,128)S(1)} %get-tuple-element.55), channel_id=1, source_target_pairs={{0,8},{4,12},{8,0},{12,4},{1,9},{5,13},{9,1},{13,5},{2,10},{6,14},... | collective-permute-start | bytes 6152 | tf_op jit(solution)/shard_map/ppermute | solution.py:372
  54.3 4.5 %collective-permute-start.16 = (f32[2,8,32]{2,1,0:T(8,128)S(1)}, f32[2,8,32]{2,1,0:T(8,128)S(1)}, u32[]{:S(2)}, u32[]{:S(2)}) collective-permute-start(f32[2,8,32]{2,1,0:T(8,128)S(1)} %get-tuple-element.56), channel_id=1, source_target_pairs={{0,4},{4,0},{8,12},{12,8},{1,5},{5,1},{9,13},{13,9},{2,6},{6,2},{1... | collective-permute-start | bytes 6152 | tf_op jit(solution)/shard_map/ppermute | solution.py:372

commit v7 on v6

--- a/solution.py
+++ b/solution.py
@@ -247,7 +247,10 @@
         mixed = jnp.dot(dscore, q, preferred_element_type=jnp.float32)
         return jnp.sum(mixed * k.astype(jnp.float32), axis=0, keepdims=True)
 
-    begins = sum(jnp.where(units[group, slot] > 0, 1 << slot, 0) for slot in range(slots))
+    table = units[...]
+    rows_of, slots_of = (lax.broadcasted_iota(jnp.int32, table.shape, dim) for dim in (0, 1))
+    starts = jnp.where((rows_of == group) & (table > 0), lax.shift_left(jnp.int32(1), slots_of), 0)
+    begins = jnp.sum(starts)
     for layout in layouts(slots):
 
         @pl.when(begins == sum(1 << slot for slot, _ in layout))
@@ -297,8 +300,7 @@
     return pl.pallas_call(
         kernel,
         out_shape=shapes,
-        in_specs=[pl.BlockSpec(memory_space=pltpu.SMEM)]
-        + [pl.BlockSpec(memory_space=pltpu.VMEM)] * (3 + len(pieces) + len(earlier)),
+        in_specs=[pl.BlockSpec(memory_space=pltpu.VMEM)] * (4 + len(pieces) + len(earlier)),
         out_specs=outs,
         scratch_shapes=held,
         compiler_params=pltpu.CompilerParams(vmem_limit_bytes=VMEM_LIMIT),

time: 60 us -> 59 us (0.983)
  Pallas kernels: 17.7 us -> 16 us
  waiting for transfers between devices: 24 us -> 25 us
    pallas_call x3, Pallas kernels: 8.25 us -> 6.51 us  [attend(): pl.pallas_call(kernel, out_shape=shapes, in_specs=[pl.BlockSpec(memory_sp...]
    ppermute x14, waiting for transfers between devices: 20.2 us -> 21.2 us  [send(): return lax.ppermute(block, 'seq', [(s, s ^ flip) for s in range(sequence)])]
  transfers between devices with their start and end apart: 17 -> 17, of which waited for: 9 -> 9; matrix products, arithmetic and copies ran while one was open for 0% -> 0% of each run, Pallas kernels for 25% -> 24%
where the time goes in v7:
time: 59 us; the launch traced here: 58.8 us
  waiting for transfers between devices  25 us (42%)
  Pallas kernels  16 us (27%)
  starting transfers between devices  15 us (25%)
  local copies, waits for them, and re-layouts  2.08 us (4%)
  other arithmetic  0.6 us (1%)
    ppermute x14, waiting for transfers between devices, send(): return lax.ppermute(block, 'seq', [(s, s ^ flip) for s in range(sequence)])  21.2 us
    ppermute x14, starting transfers between devices, send(): return lax.ppermute(block, 'seq', [(s, s ^ flip) for s in range(sequence)])  10.5 us
    pallas_call x3, Pallas kernels, pack(): pl.pallas_call(functools.partial(pack_kernel, plan, heads, len(after)), o...  7.37 us
    pallas_call x3, Pallas kernels, attend(): pl.pallas_call(kernel, out_shape=shapes, in_specs=[pl.BlockSpec(memory_sp...  6.51 us
    ppermute x3, starting transfers between devices, body(): lax.ppermute(parts[flip], 'dp', [(g, g ^ flip) for g in range(groups)])  4.43 us
    ppermute x3, waiting for transfers between devices, body(): lax.ppermute(parts[flip], 'dp', [(g, g ^ flip) for g in range(groups)])  3.74 us
    unnamed x10, local copies, waits for them, and re-layouts  2.08 us
  transfers between devices with their start and end apart: 17, of which 9 were waited for; matrix products, arithmetic and copies ran while one was open for 0% of the time, Pallas kernels for 24%

profile of v7, /device:TPU:0, one launch (start us, length us, event | category | flops | bytes accessed | tf_op | source)
XLA Modules:
  0.0 58.8 jit_solution(15624065849484550033)
XLA Ops:
  0.0 1.1 %cut.1 = (bf16[4,32,8,128]{3,2,1,0:T(8,128)(2,1)S(1)}, bf16[4,32,8,128]{3,2,1,0:T(8,128)(2,1)S(1)}, f32[8,128]{1,0:T(8,128)S(1)}) custom-call(bf16[1,4,32,32,128]{4,3,2,1,0:T(8,128)(2,1)} %refs_2_.5), custom_call_target="tpu_custom_call" | custom-call | tf_op jit(solution)/shard_map/cut/pallas_call | solution.py:53
  1.1 3.0 %collective-permute-start = (bf16[4,32,8,128]{3,2,1,0:T(8,128)(2,1)S(1)}, bf16[4,32,8,128]{3,2,1,0:T(8,128)(2,1)S(1)}, u32[]{:S(2)}, u32[]{:S(2)}) collective-permute-start(bf16[4,32,8,128]{3,2,1,0:T(8,128)(2,1)S(1)} %get-tuple-element.31), channel_id=1, source_target_pairs={{0,2},{1,3},{2,0},{3,1},{4,6},{5,7},{6,4},{7,5},{8,10},{9,11},{10,... | collective-permute-start | bytes 786440 | tf_op jit(solution)/shard_map/ppermute | solution.py:338
  4.1 0.0 collective-permute-start.1
  4.1 1.5 %pack.3 = (bf16[4,3,128,128]{3,2,1,0:T(8,128)(2,1)S(1)}, bf16[4,3,128,128]{3,2,1,0:T(8,128)(2,1)S(1)}, f32[8,128]{1,0:T(8,128)S(1)}) custom-call(bf16[1,4,32,32,128]{4,3,2,1,0:T(8,128)(2,1)} %refs_0_.5, bf16[1,4,32,32,128]{4,3,2,1,0:T(8,128)(2,1)} %refs_1_.5, bf16[1,4,32,32,128]{4,3,2,1,0:T(8,128)(2,1)} %refs_2_.5, bf16[1,4,32,32,128]{4,3,2,1,0:T(8,128)(2,1)} %refs_3_.5, ...), custom_call_target="tpu_custom_call" | custom-call | flops 2097152 | bytes 4194304 | tf_op jit(solution)/shard_map/pack/pallas_call | solution.py:145
  5.6 1.2 %collective-permute-start.4 = (bf16[4,3,128,128]{3,2,1,0:T(8,128)(2,1)S(1)}, bf16[4,3,128,128]{3,2,1,0:T(8,128)(2,1)S(1)}, u32[]{:S(2)}, u32[]{:S(2)}) collective-permute-start(bf16[4,3,128,128]{3,2,1,0:T(8,128)(2,1)S(1)} %get-tuple-element.39), channel_id=1, source_target_pairs={{0,2},{1,3},{2,0},{3,1},{4,6},{5,7},{6,4},{7,5},{8,10},{9,11},{10,... | collective-permute-start | bytes 1179656 | tf_op jit(solution)/shard_map/ppermute | solution.py:338
  6.9 0.6 %collective-permute-start.5 = (bf16[4,3,128,128]{3,2,1,0:T(8,128)(2,1)S(1)}, bf16[4,3,128,128]{3,2,1,0:T(8,128)(2,1)S(1)}, u32[]{:S(2)}, u32[]{:S(2)}) collective-permute-start(bf16[4,3,128,128]{3,2,1,0:T(8,128)(2,1)S(1)} %get-tuple-element.40), channel_id=1, source_target_pairs={{0,3},{1,2},{2,1},{3,0},{4,7},{5,6},{6,5},{7,4},{8,11},{9,10},{10,... | collective-permute-start | bytes 1179656 | tf_op jit(solution)/shard_map/ppermute | solution.py:338
  7.5 3.7 %collective-permute-done.refs_0_ = bf16[4,32,8,128]{3,2,1,0:T(8,128)(2,1)S(1)} collective-permute-done((bf16[4,32,8,128]{3,2,1,0:T(8,128)(2,1)S(1)}, bf16[4,32,8,128]{3,2,1,0:T(8,128)(2,1)S(1)}, u32[]{:S(2)}, u32[]{:S(2)}) %collective-permute-start) | collective-permute-done | bytes 262176 | tf_op jit(solution)/shard_map/ppermute | solution.py:338
  11.2 5.2 %collective-permute-done.1.refs_1_ = bf16[4,32,8,128]{3,2,1,0:T(8,128)(2,1)S(1)} collective-permute-done((bf16[4,32,8,128]{3,2,1,0:T(8,128)(2,1)S(1)}, bf16[4,32,8,128]{3,2,1,0:T(8,128)(2,1)S(1)}, u32[]{:S(2)}, u32[]{:S(2)}) %collective-permute-start.1) | collective-permute-done | bytes 262176 | tf_op jit(solution)/shard_map/ppermute | solution.py:338
  16.4 3.8 %pack.4 = (bf16[3,3,128,128]{3,2,1,0:T(8,128)(2,1)}, bf16[3,3,128,128]{3,2,1,0:T(8,128)(2,1)}, bf16[4,2,128,128]{3,2,1,0:T(8,128)(2,1)}, bf16[3,2,128,128]{3,2,1...) custom-call(bf16[1,4,32,32,128]{4,3,2,1,0:T(8,128)(2,1)} %refs_0_.5,, ...), custom_call_target="tpu_custom_call" | custom-call | flops 6291456 | bytes 12582912 | tf_op jit(solution)/shard_map/pack/pallas_call | solution.py:145
  20.2 0.3 collective-permute-start.6
  20.5 0.3 collective-permute-start.7
  20.8 0.2 collective-permute-start.2
  21.0 1.2 %collective-permute-done.2.refs_0_ = bf16[1,2,128,128]{3,2,1,0:T(8,128)(2,1)S(1)} collective-permute-done((bf16[1,2,128,128]{3,2,1,0:T(8,128)(2,1)S(1)}, bf16[1,2,128,128]{3,2,1,0:T(8,128)(2,1)S(1)}, u32[]{:S(2)}, u32[]{:S(2)}) %collective-permute-start.2) | collective-permute-done | bytes 65568 | tf_op jit(solution)/shard_map/ppermute | solution.py:338
  22.2 1.9 %collective-permute-start.12 = (bf16[3,3,128,128]{3,2,1,0:T(8,128)(2,1)}, bf16[3,3,128,128]{3,2,1,0:T(8,128)(2,1)S(1)}, u32[]{:S(2)}, u32[]{:S(2)}) collective-permute-start(bf16[3,3,128,128]{3,2,1,0:T(8,128)(2,1)} %get-tuple-element.51), channel_id=1, source_target_pairs={{0,2},{1,3},{2,0},{3,1},{4,6},{5,7},{6,4},{7,5},{8,10},{9,11},{10,... | collective-permute-start | bytes 884744 | tf_op jit(solution)/shard_map/ppermute | solution.py:338
  24.2 1.1 %collective-permute-done.4.refs_0_ = bf16[4,3,128,128]{3,2,1,0:T(8,128)(2,1)S(1)} collective-permute-done((bf16[4,3,128,128]{3,2,1,0:T(8,128)(2,1)S(1)}, bf16[4,3,128,128]{3,2,1,0:T(8,128)(2,1)S(1)}, u32[]{:S(2)}, u32[]{:S(2)}) %collective-permute-start.4) | collective-permute-done | bytes 393248 | tf_op jit(solution)/shard_map/ppermute | solution.py:338
  25.2 0.0 collective-permute-start.13
  25.2 8.0 %collective-permute-done.5.refs_1_ = bf16[4,3,128,128]{3,2,1,0:T(8,128)(2,1)S(1)} collective-permute-done((bf16[4,3,128,128]{3,2,1,0:T(8,128)(2,1)S(1)}, bf16[4,3,128,128]{3,2,1,0:T(8,128)(2,1)S(1)}, u32[]{:S(2)}, u32[]{:S(2)}) %collective-permute-start.5) | collective-permute-done | bytes 393248 | tf_op jit(solution)/shard_map/ppermute | solution.py:338
  33.2 0.2 collective-permute-start.10
  33.5 0.0 collective-permute-done.6.refs_1_
  33.5 0.3 collective-permute-start.11
  33.8 0.0 collective-permute-done.7.refs_2_
  33.8 0.2 collective-permute-start.3
  34.0 0.2 arrange.1.values
  34.2 0.0 copy-start
  34.3 0.7 %copy-done = f32[2,8,128]{2,1,0:T(8,128)S(1)} copy-done((f32[2,8,128]{2,1,0:T(8,128)S(1)}, f32[2,8,128]{2,1,0:T(8,128)}, u32[]{:S(2)}) %copy-start) | copy-done | bytes 8216
  34.9 0.3 copy-done.1
  35.2 0.1 copy-done.2
  35.3 0.4 prepare.4.close
  35.7 0.3 copy-done.4
  36.0 3.0 %attend.3.refs_4_.refs_2_ = f32[4,128]{1,0:T(4,128)S(1)} custom-call(s32[4,4]{1,0:T(4,128)S(1)} %copy-done.4, f32[2,8,128]{2,1,0:T(8,128)S(1)} %copy-done, bf16[8,4,64,128]{3,2,1,0:T(8,128)(2,1)S(1)} %arrange.1.values, bf16[4,4,4,64,128]{4,3,2,1,0:T(8,128)(2,1)S(1)} %prepare.4.close, bf16[4,3,128,128]{3,2,1,0:T(8,128)(2,1)S(1)} %collective-permute-done.4.refs_0_, ...), custom_call_target="tpu_custom_call" | custom-call | flops 402653184 | bytes 1048576 | tf_op jit(solution)/shard_map/attend/pallas_call | solution.py:300
  39.0 2.1 %pack.5 = (bf16[1,3,128,128]{3,2,1,0:T(8,128)(2,1)S(1)}, bf16[1,3,128,128]{3,2,1,0:T(8,128)(2,1)S(1)}, f32[8,128]{1,0:T(8,128)}) custom-call(bf16[1,4,32,32,128]{4,3,2,1,0:T(8,128)(2,1)} %refs_0_.5, bf16[1,4,32,32,128]{4,3,2,1,0:T(8,128)(2,1)} %refs_1_.5, bf16[1,4,32,32,128]{4,3,2,1,0:T(8,128)(2,1)} %refs_2_.5, bf16[1,4,32,32,128]{4,3,2,1,0:T(8,128)(2,1)} %refs_3_.5, ...), custom_call_target="tpu_custom_call" | custom-call | flops 2097152 | bytes 4194304 | tf_op jit(solution)/shard_map/pack/pallas_call | solution.py:145
  41.1 0.0 collective-permute-done.3.refs_1_
  41.1 2.1 %collective-permute-start.8 = (bf16[1,3,128,128]{3,2,1,0:T(8,128)(2,1)S(1)}, bf16[1,3,128,128]{3,2,1,0:T(8,128)(2,1)S(1)}, u32[]{:S(2)}, u32[]{:S(2)}) collective-permute-start(bf16[1,3,128,128]{3,2,1,0:T(8,128)(2,1)S(1)} %get-tuple-element.45), channel_id=1, source_target_pairs={{0,2},{1,3},{2,0},{3,1},{4,6},{5,7},{6,4},{7,5},{8,10},{9,11},{10,... | collective-permute-start | bytes 294920 | tf_op jit(solution)/shard_map/ppermute | solution.py:338
  43.2 0.0 collective-permute-done.10.refs_0_
  43.2 0.2 prepare.3.close
  43.4 0.8 %copy-done.3 = bf16[3,2,128,128]{3,2,1,0:T(8,128)(2,1)S(1)} copy-done((bf16[3,2,128,128]{3,2,1,0:T(8,128)(2,1)S(1)}, bf16[3,2,128,128]{3,2,1,0:T(8,128)(2,1)}, u32[]{:S(2)}) %copy-start.3) | copy-done | bytes 196632
  44.2 0.3 prepare.5.close
  44.5 1.5 %collective-permute-done.13.refs_1_ = bf16[3,3,128,128]{3,2,1,0:T(8,128)(2,1)S(1)} collective-permute-done((bf16[3,3,128,128]{3,2,1,0:T(8,128)(2,1)}, bf16[3,3,128,128]{3,2,1,0:T(8,128)(2,1)S(1)}, u32[]{:S(2)}, u32[]{:S(2)}) %collective-permute-start.13) | collective-permute-done | bytes 294944 | tf_op jit(solution)/shard_map/ppermute | solution.py:338
  46.0 2.4 %attend.4.refs_3_ = f32[3,128]{1,0:T(4,128)S(1)} custom-call(s32[4,4]{1,0:T(4,128)S(1)} %copy-done.4, f32[2,8,128]{2,1,0:T(8,128)S(1)} %copy-done, bf16[8,4,64,128]{3,2,1,0:T(8,128)(2,1)S(1)} %arrange.1.values, bf16[3,4,4,64,128]{4,3,2,1,0:T(8,128)(2,1)S(1)} %prepare.5.close, bf16[3,3,128,128]{3,2,1,0:T(8,128)(2,1)S(1)} %collective-permute-done.12.refs_0_, ...), custom_call_target="tpu_custom_call" | custom-call | flops 301989888 | bytes 786432 | tf_op jit(solution)/shard_map/attend/pallas_call | solution.py:300
  48.4 0.0 collective-permute-done.8.refs_0_
  48.5 0.5 collective-permute-done.9.refs_1_
  49.0 1.0 %attend.5 = (f32[2,8,32]{2,1,0:T(8,128)S(1)}, f32[2,8,32]{2,1,0:T(8,128)S(1)}, f32[2,8,32]{2,1,0:T(8,128)S(1)}, f32[2,8,32]{2,1,0:T(8,128)S(1)}) custom-call(s32[4,4]{1,0:T(4,128)S(1)} %copy-done.4, f32[2,8,128]{2,1,0:T(8,128)S(1)} %copy-done, bf16[8,4,64,128]{3,2,1,0:T(8,128)(2,1)S(1)} %arrange.1.values, bf16[1,4,4,64,128]{4,3,2,1,0:T(8,128)(2,1)S(1)} %prepare.3.close, ...), custom_call_target="tpu_custom_call" | custom-call | flops 100663296 | bytes 262144 | tf_op jit(solution)/shard_map/attend/pallas_call | solution.py:300
  50.0 3.6 %collective-permute-start.14 = (f32[2,8,32]{2,1,0:T(8,128)S(1)}, f32[2,8,32]{2,1,0:T(8,128)S(1)}, u32[]{:S(2)}, u32[]{:S(2)}) collective-permute-start(f32[2,8,32]{2,1,0:T(8,128)S(1)} %get-tuple-element.54), channel_id=1, source_target_pairs={{0,12},{4,8},{8,4},{12,0},{1,13},{5,9},{9,5},{13,1},{2,14},{6,10},... | collective-permute-start | bytes 6152 | tf_op jit(solution)/shard_map/ppermute | solution.py:374
  53.6 0.8 %collective-permute-start.16 = (f32[2,8,32]{2,1,0:T(8,128)S(1)}, f32[2,8,32]{2,1,0:T(8,128)S(1)}, u32[]{:S(2)}, u32[]{:S(2)}) collective-permute-start(f32[2,8,32]{2,1,0:T(8,128)S(1)} %get-tuple-element.56), channel_id=1, source_target_pairs={{0,4},{4,0},{8,12},{12,8},{1,5},{5,1},{9,13},{13,9},{2,6},{6,2},{1... | collective-permute-start | bytes 6152 | tf_op jit(solution)/shard_map/ppermute | solution.py:374
  54.4 1.0 %collective-permute-done.14 = f32[2,8,32]{2,1,0:T(8,128)S(1)} collective-permute-done((f32[2,8,32]{2,1,0:T(8,128)S(1)}, f32[2,8,32]{2,1,0:T(8,128)S(1)}, u32[]{:S(2)}, u32[]{:S(2)}) %collective-permute-start.14) | collective-permute-done | bytes 2080 | tf_op jit(solution)/shard_map/ppermute | solution.py:374
  55.5 2.7 %collective-permute-done.15 = f32[2,8,32]{2,1,0:T(8,128)S(1)} collective-permute-done((f32[2,8,32]{2,1,0:T(8,128)S(1)}, f32[2,8,32]{2,1,0:T(8,128)S(1)}, u32[]{:S(2)}, u32[]{:S(2)}) %collective-permute-start.15) | collective-permute-done | bytes 2080 | tf_op jit(solution)/shard_map/ppermute | solution.py:374
  58.2 0.0 collective-permute-done.16
  58.2 0.6 %add_add_fusion = f32[2,8,32]{2,1,0:T(8,128)} fusion(f32[2,8,32]{2,1,0:T(8,128)S(1)} %collective-permute-done.16, f32[2,8,32]{2,1,0:T(8,128)S(1)} %collective-permute-done.15, f32[2,8,32]{2,1,0:T(8,128)S(1)} %get-tuple-element.53, f32[2,8,32]{2,1,0:T(8,128)S(1)} %collective-permute-done.14), kind=kLoop, calls=%fused_computation | loop fusion | flops 1536 | bytes 10240 | tf_op jit(solution)/shard_map/add | solution.py:374
  (10 shorter events, 0.0 us)
Async XLA Ops:
  1.1 10.1 %collective-permute-start = (bf16[4,32,8,128]{3,2,1,0:T(8,128)(2,1)S(1)}, bf16[4,32,8,128]{3,2,1,0:T(8,128)(2,1)S(1)}, u32[]{:S(2)}, u32[]{:S(2)}) collective-permute-start(bf16[4,32,8,128]{3,2,1,0:T(8,128)(2,1)S(1)} %get-tuple-element.31), channel_id=1, source_target_pairs={{0,2},{1,3},{2,0},{3,1},{4,6},{5,7},{6,4},{7,5},{8,10},{9,11},{10,... | collective-permute-start | bytes 786440 | tf_op jit(solution)/shard_map/ppermute | solution.py:338
  4.1 12.3 %collective-permute-start.1 = (bf16[4,32,8,128]{3,2,1,0:T(8,128)(2,1)S(1)}, bf16[4,32,8,128]{3,2,1,0:T(8,128)(2,1)S(1)}, u32[]{:S(2)}, u32[]{:S(2)}) collective-permute-start(bf16[4,32,8,128]{3,2,1,0:T(8,128)(2,1)S(1)} %get-tuple-element.32), channel_id=1, source_target_pairs={{0,3},{1,2},{2,1},{3,0},{4,7},{5,6},{6,5},{7,4},{8,11},{9,10},{10,... | collective-permute-start | bytes 786440 | tf_op jit(solution)/shard_map/ppermute | solution.py:338
  5.6 19.6 %collective-permute-start.4 = (bf16[4,3,128,128]{3,2,1,0:T(8,128)(2,1)S(1)}, bf16[4,3,128,128]{3,2,1,0:T(8,128)(2,1)S(1)}, u32[]{:S(2)}, u32[]{:S(2)}) collective-permute-start(bf16[4,3,128,128]{3,2,1,0:T(8,128)(2,1)S(1)} %get-tuple-element.39), channel_id=1, source_target_pairs={{0,2},{1,3},{2,0},{3,1},{4,6},{5,7},{6,4},{7,5},{8,10},{9,11},{10,... | collective-permute-start | bytes 1179656 | tf_op jit(solution)/shard_map/ppermute | solution.py:338
  6.9 26.4 %collective-permute-start.5 = (bf16[4,3,128,128]{3,2,1,0:T(8,128)(2,1)S(1)}, bf16[4,3,128,128]{3,2,1,0:T(8,128)(2,1)S(1)}, u32[]{:S(2)}, u32[]{:S(2)}) collective-permute-start(bf16[4,3,128,128]{3,2,1,0:T(8,128)(2,1)S(1)} %get-tuple-element.40), channel_id=1, source_target_pairs={{0,3},{1,2},{2,1},{3,0},{4,7},{5,6},{6,5},{7,4},{8,11},{9,10},{10,... | collective-permute-start | bytes 1179656 | tf_op jit(solution)/shard_map/ppermute | solution.py:338
  20.2 13.3 %collective-permute-start.6 = (bf16[4,2,128,128]{3,2,1,0:T(8,128)(2,1)}, bf16[4,2,128,128]{3,2,1,0:T(8,128)(2,1)S(1)}, u32[]{:S(2)}, u32[]{:S(2)}) collective-permute-start(bf16[4,2,128,128]{3,2,1,0:T(8,128)(2,1)} %get-tuple-element.41), channel_id=1, source_target_pairs={{0,1},{1,0},{2,3},{3,2},{4,5},{5,4},{6,7},{7,6},{8,9},{9,8},{10,11... | collective-permute-start | bytes 786440 | tf_op jit(solution)/shard_map/ppermute | solution.py:338
  20.5 13.3 %collective-permute-start.7 = (bf16[4,2,128,128]{3,2,1,0:T(8,128)(2,1)}, bf16[4,2,128,128]{3,2,1,0:T(8,128)(2,1)S(1)}, u32[]{:S(2)}, u32[]{:S(2)}) collective-permute-start(bf16[4,2,128,128]{3,2,1,0:T(8,128)(2,1)} %get-tuple-element.42), channel_id=1, source_target_pairs={{0,1},{1,0},{2,3},{3,2},{4,5},{5,4},{6,7},{7,6},{8,9},{9,8},{10,11... | collective-permute-start | bytes 786440 | tf_op jit(solution)/shard_map/ppermute | solution.py:338
  20.8 1.5 %collective-permute-start.2 = (bf16[1,2,128,128]{3,2,1,0:T(8,128)(2,1)S(1)}, bf16[1,2,128,128]{3,2,1,0:T(8,128)(2,1)S(1)}, u32[]{:S(2)}, u32[]{:S(2)}) collective-permute-start(bf16[1,2,128,128]{3,2,1,0:T(8,128)(2,1)S(1)} %get-tuple-element.35), channel_id=1, source_target_pairs={{0,1},{1,0},{2,3},{3,2},{4,5},{5,4},{6,7},{7,6},{8,9},{9,8},{10,11... | collective-permute-start | bytes 196616 | tf_op jit(solution)/shard_map/ppermute | solution.py:338
  22.2 22.2 %collective-permute-start.12 = (bf16[3,3,128,128]{3,2,1,0:T(8,128)(2,1)}, bf16[3,3,128,128]{3,2,1,0:T(8,128)(2,1)S(1)}, u32[]{:S(2)}, u32[]{:S(2)}) collective-permute-start(bf16[3,3,128,128]{3,2,1,0:T(8,128)(2,1)} %get-tuple-element.51), channel_id=1, source_target_pairs={{0,2},{1,3},{2,0},{3,1},{4,6},{5,7},{6,4},{7,5},{8,10},{9,11},{10,... | collective-permute-start | bytes 884744 | tf_op jit(solution)/shard_map/ppermute | solution.py:338
  25.2 20.7 %collective-permute-start.13 = (bf16[3,3,128,128]{3,2,1,0:T(8,128)(2,1)}, bf16[3,3,128,128]{3,2,1,0:T(8,128)(2,1)S(1)}, u32[]{:S(2)}, u32[]{:S(2)}) collective-permute-start(bf16[3,3,128,128]{3,2,1,0:T(8,128)(2,1)} %get-tuple-element.52), channel_id=1, source_target_pairs={{0,3},{1,2},{2,1},{3,0},{4,7},{5,6},{6,5},{7,4},{8,11},{9,10},{10,... | collective-permute-start | bytes 884744 | tf_op jit(solution)/shard_map/ppermute | solution.py:338
  33.2 10.0 %collective-permute-start.10 = (bf16[3,2,128,128]{3,2,1,0:T(8,128)(2,1)S(1)}, bf16[3,2,128,128]{3,2,1,0:T(8,128)(2,1)S(1)}, u32[]{:S(2)}, u32[]{:S(2)}) collective-permute-start(bf16[3,2,128,128]{3,2,1,0:T(8,128)(2,1)S(1)} %get-tuple-element.47), channel_id=1, source_target_pairs={{0,1},{1,0},{2,3},{3,2},{4,5},{5,4},{6,7},{7,6},{8,9},{9,8},{10,11... | collective-permute-start | bytes 589832 | tf_op jit(solution)/shard_map/ppermute | solution.py:338
  33.5 9.9 %collective-permute-start.11 = (bf16[3,2,128,128]{3,2,1,0:T(8,128)(2,1)S(1)}, bf16[3,2,128,128]{3,2,1,0:T(8,128)(2,1)S(1)}, u32[]{:S(2)}, u32[]{:S(2)}) collective-permute-start(bf16[3,2,128,128]{3,2,1,0:T(8,128)(2,1)S(1)} %get-tuple-element.48), channel_id=1, source_target_pairs={{0,1},{1,0},{2,3},{3,2},{4,5},{5,4},{6,7},{7,6},{8,9},{9,8},{10,11... | collective-permute-start | bytes 589832 | tf_op jit(solution)/shard_map/ppermute | solution.py:338
  33.8 7.3 %collective-permute-start.3 = (bf16[1,2,128,128]{3,2,1,0:T(8,128)(2,1)S(1)}, bf16[1,2,128,128]{3,2,1,0:T(8,128)(2,1)S(1)}, u32[]{:S(2)}, u32[]{:S(2)}) collective-permute-start(bf16[1,2,128,128]{3,2,1,0:T(8,128)(2,1)S(1)} %get-tuple-element.36), channel_id=1, source_target_pairs={{0,1},{1,0},{2,3},{3,2},{4,5},{5,4},{6,7},{7,6},{8,9},{9,8},{10,11... | collective-permute-start | bytes 196616 | tf_op jit(solution)/shard_map/ppermute | solution.py:338
  34.2 0.7 %copy-start = (f32[2,8,128]{2,1,0:T(8,128)S(1)}, f32[2,8,128]{2,1,0:T(8,128)}, u32[]{:S(2)}) copy-start(f32[2,8,128]{2,1,0:T(8,128)} %gains.11) | copy-start | bytes 24580
  34.3 1.0 %copy-start.1 = (bf16[4,2,128,128]{3,2,1,0:T(8,128)(2,1)S(1)}, bf16[4,2,128,128]{3,2,1,0:T(8,128)(2,1)}, u32[]{:S(2)}) copy-start(bf16[4,2,128,128]{3,2,1,0:T(8,128)(2,1)} %get-tuple-element.43.refs_3_) | copy-start | bytes 786436
  34.3 1.0 %copy-start.2 = (bf16[4,2,128,128]{3,2,1,0:T(8,128)(2,1)S(1)}, bf16[4,2,128,128]{3,2,1,0:T(8,128)(2,1)}, u32[]{:S(2)}) copy-start(bf16[4,2,128,128]{3,2,1,0:T(8,128)(2,1)} %get-tuple-element.44.refs_4_) | copy-start | bytes 786436
  35.3 0.7 %copy-start.4 = (s32[4,4]{1,0:T(4,128)S(1)}, s32[4,4]{1,0:T(4,128)}, u32[]{:S(2)}) copy-start(s32[4,4]{1,0:T(4,128)} %units.5) | copy-start | bytes 196
  41.1 7.3 %collective-permute-start.8 = (bf16[1,3,128,128]{3,2,1,0:T(8,128)(2,1)S(1)}, bf16[1,3,128,128]{3,2,1,0:T(8,128)(2,1)S(1)}, u32[]{:S(2)}, u32[]{:S(2)}) collective-permute-start(bf16[1,3,128,128]{3,2,1,0:T(8,128)(2,1)S(1)} %get-tuple-element.45), channel_id=1, source_target_pairs={{0,2},{1,3},{2,0},{3,1},{4,6},{5,7},{6,4},{7,5},{8,10},{9,11},{10,... | collective-permute-start | bytes 294920 | tf_op jit(solution)/shard_map/ppermute | solution.py:338
  43.2 5.7 %collective-permute-start.9 = (bf16[1,3,128,128]{3,2,1,0:T(8,128)(2,1)S(1)}, bf16[1,3,128,128]{3,2,1,0:T(8,128)(2,1)S(1)}, u32[]{:S(2)}, u32[]{:S(2)}) collective-permute-start(bf16[1,3,128,128]{3,2,1,0:T(8,128)(2,1)S(1)} %get-tuple-element.46), channel_id=1, source_target_pairs={{0,3},{1,2},{2,1},{3,0},{4,7},{5,6},{6,5},{7,4},{8,11},{9,10},{10,... | collective-permute-start | bytes 294920 | tf_op jit(solution)/shard_map/ppermute | solution.py:338
  43.2 0.9 %copy-start.3 = (bf16[3,2,128,128]{3,2,1,0:T(8,128)(2,1)S(1)}, bf16[3,2,128,128]{3,2,1,0:T(8,128)(2,1)}, u32[]{:S(2)}) copy-start(bf16[3,2,128,128]{3,2,1,0:T(8,128)(2,1)} %get-tuple-element.50.refs_3_) | copy-start | bytes 589828
  50.0 5.5 %collective-permute-start.14 = (f32[2,8,32]{2,1,0:T(8,128)S(1)}, f32[2,8,32]{2,1,0:T(8,128)S(1)}, u32[]{:S(2)}, u32[]{:S(2)}) collective-permute-start(f32[2,8,32]{2,1,0:T(8,128)S(1)} %get-tuple-element.54), channel_id=1, source_target_pairs={{0,12},{4,8},{8,4},{12,0},{1,13},{5,9},{9,5},{13,1},{2,14},{6,10},... | collective-permute-start | bytes 6152 | tf_op jit(solution)/shard_map/ppermute | solution.py:374
  53.6 4.5 %collective-permute-start.15 = (f32[2,8,32]{2,1,0:T(8,128)S(1)}, f32[2,8,32]{2,1,0:T(8,128)S(1)}, u32[]{:S(2)}, u32[]{:S(2)}) collective-permute-start(f32[2,8,32]{2,1,0:T(8,128)S(1)} %get-tuple-element.55), channel_id=1, source_target_pairs={{0,8},{4,12},{8,0},{12,4},{1,9},{5,13},{9,1},{13,5},{2,10},{6,14},... | collective-permute-start | bytes 6152 | tf_op jit(solution)/shard_map/ppermute | solution.py:374
  53.6 4.5 %collective-permute-start.16 = (f32[2,8,32]{2,1,0:T(8,128)S(1)}, f32[2,8,32]{2,1,0:T(8,128)S(1)}, u32[]{:S(2)}, u32[]{:S(2)}) collective-permute-start(f32[2,8,32]{2,1,0:T(8,128)S(1)} %get-tuple-element.56), channel_id=1, source_target_pairs={{0,4},{4,0},{8,12},{12,8},{1,5},{5,1},{9,13},{13,9},{2,6},{6,2},{1... | collective-permute-start | bytes 6152 | tf_op jit(solution)/shard_map/ppermute | solution.py:374

commit v8 on v7

--- a/solution.py
+++ b/solution.py
@@ -264,44 +264,34 @@
     attention_chunk(low, out.shape[0], units, gains, values, close, pieces, held, out)
 
 
-def last_kernel(low, sources, earlier, peers, units, gains, values, close, *refs):
-    pieces = refs[:sources]
-    before = refs[sources : sources + earlier]
-    outs = refs[sources + earlier : sources + earlier + len(peers)]
-    held, total = refs[sources + earlier + len(peers) : -1], refs[-1]
+def last_kernel(low, sources, units, gains, values, close, *refs):
+    pieces, before = refs[:sources], refs[sources:-6]
+    out, held, total = refs[-6], refs[-5:-1], refs[-1]
+    row = 0
+    for ref in before:
+        out[row : row + ref.shape[0], :] = ref[...]
+        row += ref.shape[0]
     attention_chunk(low, total.shape[0], units, gains, values, close, pieces, held, total)
-    group = lax.axis_index("dp")
-    size = total.shape[-1]
-    width = outs[0].shape[-1]
-    scaled = jnp.concatenate([ref[...] for ref in before] + [total[...]], axis=0) * (size ** (-0.5))
-    for side in range(2):
-        grads = scaled / gains[side]
-        for out, flip in zip(outs, peers):
-            shift = lax.rem(size - jnp.bitwise_xor(group, flip) * width, size)
-            out[side] = pltpu.roll(grads, shift, 1)[:, :width]
-
-
-def attend(low, count, units, gains, values, close, pieces, earlier=None, peers=None):
+    out[row:, :] = total[...]
+
+
+def attend(low, count, units, gains, values, close, pieces, earlier=None):
     _, _, tokens, size = pieces[0].shape
     all_tokens = close.shape[2] * close.shape[3] + tokens * len(pieces)
     held = [pltpu.VMEM((count, all_tokens, size), jnp.bfloat16)] * 4
     if earlier is None:
         kernel = functools.partial(chunk_kernel, low)
-        shapes = jax.ShapeDtypeStruct((count, size), jnp.float32)
-        earlier = []
-        outs = pl.BlockSpec(memory_space=pltpu.VMEM)
+        rows, earlier = count, []
     else:
-        kernel = functools.partial(last_kernel, low, len(pieces), len(earlier), peers)
-        heads = gains.shape[1]
-        shapes = [jax.ShapeDtypeStruct((2, heads, size // len(peers)), jnp.float32)] * len(peers)
+        kernel = functools.partial(last_kernel, low, len(pieces))
+        rows = low + count
         held.append(pltpu.VMEM((count, size), jnp.float32))
-        outs = [pl.BlockSpec(memory_space=pltpu.VMEM)] * len(peers)
     pairs = count * all_tokens * all_tokens // 2
     return pl.pallas_call(
         kernel,
-        out_shape=shapes,
+        out_shape=jax.ShapeDtypeStruct((rows, size), jnp.float32),
         in_specs=[pl.BlockSpec(memory_space=pltpu.VMEM)] * (4 + len(pieces) + len(earlier)),
-        out_specs=outs,
+        out_specs=pl.BlockSpec(memory_space=pltpu.VMEM),
         scratch_shapes=held,
         compiler_params=pltpu.CompilerParams(vmem_limit_bytes=VMEM_LIMIT),
         cost_estimate=pl.CostEstimate(
@@ -309,6 +299,28 @@
         ),
         name="attend",
     )(units, gains, values, close, *pieces, *earlier)
+
+
+def finish_kernel(gains, *refs):
+    sums, out = refs[:-1], refs[-1]
+    size, width = sums[0].shape[-1], out.shape[-1]
+    shift = lax.rem(size - lax.axis_index("dp") * width, size)
+    total = sum(ref[...] for ref in sums) * (size ** (-0.5))
+    for side in range(2):
+        out[side] = pltpu.roll(total / gains[side], shift, 1)[:, :width]
+
+
+def finish(gains, sums):
+    heads, size = sums[0].shape
+    return pl.pallas_call(
+        finish_kernel,
+        out_shape=jax.ShapeDtypeStruct((2, heads, size // len(sums)), jnp.float32),
+        in_specs=[pl.BlockSpec(memory_space=pltpu.VMEM)] * (1 + len(sums)),
+        out_specs=pl.BlockSpec(memory_space=pltpu.VMEM),
+        compiler_params=pltpu.CompilerParams(vmem_limit_bytes=VMEM_LIMIT),
+        cost_estimate=pl.CostEstimate(flops=1, bytes_accessed=1, transcendentals=0),
+        name="finish",
+    )(gains, *sums)
 
 
 def seen_kernel(*refs):
@@ -366,13 +378,10 @@
         if number + 2 < len(chunks):
             waiting, _ = pack_and_send(far_plan(number + 2), sums[-1:])
     low, high = chunks[-1]
-    parts = attend(
-        low, high - low, clip_units, norm_gains, values, prepared[-1], received, sums, list(range(groups))
-    )
-    result = parts[0]
+    sums = [attend(low, high - low, clip_units, norm_gains, values, prepared[-1], received, sums)]
     for flip in reversed(range(1, groups)):
-        result = result + lax.ppermute(parts[flip], "dp", [(g, g ^ flip) for g in range(groups)])
-    return result
+        sums.append(lax.ppermute(sums[0], "dp", [(g, g ^ flip) for g in range(groups)]))
+    return finish(norm_gains, sums)
 
 
 def solution(mesh):

time: 59 us -> 59 us (level)
  Pallas kernels: 16 us -> 16.8 us
  other arithmetic: 0.6 us -> 0 us
    pallas_call x3 -> x4, Pallas kernels: 6.51 us -> 7.34 us  [the longest x3 6.66 us: attend(): pl.pallas_call(kernel, out_shape=jax.ShapeDtypeStruct((rows, size), jnp.f...]
    add x1 -> x0, other arithmetic: 0.6 us -> none  [body(): result + lax.ppermute(parts[flip], 'dp', [(g, g ^ flip) for g in range(gr...]
where the time goes in v8:
time: 59 us; the launch traced here: 58.8 us
  waiting for transfers between devices  24.8 us (42%)
  Pallas kernels  16.8 us (28%)
  starting transfers between devices  15 us (25%)
  local copies, waits for them, and re-layouts  2.08 us (4%)
    ppermute x14, waiting for transfers between devices, send(): return lax.ppermute(block, 'seq', [(s, s ^ flip) for s in range(sequence)])  21.1 us
    ppermute x14, starting transfers between devices, send(): return lax.ppermute(block, 'seq', [(s, s ^ flip) for s in range(sequence)])  10.5 us
    pallas_call x3, Pallas kernels, pack(): pl.pallas_call(functools.partial(pack_kernel, plan, heads, len(after)), o...  7.35 us
    pallas_call x3, Pallas kernels, attend(): pl.pallas_call(kernel, out_shape=jax.ShapeDtypeStruct((rows, size), jnp.f...  6.66 us
    ppermute x3, starting transfers between devices, body(): lax.ppermute(sums[0], 'dp', [(g, g ^ flip) for g in range(groups)])  4.45 us
    ppermute x3, waiting for transfers between devices, body(): lax.ppermute(sums[0], 'dp', [(g, g ^ flip) for g in range(groups)])  3.68 us
    unnamed x10, local copies, waits for them, and re-layouts  2.08 us
  transfers between devices with their start and end apart: 17, of which 9 were waited for; matrix products, arithmetic and copies ran while one was open for 0% of the time, Pallas kernels for 24%

profile of v8, /device:TPU:0, one launch (start us, length us, event | category | flops | bytes accessed | tf_op | source)
XLA Modules:
  0.0 58.8 jit_solution(6072463794123598203)
XLA Ops:
  0.0 1.1 %cut.1 = (bf16[4,32,8,128]{3,2,1,0:T(8,128)(2,1)S(1)}, bf16[4,32,8,128]{3,2,1,0:T(8,128)(2,1)S(1)}, f32[8,128]{1,0:T(8,128)S(1)}) custom-call(bf16[1,4,32,32,128]{4,3,2,1,0:T(8,128)(2,1)} %refs_2_.5), custom_call_target="tpu_custom_call" | custom-call | tf_op jit(solution)/shard_map/cut/pallas_call | solution.py:53
  1.1 3.0 %collective-permute-start = (bf16[4,32,8,128]{3,2,1,0:T(8,128)(2,1)S(1)}, bf16[4,32,8,128]{3,2,1,0:T(8,128)(2,1)S(1)}, u32[]{:S(2)}, u32[]{:S(2)}) collective-permute-start(bf16[4,32,8,128]{3,2,1,0:T(8,128)(2,1)S(1)} %get-tuple-element.27), channel_id=1, source_target_pairs={{0,2},{1,3},{2,0},{3,1},{4,6},{5,7},{6,4},{7,5},{8,10},{9,11},{10,... | collective-permute-start | bytes 786440 | tf_op jit(solution)/shard_map/ppermute | solution.py:350
  4.1 0.0 collective-permute-start.1
  4.1 1.5 %pack.3 = (bf16[4,3,128,128]{3,2,1,0:T(8,128)(2,1)S(1)}, bf16[4,3,128,128]{3,2,1,0:T(8,128)(2,1)S(1)}, f32[8,128]{1,0:T(8,128)S(1)}) custom-call(bf16[1,4,32,32,128]{4,3,2,1,0:T(8,128)(2,1)} %refs_0_.5, bf16[1,4,32,32,128]{4,3,2,1,0:T(8,128)(2,1)} %refs_1_.5, bf16[1,4,32,32,128]{4,3,2,1,0:T(8,128)(2,1)} %refs_2_.5, bf16[1,4,32,32,128]{4,3,2,1,0:T(8,128)(2,1)} %refs_3_.5, ...), custom_call_target="tpu_custom_call" | custom-call | flops 2097152 | bytes 4194304 | tf_op jit(solution)/shard_map/pack/pallas_call | solution.py:145
  5.6 1.2 %collective-permute-start.4 = (bf16[4,3,128,128]{3,2,1,0:T(8,128)(2,1)S(1)}, bf16[4,3,128,128]{3,2,1,0:T(8,128)(2,1)S(1)}, u32[]{:S(2)}, u32[]{:S(2)}) collective-permute-start(bf16[4,3,128,128]{3,2,1,0:T(8,128)(2,1)S(1)} %get-tuple-element.35), channel_id=1, source_target_pairs={{0,2},{1,3},{2,0},{3,1},{4,6},{5,7},{6,4},{7,5},{8,10},{9,11},{10,... | collective-permute-start | bytes 1179656 | tf_op jit(solution)/shard_map/ppermute | solution.py:350
  6.9 0.6 %collective-permute-start.5 = (bf16[4,3,128,128]{3,2,1,0:T(8,128)(2,1)S(1)}, bf16[4,3,128,128]{3,2,1,0:T(8,128)(2,1)S(1)}, u32[]{:S(2)}, u32[]{:S(2)}) collective-permute-start(bf16[4,3,128,128]{3,2,1,0:T(8,128)(2,1)S(1)} %get-tuple-element.36), channel_id=1, source_target_pairs={{0,3},{1,2},{2,1},{3,0},{4,7},{5,6},{6,5},{7,4},{8,11},{9,10},{10,... | collective-permute-start | bytes 1179656 | tf_op jit(solution)/shard_map/ppermute | solution.py:350
  7.5 3.7 %collective-permute-done.refs_0_ = bf16[4,32,8,128]{3,2,1,0:T(8,128)(2,1)S(1)} collective-permute-done((bf16[4,32,8,128]{3,2,1,0:T(8,128)(2,1)S(1)}, bf16[4,32,8,128]{3,2,1,0:T(8,128)(2,1)S(1)}, u32[]{:S(2)}, u32[]{:S(2)}) %collective-permute-start) | collective-permute-done | bytes 262176 | tf_op jit(solution)/shard_map/ppermute | solution.py:350
  11.2 5.2 %collective-permute-done.1.refs_1_ = bf16[4,32,8,128]{3,2,1,0:T(8,128)(2,1)S(1)} collective-permute-done((bf16[4,32,8,128]{3,2,1,0:T(8,128)(2,1)S(1)}, bf16[4,32,8,128]{3,2,1,0:T(8,128)(2,1)S(1)}, u32[]{:S(2)}, u32[]{:S(2)}) %collective-permute-start.1) | collective-permute-done | bytes 262176 | tf_op jit(solution)/shard_map/ppermute | solution.py:350
  16.4 3.8 %pack.4 = (bf16[3,3,128,128]{3,2,1,0:T(8,128)(2,1)}, bf16[3,3,128,128]{3,2,1,0:T(8,128)(2,1)}, bf16[4,2,128,128]{3,2,1,0:T(8,128)(2,1)}, bf16[3,2,128,128]{3,2,1...) custom-call(bf16[1,4,32,32,128]{4,3,2,1,0:T(8,128)(2,1)} %refs_0_.5,, ...), custom_call_target="tpu_custom_call" | custom-call | flops 6291456 | bytes 12582912 | tf_op jit(solution)/shard_map/pack/pallas_call | solution.py:145
  20.2 0.3 collective-permute-start.6
  20.5 0.3 collective-permute-start.7
  20.7 0.2 collective-permute-start.2
  21.0 1.2 %collective-permute-done.2.refs_0_ = bf16[1,2,128,128]{3,2,1,0:T(8,128)(2,1)S(1)} collective-permute-done((bf16[1,2,128,128]{3,2,1,0:T(8,128)(2,1)S(1)}, bf16[1,2,128,128]{3,2,1,0:T(8,128)(2,1)S(1)}, u32[]{:S(2)}, u32[]{:S(2)}) %collective-permute-start.2) | collective-permute-done | bytes 65568 | tf_op jit(solution)/shard_map/ppermute | solution.py:350
  22.2 1.9 %collective-permute-start.12 = (bf16[3,3,128,128]{3,2,1,0:T(8,128)(2,1)}, bf16[3,3,128,128]{3,2,1,0:T(8,128)(2,1)S(1)}, u32[]{:S(2)}, u32[]{:S(2)}) collective-permute-start(bf16[3,3,128,128]{3,2,1,0:T(8,128)(2,1)} %get-tuple-element.47), channel_id=1, source_target_pairs={{0,2},{1,3},{2,0},{3,1},{4,6},{5,7},{6,4},{7,5},{8,10},{9,11},{10,... | collective-permute-start | bytes 884744 | tf_op jit(solution)/shard_map/ppermute | solution.py:350
  24.2 1.1 %collective-permute-done.4.refs_0_ = bf16[4,3,128,128]{3,2,1,0:T(8,128)(2,1)S(1)} collective-permute-done((bf16[4,3,128,128]{3,2,1,0:T(8,128)(2,1)S(1)}, bf16[4,3,128,128]{3,2,1,0:T(8,128)(2,1)S(1)}, u32[]{:S(2)}, u32[]{:S(2)}) %collective-permute-start.4) | collective-permute-done | bytes 393248 | tf_op jit(solution)/shard_map/ppermute | solution.py:350
  25.2 0.0 collective-permute-start.13
  25.2 8.0 %collective-permute-done.5.refs_1_ = bf16[4,3,128,128]{3,2,1,0:T(8,128)(2,1)S(1)} collective-permute-done((bf16[4,3,128,128]{3,2,1,0:T(8,128)(2,1)S(1)}, bf16[4,3,128,128]{3,2,1,0:T(8,128)(2,1)S(1)}, u32[]{:S(2)}, u32[]{:S(2)}) %collective-permute-start.5) | collective-permute-done | bytes 393248 | tf_op jit(solution)/shard_map/ppermute | solution.py:350
  33.2 0.2 collective-permute-start.10
  33.5 0.0 collective-permute-done.6.refs_1_
  33.5 0.3 collective-permute-start.11
  33.8 0.0 collective-permute-done.7.refs_2_
  33.8 0.2 collective-permute-start.3
  34.0 0.2 arrange.1.values
  34.2 0.0 copy-start
  34.3 0.7 %copy-done = f32[2,8,128]{2,1,0:T(8,128)S(1)} copy-done((f32[2,8,128]{2,1,0:T(8,128)S(1)}, f32[2,8,128]{2,1,0:T(8,128)}, u32[]{:S(2)}) %copy-start) | copy-done | bytes 8216
  34.9 0.3 copy-done.1
  35.2 0.1 copy-done.2
  35.3 0.4 prepare.4.close
  35.7 0.3 copy-done.4
  36.0 3.1 %attend.3.refs_4_.refs_2_ = f32[4,128]{1,0:T(4,128)S(1)} custom-call(s32[4,4]{1,0:T(4,128)S(1)} %copy-done.4, f32[2,8,128]{2,1,0:T(8,128)S(1)} %copy-done, bf16[8,4,64,128]{3,2,1,0:T(8,128)(2,1)S(1)} %arrange.1.values, bf16[4,4,4,64,128]{4,3,2,1,0:T(8,128)(2,1)S(1)} %prepare.4.close, bf16[4,3,128,128]{3,2,1,0:T(8,128)(2,1)S(1)} %collective-permute-done.4.refs_0_, ...), custom_call_target="tpu_custom_call" | custom-call | flops 402653184 | bytes 1048576 | tf_op jit(solution)/shard_map/attend/pallas_call | solution.py:290
  39.1 2.1 %pack.5 = (bf16[1,3,128,128]{3,2,1,0:T(8,128)(2,1)S(1)}, bf16[1,3,128,128]{3,2,1,0:T(8,128)(2,1)S(1)}, f32[8,128]{1,0:T(8,128)}) custom-call(bf16[1,4,32,32,128]{4,3,2,1,0:T(8,128)(2,1)} %refs_0_.5, bf16[1,4,32,32,128]{4,3,2,1,0:T(8,128)(2,1)} %refs_1_.5, bf16[1,4,32,32,128]{4,3,2,1,0:T(8,128)(2,1)} %refs_2_.5, bf16[1,4,32,32,128]{4,3,2,1,0:T(8,128)(2,1)} %refs_3_.5, ...), custom_call_target="tpu_custom_call" | custom-call | flops 2097152 | bytes 4194304 | tf_op jit(solution)/shard_map/pack/pallas_call | solution.py:145
  41.2 2.1 %collective-permute-start.8 = (bf16[1,3,128,128]{3,2,1,0:T(8,128)(2,1)S(1)}, bf16[1,3,128,128]{3,2,1,0:T(8,128)(2,1)S(1)}, u32[]{:S(2)}, u32[]{:S(2)}) collective-permute-start(bf16[1,3,128,128]{3,2,1,0:T(8,128)(2,1)S(1)} %get-tuple-element.41), channel_id=1, source_target_pairs={{0,2},{1,3},{2,0},{3,1},{4,6},{5,7},{6,4},{7,5},{8,10},{9,11},{10,... | collective-permute-start | bytes 294920 | tf_op jit(solution)/shard_map/ppermute | solution.py:350
  43.3 0.0 collective-permute-start.9
  43.3 0.2 prepare.3.close
  43.5 0.8 %copy-done.3 = bf16[3,2,128,128]{3,2,1,0:T(8,128)(2,1)S(1)} copy-done((bf16[3,2,128,128]{3,2,1,0:T(8,128)(2,1)S(1)}, bf16[3,2,128,128]{3,2,1,0:T(8,128)(2,1)}, u32[]{:S(2)}) %copy-start.3) | copy-done | bytes 196632
  44.3 0.3 prepare.5.close
  44.6 0.0 collective-permute-done.12.refs_0_
  44.6 1.4 %collective-permute-done.13.refs_1_ = bf16[3,3,128,128]{3,2,1,0:T(8,128)(2,1)S(1)} collective-permute-done((bf16[3,3,128,128]{3,2,1,0:T(8,128)(2,1)}, bf16[3,3,128,128]{3,2,1,0:T(8,128)(2,1)S(1)}, u32[]{:S(2)}, u32[]{:S(2)}) %collective-permute-start.13) | collective-permute-done | bytes 294944 | tf_op jit(solution)/shard_map/ppermute | solution.py:350
  46.0 2.5 %attend.4.refs_3_ = f32[3,128]{1,0:T(4,128)S(1)} custom-call(s32[4,4]{1,0:T(4,128)S(1)} %copy-done.4, f32[2,8,128]{2,1,0:T(8,128)S(1)} %copy-done, bf16[8,4,64,128]{3,2,1,0:T(8,128)(2,1)S(1)} %arrange.1.values, bf16[3,4,4,64,128]{4,3,2,1,0:T(8,128)(2,1)S(1)} %prepare.5.close, bf16[3,3,128,128]{3,2,1,0:T(8,128)(2,1)S(1)} %collective-permute-done.12.refs_0_, ...), custom_call_target="tpu_custom_call" | custom-call | flops 301989888 | bytes 786432 | tf_op jit(solution)/shard_map/attend/pallas_call | solution.py:290
  48.5 0.4 collective-permute-done.9.refs_1_
  49.0 1.0 %attend.5.refs_0_ = f32[8,128]{1,0:T(8,128)S(1)} custom-call(s32[4,4]{1,0:T(4,128)S(1)} %copy-done.4, f32[2,8,128]{2,1,0:T(8,128)S(1)} %copy-done, bf16[8,4,64,128]{3,2,1,0:T(8,128)(2,1)S(1)} %arrange.1.values, bf16[1,4,4,64,128]{4,3,2,1,0:T(8,128)(2,1)S(1)} %prepare.3.close, bf16[1,3,128,128]{3,2,1,0:T(8,128)(2,1)S(1)} %collective-permute-done.8.refs_0_, ...), custom_call_target="tpu_custom_call" | custom-call | flops 100663296 | bytes 262144 | tf_op jit(solution)/shard_map/attend/pallas_call | solution.py:290
  50.0 3.6 %collective-permute-start.14 = (f32[8,128]{1,0:T(8,128)S(1)}, f32[8,128]{1,0:T(8,128)S(1)}, u32[]{:S(2)}, u32[]{:S(2)}) collective-permute-start(f32[8,128]{1,0:T(8,128)S(1)} %attend.5.refs_0_), channel_id=1, source_target_pairs={{0,12},{4,8},{8,4},{12,0},{1,13},{5,9},{9,5},{13,1},{2,14},{6,10},... | collective-permute-start | bytes 12296 | tf_op jit(solution)/shard_map/ppermute | solution.py:383
  53.6 0.0 collective-permute-start.15
  53.6 0.8 %collective-permute-start.16 = (f32[8,128]{1,0:T(8,128)S(1)}, f32[8,128]{1,0:T(8,128)S(1)}, u32[]{:S(2)}, u32[]{:S(2)}) collective-permute-start(f32[8,128]{1,0:T(8,128)S(1)} %attend.5.refs_0_), channel_id=1, source_target_pairs={{0,4},{4,0},{8,12},{12,8},{1,5},{5,1},{9,13},{13,9},{2,6},{6,2},{1... | collective-permute-start | bytes 12296 | tf_op jit(solution)/shard_map/ppermute | solution.py:383
  54.4 1.0 %collective-permute-done.14.refs_1_ = f32[8,128]{1,0:T(8,128)S(1)} collective-permute-done((f32[8,128]{1,0:T(8,128)S(1)}, f32[8,128]{1,0:T(8,128)S(1)}, u32[]{:S(2)}, u32[]{:S(2)}) %collective-permute-start.14) | collective-permute-done | bytes 4128 | tf_op jit(solution)/shard_map/ppermute | solution.py:383
  55.4 2.7 %collective-permute-done.15.refs_2_ = f32[8,128]{1,0:T(8,128)S(1)} collective-permute-done((f32[8,128]{1,0:T(8,128)S(1)}, f32[8,128]{1,0:T(8,128)S(1)}, u32[]{:S(2)}, u32[]{:S(2)}) %collective-permute-start.15) | collective-permute-done | bytes 4128 | tf_op jit(solution)/shard_map/ppermute | solution.py:383
  58.1 0.0 collective-permute-done.16.refs_3_
  58.1 0.7 %finish.1 = f32[2,8,32]{2,1,0:T(8,128)} custom-call(f32[2,8,128]{2,1,0:T(8,128)S(1)} %copy-done, f32[8,128]{1,0:T(8,128)S(1)} %attend.5.refs_0_, f32[8,128]{1,0:T(8,128)S(1)} %collective-permute-done.14.refs_1_, f32[8,128]{1,0:T(8,128)S(1)} %collective-permute-done.15.refs_2_, f32[8,128]{1,0:T(8,128)S(1)} %collective-permute-done.16.refs_3_), custom_call_target="tpu_custom_call" | custom-call | flops 1 | bytes 1 | tf_op jit(solution)/shard_map/finish/pallas_call | solution.py:315
  (10 shorter events, 0.0 us)
Async XLA Ops:
  1.1 10.1 %collective-permute-start = (bf16[4,32,8,128]{3,2,1,0:T(8,128)(2,1)S(1)}, bf16[4,32,8,128]{3,2,1,0:T(8,128)(2,1)S(1)}, u32[]{:S(2)}, u32[]{:S(2)}) collective-permute-start(bf16[4,32,8,128]{3,2,1,0:T(8,128)(2,1)S(1)} %get-tuple-element.27), channel_id=1, source_target_pairs={{0,2},{1,3},{2,0},{3,1},{4,6},{5,7},{6,4},{7,5},{8,10},{9,11},{10,... | collective-permute-start | bytes 786440 | tf_op jit(solution)/shard_map/ppermute | solution.py:350
  4.1 12.3 %collective-permute-start.1 = (bf16[4,32,8,128]{3,2,1,0:T(8,128)(2,1)S(1)}, bf16[4,32,8,128]{3,2,1,0:T(8,128)(2,1)S(1)}, u32[]{:S(2)}, u32[]{:S(2)}) collective-permute-start(bf16[4,32,8,128]{3,2,1,0:T(8,128)(2,1)S(1)} %get-tuple-element.28), channel_id=1, source_target_pairs={{0,3},{1,2},{2,1},{3,0},{4,7},{5,6},{6,5},{7,4},{8,11},{9,10},{10,... | collective-permute-start | bytes 786440 | tf_op jit(solution)/shard_map/ppermute | solution.py:350
  5.6 19.6 %collective-permute-start.4 = (bf16[4,3,128,128]{3,2,1,0:T(8,128)(2,1)S(1)}, bf16[4,3,128,128]{3,2,1,0:T(8,128)(2,1)S(1)}, u32[]{:S(2)}, u32[]{:S(2)}) collective-permute-start(bf16[4,3,128,128]{3,2,1,0:T(8,128)(2,1)S(1)} %get-tuple-element.35), channel_id=1, source_target_pairs={{0,2},{1,3},{2,0},{3,1},{4,6},{5,7},{6,4},{7,5},{8,10},{9,11},{10,... | collective-permute-start | bytes 1179656 | tf_op jit(solution)/shard_map/ppermute | solution.py:350
  6.9 26.4 %collective-permute-start.5 = (bf16[4,3,128,128]{3,2,1,0:T(8,128)(2,1)S(1)}, bf16[4,3,128,128]{3,2,1,0:T(8,128)(2,1)S(1)}, u32[]{:S(2)}, u32[]{:S(2)}) collective-permute-start(bf16[4,3,128,128]{3,2,1,0:T(8,128)(2,1)S(1)} %get-tuple-element.36), channel_id=1, source_target_pairs={{0,3},{1,2},{2,1},{3,0},{4,7},{5,6},{6,5},{7,4},{8,11},{9,10},{10,... | collective-permute-start | bytes 1179656 | tf_op jit(solution)/shard_map/ppermute | solution.py:350
  20.2 13.3 %collective-permute-start.6 = (bf16[4,2,128,128]{3,2,1,0:T(8,128)(2,1)}, bf16[4,2,128,128]{3,2,1,0:T(8,128)(2,1)S(1)}, u32[]{:S(2)}, u32[]{:S(2)}) collective-permute-start(bf16[4,2,128,128]{3,2,1,0:T(8,128)(2,1)} %get-tuple-element.37), channel_id=1, source_target_pairs={{0,1},{1,0},{2,3},{3,2},{4,5},{5,4},{6,7},{7,6},{8,9},{9,8},{10,11... | collective-permute-start | bytes 786440 | tf_op jit(solution)/shard_map/ppermute | solution.py:350
  20.5 13.3 %collective-permute-start.7 = (bf16[4,2,128,128]{3,2,1,0:T(8,128)(2,1)}, bf16[4,2,128,128]{3,2,1,0:T(8,128)(2,1)S(1)}, u32[]{:S(2)}, u32[]{:S(2)}) collective-permute-start(bf16[4,2,128,128]{3,2,1,0:T(8,128)(2,1)} %get-tuple-element.38), channel_id=1, source_target_pairs={{0,1},{1,0},{2,3},{3,2},{4,5},{5,4},{6,7},{7,6},{8,9},{9,8},{10,11... | collective-permute-start | bytes 786440 | tf_op jit(solution)/shard_map/ppermute | solution.py:350
  20.7 1.5 %collective-permute-start.2 = (bf16[1,2,128,128]{3,2,1,0:T(8,128)(2,1)S(1)}, bf16[1,2,128,128]{3,2,1,0:T(8,128)(2,1)S(1)}, u32[]{:S(2)}, u32[]{:S(2)}) collective-permute-start(bf16[1,2,128,128]{3,2,1,0:T(8,128)(2,1)S(1)} %get-tuple-element.31), channel_id=1, source_target_pairs={{0,1},{1,0},{2,3},{3,2},{4,5},{5,4},{6,7},{7,6},{8,9},{9,8},{10,11... | collective-permute-start | bytes 196616 | tf_op jit(solution)/shard_map/ppermute | solution.py:350
  22.2 22.3 %collective-permute-start.12 = (bf16[3,3,128,128]{3,2,1,0:T(8,128)(2,1)}, bf16[3,3,128,128]{3,2,1,0:T(8,128)(2,1)S(1)}, u32[]{:S(2)}, u32[]{:S(2)}) collective-permute-start(bf16[3,3,128,128]{3,2,1,0:T(8,128)(2,1)} %get-tuple-element.47), channel_id=1, source_target_pairs={{0,2},{1,3},{2,0},{3,1},{4,6},{5,7},{6,4},{7,5},{8,10},{9,11},{10,... | collective-permute-start | bytes 884744 | tf_op jit(solution)/shard_map/ppermute | solution.py:350
  25.2 20.7 %collective-permute-start.13 = (bf16[3,3,128,128]{3,2,1,0:T(8,128)(2,1)}, bf16[3,3,128,128]{3,2,1,0:T(8,128)(2,1)S(1)}, u32[]{:S(2)}, u32[]{:S(2)}) collective-permute-start(bf16[3,3,128,128]{3,2,1,0:T(8,128)(2,1)} %get-tuple-element.48), channel_id=1, source_target_pairs={{0,3},{1,2},{2,1},{3,0},{4,7},{5,6},{6,5},{7,4},{8,11},{9,10},{10,... | collective-permute-start | bytes 884744 | tf_op jit(solution)/shard_map/ppermute | solution.py:350
  33.2 10.1 %collective-permute-start.10 = (bf16[3,2,128,128]{3,2,1,0:T(8,128)(2,1)S(1)}, bf16[3,2,128,128]{3,2,1,0:T(8,128)(2,1)S(1)}, u32[]{:S(2)}, u32[]{:S(2)}) collective-permute-start(bf16[3,2,128,128]{3,2,1,0:T(8,128)(2,1)S(1)} %get-tuple-element.43), channel_id=1, source_target_pairs={{0,1},{1,0},{2,3},{3,2},{4,5},{5,4},{6,7},{7,6},{8,9},{9,8},{10,11... | collective-permute-start | bytes 589832 | tf_op jit(solution)/shard_map/ppermute | solution.py:350
  33.5 10.0 %collective-permute-start.11 = (bf16[3,2,128,128]{3,2,1,0:T(8,128)(2,1)S(1)}, bf16[3,2,128,128]{3,2,1,0:T(8,128)(2,1)S(1)}, u32[]{:S(2)}, u32[]{:S(2)}) collective-permute-start(bf16[3,2,128,128]{3,2,1,0:T(8,128)(2,1)S(1)} %get-tuple-element.44), channel_id=1, source_target_pairs={{0,1},{1,0},{2,3},{3,2},{4,5},{5,4},{6,7},{7,6},{8,9},{9,8},{10,11... | collective-permute-start | bytes 589832 | tf_op jit(solution)/shard_map/ppermute | solution.py:350
  33.8 7.4 %collective-permute-start.3 = (bf16[1,2,128,128]{3,2,1,0:T(8,128)(2,1)S(1)}, bf16[1,2,128,128]{3,2,1,0:T(8,128)(2,1)S(1)}, u32[]{:S(2)}, u32[]{:S(2)}) collective-permute-start(bf16[1,2,128,128]{3,2,1,0:T(8,128)(2,1)S(1)} %get-tuple-element.32), channel_id=1, source_target_pairs={{0,1},{1,0},{2,3},{3,2},{4,5},{5,4},{6,7},{7,6},{8,9},{9,8},{10,11... | collective-permute-start | bytes 196616 | tf_op jit(solution)/shard_map/ppermute | solution.py:350
  34.2 0.7 %copy-start = (f32[2,8,128]{2,1,0:T(8,128)S(1)}, f32[2,8,128]{2,1,0:T(8,128)}, u32[]{:S(2)}) copy-start(f32[2,8,128]{2,1,0:T(8,128)} %gains.13) | copy-start | bytes 24580
  34.3 1.0 %copy-start.1 = (bf16[4,2,128,128]{3,2,1,0:T(8,128)(2,1)S(1)}, bf16[4,2,128,128]{3,2,1,0:T(8,128)(2,1)}, u32[]{:S(2)}) copy-start(bf16[4,2,128,128]{3,2,1,0:T(8,128)(2,1)} %get-tuple-element.39.refs_3_) | copy-start | bytes 786436
  34.3 1.0 %copy-start.2 = (bf16[4,2,128,128]{3,2,1,0:T(8,128)(2,1)S(1)}, bf16[4,2,128,128]{3,2,1,0:T(8,128)(2,1)}, u32[]{:S(2)}) copy-start(bf16[4,2,128,128]{3,2,1,0:T(8,128)(2,1)} %get-tuple-element.40.refs_4_) | copy-start | bytes 786436
  35.3 0.7 %copy-start.4 = (s32[4,4]{1,0:T(4,128)S(1)}, s32[4,4]{1,0:T(4,128)}, u32[]{:S(2)}) copy-start(s32[4,4]{1,0:T(4,128)} %units.5) | copy-start | bytes 196
  41.2 7.3 %collective-permute-start.8 = (bf16[1,3,128,128]{3,2,1,0:T(8,128)(2,1)S(1)}, bf16[1,3,128,128]{3,2,1,0:T(8,128)(2,1)S(1)}, u32[]{:S(2)}, u32[]{:S(2)}) collective-permute-start(bf16[1,3,128,128]{3,2,1,0:T(8,128)(2,1)S(1)} %get-tuple-element.41), channel_id=1, source_target_pairs={{0,2},{1,3},{2,0},{3,1},{4,6},{5,7},{6,4},{7,5},{8,10},{9,11},{10,... | collective-permute-start | bytes 294920 | tf_op jit(solution)/shard_map/ppermute | solution.py:350
  43.3 5.6 %collective-permute-start.9 = (bf16[1,3,128,128]{3,2,1,0:T(8,128)(2,1)S(1)}, bf16[1,3,128,128]{3,2,1,0:T(8,128)(2,1)S(1)}, u32[]{:S(2)}, u32[]{:S(2)}) collective-permute-start(bf16[1,3,128,128]{3,2,1,0:T(8,128)(2,1)S(1)} %get-tuple-element.42), channel_id=1, source_target_pairs={{0,3},{1,2},{2,1},{3,0},{4,7},{5,6},{6,5},{7,4},{8,11},{9,10},{10,... | collective-permute-start | bytes 294920 | tf_op jit(solution)/shard_map/ppermute | solution.py:350
  43.3 0.9 %copy-start.3 = (bf16[3,2,128,128]{3,2,1,0:T(8,128)(2,1)S(1)}, bf16[3,2,128,128]{3,2,1,0:T(8,128)(2,1)}, u32[]{:S(2)}) copy-start(bf16[3,2,128,128]{3,2,1,0:T(8,128)(2,1)} %get-tuple-element.46.refs_3_) | copy-start | bytes 589828
  50.0 5.5 %collective-permute-start.14 = (f32[8,128]{1,0:T(8,128)S(1)}, f32[8,128]{1,0:T(8,128)S(1)}, u32[]{:S(2)}, u32[]{:S(2)}) collective-permute-start(f32[8,128]{1,0:T(8,128)S(1)} %attend.5.refs_0_), channel_id=1, source_target_pairs={{0,12},{4,8},{8,4},{12,0},{1,13},{5,9},{9,5},{13,1},{2,14},{6,10},... | collective-permute-start | bytes 12296 | tf_op jit(solution)/shard_map/ppermute | solution.py:383
  53.6 4.5 %collective-permute-start.15 = (f32[8,128]{1,0:T(8,128)S(1)}, f32[8,128]{1,0:T(8,128)S(1)}, u32[]{:S(2)}, u32[]{:S(2)}) collective-permute-start(f32[8,128]{1,0:T(8,128)S(1)} %attend.5.refs_0_), channel_id=1, source_target_pairs={{0,8},{4,12},{8,0},{12,4},{1,9},{5,13},{9,1},{13,5},{2,10},{6,14},... | collective-permute-start | bytes 12296 | tf_op jit(solution)/shard_map/ppermute | solution.py:383
  53.6 4.5 %collective-permute-start.16 = (f32[8,128]{1,0:T(8,128)S(1)}, f32[8,128]{1,0:T(8,128)S(1)}, u32[]{:S(2)}, u32[]{:S(2)}) collective-permute-start(f32[8,128]{1,0:T(8,128)S(1)} %attend.5.refs_0_), channel_id=1, source_target_pairs={{0,4},{4,0},{8,12},{12,8},{1,5},{5,1},{9,13},{13,9},{2,6},{6,2},{1... | collective-permute-start | bytes 12296 | tf_op jit(solution)/shard_map/ppermute | solution.py:383

commit v9 on v7

--- a/solution.py
+++ b/solution.py
@@ -276,8 +276,9 @@
     scaled = jnp.concatenate([ref[...] for ref in before] + [total[...]], axis=0) * (size ** (-0.5))
     for side in range(2):
         grads = scaled / gains[side]
-        for out, flip in zip(outs, peers):
-            shift = lax.rem(size - jnp.bitwise_xor(group, flip) * width, size)
+        for out, targets in zip(outs, peers):
+            target = sum(jnp.where(group == place, whom, 0) for place, whom in enumerate(targets))
+            shift = lax.rem(size - target * width, size)
             out[side] = pltpu.roll(grads, shift, 1)[:, :width]
 
 
@@ -327,6 +328,11 @@
     )(*blocks)
 
 
+def ring_targets(groups):
+    ring = [0] + list(range(1, groups, 2)) + list(range(2, groups, 2))[::-1]
+    return [[ring[(ring.index(place) + step) % groups] for place in range(groups)] for step in range(groups)]
+
+
 def body(sequence, groups, queries, key_rows, value_rows, out_grad, norm_gains, clip_units):
     arrays = (queries, key_rows, value_rows, out_grad)
     heads = norm_gains.shape[1]
@@ -338,6 +344,7 @@
         return lax.ppermute(block, "seq", [(s, s ^ flip) for s in range(sequence)])
 
     slots = clip_units.shape[1]
+    peers = ring_targets(groups)
     close = near + [0]
 
     def pack_and_send(plan, after):
@@ -367,11 +374,11 @@
             waiting, _ = pack_and_send(far_plan(number + 2), sums[-1:])
     low, high = chunks[-1]
     parts = attend(
-        low, high - low, clip_units, norm_gains, values, prepared[-1], received, sums, list(range(groups))
+        low, high - low, clip_units, norm_gains, values, prepared[-1], received, sums, peers
     )
     result = parts[0]
-    for flip in reversed(range(1, groups)):
-        result = result + lax.ppermute(parts[flip], "dp", [(g, g ^ flip) for g in range(groups)])
+    for part, targets in zip(parts[1:], peers[1:]):
+        result = result + lax.ppermute(part, "dp", list(enumerate(targets)))
     return result
 
 

time: 59 us -> 58.5 us (level)
  waiting for transfers between devices: 25 us -> 23.1 us
  starting transfers between devices: 15 us -> 16.2 us
    ppermute x3, waiting for transfers between devices: 3.74 us -> 1.97 us  [body(): result = result + lax.ppermute(part, 'dp', list(enumerate(targets)))]
    ppermute x3, starting transfers between devices: 4.43 us -> 5.62 us  [body(): result = result + lax.ppermute(part, 'dp', list(enumerate(targets)))]
where the time goes in v9:
time: 58.5 us; the launch traced here: 58.2 us
  waiting for transfers between devices  23.1 us (39%)
  starting transfers between devices  16.2 us (28%)
  Pallas kernels  16.1 us (28%)
  local copies, waits for them, and re-layouts  2.08 us (4%)
  other arithmetic  0.6 us (1%)
    ppermute x14, waiting for transfers between devices, send(): return lax.ppermute(block, 'seq', [(s, s ^ flip) for s in range(sequence)])  21.2 us
    ppermute x14, starting transfers between devices, send(): return lax.ppermute(block, 'seq', [(s, s ^ flip) for s in range(sequence)])  10.6 us
    pallas_call x3, Pallas kernels, pack(): pl.pallas_call(functools.partial(pack_kernel, plan, heads, len(after)), o...  7.37 us
    pallas_call x3, Pallas kernels, attend(): pl.pallas_call(kernel, out_shape=shapes, in_specs=[pl.BlockSpec(memory_sp...  6.62 us
    ppermute x3, starting transfers between devices, body(): result = result + lax.ppermute(part, 'dp', list(enumerate(targets)))  5.62 us
    unnamed x10, local copies, waits for them, and re-layouts  2.08 us
    ppermute x3, waiting for transfers between devices, body(): result = result + lax.ppermute(part, 'dp', list(enumerate(targets)))  1.97 us
  transfers between devices with their start and end apart: 17, of which 9 were waited for; matrix products, arithmetic and copies ran while one was open for 0% of the time, Pallas kernels for 24%

profile of v9, /device:TPU:0, one launch (start us, length us, event | category | flops | bytes accessed | tf_op | source)
XLA Modules:
  0.0 58.2 jit_solution(5715611067373060189)
XLA Ops:
  0.0 1.1 %cut.1 = (bf16[4,32,8,128]{3,2,1,0:T(8,128)(2,1)S(1)}, bf16[4,32,8,128]{3,2,1,0:T(8,128)(2,1)S(1)}, f32[8,128]{1,0:T(8,128)S(1)}) custom-call(bf16[1,4,32,32,128]{4,3,2,1,0:T(8,128)(2,1)} %refs_2_.5), custom_call_target="tpu_custom_call" | custom-call | tf_op jit(solution)/shard_map/cut/pallas_call | solution.py:53
  1.1 3.0 %collective-permute-start = (bf16[4,32,8,128]{3,2,1,0:T(8,128)(2,1)S(1)}, bf16[4,32,8,128]{3,2,1,0:T(8,128)(2,1)S(1)}, u32[]{:S(2)}, u32[]{:S(2)}) collective-permute-start(bf16[4,32,8,128]{3,2,1,0:T(8,128)(2,1)S(1)} %get-tuple-element.31), channel_id=1, source_target_pairs={{0,2},{1,3},{2,0},{3,1},{4,6},{5,7},{6,4},{7,5},{8,10},{9,11},{10,... | collective-permute-start | bytes 786440 | tf_op jit(solution)/shard_map/ppermute | solution.py:344
  4.1 0.0 collective-permute-start.1
  4.1 1.5 %pack.3 = (bf16[4,3,128,128]{3,2,1,0:T(8,128)(2,1)S(1)}, bf16[4,3,128,128]{3,2,1,0:T(8,128)(2,1)S(1)}, f32[8,128]{1,0:T(8,128)S(1)}) custom-call(bf16[1,4,32,32,128]{4,3,2,1,0:T(8,128)(2,1)} %refs_0_.5, bf16[1,4,32,32,128]{4,3,2,1,0:T(8,128)(2,1)} %refs_1_.5, bf16[1,4,32,32,128]{4,3,2,1,0:T(8,128)(2,1)} %refs_2_.5, bf16[1,4,32,32,128]{4,3,2,1,0:T(8,128)(2,1)} %refs_3_.5, ...), custom_call_target="tpu_custom_call" | custom-call | flops 2097152 | bytes 4194304 | tf_op jit(solution)/shard_map/pack/pallas_call | solution.py:145
  5.6 1.2 %collective-permute-start.4 = (bf16[4,3,128,128]{3,2,1,0:T(8,128)(2,1)S(1)}, bf16[4,3,128,128]{3,2,1,0:T(8,128)(2,1)S(1)}, u32[]{:S(2)}, u32[]{:S(2)}) collective-permute-start(bf16[4,3,128,128]{3,2,1,0:T(8,128)(2,1)S(1)} %get-tuple-element.39), channel_id=1, source_target_pairs={{0,2},{1,3},{2,0},{3,1},{4,6},{5,7},{6,4},{7,5},{8,10},{9,11},{10,... | collective-permute-start | bytes 1179656 | tf_op jit(solution)/shard_map/ppermute | solution.py:344
  6.9 0.6 %collective-permute-start.5 = (bf16[4,3,128,128]{3,2,1,0:T(8,128)(2,1)S(1)}, bf16[4,3,128,128]{3,2,1,0:T(8,128)(2,1)S(1)}, u32[]{:S(2)}, u32[]{:S(2)}) collective-permute-start(bf16[4,3,128,128]{3,2,1,0:T(8,128)(2,1)S(1)} %get-tuple-element.40), channel_id=1, source_target_pairs={{0,3},{1,2},{2,1},{3,0},{4,7},{5,6},{6,5},{7,4},{8,11},{9,10},{10,... | collective-permute-start | bytes 1179656 | tf_op jit(solution)/shard_map/ppermute | solution.py:344
  7.5 3.7 %collective-permute-done.refs_0_ = bf16[4,32,8,128]{3,2,1,0:T(8,128)(2,1)S(1)} collective-permute-done((bf16[4,32,8,128]{3,2,1,0:T(8,128)(2,1)S(1)}, bf16[4,32,8,128]{3,2,1,0:T(8,128)(2,1)S(1)}, u32[]{:S(2)}, u32[]{:S(2)}) %collective-permute-start) | collective-permute-done | bytes 262176 | tf_op jit(solution)/shard_map/ppermute | solution.py:344
  11.2 5.2 %collective-permute-done.1.refs_1_ = bf16[4,32,8,128]{3,2,1,0:T(8,128)(2,1)S(1)} collective-permute-done((bf16[4,32,8,128]{3,2,1,0:T(8,128)(2,1)S(1)}, bf16[4,32,8,128]{3,2,1,0:T(8,128)(2,1)S(1)}, u32[]{:S(2)}, u32[]{:S(2)}) %collective-permute-start.1) | collective-permute-done | bytes 262176 | tf_op jit(solution)/shard_map/ppermute | solution.py:344
  16.4 3.8 %pack.4 = (bf16[3,3,128,128]{3,2,1,0:T(8,128)(2,1)}, bf16[3,3,128,128]{3,2,1,0:T(8,128)(2,1)}, bf16[4,2,128,128]{3,2,1,0:T(8,128)(2,1)}, bf16[3,2,128,128]{3,2,1...) custom-call(bf16[1,4,32,32,128]{4,3,2,1,0:T(8,128)(2,1)} %refs_0_.5,, ...), custom_call_target="tpu_custom_call" | custom-call | flops 6291456 | bytes 12582912 | tf_op jit(solution)/shard_map/pack/pallas_call | solution.py:145
  20.2 0.3 collective-permute-start.6
  20.5 0.3 collective-permute-start.7
  20.8 0.2 collective-permute-start.2
  21.0 1.2 %collective-permute-done.2.refs_0_ = bf16[1,2,128,128]{3,2,1,0:T(8,128)(2,1)S(1)} collective-permute-done((bf16[1,2,128,128]{3,2,1,0:T(8,128)(2,1)S(1)}, bf16[1,2,128,128]{3,2,1,0:T(8,128)(2,1)S(1)}, u32[]{:S(2)}, u32[]{:S(2)}) %collective-permute-start.2) | collective-permute-done | bytes 65568 | tf_op jit(solution)/shard_map/ppermute | solution.py:344
  22.2 1.9 %collective-permute-start.12 = (bf16[3,3,128,128]{3,2,1,0:T(8,128)(2,1)}, bf16[3,3,128,128]{3,2,1,0:T(8,128)(2,1)S(1)}, u32[]{:S(2)}, u32[]{:S(2)}) collective-permute-start(bf16[3,3,128,128]{3,2,1,0:T(8,128)(2,1)} %get-tuple-element.51), channel_id=1, source_target_pairs={{0,2},{1,3},{2,0},{3,1},{4,6},{5,7},{6,4},{7,5},{8,10},{9,11},{10,... | collective-permute-start | bytes 884744 | tf_op jit(solution)/shard_map/ppermute | solution.py:344
  24.2 1.1 %collective-permute-done.4.refs_0_ = bf16[4,3,128,128]{3,2,1,0:T(8,128)(2,1)S(1)} collective-permute-done((bf16[4,3,128,128]{3,2,1,0:T(8,128)(2,1)S(1)}, bf16[4,3,128,128]{3,2,1,0:T(8,128)(2,1)S(1)}, u32[]{:S(2)}, u32[]{:S(2)}) %collective-permute-start.4) | collective-permute-done | bytes 393248 | tf_op jit(solution)/shard_map/ppermute | solution.py:344
  25.2 0.0 collective-permute-start.13
  25.2 8.0 %collective-permute-done.5.refs_1_ = bf16[4,3,128,128]{3,2,1,0:T(8,128)(2,1)S(1)} collective-permute-done((bf16[4,3,128,128]{3,2,1,0:T(8,128)(2,1)S(1)}, bf16[4,3,128,128]{3,2,1,0:T(8,128)(2,1)S(1)}, u32[]{:S(2)}, u32[]{:S(2)}) %collective-permute-start.5) | collective-permute-done | bytes 393248 | tf_op jit(solution)/shard_map/ppermute | solution.py:344
  33.2 0.2 collective-permute-start.10
  33.5 0.0 collective-permute-done.6.refs_1_
  33.5 0.3 collective-permute-start.11
  33.8 0.0 collective-permute-done.7.refs_2_
  33.8 0.2 collective-permute-start.3
  34.0 0.2 arrange.1.values
  34.2 0.0 copy-start
  34.3 0.7 %copy-done = f32[2,8,128]{2,1,0:T(8,128)S(1)} copy-done((f32[2,8,128]{2,1,0:T(8,128)S(1)}, f32[2,8,128]{2,1,0:T(8,128)}, u32[]{:S(2)}) %copy-start) | copy-done | bytes 8216
  34.9 0.3 copy-done.1
  35.2 0.1 copy-done.2
  35.3 0.4 prepare.4.close
  35.7 0.3 copy-done.4
  36.0 3.1 %attend.3.refs_4_.refs_2_ = f32[4,128]{1,0:T(4,128)S(1)} custom-call(s32[4,4]{1,0:T(4,128)S(1)} %copy-done.4, f32[2,8,128]{2,1,0:T(8,128)S(1)} %copy-done, bf16[8,4,64,128]{3,2,1,0:T(8,128)(2,1)S(1)} %arrange.1.values, bf16[4,4,4,64,128]{4,3,2,1,0:T(8,128)(2,1)S(1)} %prepare.4.close, bf16[4,3,128,128]{3,2,1,0:T(8,128)(2,1)S(1)} %collective-permute-done.4.refs_0_, ...), custom_call_target="tpu_custom_call" | custom-call | flops 402653184 | bytes 1048576 | tf_op jit(solution)/shard_map/attend/pallas_call | solution.py:301
  39.1 2.1 %pack.5 = (bf16[1,3,128,128]{3,2,1,0:T(8,128)(2,1)S(1)}, bf16[1,3,128,128]{3,2,1,0:T(8,128)(2,1)S(1)}, f32[8,128]{1,0:T(8,128)}) custom-call(bf16[1,4,32,32,128]{4,3,2,1,0:T(8,128)(2,1)} %refs_0_.5, bf16[1,4,32,32,128]{4,3,2,1,0:T(8,128)(2,1)} %refs_1_.5, bf16[1,4,32,32,128]{4,3,2,1,0:T(8,128)(2,1)} %refs_2_.5, bf16[1,4,32,32,128]{4,3,2,1,0:T(8,128)(2,1)} %refs_3_.5, ...), custom_call_target="tpu_custom_call" | custom-call | flops 2097152 | bytes 4194304 | tf_op jit(solution)/shard_map/pack/pallas_call | solution.py:145
  41.1 0.0 collective-permute-done.3.refs_1_
  41.1 2.1 %collective-permute-start.8 = (bf16[1,3,128,128]{3,2,1,0:T(8,128)(2,1)S(1)}, bf16[1,3,128,128]{3,2,1,0:T(8,128)(2,1)S(1)}, u32[]{:S(2)}, u32[]{:S(2)}) collective-permute-start(bf16[1,3,128,128]{3,2,1,0:T(8,128)(2,1)S(1)} %get-tuple-element.45), channel_id=1, source_target_pairs={{0,2},{1,3},{2,0},{3,1},{4,6},{5,7},{6,4},{7,5},{8,10},{9,11},{10,... | collective-permute-start | bytes 294920 | tf_op jit(solution)/shard_map/ppermute | solution.py:344
  43.3 0.0 collective-permute-done.10.refs_0_
  43.3 0.0 collective-permute-start.9
  43.3 0.2 prepare.3.close
  43.5 0.8 %copy-done.3 = bf16[3,2,128,128]{3,2,1,0:T(8,128)(2,1)S(1)} copy-done((bf16[3,2,128,128]{3,2,1,0:T(8,128)(2,1)S(1)}, bf16[3,2,128,128]{3,2,1,0:T(8,128)(2,1)}, u32[]{:S(2)}) %copy-start.3) | copy-done | bytes 196632
  44.2 0.3 prepare.5.close
  44.5 1.5 %collective-permute-done.13.refs_1_ = bf16[3,3,128,128]{3,2,1,0:T(8,128)(2,1)S(1)} collective-permute-done((bf16[3,3,128,128]{3,2,1,0:T(8,128)(2,1)}, bf16[3,3,128,128]{3,2,1,0:T(8,128)(2,1)S(1)}, u32[]{:S(2)}, u32[]{:S(2)}) %collective-permute-start.13) | collective-permute-done | bytes 294944 | tf_op jit(solution)/shard_map/ppermute | solution.py:344
  46.0 2.5 %attend.4.refs_3_ = f32[3,128]{1,0:T(4,128)S(1)} custom-call(s32[4,4]{1,0:T(4,128)S(1)} %copy-done.4, f32[2,8,128]{2,1,0:T(8,128)S(1)} %copy-done, bf16[8,4,64,128]{3,2,1,0:T(8,128)(2,1)S(1)} %arrange.1.values, bf16[3,4,4,64,128]{4,3,2,1,0:T(8,128)(2,1)S(1)} %prepare.5.close, bf16[3,3,128,128]{3,2,1,0:T(8,128)(2,1)S(1)} %collective-permute-done.12.refs_0_, ...), custom_call_target="tpu_custom_call" | custom-call | flops 301989888 | bytes 786432 | tf_op jit(solution)/shard_map/attend/pallas_call | solution.py:301
  48.5 0.5 collective-permute-done.9.refs_1_
  49.0 1.1 %attend.5 = (f32[2,8,32]{2,1,0:T(8,128)S(1)}, f32[2,8,32]{2,1,0:T(8,128)S(1)}, f32[2,8,32]{2,1,0:T(8,128)S(1)}, f32[2,8,32]{2,1,0:T(8,128)S(1)}) custom-call(s32[4,4]{1,0:T(4,128)S(1)} %copy-done.4, f32[2,8,128]{2,1,0:T(8,128)S(1)} %copy-done, bf16[8,4,64,128]{3,2,1,0:T(8,128)(2,1)S(1)} %arrange.1.values, bf16[1,4,4,64,128]{4,3,2,1,0:T(8,128)(2,1)S(1)} %prepare.3.close, ...), custom_call_target="tpu_custom_call" | custom-call | flops 100663296 | bytes 262144 | tf_op jit(solution)/shard_map/attend/pallas_call | solution.py:301
  50.0 1.6 %collective-permute-start.14 = (f32[2,8,32]{2,1,0:T(8,128)S(1)}, f32[2,8,32]{2,1,0:T(8,128)S(1)}, u32[]{:S(2)}, u32[]{:S(2)}) collective-permute-start(f32[2,8,32]{2,1,0:T(8,128)S(1)} %get-tuple-element.54), channel_id=1, source_target_pairs={{0,4},{4,12},{8,0},{12,8},{1,5},{5,13},{9,1},{13,9},{2,6},{6,14},{... | collective-permute-start | bytes 6152 | tf_op jit(solution)/shard_map/ppermute | solution.py:381
  51.6 2.4 %collective-permute-start.15 = (f32[2,8,32]{2,1,0:T(8,128)S(1)}, f32[2,8,32]{2,1,0:T(8,128)S(1)}, u32[]{:S(2)}, u32[]{:S(2)}) collective-permute-start(f32[2,8,32]{2,1,0:T(8,128)S(1)} %get-tuple-element.55), channel_id=1, source_target_pairs={{0,12},{4,8},{8,4},{12,0},{1,13},{5,9},{9,5},{13,1},{2,14},{6,10},... | collective-permute-start | bytes 6152 | tf_op jit(solution)/shard_map/ppermute | solution.py:381
  54.0 1.7 %collective-permute-start.16 = (f32[2,8,32]{2,1,0:T(8,128)S(1)}, f32[2,8,32]{2,1,0:T(8,128)S(1)}, u32[]{:S(2)}, u32[]{:S(2)}) collective-permute-start(f32[2,8,32]{2,1,0:T(8,128)S(1)} %get-tuple-element.56), channel_id=1, source_target_pairs={{0,8},{4,0},{8,12},{12,4},{1,9},{5,1},{9,13},{13,5},{2,10},{6,2},{... | collective-permute-start | bytes 6152 | tf_op jit(solution)/shard_map/ppermute | solution.py:381
  55.7 1.4 %collective-permute-done.15 = f32[2,8,32]{2,1,0:T(8,128)S(1)} collective-permute-done((f32[2,8,32]{2,1,0:T(8,128)S(1)}, f32[2,8,32]{2,1,0:T(8,128)S(1)}, u32[]{:S(2)}, u32[]{:S(2)}) %collective-permute-start.15) | collective-permute-done | bytes 2080 | tf_op jit(solution)/shard_map/ppermute | solution.py:381
  57.1 0.6 collective-permute-done.16
  57.6 0.6 %add_add_fusion = f32[2,8,32]{2,1,0:T(8,128)} fusion(f32[2,8,32]{2,1,0:T(8,128)S(1)} %collective-permute-done.16, f32[2,8,32]{2,1,0:T(8,128)S(1)} %collective-permute-done.15, f32[2,8,32]{2,1,0:T(8,128)S(1)} %get-tuple-element.53, f32[2,8,32]{2,1,0:T(8,128)S(1)} %collective-permute-done.14), kind=kLoop, calls=%fused_computation | loop fusion | flops 1536 | bytes 10240 | tf_op jit(solution)/shard_map/add | solution.py:381
  (10 shorter events, 0.0 us)
Async XLA Ops:
  1.1 10.1 %collective-permute-start = (bf16[4,32,8,128]{3,2,1,0:T(8,128)(2,1)S(1)}, bf16[4,32,8,128]{3,2,1,0:T(8,128)(2,1)S(1)}, u32[]{:S(2)}, u32[]{:S(2)}) collective-permute-start(bf16[4,32,8,128]{3,2,1,0:T(8,128)(2,1)S(1)} %get-tuple-element.31), channel_id=1, source_target_pairs={{0,2},{1,3},{2,0},{3,1},{4,6},{5,7},{6,4},{7,5},{8,10},{9,11},{10,... | collective-permute-start | bytes 786440 | tf_op jit(solution)/shard_map/ppermute | solution.py:344
  4.1 12.3 %collective-permute-start.1 = (bf16[4,32,8,128]{3,2,1,0:T(8,128)(2,1)S(1)}, bf16[4,32,8,128]{3,2,1,0:T(8,128)(2,1)S(1)}, u32[]{:S(2)}, u32[]{:S(2)}) collective-permute-start(bf16[4,32,8,128]{3,2,1,0:T(8,128)(2,1)S(1)} %get-tuple-element.32), channel_id=1, source_target_pairs={{0,3},{1,2},{2,1},{3,0},{4,7},{5,6},{6,5},{7,4},{8,11},{9,10},{10,... | collective-permute-start | bytes 786440 | tf_op jit(solution)/shard_map/ppermute | solution.py:344
  5.6 19.6 %collective-permute-start.4 = (bf16[4,3,128,128]{3,2,1,0:T(8,128)(2,1)S(1)}, bf16[4,3,128,128]{3,2,1,0:T(8,128)(2,1)S(1)}, u32[]{:S(2)}, u32[]{:S(2)}) collective-permute-start(bf16[4,3,128,128]{3,2,1,0:T(8,128)(2,1)S(1)} %get-tuple-element.39), channel_id=1, source_target_pairs={{0,2},{1,3},{2,0},{3,1},{4,6},{5,7},{6,4},{7,5},{8,10},{9,11},{10,... | collective-permute-start | bytes 1179656 | tf_op jit(solution)/shard_map/ppermute | solution.py:344
  6.9 26.4 %collective-permute-start.5 = (bf16[4,3,128,128]{3,2,1,0:T(8,128)(2,1)S(1)}, bf16[4,3,128,128]{3,2,1,0:T(8,128)(2,1)S(1)}, u32[]{:S(2)}, u32[]{:S(2)}) collective-permute-start(bf16[4,3,128,128]{3,2,1,0:T(8,128)(2,1)S(1)} %get-tuple-element.40), channel_id=1, source_target_pairs={{0,3},{1,2},{2,1},{3,0},{4,7},{5,6},{6,5},{7,4},{8,11},{9,10},{10,... | collective-permute-start | bytes 1179656 | tf_op jit(solution)/shard_map/ppermute | solution.py:344
  20.2 13.3 %collective-permute-start.6 = (bf16[4,2,128,128]{3,2,1,0:T(8,128)(2,1)}, bf16[4,2,128,128]{3,2,1,0:T(8,128)(2,1)S(1)}, u32[]{:S(2)}, u32[]{:S(2)}) collective-permute-start(bf16[4,2,128,128]{3,2,1,0:T(8,128)(2,1)} %get-tuple-element.41), channel_id=1, source_target_pairs={{0,1},{1,0},{2,3},{3,2},{4,5},{5,4},{6,7},{7,6},{8,9},{9,8},{10,11... | collective-permute-start | bytes 786440 | tf_op jit(solution)/shard_map/ppermute | solution.py:344
  20.5 13.3 %collective-permute-start.7 = (bf16[4,2,128,128]{3,2,1,0:T(8,128)(2,1)}, bf16[4,2,128,128]{3,2,1,0:T(8,128)(2,1)S(1)}, u32[]{:S(2)}, u32[]{:S(2)}) collective-permute-start(bf16[4,2,128,128]{3,2,1,0:T(8,128)(2,1)} %get-tuple-element.42), channel_id=1, source_target_pairs={{0,1},{1,0},{2,3},{3,2},{4,5},{5,4},{6,7},{7,6},{8,9},{9,8},{10,11... | collective-permute-start | bytes 786440 | tf_op jit(solution)/shard_map/ppermute | solution.py:344
  20.8 1.5 %collective-permute-start.2 = (bf16[1,2,128,128]{3,2,1,0:T(8,128)(2,1)S(1)}, bf16[1,2,128,128]{3,2,1,0:T(8,128)(2,1)S(1)}, u32[]{:S(2)}, u32[]{:S(2)}) collective-permute-start(bf16[1,2,128,128]{3,2,1,0:T(8,128)(2,1)S(1)} %get-tuple-element.35), channel_id=1, source_target_pairs={{0,1},{1,0},{2,3},{3,2},{4,5},{5,4},{6,7},{7,6},{8,9},{9,8},{10,11... | collective-permute-start | bytes 196616 | tf_op jit(solution)/shard_map/ppermute | solution.py:344
  22.2 22.3 %collective-permute-start.12 = (bf16[3,3,128,128]{3,2,1,0:T(8,128)(2,1)}, bf16[3,3,128,128]{3,2,1,0:T(8,128)(2,1)S(1)}, u32[]{:S(2)}, u32[]{:S(2)}) collective-permute-start(bf16[3,3,128,128]{3,2,1,0:T(8,128)(2,1)} %get-tuple-element.51), channel_id=1, source_target_pairs={{0,2},{1,3},{2,0},{3,1},{4,6},{5,7},{6,4},{7,5},{8,10},{9,11},{10,... | collective-permute-start | bytes 884744 | tf_op jit(solution)/shard_map/ppermute | solution.py:344
  25.2 20.7 %collective-permute-start.13 = (bf16[3,3,128,128]{3,2,1,0:T(8,128)(2,1)}, bf16[3,3,128,128]{3,2,1,0:T(8,128)(2,1)S(1)}, u32[]{:S(2)}, u32[]{:S(2)}) collective-permute-start(bf16[3,3,128,128]{3,2,1,0:T(8,128)(2,1)} %get-tuple-element.52), channel_id=1, source_target_pairs={{0,3},{1,2},{2,1},{3,0},{4,7},{5,6},{6,5},{7,4},{8,11},{9,10},{10,... | collective-permute-start | bytes 884744 | tf_op jit(solution)/shard_map/ppermute | solution.py:344
  33.2 10.0 %collective-permute-start.10 = (bf16[3,2,128,128]{3,2,1,0:T(8,128)(2,1)S(1)}, bf16[3,2,128,128]{3,2,1,0:T(8,128)(2,1)S(1)}, u32[]{:S(2)}, u32[]{:S(2)}) collective-permute-start(bf16[3,2,128,128]{3,2,1,0:T(8,128)(2,1)S(1)} %get-tuple-element.47), channel_id=1, source_target_pairs={{0,1},{1,0},{2,3},{3,2},{4,5},{5,4},{6,7},{7,6},{8,9},{9,8},{10,11... | collective-permute-start | bytes 589832 | tf_op jit(solution)/shard_map/ppermute | solution.py:344
  33.5 10.0 %collective-permute-start.11 = (bf16[3,2,128,128]{3,2,1,0:T(8,128)(2,1)S(1)}, bf16[3,2,128,128]{3,2,1,0:T(8,128)(2,1)S(1)}, u32[]{:S(2)}, u32[]{:S(2)}) collective-permute-start(bf16[3,2,128,128]{3,2,1,0:T(8,128)(2,1)S(1)} %get-tuple-element.48), channel_id=1, source_target_pairs={{0,1},{1,0},{2,3},{3,2},{4,5},{5,4},{6,7},{7,6},{8,9},{9,8},{10,11... | collective-permute-start | bytes 589832 | tf_op jit(solution)/shard_map/ppermute | solution.py:344
  33.8 7.4 %collective-permute-start.3 = (bf16[1,2,128,128]{3,2,1,0:T(8,128)(2,1)S(1)}, bf16[1,2,128,128]{3,2,1,0:T(8,128)(2,1)S(1)}, u32[]{:S(2)}, u32[]{:S(2)}) collective-permute-start(bf16[1,2,128,128]{3,2,1,0:T(8,128)(2,1)S(1)} %get-tuple-element.36), channel_id=1, source_target_pairs={{0,1},{1,0},{2,3},{3,2},{4,5},{5,4},{6,7},{7,6},{8,9},{9,8},{10,11... | collective-permute-start | bytes 196616 | tf_op jit(solution)/shard_map/ppermute | solution.py:344
  34.2 0.7 %copy-start = (f32[2,8,128]{2,1,0:T(8,128)S(1)}, f32[2,8,128]{2,1,0:T(8,128)}, u32[]{:S(2)}) copy-start(f32[2,8,128]{2,1,0:T(8,128)} %gains.11) | copy-start | bytes 24580
  34.3 1.0 %copy-start.1 = (bf16[4,2,128,128]{3,2,1,0:T(8,128)(2,1)S(1)}, bf16[4,2,128,128]{3,2,1,0:T(8,128)(2,1)}, u32[]{:S(2)}) copy-start(bf16[4,2,128,128]{3,2,1,0:T(8,128)(2,1)} %get-tuple-element.43.refs_3_) | copy-start | bytes 786436
  34.3 1.0 %copy-start.2 = (bf16[4,2,128,128]{3,2,1,0:T(8,128)(2,1)S(1)}, bf16[4,2,128,128]{3,2,1,0:T(8,128)(2,1)}, u32[]{:S(2)}) copy-start(bf16[4,2,128,128]{3,2,1,0:T(8,128)(2,1)} %get-tuple-element.44.refs_4_) | copy-start | bytes 786436
  35.3 0.7 %copy-start.4 = (s32[4,4]{1,0:T(4,128)S(1)}, s32[4,4]{1,0:T(4,128)}, u32[]{:S(2)}) copy-start(s32[4,4]{1,0:T(4,128)} %units.5) | copy-start | bytes 196
  41.1 7.3 %collective-permute-start.8 = (bf16[1,3,128,128]{3,2,1,0:T(8,128)(2,1)S(1)}, bf16[1,3,128,128]{3,2,1,0:T(8,128)(2,1)S(1)}, u32[]{:S(2)}, u32[]{:S(2)}) collective-permute-start(bf16[1,3,128,128]{3,2,1,0:T(8,128)(2,1)S(1)} %get-tuple-element.45), channel_id=1, source_target_pairs={{0,2},{1,3},{2,0},{3,1},{4,6},{5,7},{6,4},{7,5},{8,10},{9,11},{10,... | collective-permute-start | bytes 294920 | tf_op jit(solution)/shard_map/ppermute | solution.py:344
  43.3 5.7 %collective-permute-start.9 = (bf16[1,3,128,128]{3,2,1,0:T(8,128)(2,1)S(1)}, bf16[1,3,128,128]{3,2,1,0:T(8,128)(2,1)S(1)}, u32[]{:S(2)}, u32[]{:S(2)}) collective-permute-start(bf16[1,3,128,128]{3,2,1,0:T(8,128)(2,1)S(1)} %get-tuple-element.46), channel_id=1, source_target_pairs={{0,3},{1,2},{2,1},{3,0},{4,7},{5,6},{6,5},{7,4},{8,11},{9,10},{10,... | collective-permute-start | bytes 294920 | tf_op jit(solution)/shard_map/ppermute | solution.py:344
  43.3 0.9 %copy-start.3 = (bf16[3,2,128,128]{3,2,1,0:T(8,128)(2,1)S(1)}, bf16[3,2,128,128]{3,2,1,0:T(8,128)(2,1)}, u32[]{:S(2)}) copy-start(bf16[3,2,128,128]{3,2,1,0:T(8,128)(2,1)} %get-tuple-element.50.refs_3_) | copy-start | bytes 589828
  50.0 5.6 %collective-permute-start.14 = (f32[2,8,32]{2,1,0:T(8,128)S(1)}, f32[2,8,32]{2,1,0:T(8,128)S(1)}, u32[]{:S(2)}, u32[]{:S(2)}) collective-permute-start(f32[2,8,32]{2,1,0:T(8,128)S(1)} %get-tuple-element.54), channel_id=1, source_target_pairs={{0,4},{4,12},{8,0},{12,8},{1,5},{5,13},{9,1},{13,9},{2,6},{6,14},{... | collective-permute-start | bytes 6152 | tf_op jit(solution)/shard_map/ppermute | solution.py:381
  51.6 5.4 %collective-permute-start.15 = (f32[2,8,32]{2,1,0:T(8,128)S(1)}, f32[2,8,32]{2,1,0:T(8,128)S(1)}, u32[]{:S(2)}, u32[]{:S(2)}) collective-permute-start(f32[2,8,32]{2,1,0:T(8,128)S(1)} %get-tuple-element.55), channel_id=1, source_target_pairs={{0,12},{4,8},{8,4},{12,0},{1,13},{5,9},{9,5},{13,1},{2,14},{6,10},... | collective-permute-start | bytes 6152 | tf_op jit(solution)/shard_map/ppermute | solution.py:381
  54.0 3.7 %collective-permute-start.16 = (f32[2,8,32]{2,1,0:T(8,128)S(1)}, f32[2,8,32]{2,1,0:T(8,128)S(1)}, u32[]{:S(2)}, u32[]{:S(2)}) collective-permute-start(f32[2,8,32]{2,1,0:T(8,128)S(1)} %get-tuple-element.56), channel_id=1, source_target_pairs={{0,8},{4,0},{8,12},{12,4},{1,9},{5,1},{9,13},{13,5},{2,10},{6,2},{... | collective-permute-start | bytes 6152 | tf_op jit(solution)/shard_map/ppermute | solution.py:381

commit v10 on v9

--- a/solution.py
+++ b/solution.py
@@ -34,8 +34,8 @@
     return pl.multiple_of((head // TILE) * TILE, TILE), offset
 
 
-def cut_kernel(flips, heads, array, *refs):
-    outs, token, sems = refs[:-2], refs[-2], refs[-1]
+def cut_kernel(flips, heads, after, array, *refs):
+    outs, token, sems = refs[after:-2], refs[-2], refs[-1]
     token[...] = jnp.zeros_like(token)
     copies = []
     for index, flip in enumerate(flips):
@@ -47,18 +47,18 @@
         copy.wait()
 
 
-def cut(array, flips, heads):
+def cut(array, flips, heads, after):
     _, slots, rows, _, size = array.shape
     shape = jax.ShapeDtypeStruct((slots, rows, max(heads, TILE), size), array.dtype)
     return pl.pallas_call(
-        functools.partial(cut_kernel, flips, heads),
+        functools.partial(cut_kernel, flips, heads, len(after)),
         out_shape=[shape] * len(flips) + [jax.ShapeDtypeStruct((TILE, size), jnp.float32)],
-        in_specs=[pl.BlockSpec(memory_space=pltpu.HBM)],
+        in_specs=[pl.BlockSpec(memory_space=pltpu.HBM)] + [pl.BlockSpec(memory_space=pl.ANY)] * len(after),
         out_specs=[pl.BlockSpec(memory_space=pltpu.VMEM)] * (len(flips) + 1),
         scratch_shapes=[pltpu.SemaphoreType.DMA((len(flips),))],
         compiler_params=pltpu.CompilerParams(vmem_limit_bytes=PACK_VMEM_LIMIT),
         name="cut",
-    )(array)
+    )(array, *after)
 
 
 def arrange_kernel(*refs):
@@ -355,12 +355,18 @@
     def far_plan(number):
         return [(flip, OTHERS, chunks[number : number + 1]) for flip in far]
 
-    *tiles, token = cut(arrays[VALUES], far, heads)
-    tiles = [send(block, flip) for flip, block in zip(far, tiles)]
-    received, token = pack_and_send(far_plan(0), [token])
+    tiles, tokens = [], []
+    for flip in far:
+        block, token = cut(arrays[VALUES], [flip], heads, tokens)
+        tiles.append(send(block, flip))
+        tokens = [token]
+    received, token = pack_and_send(far_plan(0), tokens)
     later = far_plan(1) if len(chunks) > 1 else []
     whole = [(flip, pair, chunks) for flip in close for pair in ((0, 1), (2, 3))]
-    blocks, _ = pack_and_send(later + whole, [token, seen(tiles)])
+    arrived = []
+    for tile in tiles:
+        arrived = [seen([tile] + arrived)]
+    blocks, _ = pack_and_send(later + whole, [token] + arrived)
     values = arrange(tiles, heads)
     prepared = [
         prepare(low, norm_gains, blocks[len(later) + number :: len(chunks)], slots, [] if number else [seen(received)])

time: 58.5 us -> 58.6 us (level)
  Pallas kernels: 16.1 us -> 17 us
  waiting for transfers between devices: 23.1 us -> 22.3 us
    ppermute x14, waiting for transfers between devices: 21.2 us -> 20.2 us  [send(): return lax.ppermute(block, 'seq', [(s, s ^ flip) for s in range(sequence)])]
    pallas_call x1 -> x2, Pallas kernels: 1.05 us -> 1.92 us  [cut(): pl.pallas_call(functools.partial(cut_kernel, flips, heads, len(after)), o...]
  transfers between devices with their start and end apart: 17 -> 17, of which waited for: 9 -> 9; matrix products, arithmetic and copies ran while one was open for 0% -> 0% of each run, Pallas kernels for 24% -> 26%
where the time goes in v10:
time: 58.6 us; the launch traced here: 58.3 us
  waiting for transfers between devices  22.3 us (38%)
  Pallas kernels  17 us (29%)
  starting transfers between devices  16.2 us (28%)
  local copies, waits for them, and re-layouts  2.08 us (4%)
  other arithmetic  0.6 us (1%)
    ppermute x14, waiting for transfers between devices, send(): return lax.ppermute(block, 'seq', [(s, s ^ flip) for s in range(sequence)])  20.2 us
    ppermute x14, starting transfers between devices, send(): return lax.ppermute(block, 'seq', [(s, s ^ flip) for s in range(sequence)])  10.6 us
    pallas_call x3, Pallas kernels, pack(): pl.pallas_call(functools.partial(pack_kernel, plan, heads, len(after)), o...  7.37 us
    pallas_call x3, Pallas kernels, attend(): pl.pallas_call(kernel, out_shape=shapes, in_specs=[pl.BlockSpec(memory_sp...  6.62 us
    ppermute x3, starting transfers between devices, body(): result = result + lax.ppermute(part, 'dp', list(enumerate(targets)))  5.62 us
    ppermute x3, waiting for transfers between devices, body(): result = result + lax.ppermute(part, 'dp', list(enumerate(targets)))  2.13 us
    unnamed x10, local copies, waits for them, and re-layouts  2.08 us
    pallas_call x2, Pallas kernels, cut(): pl.pallas_call(functools.partial(cut_kernel, flips, heads, len(after)), o...  1.92 us
  transfers between devices with their start and end apart: 17, of which 9 were waited for; matrix products, arithmetic and copies ran while one was open for 0% of the time, Pallas kernels for 26%

profile of v10, /device:TPU:0, one launch (start us, length us, event | category | flops | bytes accessed | tf_op | source)
XLA Modules:
  0.0 58.3 jit_solution(1729724771307205114)
XLA Ops:
  0.0 1.0 %cut.2 = (bf16[4,32,8,128]{3,2,1,0:T(8,128)(2,1)S(1)}, f32[8,128]{1,0:T(8,128)S(1)}) custom-call(bf16[1,4,32,32,128]{4,3,2,1,0:T(8,128)(2,1)} %refs_2_.5), custom_call_target="tpu_custom_call" | custom-call | tf_op jit(solution)/shard_map/cut/pallas_call | solution.py:53
  1.0 3.0 %collective-permute-start = (bf16[4,32,8,128]{3,2,1,0:T(8,128)(2,1)S(1)}, bf16[4,32,8,128]{3,2,1,0:T(8,128)(2,1)S(1)}, u32[]{:S(2)}, u32[]{:S(2)}) collective-permute-start(bf16[4,32,8,128]{3,2,1,0:T(8,128)(2,1)S(1)} %get-tuple-element.32), channel_id=1, source_target_pairs={{0,2},{1,3},{2,0},{3,1},{4,6},{5,7},{6,4},{7,5},{8,10},{9,11},{10,... | collective-permute-start | bytes 786440 | tf_op jit(solution)/shard_map/ppermute | solution.py:344
  4.0 1.0 %cut.3 = (bf16[4,32,8,128]{3,2,1,0:T(8,128)(2,1)S(1)}, f32[8,128]{1,0:T(8,128)S(1)}) custom-call(bf16[1,4,32,32,128]{4,3,2,1,0:T(8,128)(2,1)} %refs_2_.5, f32[8,128]{1,0:T(8,128)S(1)} %get-tuple-element.33.refs_0_), custom_call_target="tpu_custom_call" | custom-call | tf_op jit(solution)/shard_map/cut/pallas_call | solution.py:53
  4.9 0.1 collective-permute-start.1
  5.0 1.5 %pack.3 = (bf16[4,3,128,128]{3,2,1,0:T(8,128)(2,1)S(1)}, bf16[4,3,128,128]{3,2,1,0:T(8,128)(2,1)S(1)}, f32[8,128]{1,0:T(8,128)S(1)}) custom-call(bf16[1,4,32,32,128]{4,3,2,1,0:T(8,128)(2,1)} %refs_0_.5, bf16[1,4,32,32,128]{4,3,2,1,0:T(8,128)(2,1)} %refs_1_.5, bf16[1,4,32,32,128]{4,3,2,1,0:T(8,128)(2,1)} %refs_2_.5, bf16[1,4,32,32,128]{4,3,2,1,0:T(8,128)(2,1)} %refs_3_.5, ...), custom_call_target="tpu_custom_call" | custom-call | flops 2097152 | bytes 4194304 | tf_op jit(solution)/shard_map/pack/pallas_call | solution.py:145
  6.6 1.2 %collective-permute-start.4 = (bf16[4,3,128,128]{3,2,1,0:T(8,128)(2,1)S(1)}, bf16[4,3,128,128]{3,2,1,0:T(8,128)(2,1)S(1)}, u32[]{:S(2)}, u32[]{:S(2)}) collective-permute-start(bf16[4,3,128,128]{3,2,1,0:T(8,128)(2,1)S(1)} %get-tuple-element.41), channel_id=1, source_target_pairs={{0,2},{1,3},{2,0},{3,1},{4,6},{5,7},{6,4},{7,5},{8,10},{9,11},{10,... | collective-permute-start | bytes 1179656 | tf_op jit(solution)/shard_map/ppermute | solution.py:344
  7.8 0.6 %collective-permute-start.5 = (bf16[4,3,128,128]{3,2,1,0:T(8,128)(2,1)S(1)}, bf16[4,3,128,128]{3,2,1,0:T(8,128)(2,1)S(1)}, u32[]{:S(2)}, u32[]{:S(2)}) collective-permute-start(bf16[4,3,128,128]{3,2,1,0:T(8,128)(2,1)S(1)} %get-tuple-element.42), channel_id=1, source_target_pairs={{0,3},{1,2},{2,1},{3,0},{4,7},{5,6},{6,5},{7,4},{8,11},{9,10},{10,... | collective-permute-start | bytes 1179656 | tf_op jit(solution)/shard_map/ppermute | solution.py:344
  8.4 2.7 %collective-permute-done.refs_0_ = bf16[4,32,8,128]{3,2,1,0:T(8,128)(2,1)S(1)} collective-permute-done((bf16[4,32,8,128]{3,2,1,0:T(8,128)(2,1)S(1)}, bf16[4,32,8,128]{3,2,1,0:T(8,128)(2,1)S(1)}, u32[]{:S(2)}, u32[]{:S(2)}) %collective-permute-start) | collective-permute-done | bytes 262176 | tf_op jit(solution)/shard_map/ppermute | solution.py:344
  11.1 5.2 %collective-permute-done.1.refs_1_.refs_0_ = bf16[4,32,8,128]{3,2,1,0:T(8,128)(2,1)S(1)} collective-permute-done((bf16[4,32,8,128]{3,2,1,0:T(8,128)(2,1)S(1)}, bf16[4,32,8,128]{3,2,1,0:T(8,128)(2,1)S(1)}, u32[]{:S(2)}, u32[]{:S(2)}) %collective-permute-start.1) | collective-permute-done | bytes 262176 | tf_op jit(solution)/shard_map/ppermute | solution.py:344
  16.3 3.8 %pack.4 = (bf16[3,3,128,128]{3,2,1,0:T(8,128)(2,1)}, bf16[3,3,128,128]{3,2,1,0:T(8,128)(2,1)}, bf16[4,2,128,128]{3,2,1,0:T(8,128)(2,1)}, bf16[3,2,128,128]{3,2,1...) custom-call(bf16[1,4,32,32,128]{4,3,2,1,0:T(8,128)(2,1)} %refs_0_.5,, ...), custom_call_target="tpu_custom_call" | custom-call | flops 6291456 | bytes 12582912 | tf_op jit(solution)/shard_map/pack/pallas_call | solution.py:145
  20.1 0.3 collective-permute-start.6
  20.4 0.3 collective-permute-start.7
  20.6 0.2 collective-permute-start.2
  20.9 1.2 %collective-permute-done.2.refs_0_ = bf16[1,2,128,128]{3,2,1,0:T(8,128)(2,1)S(1)} collective-permute-done((bf16[1,2,128,128]{3,2,1,0:T(8,128)(2,1)S(1)}, bf16[1,2,128,128]{3,2,1,0:T(8,128)(2,1)S(1)}, u32[]{:S(2)}, u32[]{:S(2)}) %collective-permute-start.2) | collective-permute-done | bytes 65568 | tf_op jit(solution)/shard_map/ppermute | solution.py:344
  22.1 1.9 %collective-permute-start.12 = (bf16[3,3,128,128]{3,2,1,0:T(8,128)(2,1)}, bf16[3,3,128,128]{3,2,1,0:T(8,128)(2,1)S(1)}, u32[]{:S(2)}, u32[]{:S(2)}) collective-permute-start(bf16[3,3,128,128]{3,2,1,0:T(8,128)(2,1)} %get-tuple-element.53), channel_id=1, source_target_pairs={{0,2},{1,3},{2,0},{3,1},{4,6},{5,7},{6,4},{7,5},{8,10},{9,11},{10,... | collective-permute-start | bytes 884744 | tf_op jit(solution)/shard_map/ppermute | solution.py:344
  24.1 1.1 %collective-permute-done.4.refs_0_ = bf16[4,3,128,128]{3,2,1,0:T(8,128)(2,1)S(1)} collective-permute-done((bf16[4,3,128,128]{3,2,1,0:T(8,128)(2,1)S(1)}, bf16[4,3,128,128]{3,2,1,0:T(8,128)(2,1)S(1)}, u32[]{:S(2)}, u32[]{:S(2)}) %collective-permute-start.4) | collective-permute-done | bytes 393248 | tf_op jit(solution)/shard_map/ppermute | solution.py:344
  25.1 0.0 collective-permute-start.13
  25.2 8.0 %collective-permute-done.5.refs_1_ = bf16[4,3,128,128]{3,2,1,0:T(8,128)(2,1)S(1)} collective-permute-done((bf16[4,3,128,128]{3,2,1,0:T(8,128)(2,1)S(1)}, bf16[4,3,128,128]{3,2,1,0:T(8,128)(2,1)S(1)}, u32[]{:S(2)}, u32[]{:S(2)}) %collective-permute-start.5) | collective-permute-done | bytes 393248 | tf_op jit(solution)/shard_map/ppermute | solution.py:344
  33.2 0.2 collective-permute-start.10
  33.4 0.3 collective-permute-start.11
  33.7 0.0 collective-permute-done.7.refs_2_
  33.7 0.2 collective-permute-start.3
  33.9 0.2 arrange.1.values
  34.2 0.0 copy-start
  34.2 0.7 %copy-done = f32[2,8,128]{2,1,0:T(8,128)S(1)} copy-done((f32[2,8,128]{2,1,0:T(8,128)S(1)}, f32[2,8,128]{2,1,0:T(8,128)}, u32[]{:S(2)}) %copy-start) | copy-done | bytes 8216
  34.9 0.3 copy-done.1
  35.1 0.1 copy-done.2
  35.2 0.4 prepare.4.close
  35.6 0.3 copy-done.4
  35.9 3.1 %attend.3.refs_4_.refs_2_ = f32[4,128]{1,0:T(4,128)S(1)} custom-call(s32[4,4]{1,0:T(4,128)S(1)} %copy-done.4, f32[2,8,128]{2,1,0:T(8,128)S(1)} %copy-done, bf16[8,4,64,128]{3,2,1,0:T(8,128)(2,1)S(1)} %arrange.1.values, bf16[4,4,4,64,128]{4,3,2,1,0:T(8,128)(2,1)S(1)} %prepare.4.close, bf16[4,3,128,128]{3,2,1,0:T(8,128)(2,1)S(1)} %collective-permute-done.4.refs_0_, ...), custom_call_target="tpu_custom_call" | custom-call | flops 402653184 | bytes 1048576 | tf_op jit(solution)/shard_map/attend/pallas_call | solution.py:301
  39.0 2.1 %pack.5 = (bf16[1,3,128,128]{3,2,1,0:T(8,128)(2,1)S(1)}, bf16[1,3,128,128]{3,2,1,0:T(8,128)(2,1)S(1)}, f32[8,128]{1,0:T(8,128)}) custom-call(bf16[1,4,32,32,128]{4,3,2,1,0:T(8,128)(2,1)} %refs_0_.5, bf16[1,4,32,32,128]{4,3,2,1,0:T(8,128)(2,1)} %refs_1_.5, bf16[1,4,32,32,128]{4,3,2,1,0:T(8,128)(2,1)} %refs_2_.5, bf16[1,4,32,32,128]{4,3,2,1,0:T(8,128)(2,1)} %refs_3_.5, ...), custom_call_target="tpu_custom_call" | custom-call | flops 2097152 | bytes 4194304 | tf_op jit(solution)/shard_map/pack/pallas_call | solution.py:145
  41.0 0.0 collective-permute-done.3.refs_1_
  41.0 2.1 %collective-permute-start.8 = (bf16[1,3,128,128]{3,2,1,0:T(8,128)(2,1)S(1)}, bf16[1,3,128,128]{3,2,1,0:T(8,128)(2,1)S(1)}, u32[]{:S(2)}, u32[]{:S(2)}) collective-permute-start(bf16[1,3,128,128]{3,2,1,0:T(8,128)(2,1)S(1)} %get-tuple-element.47), channel_id=1, source_target_pairs={{0,2},{1,3},{2,0},{3,1},{4,6},{5,7},{6,4},{7,5},{8,10},{9,11},{10,... | collective-permute-start | bytes 294920 | tf_op jit(solution)/shard_map/ppermute | solution.py:344
  43.2 0.2 prepare.3.close
  43.4 0.8 %copy-done.3 = bf16[3,2,128,128]{3,2,1,0:T(8,128)(2,1)S(1)} copy-done((bf16[3,2,128,128]{3,2,1,0:T(8,128)(2,1)S(1)}, bf16[3,2,128,128]{3,2,1,0:T(8,128)(2,1)}, u32[]{:S(2)}) %copy-start.3) | copy-done | bytes 196632
  44.1 0.3 prepare.5.close
  44.4 1.5 %collective-permute-done.13.refs_1_ = bf16[3,3,128,128]{3,2,1,0:T(8,128)(2,1)S(1)} collective-permute-done((bf16[3,3,128,128]{3,2,1,0:T(8,128)(2,1)}, bf16[3,3,128,128]{3,2,1,0:T(8,128)(2,1)S(1)}, u32[]{:S(2)}, u32[]{:S(2)}) %collective-permute-start.13) | collective-permute-done | bytes 294944 | tf_op jit(solution)/shard_map/ppermute | solution.py:344
  45.9 2.5 %attend.4.refs_3_ = f32[3,128]{1,0:T(4,128)S(1)} custom-call(s32[4,4]{1,0:T(4,128)S(1)} %copy-done.4, f32[2,8,128]{2,1,0:T(8,128)S(1)} %copy-done, bf16[8,4,64,128]{3,2,1,0:T(8,128)(2,1)S(1)} %arrange.1.values, bf16[3,4,4,64,128]{4,3,2,1,0:T(8,128)(2,1)S(1)} %prepare.5.close, bf16[3,3,128,128]{3,2,1,0:T(8,128)(2,1)S(1)} %collective-permute-done.12.refs_0_, ...), custom_call_target="tpu_custom_call" | custom-call | flops 301989888 | bytes 786432 | tf_op jit(solution)/shard_map/attend/pallas_call | solution.py:301
  48.4 0.0 collective-permute-done.8.refs_0_
  48.4 0.5 collective-permute-done.9.refs_1_
  48.9 1.1 %attend.5 = (f32[2,8,32]{2,1,0:T(8,128)S(1)}, f32[2,8,32]{2,1,0:T(8,128)S(1)}, f32[2,8,32]{2,1,0:T(8,128)S(1)}, f32[2,8,32]{2,1,0:T(8,128)S(1)}) custom-call(s32[4,4]{1,0:T(4,128)S(1)} %copy-done.4, f32[2,8,128]{2,1,0:T(8,128)S(1)} %copy-done, bf16[8,4,64,128]{3,2,1,0:T(8,128)(2,1)S(1)} %arrange.1.values, bf16[1,4,4,64,128]{4,3,2,1,0:T(8,128)(2,1)S(1)} %prepare.3.close, ...), custom_call_target="tpu_custom_call" | custom-call | flops 100663296 | bytes 262144 | tf_op jit(solution)/shard_map/attend/pallas_call | solution.py:301
  49.9 1.5 %collective-permute-start.14 = (f32[2,8,32]{2,1,0:T(8,128)S(1)}, f32[2,8,32]{2,1,0:T(8,128)S(1)}, u32[]{:S(2)}, u32[]{:S(2)}) collective-permute-start(f32[2,8,32]{2,1,0:T(8,128)S(1)} %get-tuple-element.56), channel_id=1, source_target_pairs={{0,4},{4,12},{8,0},{12,8},{1,5},{5,13},{9,1},{13,9},{2,6},{6,14},{... | collective-permute-start | bytes 6152 | tf_op jit(solution)/shard_map/ppermute | solution.py:387
  51.4 2.6 %collective-permute-start.15 = (f32[2,8,32]{2,1,0:T(8,128)S(1)}, f32[2,8,32]{2,1,0:T(8,128)S(1)}, u32[]{:S(2)}, u32[]{:S(2)}) collective-permute-start(f32[2,8,32]{2,1,0:T(8,128)S(1)} %get-tuple-element.57), channel_id=1, source_target_pairs={{0,12},{4,8},{8,4},{12,0},{1,13},{5,9},{9,5},{13,1},{2,14},{6,10},... | collective-permute-start | bytes 6152 | tf_op jit(solution)/shard_map/ppermute | solution.py:387
  54.0 1.5 %collective-permute-start.16 = (f32[2,8,32]{2,1,0:T(8,128)S(1)}, f32[2,8,32]{2,1,0:T(8,128)S(1)}, u32[]{:S(2)}, u32[]{:S(2)}) collective-permute-start(f32[2,8,32]{2,1,0:T(8,128)S(1)} %get-tuple-element.58), channel_id=1, source_target_pairs={{0,8},{4,0},{8,12},{12,4},{1,9},{5,1},{9,13},{13,5},{2,10},{6,2},{... | collective-permute-start | bytes 6152 | tf_op jit(solution)/shard_map/ppermute | solution.py:387
  55.5 0.0 collective-permute-done.14
  55.6 1.3 %collective-permute-done.15 = f32[2,8,32]{2,1,0:T(8,128)S(1)} collective-permute-done((f32[2,8,32]{2,1,0:T(8,128)S(1)}, f32[2,8,32]{2,1,0:T(8,128)S(1)}, u32[]{:S(2)}, u32[]{:S(2)}) %collective-permute-start.15) | collective-permute-done | bytes 2080 | tf_op jit(solution)/shard_map/ppermute | solution.py:387
  56.8 0.8 %collective-permute-done.16 = f32[2,8,32]{2,1,0:T(8,128)S(1)} collective-permute-done((f32[2,8,32]{2,1,0:T(8,128)S(1)}, f32[2,8,32]{2,1,0:T(8,128)S(1)}, u32[]{:S(2)}, u32[]{:S(2)}) %collective-permute-start.16) | collective-permute-done | bytes 2080 | tf_op jit(solution)/shard_map/ppermute | solution.py:387
  57.7 0.6 %add_add_fusion = f32[2,8,32]{2,1,0:T(8,128)} fusion(f32[2,8,32]{2,1,0:T(8,128)S(1)} %collective-permute-done.16, f32[2,8,32]{2,1,0:T(8,128)S(1)} %collective-permute-done.15, f32[2,8,32]{2,1,0:T(8,128)S(1)} %get-tuple-element.55, f32[2,8,32]{2,1,0:T(8,128)S(1)} %collective-permute-done.14), kind=kLoop, calls=%fused_computation | loop fusion | flops 1536 | bytes 10240 | tf_op jit(solution)/shard_map/add | solution.py:387
  (12 shorter events, 0.0 us)
Async XLA Ops:
  1.0 10.1 %collective-permute-start = (bf16[4,32,8,128]{3,2,1,0:T(8,128)(2,1)S(1)}, bf16[4,32,8,128]{3,2,1,0:T(8,128)(2,1)S(1)}, u32[]{:S(2)}, u32[]{:S(2)}) collective-permute-start(bf16[4,32,8,128]{3,2,1,0:T(8,128)(2,1)S(1)} %get-tuple-element.32), channel_id=1, source_target_pairs={{0,2},{1,3},{2,0},{3,1},{4,6},{5,7},{6,4},{7,5},{8,10},{9,11},{10,... | collective-permute-start | bytes 786440 | tf_op jit(solution)/shard_map/ppermute | solution.py:344
  4.9 11.4 %collective-permute-start.1 = (bf16[4,32,8,128]{3,2,1,0:T(8,128)(2,1)S(1)}, bf16[4,32,8,128]{3,2,1,0:T(8,128)(2,1)S(1)}, u32[]{:S(2)}, u32[]{:S(2)}) collective-permute-start(bf16[4,32,8,128]{3,2,1,0:T(8,128)(2,1)S(1)} %get-tuple-element.34), channel_id=1, source_target_pairs={{0,3},{1,2},{2,1},{3,0},{4,7},{5,6},{6,5},{7,4},{8,11},{9,10},{10,... | collective-permute-start | bytes 786440 | tf_op jit(solution)/shard_map/ppermute | solution.py:344
  6.6 18.6 %collective-permute-start.4 = (bf16[4,3,128,128]{3,2,1,0:T(8,128)(2,1)S(1)}, bf16[4,3,128,128]{3,2,1,0:T(8,128)(2,1)S(1)}, u32[]{:S(2)}, u32[]{:S(2)}) collective-permute-start(bf16[4,3,128,128]{3,2,1,0:T(8,128)(2,1)S(1)} %get-tuple-element.41), channel_id=1, source_target_pairs={{0,2},{1,3},{2,0},{3,1},{4,6},{5,7},{6,4},{7,5},{8,10},{9,11},{10,... | collective-permute-start | bytes 1179656 | tf_op jit(solution)/shard_map/ppermute | solution.py:344
  7.8 25.4 %collective-permute-start.5 = (bf16[4,3,128,128]{3,2,1,0:T(8,128)(2,1)S(1)}, bf16[4,3,128,128]{3,2,1,0:T(8,128)(2,1)S(1)}, u32[]{:S(2)}, u32[]{:S(2)}) collective-permute-start(bf16[4,3,128,128]{3,2,1,0:T(8,128)(2,1)S(1)} %get-tuple-element.42), channel_id=1, source_target_pairs={{0,3},{1,2},{2,1},{3,0},{4,7},{5,6},{6,5},{7,4},{8,11},{9,10},{10,... | collective-permute-start | bytes 1179656 | tf_op jit(solution)/shard_map/ppermute | solution.py:344
  20.1 13.3 %collective-permute-start.6 = (bf16[4,2,128,128]{3,2,1,0:T(8,128)(2,1)}, bf16[4,2,128,128]{3,2,1,0:T(8,128)(2,1)S(1)}, u32[]{:S(2)}, u32[]{:S(2)}) collective-permute-start(bf16[4,2,128,128]{3,2,1,0:T(8,128)(2,1)} %get-tuple-element.43), channel_id=1, source_target_pairs={{0,1},{1,0},{2,3},{3,2},{4,5},{5,4},{6,7},{7,6},{8,9},{9,8},{10,11... | collective-permute-start | bytes 786440 | tf_op jit(solution)/shard_map/ppermute | solution.py:344
  20.4 13.3 %collective-permute-start.7 = (bf16[4,2,128,128]{3,2,1,0:T(8,128)(2,1)}, bf16[4,2,128,128]{3,2,1,0:T(8,128)(2,1)S(1)}, u32[]{:S(2)}, u32[]{:S(2)}) collective-permute-start(bf16[4,2,128,128]{3,2,1,0:T(8,128)(2,1)} %get-tuple-element.44), channel_id=1, source_target_pairs={{0,1},{1,0},{2,3},{3,2},{4,5},{5,4},{6,7},{7,6},{8,9},{9,8},{10,11... | collective-permute-start | bytes 786440 | tf_op jit(solution)/shard_map/ppermute | solution.py:344
  20.6 1.5 %collective-permute-start.2 = (bf16[1,2,128,128]{3,2,1,0:T(8,128)(2,1)S(1)}, bf16[1,2,128,128]{3,2,1,0:T(8,128)(2,1)S(1)}, u32[]{:S(2)}, u32[]{:S(2)}) collective-permute-start(bf16[1,2,128,128]{3,2,1,0:T(8,128)(2,1)S(1)} %get-tuple-element.37), channel_id=1, source_target_pairs={{0,1},{1,0},{2,3},{3,2},{4,5},{5,4},{6,7},{7,6},{8,9},{9,8},{10,11... | collective-permute-start | bytes 196616 | tf_op jit(solution)/shard_map/ppermute | solution.py:344
  22.1 22.3 %collective-permute-start.12 = (bf16[3,3,128,128]{3,2,1,0:T(8,128)(2,1)}, bf16[3,3,128,128]{3,2,1,0:T(8,128)(2,1)S(1)}, u32[]{:S(2)}, u32[]{:S(2)}) collective-permute-start(bf16[3,3,128,128]{3,2,1,0:T(8,128)(2,1)} %get-tuple-element.53), channel_id=1, source_target_pairs={{0,2},{1,3},{2,0},{3,1},{4,6},{5,7},{6,4},{7,5},{8,10},{9,11},{10,... | collective-permute-start | bytes 884744 | tf_op jit(solution)/shard_map/ppermute | solution.py:344
  25.1 20.7 %collective-permute-start.13 = (bf16[3,3,128,128]{3,2,1,0:T(8,128)(2,1)}, bf16[3,3,128,128]{3,2,1,0:T(8,128)(2,1)S(1)}, u32[]{:S(2)}, u32[]{:S(2)}) collective-permute-start(bf16[3,3,128,128]{3,2,1,0:T(8,128)(2,1)} %get-tuple-element.54), channel_id=1, source_target_pairs={{0,3},{1,2},{2,1},{3,0},{4,7},{5,6},{6,5},{7,4},{8,11},{9,10},{10,... | collective-permute-start | bytes 884744 | tf_op jit(solution)/shard_map/ppermute | solution.py:344
  33.2 10.0 %collective-permute-start.10 = (bf16[3,2,128,128]{3,2,1,0:T(8,128)(2,1)S(1)}, bf16[3,2,128,128]{3,2,1,0:T(8,128)(2,1)S(1)}, u32[]{:S(2)}, u32[]{:S(2)}) collective-permute-start(bf16[3,2,128,128]{3,2,1,0:T(8,128)(2,1)S(1)} %get-tuple-element.49), channel_id=1, source_target_pairs={{0,1},{1,0},{2,3},{3,2},{4,5},{5,4},{6,7},{7,6},{8,9},{9,8},{10,11... | collective-permute-start | bytes 589832 | tf_op jit(solution)/shard_map/ppermute | solution.py:344
  33.4 9.9 %collective-permute-start.11 = (bf16[3,2,128,128]{3,2,1,0:T(8,128)(2,1)S(1)}, bf16[3,2,128,128]{3,2,1,0:T(8,128)(2,1)S(1)}, u32[]{:S(2)}, u32[]{:S(2)}) collective-permute-start(bf16[3,2,128,128]{3,2,1,0:T(8,128)(2,1)S(1)} %get-tuple-element.50), channel_id=1, source_target_pairs={{0,1},{1,0},{2,3},{3,2},{4,5},{5,4},{6,7},{7,6},{8,9},{9,8},{10,11... | collective-permute-start | bytes 589832 | tf_op jit(solution)/shard_map/ppermute | solution.py:344
  33.7 7.4 %collective-permute-start.3 = (bf16[1,2,128,128]{3,2,1,0:T(8,128)(2,1)S(1)}, bf16[1,2,128,128]{3,2,1,0:T(8,128)(2,1)S(1)}, u32[]{:S(2)}, u32[]{:S(2)}) collective-permute-start(bf16[1,2,128,128]{3,2,1,0:T(8,128)(2,1)S(1)} %get-tuple-element.38), channel_id=1, source_target_pairs={{0,1},{1,0},{2,3},{3,2},{4,5},{5,4},{6,7},{7,6},{8,9},{9,8},{10,11... | collective-permute-start | bytes 196616 | tf_op jit(solution)/shard_map/ppermute | solution.py:344
  34.2 0.7 %copy-start = (f32[2,8,128]{2,1,0:T(8,128)S(1)}, f32[2,8,128]{2,1,0:T(8,128)}, u32[]{:S(2)}) copy-start(f32[2,8,128]{2,1,0:T(8,128)} %gains.11) | copy-start | bytes 24580
  34.2 1.0 %copy-start.1 = (bf16[4,2,128,128]{3,2,1,0:T(8,128)(2,1)S(1)}, bf16[4,2,128,128]{3,2,1,0:T(8,128)(2,1)}, u32[]{:S(2)}) copy-start(bf16[4,2,128,128]{3,2,1,0:T(8,128)(2,1)} %get-tuple-element.45.refs_3_) | copy-start | bytes 786436
  34.2 1.0 %copy-start.2 = (bf16[4,2,128,128]{3,2,1,0:T(8,128)(2,1)S(1)}, bf16[4,2,128,128]{3,2,1,0:T(8,128)(2,1)}, u32[]{:S(2)}) copy-start(bf16[4,2,128,128]{3,2,1,0:T(8,128)(2,1)} %get-tuple-element.46.refs_4_) | copy-start | bytes 786436
  35.2 0.7 %copy-start.4 = (s32[4,4]{1,0:T(4,128)S(1)}, s32[4,4]{1,0:T(4,128)}, u32[]{:S(2)}) copy-start(s32[4,4]{1,0:T(4,128)} %units.5) | copy-start | bytes 196
  41.0 7.3 %collective-permute-start.8 = (bf16[1,3,128,128]{3,2,1,0:T(8,128)(2,1)S(1)}, bf16[1,3,128,128]{3,2,1,0:T(8,128)(2,1)S(1)}, u32[]{:S(2)}, u32[]{:S(2)}) collective-permute-start(bf16[1,3,128,128]{3,2,1,0:T(8,128)(2,1)S(1)} %get-tuple-element.47), channel_id=1, source_target_pairs={{0,2},{1,3},{2,0},{3,1},{4,6},{5,7},{6,4},{7,5},{8,10},{9,11},{10,... | collective-permute-start | bytes 294920 | tf_op jit(solution)/shard_map/ppermute | solution.py:344
  43.2 5.7 %collective-permute-start.9 = (bf16[1,3,128,128]{3,2,1,0:T(8,128)(2,1)S(1)}, bf16[1,3,128,128]{3,2,1,0:T(8,128)(2,1)S(1)}, u32[]{:S(2)}, u32[]{:S(2)}) collective-permute-start(bf16[1,3,128,128]{3,2,1,0:T(8,128)(2,1)S(1)} %get-tuple-element.48), channel_id=1, source_target_pairs={{0,3},{1,2},{2,1},{3,0},{4,7},{5,6},{6,5},{7,4},{8,11},{9,10},{10,... | collective-permute-start | bytes 294920 | tf_op jit(solution)/shard_map/ppermute | solution.py:344
  43.2 0.9 %copy-start.3 = (bf16[3,2,128,128]{3,2,1,0:T(8,128)(2,1)S(1)}, bf16[3,2,128,128]{3,2,1,0:T(8,128)(2,1)}, u32[]{:S(2)}) copy-start(bf16[3,2,128,128]{3,2,1,0:T(8,128)(2,1)} %get-tuple-element.52.refs_3_) | copy-start | bytes 589828
  49.9 5.6 %collective-permute-start.14 = (f32[2,8,32]{2,1,0:T(8,128)S(1)}, f32[2,8,32]{2,1,0:T(8,128)S(1)}, u32[]{:S(2)}, u32[]{:S(2)}) collective-permute-start(f32[2,8,32]{2,1,0:T(8,128)S(1)} %get-tuple-element.56), channel_id=1, source_target_pairs={{0,4},{4,12},{8,0},{12,8},{1,5},{5,13},{9,1},{13,9},{2,6},{6,14},{... | collective-permute-start | bytes 6152 | tf_op jit(solution)/shard_map/ppermute | solution.py:387
  51.4 5.4 %collective-permute-start.15 = (f32[2,8,32]{2,1,0:T(8,128)S(1)}, f32[2,8,32]{2,1,0:T(8,128)S(1)}, u32[]{:S(2)}, u32[]{:S(2)}) collective-permute-start(f32[2,8,32]{2,1,0:T(8,128)S(1)} %get-tuple-element.57), channel_id=1, source_target_pairs={{0,12},{4,8},{8,4},{12,0},{1,13},{5,9},{9,5},{13,1},{2,14},{6,10},... | collective-permute-start | bytes 6152 | tf_op jit(solution)/shard_map/ppermute | solution.py:387
  54.0 3.7 %collective-permute-start.16 = (f32[2,8,32]{2,1,0:T(8,128)S(1)}, f32[2,8,32]{2,1,0:T(8,128)S(1)}, u32[]{:S(2)}, u32[]{:S(2)}) collective-permute-start(f32[2,8,32]{2,1,0:T(8,128)S(1)} %get-tuple-element.58), channel_id=1, source_target_pairs={{0,8},{4,0},{8,12},{12,4},{1,9},{5,1},{9,13},{13,5},{2,10},{6,2},{... | collective-permute-start | bytes 6152 | tf_op jit(solution)/shard_map/ppermute | solution.py:387

commit v11 on v9

--- a/solution.py
+++ b/solution.py
@@ -236,16 +236,29 @@
                     kept[head, start : start + rows, :] = block[slot * rows : (slot + 1) * rows]
     factor = size ** (-0.5) * math.log2(math.e)
 
-    def clip(head, slot, span):
-        where = slice(slot * unit, (slot + span) * unit)
-        q, k = query[head, where, :], key[head, where, :]
-        expo = jnp.exp2(contract_last(k, q) * factor)
-        dprob = contract_last(value[head, where, :], grad[head, where, :])
-        prob = expo * (1.0 / jnp.sum(expo, axis=0, keepdims=True))
-        delta = jnp.sum(prob * dprob, axis=0, keepdims=True)
-        dscore = (prob * (dprob - delta)).astype(jnp.bfloat16)
-        mixed = jnp.dot(dscore, q, preferred_element_type=jnp.float32)
-        return jnp.sum(mixed * k.astype(jnp.float32), axis=0, keepdims=True)
+    def attention(head, layout):
+        blocks = [
+            (slice(slot * unit, (slot + span) * unit), slice(place * unit, (place + 1) * unit))
+            for slot, span in layout
+            for place in range(slot, slot + span)
+        ]
+        scores = [contract_last(key[head, keys, :], query[head, own, :]) for keys, own in blocks]
+        dprobs = [contract_last(value[head, keys, :], grad[head, own, :]) for keys, own in blocks]
+        expos = [jnp.exp2(score * factor) for score in scores]
+        shares = [1.0 / jnp.sum(expo, axis=0, keepdims=True) for expo in expos]
+        probs = [expo * share for expo, share in zip(expos, shares)]
+        deltas = [jnp.sum(prob * dprob, axis=0, keepdims=True) for prob, dprob in zip(probs, dprobs)]
+        dscores = [
+            (prob * (dprob - delta)).astype(jnp.bfloat16) for prob, dprob, delta in zip(probs, dprobs, deltas)
+        ]
+        mixed = [
+            jnp.dot(dscore, query[head, own, :], preferred_element_type=jnp.float32)
+            for dscore, (_, own) in zip(dscores, blocks)
+        ]
+        return sum(
+            jnp.sum(part * key[head, keys, :].astype(jnp.float32), axis=0, keepdims=True)
+            for part, (keys, _) in zip(mixed, blocks)
+        )
 
     table = units[...]
     rows_of, slots_of = (lax.broadcasted_iota(jnp.int32, table.shape, dim) for dim in (0, 1))
@@ -256,7 +269,7 @@
         @pl.when(begins == sum(1 << slot for slot, _ in layout))
         def _():
             for head in range(count):
-                total[head : head + 1, :] = sum(clip(head, slot, span) for slot, span in layout)
+                total[head : head + 1, :] = attention(head, layout)
 
 
 def chunk_kernel(low, units, gains, values, close, *refs):

time: 58.5 us -> 58.3 us (level)
  Pallas kernels: 16.1 us -> 14.2 us
  waiting for transfers between devices: 23.1 us -> 24.9 us
    pallas_call x3, Pallas kernels: 6.62 us -> 4.7 us  [attend(): pl.pallas_call(kernel, out_shape=shapes, in_specs=[pl.BlockSpec(memory_sp...]
    ppermute x14, waiting for transfers between devices: 21.2 us -> 22.8 us  [send(): return lax.ppermute(block, 'seq', [(s, s ^ flip) for s in range(sequence)])]
  transfers between devices with their start and end apart: 17 -> 17, of which waited for: 9 -> 10; matrix products, arithmetic and copies ran while one was open for 0% -> 0% of each run, Pallas kernels for 24% -> 21%
where the time goes in v11:
time: 58.3 us; the launch traced here: 58.1 us
  waiting for transfers between devices  24.9 us (43%)
  starting transfers between devices  16.2 us (28%)
  Pallas kernels  14.2 us (24%)
  local copies, waits for them, and re-layouts  2.08 us (4%)
  other arithmetic  0.6 us (1%)
    ppermute x14, waiting for transfers between devices, send(): return lax.ppermute(block, 'seq', [(s, s ^ flip) for s in range(sequence)])  22.8 us
    ppermute x14, starting transfers between devices, send(): return lax.ppermute(block, 'seq', [(s, s ^ flip) for s in range(sequence)])  10.5 us
    pallas_call x3, Pallas kernels, pack(): pl.pallas_call(functools.partial(pack_kernel, plan, heads, len(after)), o...  7.37 us
    ppermute x3, starting transfers between devices, body(): result = result + lax.ppermute(part, 'dp', list(enumerate(targets)))  5.64 us
    pallas_call x3, Pallas kernels, attend(): pl.pallas_call(kernel, out_shape=shapes, in_specs=[pl.BlockSpec(memory_sp...  4.7 us
    unnamed x10, local copies, waits for them, and re-layouts  2.08 us
    ppermute x3, waiting for transfers between devices, body(): result = result + lax.ppermute(part, 'dp', list(enumerate(targets)))  2.07 us
  transfers between devices with their start and end apart: 17, of which 10 were waited for; matrix products, arithmetic and copies ran while one was open for 0% of the time, Pallas kernels for 21%

profile of v11, /device:TPU:0, one launch (start us, length us, event | category | flops | bytes accessed | tf_op | source)
XLA Modules:
  0.0 58.1 jit_solution(16054710537667473263)
XLA Ops:
  0.0 1.1 %cut.1 = (bf16[4,32,8,128]{3,2,1,0:T(8,128)(2,1)S(1)}, bf16[4,32,8,128]{3,2,1,0:T(8,128)(2,1)S(1)}, f32[8,128]{1,0:T(8,128)S(1)}) custom-call(bf16[1,4,32,32,128]{4,3,2,1,0:T(8,128)(2,1)} %refs_2_.5), custom_call_target="tpu_custom_call" | custom-call | tf_op jit(solution)/shard_map/cut/pallas_call | solution.py:53
  1.1 3.0 %collective-permute-start = (bf16[4,32,8,128]{3,2,1,0:T(8,128)(2,1)S(1)}, bf16[4,32,8,128]{3,2,1,0:T(8,128)(2,1)S(1)}, u32[]{:S(2)}, u32[]{:S(2)}) collective-permute-start(bf16[4,32,8,128]{3,2,1,0:T(8,128)(2,1)S(1)} %get-tuple-element.31), channel_id=1, source_target_pairs={{0,2},{1,3},{2,0},{3,1},{4,6},{5,7},{6,4},{7,5},{8,10},{9,11},{10,... | collective-permute-start | bytes 786440 | tf_op jit(solution)/shard_map/ppermute | solution.py:357
  4.1 1.5 %pack.3 = (bf16[4,3,128,128]{3,2,1,0:T(8,128)(2,1)S(1)}, bf16[4,3,128,128]{3,2,1,0:T(8,128)(2,1)S(1)}, f32[8,128]{1,0:T(8,128)S(1)}) custom-call(bf16[1,4,32,32,128]{4,3,2,1,0:T(8,128)(2,1)} %refs_0_.5, bf16[1,4,32,32,128]{4,3,2,1,0:T(8,128)(2,1)} %refs_1_.5, bf16[1,4,32,32,128]{4,3,2,1,0:T(8,128)(2,1)} %refs_2_.5, bf16[1,4,32,32,128]{4,3,2,1,0:T(8,128)(2,1)} %refs_3_.5, ...), custom_call_target="tpu_custom_call" | custom-call | flops 2097152 | bytes 4194304 | tf_op jit(solution)/shard_map/pack/pallas_call | solution.py:145
  5.6 1.2 %collective-permute-start.4 = (bf16[4,3,128,128]{3,2,1,0:T(8,128)(2,1)S(1)}, bf16[4,3,128,128]{3,2,1,0:T(8,128)(2,1)S(1)}, u32[]{:S(2)}, u32[]{:S(2)}) collective-permute-start(bf16[4,3,128,128]{3,2,1,0:T(8,128)(2,1)S(1)} %get-tuple-element.39), channel_id=1, source_target_pairs={{0,2},{1,3},{2,0},{3,1},{4,6},{5,7},{6,4},{7,5},{8,10},{9,11},{10,... | collective-permute-start | bytes 1179656 | tf_op jit(solution)/shard_map/ppermute | solution.py:357
  6.9 0.6 %collective-permute-start.5 = (bf16[4,3,128,128]{3,2,1,0:T(8,128)(2,1)S(1)}, bf16[4,3,128,128]{3,2,1,0:T(8,128)(2,1)S(1)}, u32[]{:S(2)}, u32[]{:S(2)}) collective-permute-start(bf16[4,3,128,128]{3,2,1,0:T(8,128)(2,1)S(1)} %get-tuple-element.40), channel_id=1, source_target_pairs={{0,3},{1,2},{2,1},{3,0},{4,7},{5,6},{6,5},{7,4},{8,11},{9,10},{10,... | collective-permute-start | bytes 1179656 | tf_op jit(solution)/shard_map/ppermute | solution.py:357
  7.5 3.7 %collective-permute-done.refs_0_ = bf16[4,32,8,128]{3,2,1,0:T(8,128)(2,1)S(1)} collective-permute-done((bf16[4,32,8,128]{3,2,1,0:T(8,128)(2,1)S(1)}, bf16[4,32,8,128]{3,2,1,0:T(8,128)(2,1)S(1)}, u32[]{:S(2)}, u32[]{:S(2)}) %collective-permute-start) | collective-permute-done | bytes 262176 | tf_op jit(solution)/shard_map/ppermute | solution.py:357
  11.2 5.2 %collective-permute-done.1.refs_1_ = bf16[4,32,8,128]{3,2,1,0:T(8,128)(2,1)S(1)} collective-permute-done((bf16[4,32,8,128]{3,2,1,0:T(8,128)(2,1)S(1)}, bf16[4,32,8,128]{3,2,1,0:T(8,128)(2,1)S(1)}, u32[]{:S(2)}, u32[]{:S(2)}) %collective-permute-start.1) | collective-permute-done | bytes 262176 | tf_op jit(solution)/shard_map/ppermute | solution.py:357
  16.4 3.8 %pack.4 = (bf16[3,3,128,128]{3,2,1,0:T(8,128)(2,1)}, bf16[3,3,128,128]{3,2,1,0:T(8,128)(2,1)}, bf16[4,2,128,128]{3,2,1,0:T(8,128)(2,1)}, bf16[3,2,128,128]{3,2,1...) custom-call(bf16[1,4,32,32,128]{4,3,2,1,0:T(8,128)(2,1)} %refs_0_.5,, ...), custom_call_target="tpu_custom_call" | custom-call | flops 6291456 | bytes 12582912 | tf_op jit(solution)/shard_map/pack/pallas_call | solution.py:145
  20.2 0.3 collective-permute-start.6
  20.5 0.3 collective-permute-start.7
  20.8 0.2 collective-permute-start.2
  21.0 1.2 %collective-permute-done.2.refs_0_ = bf16[1,2,128,128]{3,2,1,0:T(8,128)(2,1)S(1)} collective-permute-done((bf16[1,2,128,128]{3,2,1,0:T(8,128)(2,1)S(1)}, bf16[1,2,128,128]{3,2,1,0:T(8,128)(2,1)S(1)}, u32[]{:S(2)}, u32[]{:S(2)}) %collective-permute-start.2) | collective-permute-done | bytes 65568 | tf_op jit(solution)/shard_map/ppermute | solution.py:357
  22.2 1.9 %collective-permute-start.12 = (bf16[3,3,128,128]{3,2,1,0:T(8,128)(2,1)}, bf16[3,3,128,128]{3,2,1,0:T(8,128)(2,1)S(1)}, u32[]{:S(2)}, u32[]{:S(2)}) collective-permute-start(bf16[3,3,128,128]{3,2,1,0:T(8,128)(2,1)} %get-tuple-element.51), channel_id=1, source_target_pairs={{0,2},{1,3},{2,0},{3,1},{4,6},{5,7},{6,4},{7,5},{8,10},{9,11},{10,... | collective-permute-start | bytes 884744 | tf_op jit(solution)/shard_map/ppermute | solution.py:357
  24.2 1.1 %collective-permute-done.4.refs_0_ = bf16[4,3,128,128]{3,2,1,0:T(8,128)(2,1)S(1)} collective-permute-done((bf16[4,3,128,128]{3,2,1,0:T(8,128)(2,1)S(1)}, bf16[4,3,128,128]{3,2,1,0:T(8,128)(2,1)S(1)}, u32[]{:S(2)}, u32[]{:S(2)}) %collective-permute-start.4) | collective-permute-done | bytes 393248 | tf_op jit(solution)/shard_map/ppermute | solution.py:357
  25.2 0.0 collective-permute-start.13
  25.2 8.0 %collective-permute-done.5.refs_1_ = bf16[4,3,128,128]{3,2,1,0:T(8,128)(2,1)S(1)} collective-permute-done((bf16[4,3,128,128]{3,2,1,0:T(8,128)(2,1)S(1)}, bf16[4,3,128,128]{3,2,1,0:T(8,128)(2,1)S(1)}, u32[]{:S(2)}, u32[]{:S(2)}) %collective-permute-start.5) | collective-permute-done | bytes 393248 | tf_op jit(solution)/shard_map/ppermute | solution.py:357
  33.2 0.2 collective-permute-start.10
  33.5 0.3 collective-permute-start.11
  33.8 0.0 collective-permute-done.7.refs_2_
  33.8 0.2 collective-permute-start.3
  34.0 0.2 arrange.1.values
  34.2 0.0 copy-start
  34.3 0.7 %copy-done = f32[2,8,128]{2,1,0:T(8,128)S(1)} copy-done((f32[2,8,128]{2,1,0:T(8,128)S(1)}, f32[2,8,128]{2,1,0:T(8,128)}, u32[]{:S(2)}) %copy-start) | copy-done | bytes 8216
  34.9 0.3 copy-done.1
  35.2 0.1 copy-done.2
  35.3 0.4 prepare.4.close
  35.7 0.3 copy-done.4
  36.0 2.3 %attend.3.refs_4_.refs_2_ = f32[4,128]{1,0:T(4,128)S(1)} custom-call(s32[4,4]{1,0:T(4,128)S(1)} %copy-done.4, f32[2,8,128]{2,1,0:T(8,128)S(1)} %copy-done, bf16[8,4,64,128]{3,2,1,0:T(8,128)(2,1)S(1)} %arrange.1.values, bf16[4,4,4,64,128]{4,3,2,1,0:T(8,128)(2,1)S(1)} %prepare.4.close, bf16[4,3,128,128]{3,2,1,0:T(8,128)(2,1)S(1)} %collective-permute-done.4.refs_0_, ...), custom_call_target="tpu_custom_call" | custom-call | flops 402653184 | bytes 1048576 | tf_op jit(solution)/shard_map/attend/pallas_call | solution.py:314
  38.2 2.1 %pack.5 = (bf16[1,3,128,128]{3,2,1,0:T(8,128)(2,1)S(1)}, bf16[1,3,128,128]{3,2,1,0:T(8,128)(2,1)S(1)}, f32[8,128]{1,0:T(8,128)}) custom-call(bf16[1,4,32,32,128]{4,3,2,1,0:T(8,128)(2,1)} %refs_0_.5, bf16[1,4,32,32,128]{4,3,2,1,0:T(8,128)(2,1)} %refs_1_.5, bf16[1,4,32,32,128]{4,3,2,1,0:T(8,128)(2,1)} %refs_2_.5, bf16[1,4,32,32,128]{4,3,2,1,0:T(8,128)(2,1)} %refs_3_.5, ...), custom_call_target="tpu_custom_call" | custom-call | flops 2097152 | bytes 4194304 | tf_op jit(solution)/shard_map/pack/pallas_call | solution.py:145
  40.3 2.1 %collective-permute-start.8 = (bf16[1,3,128,128]{3,2,1,0:T(8,128)(2,1)S(1)}, bf16[1,3,128,128]{3,2,1,0:T(8,128)(2,1)S(1)}, u32[]{:S(2)}, u32[]{:S(2)}) collective-permute-start(bf16[1,3,128,128]{3,2,1,0:T(8,128)(2,1)S(1)} %get-tuple-element.45), channel_id=1, source_target_pairs={{0,2},{1,3},{2,0},{3,1},{4,6},{5,7},{6,4},{7,5},{8,10},{9,11},{10,... | collective-permute-start | bytes 294920 | tf_op jit(solution)/shard_map/ppermute | solution.py:357
  42.4 0.0 collective-permute-done.10.refs_0_
  42.5 0.0 collective-permute-start.9
  42.5 0.2 prepare.3.close
  42.6 0.0 collective-permute-done.11.refs_1_
  42.6 0.8 %copy-done.3 = bf16[3,2,128,128]{3,2,1,0:T(8,128)(2,1)S(1)} copy-done((bf16[3,2,128,128]{3,2,1,0:T(8,128)(2,1)S(1)}, bf16[3,2,128,128]{3,2,1,0:T(8,128)(2,1)}, u32[]{:S(2)}) %copy-start.3) | copy-done | bytes 196632
  43.4 0.3 prepare.5.close
  43.7 0.0 collective-permute-done.12.refs_0_
  43.7 2.3 %collective-permute-done.13.refs_1_ = bf16[3,3,128,128]{3,2,1,0:T(8,128)(2,1)S(1)} collective-permute-done((bf16[3,3,128,128]{3,2,1,0:T(8,128)(2,1)}, bf16[3,3,128,128]{3,2,1,0:T(8,128)(2,1)S(1)}, u32[]{:S(2)}, u32[]{:S(2)}) %collective-permute-start.13) | collective-permute-done | bytes 294944 | tf_op jit(solution)/shard_map/ppermute | solution.py:357
  46.0 1.6 %attend.4.refs_3_ = f32[3,128]{1,0:T(4,128)S(1)} custom-call(s32[4,4]{1,0:T(4,128)S(1)} %copy-done.4, f32[2,8,128]{2,1,0:T(8,128)S(1)} %copy-done, bf16[8,4,64,128]{3,2,1,0:T(8,128)(2,1)S(1)} %arrange.1.values, bf16[3,4,4,64,128]{4,3,2,1,0:T(8,128)(2,1)S(1)} %prepare.5.close, bf16[3,3,128,128]{3,2,1,0:T(8,128)(2,1)S(1)} %collective-permute-done.12.refs_0_, ...), custom_call_target="tpu_custom_call" | custom-call | flops 301989888 | bytes 786432 | tf_op jit(solution)/shard_map/attend/pallas_call | solution.py:314
  47.6 0.8 %collective-permute-done.8.refs_0_ = bf16[1,3,128,128]{3,2,1,0:T(8,128)(2,1)S(1)} collective-permute-done((bf16[1,3,128,128]{3,2,1,0:T(8,128)(2,1)S(1)}, bf16[1,3,128,128]{3,2,1,0:T(8,128)(2,1)S(1)}, u32[]{:S(2)}, u32[]{:S(2)}) %collective-permute-start.8) | collective-permute-done | bytes 98336 | tf_op jit(solution)/shard_map/ppermute | solution.py:357
  48.4 0.5 collective-permute-done.9.refs_1_
  49.0 0.8 %attend.5 = (f32[2,8,32]{2,1,0:T(8,128)S(1)}, f32[2,8,32]{2,1,0:T(8,128)S(1)}, f32[2,8,32]{2,1,0:T(8,128)S(1)}, f32[2,8,32]{2,1,0:T(8,128)S(1)}) custom-call(s32[4,4]{1,0:T(4,128)S(1)} %copy-done.4, f32[2,8,128]{2,1,0:T(8,128)S(1)} %copy-done, bf16[8,4,64,128]{3,2,1,0:T(8,128)(2,1)S(1)} %arrange.1.values, bf16[1,4,4,64,128]{4,3,2,1,0:T(8,128)(2,1)S(1)} %prepare.3.close, ...), custom_call_target="tpu_custom_call" | custom-call | flops 100663296 | bytes 262144 | tf_op jit(solution)/shard_map/attend/pallas_call | solution.py:314
  49.8 1.6 %collective-permute-start.14 = (f32[2,8,32]{2,1,0:T(8,128)S(1)}, f32[2,8,32]{2,1,0:T(8,128)S(1)}, u32[]{:S(2)}, u32[]{:S(2)}) collective-permute-start(f32[2,8,32]{2,1,0:T(8,128)S(1)} %get-tuple-element.54), channel_id=1, source_target_pairs={{0,4},{4,12},{8,0},{12,8},{1,5},{5,13},{9,1},{13,9},{2,6},{6,14},{... | collective-permute-start | bytes 6152 | tf_op jit(solution)/shard_map/ppermute | solution.py:394
  51.4 2.4 %collective-permute-start.15 = (f32[2,8,32]{2,1,0:T(8,128)S(1)}, f32[2,8,32]{2,1,0:T(8,128)S(1)}, u32[]{:S(2)}, u32[]{:S(2)}) collective-permute-start(f32[2,8,32]{2,1,0:T(8,128)S(1)} %get-tuple-element.55), channel_id=1, source_target_pairs={{0,12},{4,8},{8,4},{12,0},{1,13},{5,9},{9,5},{13,1},{2,14},{6,10},... | collective-permute-start | bytes 6152 | tf_op jit(solution)/shard_map/ppermute | solution.py:394
  53.8 1.6 %collective-permute-start.16 = (f32[2,8,32]{2,1,0:T(8,128)S(1)}, f32[2,8,32]{2,1,0:T(8,128)S(1)}, u32[]{:S(2)}, u32[]{:S(2)}) collective-permute-start(f32[2,8,32]{2,1,0:T(8,128)S(1)} %get-tuple-element.56), channel_id=1, source_target_pairs={{0,8},{4,0},{8,12},{12,4},{1,9},{5,1},{9,13},{13,5},{2,10},{6,2},{... | collective-permute-start | bytes 6152 | tf_op jit(solution)/shard_map/ppermute | solution.py:394
  55.4 1.4 %collective-permute-done.15 = f32[2,8,32]{2,1,0:T(8,128)S(1)} collective-permute-done((f32[2,8,32]{2,1,0:T(8,128)S(1)}, f32[2,8,32]{2,1,0:T(8,128)S(1)}, u32[]{:S(2)}, u32[]{:S(2)}) %collective-permute-start.15) | collective-permute-done | bytes 2080 | tf_op jit(solution)/shard_map/ppermute | solution.py:394
  56.9 0.6 %collective-permute-done.16 = f32[2,8,32]{2,1,0:T(8,128)S(1)} collective-permute-done((f32[2,8,32]{2,1,0:T(8,128)S(1)}, f32[2,8,32]{2,1,0:T(8,128)S(1)}, u32[]{:S(2)}, u32[]{:S(2)}) %collective-permute-start.16) | collective-permute-done | bytes 2080 | tf_op jit(solution)/shard_map/ppermute | solution.py:394
  57.5 0.6 %add_add_fusion = f32[2,8,32]{2,1,0:T(8,128)} fusion(f32[2,8,32]{2,1,0:T(8,128)S(1)} %collective-permute-done.16, f32[2,8,32]{2,1,0:T(8,128)S(1)} %collective-permute-done.15, f32[2,8,32]{2,1,0:T(8,128)S(1)} %get-tuple-element.53, f32[2,8,32]{2,1,0:T(8,128)S(1)} %collective-permute-done.14), kind=kLoop, calls=%fused_computation | loop fusion | flops 1536 | bytes 10240 | tf_op jit(solution)/shard_map/add | solution.py:394
  (10 shorter events, 0.0 us)
Async XLA Ops:
  1.1 10.1 %collective-permute-start = (bf16[4,32,8,128]{3,2,1,0:T(8,128)(2,1)S(1)}, bf16[4,32,8,128]{3,2,1,0:T(8,128)(2,1)S(1)}, u32[]{:S(2)}, u32[]{:S(2)}) collective-permute-start(bf16[4,32,8,128]{3,2,1,0:T(8,128)(2,1)S(1)} %get-tuple-element.31), channel_id=1, source_target_pairs={{0,2},{1,3},{2,0},{3,1},{4,6},{5,7},{6,4},{7,5},{8,10},{9,11},{10,... | collective-permute-start | bytes 786440 | tf_op jit(solution)/shard_map/ppermute | solution.py:357
  4.1 12.3 %collective-permute-start.1 = (bf16[4,32,8,128]{3,2,1,0:T(8,128)(2,1)S(1)}, bf16[4,32,8,128]{3,2,1,0:T(8,128)(2,1)S(1)}, u32[]{:S(2)}, u32[]{:S(2)}) collective-permute-start(bf16[4,32,8,128]{3,2,1,0:T(8,128)(2,1)S(1)} %get-tuple-element.32), channel_id=1, source_target_pairs={{0,3},{1,2},{2,1},{3,0},{4,7},{5,6},{6,5},{7,4},{8,11},{9,10},{10,... | collective-permute-start | bytes 786440 | tf_op jit(solution)/shard_map/ppermute | solution.py:357
  5.6 19.6 %collective-permute-start.4 = (bf16[4,3,128,128]{3,2,1,0:T(8,128)(2,1)S(1)}, bf16[4,3,128,128]{3,2,1,0:T(8,128)(2,1)S(1)}, u32[]{:S(2)}, u32[]{:S(2)}) collective-permute-start(bf16[4,3,128,128]{3,2,1,0:T(8,128)(2,1)S(1)} %get-tuple-element.39), channel_id=1, source_target_pairs={{0,2},{1,3},{2,0},{3,1},{4,6},{5,7},{6,4},{7,5},{8,10},{9,11},{10,... | collective-permute-start | bytes 1179656 | tf_op jit(solution)/shard_map/ppermute | solution.py:357
  6.9 26.4 %collective-permute-start.5 = (bf16[4,3,128,128]{3,2,1,0:T(8,128)(2,1)S(1)}, bf16[4,3,128,128]{3,2,1,0:T(8,128)(2,1)S(1)}, u32[]{:S(2)}, u32[]{:S(2)}) collective-permute-start(bf16[4,3,128,128]{3,2,1,0:T(8,128)(2,1)S(1)} %get-tuple-element.40), channel_id=1, source_target_pairs={{0,3},{1,2},{2,1},{3,0},{4,7},{5,6},{6,5},{7,4},{8,11},{9,10},{10,... | collective-permute-start | bytes 1179656 | tf_op jit(solution)/shard_map/ppermute | solution.py:357
  20.2 13.3 %collective-permute-start.6 = (bf16[4,2,128,128]{3,2,1,0:T(8,128)(2,1)}, bf16[4,2,128,128]{3,2,1,0:T(8,128)(2,1)S(1)}, u32[]{:S(2)}, u32[]{:S(2)}) collective-permute-start(bf16[4,2,128,128]{3,2,1,0:T(8,128)(2,1)} %get-tuple-element.41), channel_id=1, source_target_pairs={{0,1},{1,0},{2,3},{3,2},{4,5},{5,4},{6,7},{7,6},{8,9},{9,8},{10,11... | collective-permute-start | bytes 786440 | tf_op jit(solution)/shard_map/ppermute | solution.py:357
  20.5 13.3 %collective-permute-start.7 = (bf16[4,2,128,128]{3,2,1,0:T(8,128)(2,1)}, bf16[4,2,128,128]{3,2,1,0:T(8,128)(2,1)S(1)}, u32[]{:S(2)}, u32[]{:S(2)}) collective-permute-start(bf16[4,2,128,128]{3,2,1,0:T(8,128)(2,1)} %get-tuple-element.42), channel_id=1, source_target_pairs={{0,1},{1,0},{2,3},{3,2},{4,5},{5,4},{6,7},{7,6},{8,9},{9,8},{10,11... | collective-permute-start | bytes 786440 | tf_op jit(solution)/shard_map/ppermute | solution.py:357
  20.8 1.5 %collective-permute-start.2 = (bf16[1,2,128,128]{3,2,1,0:T(8,128)(2,1)S(1)}, bf16[1,2,128,128]{3,2,1,0:T(8,128)(2,1)S(1)}, u32[]{:S(2)}, u32[]{:S(2)}) collective-permute-start(bf16[1,2,128,128]{3,2,1,0:T(8,128)(2,1)S(1)} %get-tuple-element.35), channel_id=1, source_target_pairs={{0,1},{1,0},{2,3},{3,2},{4,5},{5,4},{6,7},{7,6},{8,9},{9,8},{10,11... | collective-permute-start | bytes 196616 | tf_op jit(solution)/shard_map/ppermute | solution.py:357
  22.2 21.4 %collective-permute-start.12 = (bf16[3,3,128,128]{3,2,1,0:T(8,128)(2,1)}, bf16[3,3,128,128]{3,2,1,0:T(8,128)(2,1)S(1)}, u32[]{:S(2)}, u32[]{:S(2)}) collective-permute-start(bf16[3,3,128,128]{3,2,1,0:T(8,128)(2,1)} %get-tuple-element.51), channel_id=1, source_target_pairs={{0,2},{1,3},{2,0},{3,1},{4,6},{5,7},{6,4},{7,5},{8,10},{9,11},{10,... | collective-permute-start | bytes 884744 | tf_op jit(solution)/shard_map/ppermute | solution.py:357
  25.2 20.7 %collective-permute-start.13 = (bf16[3,3,128,128]{3,2,1,0:T(8,128)(2,1)}, bf16[3,3,128,128]{3,2,1,0:T(8,128)(2,1)S(1)}, u32[]{:S(2)}, u32[]{:S(2)}) collective-permute-start(bf16[3,3,128,128]{3,2,1,0:T(8,128)(2,1)} %get-tuple-element.52), channel_id=1, source_target_pairs={{0,3},{1,2},{2,1},{3,0},{4,7},{5,6},{6,5},{7,4},{8,11},{9,10},{10,... | collective-permute-start | bytes 884744 | tf_op jit(solution)/shard_map/ppermute | solution.py:357
  33.2 9.2 %collective-permute-start.10 = (bf16[3,2,128,128]{3,2,1,0:T(8,128)(2,1)S(1)}, bf16[3,2,128,128]{3,2,1,0:T(8,128)(2,1)S(1)}, u32[]{:S(2)}, u32[]{:S(2)}) collective-permute-start(bf16[3,2,128,128]{3,2,1,0:T(8,128)(2,1)S(1)} %get-tuple-element.47), channel_id=1, source_target_pairs={{0,1},{1,0},{2,3},{3,2},{4,5},{5,4},{6,7},{7,6},{8,9},{9,8},{10,11... | collective-permute-start | bytes 589832 | tf_op jit(solution)/shard_map/ppermute | solution.py:357
  33.5 9.1 %collective-permute-start.11 = (bf16[3,2,128,128]{3,2,1,0:T(8,128)(2,1)S(1)}, bf16[3,2,128,128]{3,2,1,0:T(8,128)(2,1)S(1)}, u32[]{:S(2)}, u32[]{:S(2)}) collective-permute-start(bf16[3,2,128,128]{3,2,1,0:T(8,128)(2,1)S(1)} %get-tuple-element.48), channel_id=1, source_target_pairs={{0,1},{1,0},{2,3},{3,2},{4,5},{5,4},{6,7},{7,6},{8,9},{9,8},{10,11... | collective-permute-start | bytes 589832 | tf_op jit(solution)/shard_map/ppermute | solution.py:357
  33.8 6.6 %collective-permute-start.3 = (bf16[1,2,128,128]{3,2,1,0:T(8,128)(2,1)S(1)}, bf16[1,2,128,128]{3,2,1,0:T(8,128)(2,1)S(1)}, u32[]{:S(2)}, u32[]{:S(2)}) collective-permute-start(bf16[1,2,128,128]{3,2,1,0:T(8,128)(2,1)S(1)} %get-tuple-element.36), channel_id=1, source_target_pairs={{0,1},{1,0},{2,3},{3,2},{4,5},{5,4},{6,7},{7,6},{8,9},{9,8},{10,11... | collective-permute-start | bytes 196616 | tf_op jit(solution)/shard_map/ppermute | solution.py:357
  34.2 0.7 %copy-start = (f32[2,8,128]{2,1,0:T(8,128)S(1)}, f32[2,8,128]{2,1,0:T(8,128)}, u32[]{:S(2)}) copy-start(f32[2,8,128]{2,1,0:T(8,128)} %gains.11) | copy-start | bytes 24580
  34.3 1.0 %copy-start.1 = (bf16[4,2,128,128]{3,2,1,0:T(8,128)(2,1)S(1)}, bf16[4,2,128,128]{3,2,1,0:T(8,128)(2,1)}, u32[]{:S(2)}) copy-start(bf16[4,2,128,128]{3,2,1,0:T(8,128)(2,1)} %get-tuple-element.43.refs_3_) | copy-start | bytes 786436
  34.3 1.0 %copy-start.2 = (bf16[4,2,128,128]{3,2,1,0:T(8,128)(2,1)S(1)}, bf16[4,2,128,128]{3,2,1,0:T(8,128)(2,1)}, u32[]{:S(2)}) copy-start(bf16[4,2,128,128]{3,2,1,0:T(8,128)(2,1)} %get-tuple-element.44.refs_4_) | copy-start | bytes 786436
  35.3 0.7 %copy-start.4 = (s32[4,4]{1,0:T(4,128)S(1)}, s32[4,4]{1,0:T(4,128)}, u32[]{:S(2)}) copy-start(s32[4,4]{1,0:T(4,128)} %units.5) | copy-start | bytes 196
  40.3 8.1 %collective-permute-start.8 = (bf16[1,3,128,128]{3,2,1,0:T(8,128)(2,1)S(1)}, bf16[1,3,128,128]{3,2,1,0:T(8,128)(2,1)S(1)}, u32[]{:S(2)}, u32[]{:S(2)}) collective-permute-start(bf16[1,3,128,128]{3,2,1,0:T(8,128)(2,1)S(1)} %get-tuple-element.45), channel_id=1, source_target_pairs={{0,2},{1,3},{2,0},{3,1},{4,6},{5,7},{6,4},{7,5},{8,10},{9,11},{10,... | collective-permute-start | bytes 294920 | tf_op jit(solution)/shard_map/ppermute | solution.py:357
  42.5 6.5 %collective-permute-start.9 = (bf16[1,3,128,128]{3,2,1,0:T(8,128)(2,1)S(1)}, bf16[1,3,128,128]{3,2,1,0:T(8,128)(2,1)S(1)}, u32[]{:S(2)}, u32[]{:S(2)}) collective-permute-start(bf16[1,3,128,128]{3,2,1,0:T(8,128)(2,1)S(1)} %get-tuple-element.46), channel_id=1, source_target_pairs={{0,3},{1,2},{2,1},{3,0},{4,7},{5,6},{6,5},{7,4},{8,11},{9,10},{10,... | collective-permute-start | bytes 294920 | tf_op jit(solution)/shard_map/ppermute | solution.py:357
  42.5 0.9 %copy-start.3 = (bf16[3,2,128,128]{3,2,1,0:T(8,128)(2,1)S(1)}, bf16[3,2,128,128]{3,2,1,0:T(8,128)(2,1)}, u32[]{:S(2)}) copy-start(bf16[3,2,128,128]{3,2,1,0:T(8,128)(2,1)} %get-tuple-element.50.refs_3_) | copy-start | bytes 589828
  49.8 5.6 %collective-permute-start.14 = (f32[2,8,32]{2,1,0:T(8,128)S(1)}, f32[2,8,32]{2,1,0:T(8,128)S(1)}, u32[]{:S(2)}, u32[]{:S(2)}) collective-permute-start(f32[2,8,32]{2,1,0:T(8,128)S(1)} %get-tuple-element.54), channel_id=1, source_target_pairs={{0,4},{4,12},{8,0},{12,8},{1,5},{5,13},{9,1},{13,9},{2,6},{6,14},{... | collective-permute-start | bytes 6152 | tf_op jit(solution)/shard_map/ppermute | solution.py:394
  51.4 5.4 %collective-permute-start.15 = (f32[2,8,32]{2,1,0:T(8,128)S(1)}, f32[2,8,32]{2,1,0:T(8,128)S(1)}, u32[]{:S(2)}, u32[]{:S(2)}) collective-permute-start(f32[2,8,32]{2,1,0:T(8,128)S(1)} %get-tuple-element.55), channel_id=1, source_target_pairs={{0,12},{4,8},{8,4},{12,0},{1,13},{5,9},{9,5},{13,1},{2,14},{6,10},... | collective-permute-start | bytes 6152 | tf_op jit(solution)/shard_map/ppermute | solution.py:394
  53.8 3.7 %collective-permute-start.16 = (f32[2,8,32]{2,1,0:T(8,128)S(1)}, f32[2,8,32]{2,1,0:T(8,128)S(1)}, u32[]{:S(2)}, u32[]{:S(2)}) collective-permute-start(f32[2,8,32]{2,1,0:T(8,128)S(1)} %get-tuple-element.56), channel_id=1, source_target_pairs={{0,8},{4,0},{8,12},{12,4},{1,9},{5,1},{9,13},{13,5},{2,10},{6,2},{... | collective-permute-start | bytes 6152 | tf_op jit(solution)/shard_map/ppermute | solution.py:394

commit v12 on v11

--- a/solution.py
+++ b/solution.py
@@ -350,7 +350,7 @@
     arrays = (queries, key_rows, value_rows, out_grad)
     heads = norm_gains.shape[1]
     chunks = head_chunks(heads)
-    far = list(range(2, sequence)) or [1]
+    far = list(range(2, sequence))[::-1] or [1]
     near = [flip for flip in range(1, sequence) if flip not in far]
 
     def send(block, flip):

time: 58.3 us -> 60 us (1.029)
  starting transfers between devices: 16.2 us -> 18.3 us
  waiting for transfers between devices: 24.9 us -> 23.9 us
    ppermute x14, starting transfers between devices: 10.5 us -> 11.9 us  [send(): return lax.ppermute(block, 'seq', [(s, s ^ flip) for s in range(sequence)])]
    ppermute x14, waiting for transfers between devices: 22.8 us -> 21.8 us  [send(): return lax.ppermute(block, 'seq', [(s, s ^ flip) for s in range(sequence)])]
    ppermute x3, starting transfers between devices: 5.64 us -> 6.44 us  [body(): result = result + lax.ppermute(part, 'dp', list(enumerate(targets)))]
  transfers between devices with their start and end apart: 17 -> 17, of which waited for: 10 -> 9; matrix products, arithmetic and copies ran while one was open for 0% -> 0% of each run, Pallas kernels for 21% -> 21%
where the time goes in v12:
time: 60 us; the launch traced here: 59.7 us
  waiting for transfers between devices  23.9 us (40%)
  starting transfers between devices  18.3 us (30%)
  Pallas kernels  14.7 us (24%)
  local copies, waits for them, and re-layouts  2.08 us (3%)
  other arithmetic  0.6 us (1%)
    ppermute x14, waiting for transfers between devices, send(): return lax.ppermute(block, 'seq', [(s, s ^ flip) for s in range(sequence)])  21.8 us
    ppermute x14, starting transfers between devices, send(): return lax.ppermute(block, 'seq', [(s, s ^ flip) for s in range(sequence)])  11.9 us
    pallas_call x3, Pallas kernels, pack(): pl.pallas_call(functools.partial(pack_kernel, plan, heads, len(after)), o...  7.37 us
    ppermute x3, starting transfers between devices, body(): result = result + lax.ppermute(part, 'dp', list(enumerate(targets)))  6.44 us
    pallas_call x3, Pallas kernels, attend(): pl.pallas_call(kernel, out_shape=shapes, in_specs=[pl.BlockSpec(memory_sp...  5.19 us
    unnamed x10, local copies, waits for them, and re-layouts  2.08 us
    ppermute x3, waiting for transfers between devices, body(): result = result + lax.ppermute(part, 'dp', list(enumerate(targets)))  2.07 us
  transfers between devices with their start and end apart: 17, of which 9 were waited for; matrix products, arithmetic and copies ran while one was open for 0% of the time, Pallas kernels for 21%

profile of v12, /device:TPU:0, one launch (start us, length us, event | category | flops | bytes accessed | tf_op | source)
XLA Modules:
  0.0 59.7 jit_solution(5960602690354361619)
XLA Ops:
  0.0 1.1 %cut.1 = (bf16[4,32,8,128]{3,2,1,0:T(8,128)(2,1)S(1)}, bf16[4,32,8,128]{3,2,1,0:T(8,128)(2,1)S(1)}, f32[8,128]{1,0:T(8,128)S(1)}) custom-call(bf16[1,4,32,32,128]{4,3,2,1,0:T(8,128)(2,1)} %refs_2_.5), custom_call_target="tpu_custom_call" | custom-call | tf_op jit(solution)/shard_map/cut/pallas_call | solution.py:53
  1.1 2.4 %collective-permute-start = (bf16[4,32,8,128]{3,2,1,0:T(8,128)(2,1)S(1)}, bf16[4,32,8,128]{3,2,1,0:T(8,128)(2,1)S(1)}, u32[]{:S(2)}, u32[]{:S(2)}) collective-permute-start(bf16[4,32,8,128]{3,2,1,0:T(8,128)(2,1)S(1)} %get-tuple-element.31), channel_id=1, source_target_pairs={{0,3},{1,2},{2,1},{3,0},{4,7},{5,6},{6,5},{7,4},{8,11},{9,10},{10,... | collective-permute-start | bytes 786440 | tf_op jit(solution)/shard_map/ppermute | solution.py:357
  3.5 0.6 %collective-permute-start.1 = (bf16[4,32,8,128]{3,2,1,0:T(8,128)(2,1)S(1)}, bf16[4,32,8,128]{3,2,1,0:T(8,128)(2,1)S(1)}, u32[]{:S(2)}, u32[]{:S(2)}) collective-permute-start(bf16[4,32,8,128]{3,2,1,0:T(8,128)(2,1)S(1)} %get-tuple-element.32), channel_id=1, source_target_pairs={{0,2},{1,3},{2,0},{3,1},{4,6},{5,7},{6,4},{7,5},{8,10},{9,11},{10,... | collective-permute-start | bytes 786440 | tf_op jit(solution)/shard_map/ppermute | solution.py:357
  4.1 1.5 %pack.3 = (bf16[4,3,128,128]{3,2,1,0:T(8,128)(2,1)S(1)}, bf16[4,3,128,128]{3,2,1,0:T(8,128)(2,1)S(1)}, f32[8,128]{1,0:T(8,128)S(1)}) custom-call(bf16[1,4,32,32,128]{4,3,2,1,0:T(8,128)(2,1)} %refs_0_.5, bf16[1,4,32,32,128]{4,3,2,1,0:T(8,128)(2,1)} %refs_1_.5, bf16[1,4,32,32,128]{4,3,2,1,0:T(8,128)(2,1)} %refs_2_.5, bf16[1,4,32,32,128]{4,3,2,1,0:T(8,128)(2,1)} %refs_3_.5, ...), custom_call_target="tpu_custom_call" | custom-call | flops 2097152 | bytes 4194304 | tf_op jit(solution)/shard_map/pack/pallas_call | solution.py:145
  5.7 1.5 %collective-permute-start.4 = (bf16[4,3,128,128]{3,2,1,0:T(8,128)(2,1)S(1)}, bf16[4,3,128,128]{3,2,1,0:T(8,128)(2,1)S(1)}, u32[]{:S(2)}, u32[]{:S(2)}) collective-permute-start(bf16[4,3,128,128]{3,2,1,0:T(8,128)(2,1)S(1)} %get-tuple-element.39), channel_id=1, source_target_pairs={{0,3},{1,2},{2,1},{3,0},{4,7},{5,6},{6,5},{7,4},{8,11},{9,10},{10,... | collective-permute-start | bytes 1179656 | tf_op jit(solution)/shard_map/ppermute | solution.py:357
  7.2 0.2 collective-permute-start.5
  7.4 2.8 %collective-permute-done.refs_0_ = bf16[4,32,8,128]{3,2,1,0:T(8,128)(2,1)S(1)} collective-permute-done((bf16[4,32,8,128]{3,2,1,0:T(8,128)(2,1)S(1)}, bf16[4,32,8,128]{3,2,1,0:T(8,128)(2,1)S(1)}, u32[]{:S(2)}, u32[]{:S(2)}) %collective-permute-start) | collective-permute-done | bytes 262176 | tf_op jit(solution)/shard_map/ppermute | solution.py:357
  10.2 6.6 %collective-permute-done.1.refs_1_ = bf16[4,32,8,128]{3,2,1,0:T(8,128)(2,1)S(1)} collective-permute-done((bf16[4,32,8,128]{3,2,1,0:T(8,128)(2,1)S(1)}, bf16[4,32,8,128]{3,2,1,0:T(8,128)(2,1)S(1)}, u32[]{:S(2)}, u32[]{:S(2)}) %collective-permute-start.1) | collective-permute-done | bytes 262176 | tf_op jit(solution)/shard_map/ppermute | solution.py:357
  16.8 3.8 %pack.4 = (bf16[3,3,128,128]{3,2,1,0:T(8,128)(2,1)}, bf16[3,3,128,128]{3,2,1,0:T(8,128)(2,1)}, bf16[4,2,128,128]{3,2,1,0:T(8,128)(2,1)}, bf16[3,2,128,128]{3,2,1...) custom-call(bf16[1,4,32,32,128]{4,3,2,1,0:T(8,128)(2,1)} %refs_0_.5,, ...), custom_call_target="tpu_custom_call" | custom-call | flops 6291456 | bytes 12582912 | tf_op jit(solution)/shard_map/pack/pallas_call | solution.py:145
  20.6 0.1 collective-permute-start.6
  20.7 0.5 collective-permute-start.7
  21.2 0.1 collective-permute-start.2
  21.3 1.4 %collective-permute-done.2.refs_0_ = bf16[1,2,128,128]{3,2,1,0:T(8,128)(2,1)S(1)} collective-permute-done((bf16[1,2,128,128]{3,2,1,0:T(8,128)(2,1)S(1)}, bf16[1,2,128,128]{3,2,1,0:T(8,128)(2,1)S(1)}, u32[]{:S(2)}, u32[]{:S(2)}) %collective-permute-start.2) | collective-permute-done | bytes 65568 | tf_op jit(solution)/shard_map/ppermute | solution.py:357
  22.7 1.2 %collective-permute-start.12 = (bf16[3,3,128,128]{3,2,1,0:T(8,128)(2,1)}, bf16[3,3,128,128]{3,2,1,0:T(8,128)(2,1)S(1)}, u32[]{:S(2)}, u32[]{:S(2)}) collective-permute-start(bf16[3,3,128,128]{3,2,1,0:T(8,128)(2,1)} %get-tuple-element.51), channel_id=1, source_target_pairs={{0,3},{1,2},{2,1},{3,0},{4,7},{5,6},{6,5},{7,4},{8,11},{9,10},{10,... | collective-permute-start | bytes 884744 | tf_op jit(solution)/shard_map/ppermute | solution.py:357
  23.9 0.4 collective-permute-done.4.refs_0_
  24.2 2.5 %collective-permute-start.13 = (bf16[3,3,128,128]{3,2,1,0:T(8,128)(2,1)}, bf16[3,3,128,128]{3,2,1,0:T(8,128)(2,1)S(1)}, u32[]{:S(2)}, u32[]{:S(2)}) collective-permute-start(bf16[3,3,128,128]{3,2,1,0:T(8,128)(2,1)} %get-tuple-element.52), channel_id=1, source_target_pairs={{0,2},{1,3},{2,0},{3,1},{4,6},{5,7},{6,4},{7,5},{8,10},{9,11},{10,... | collective-permute-start | bytes 884744 | tf_op jit(solution)/shard_map/ppermute | solution.py:357
  26.7 7.0 %collective-permute-done.5.refs_1_ = bf16[4,3,128,128]{3,2,1,0:T(8,128)(2,1)S(1)} collective-permute-done((bf16[4,3,128,128]{3,2,1,0:T(8,128)(2,1)S(1)}, bf16[4,3,128,128]{3,2,1,0:T(8,128)(2,1)S(1)}, u32[]{:S(2)}, u32[]{:S(2)}) %collective-permute-start.5) | collective-permute-done | bytes 393248 | tf_op jit(solution)/shard_map/ppermute | solution.py:357
  33.7 0.0 collective-permute-start.10
  33.7 0.0 collective-permute-done.6.refs_1_
  33.7 0.5 collective-permute-start.11
  34.2 0.0 collective-permute-done.7.refs_2_
  34.2 0.1 collective-permute-start.3
  34.3 0.2 arrange.1.values
  34.5 0.0 copy-start
  34.5 0.7 %copy-done = f32[2,8,128]{2,1,0:T(8,128)S(1)} copy-done((f32[2,8,128]{2,1,0:T(8,128)S(1)}, f32[2,8,128]{2,1,0:T(8,128)}, u32[]{:S(2)}) %copy-start) | copy-done | bytes 8216
  35.2 0.3 copy-done.1
  35.5 0.1 copy-done.2
  35.5 0.4 prepare.4.close
  35.9 0.3 copy-done.4
  36.2 2.5 %attend.3.refs_4_.refs_2_ = f32[4,128]{1,0:T(4,128)S(1)} custom-call(s32[4,4]{1,0:T(4,128)S(1)} %copy-done.4, f32[2,8,128]{2,1,0:T(8,128)S(1)} %copy-done, bf16[8,4,64,128]{3,2,1,0:T(8,128)(2,1)S(1)} %arrange.1.values, bf16[4,4,4,64,128]{4,3,2,1,0:T(8,128)(2,1)S(1)} %prepare.4.close, bf16[4,3,128,128]{3,2,1,0:T(8,128)(2,1)S(1)} %collective-permute-done.4.refs_0_, ...), custom_call_target="tpu_custom_call" | custom-call | flops 402653184 | bytes 1048576 | tf_op jit(solution)/shard_map/attend/pallas_call | solution.py:314
  38.7 2.1 %pack.5 = (bf16[1,3,128,128]{3,2,1,0:T(8,128)(2,1)S(1)}, bf16[1,3,128,128]{3,2,1,0:T(8,128)(2,1)S(1)}, f32[8,128]{1,0:T(8,128)}) custom-call(bf16[1,4,32,32,128]{4,3,2,1,0:T(8,128)(2,1)} %refs_0_.5, bf16[1,4,32,32,128]{4,3,2,1,0:T(8,128)(2,1)} %refs_1_.5, bf16[1,4,32,32,128]{4,3,2,1,0:T(8,128)(2,1)} %refs_2_.5, bf16[1,4,32,32,128]{4,3,2,1,0:T(8,128)(2,1)} %refs_3_.5, ...), custom_call_target="tpu_custom_call" | custom-call | flops 2097152 | bytes 4194304 | tf_op jit(solution)/shard_map/pack/pallas_call | solution.py:145
  40.8 0.0 collective-permute-done.3.refs_1_
  40.8 1.6 %collective-permute-start.8 = (bf16[1,3,128,128]{3,2,1,0:T(8,128)(2,1)S(1)}, bf16[1,3,128,128]{3,2,1,0:T(8,128)(2,1)S(1)}, u32[]{:S(2)}, u32[]{:S(2)}) collective-permute-start(bf16[1,3,128,128]{3,2,1,0:T(8,128)(2,1)S(1)} %get-tuple-element.45), channel_id=1, source_target_pairs={{0,3},{1,2},{2,1},{3,0},{4,7},{5,6},{6,5},{7,4},{8,11},{9,10},{10,... | collective-permute-start | bytes 294920 | tf_op jit(solution)/shard_map/ppermute | solution.py:357
  42.4 0.5 collective-permute-start.9
  42.9 0.2 prepare.3.close
  43.1 0.8 %copy-done.3 = bf16[3,2,128,128]{3,2,1,0:T(8,128)(2,1)S(1)} copy-done((bf16[3,2,128,128]{3,2,1,0:T(8,128)(2,1)S(1)}, bf16[3,2,128,128]{3,2,1,0:T(8,128)(2,1)}, u32[]{:S(2)}) %copy-start.3) | copy-done | bytes 196632
  43.9 0.3 prepare.5.close
  44.2 0.0 collective-permute-done.12.refs_0_
  44.2 2.1 %collective-permute-done.13.refs_1_ = bf16[3,3,128,128]{3,2,1,0:T(8,128)(2,1)S(1)} collective-permute-done((bf16[3,3,128,128]{3,2,1,0:T(8,128)(2,1)}, bf16[3,3,128,128]{3,2,1,0:T(8,128)(2,1)S(1)}, u32[]{:S(2)}, u32[]{:S(2)}) %collective-permute-start.13) | collective-permute-done | bytes 294944 | tf_op jit(solution)/shard_map/ppermute | solution.py:357
  46.3 1.8 %attend.4.refs_3_ = f32[3,128]{1,0:T(4,128)S(1)} custom-call(s32[4,4]{1,0:T(4,128)S(1)} %copy-done.4, f32[2,8,128]{2,1,0:T(8,128)S(1)} %copy-done, bf16[8,4,64,128]{3,2,1,0:T(8,128)(2,1)S(1)} %arrange.1.values, bf16[3,4,4,64,128]{4,3,2,1,0:T(8,128)(2,1)S(1)} %prepare.5.close, bf16[3,3,128,128]{3,2,1,0:T(8,128)(2,1)S(1)} %collective-permute-done.12.refs_0_, ...), custom_call_target="tpu_custom_call" | custom-call | flops 301989888 | bytes 786432 | tf_op jit(solution)/shard_map/attend/pallas_call | solution.py:314
  48.1 1.6 %collective-permute-done.9.refs_1_ = bf16[1,3,128,128]{3,2,1,0:T(8,128)(2,1)S(1)} collective-permute-done((bf16[1,3,128,128]{3,2,1,0:T(8,128)(2,1)S(1)}, bf16[1,3,128,128]{3,2,1,0:T(8,128)(2,1)S(1)}, u32[]{:S(2)}, u32[]{:S(2)}) %collective-permute-start.9) | collective-permute-done | bytes 98336 | tf_op jit(solution)/shard_map/ppermute | solution.py:357
  49.7 0.9 %attend.5 = (f32[2,8,32]{2,1,0:T(8,128)S(1)}, f32[2,8,32]{2,1,0:T(8,128)S(1)}, f32[2,8,32]{2,1,0:T(8,128)S(1)}, f32[2,8,32]{2,1,0:T(8,128)S(1)}) custom-call(s32[4,4]{1,0:T(4,128)S(1)} %copy-done.4, f32[2,8,128]{2,1,0:T(8,128)S(1)} %copy-done, bf16[8,4,64,128]{3,2,1,0:T(8,128)(2,1)S(1)} %arrange.1.values, bf16[1,4,4,64,128]{4,3,2,1,0:T(8,128)(2,1)S(1)} %prepare.3.close, ...), custom_call_target="tpu_custom_call" | custom-call | flops 100663296 | bytes 262144 | tf_op jit(solution)/shard_map/attend/pallas_call | solution.py:314
  50.6 2.3 %collective-permute-start.14 = (f32[2,8,32]{2,1,0:T(8,128)S(1)}, f32[2,8,32]{2,1,0:T(8,128)S(1)}, u32[]{:S(2)}, u32[]{:S(2)}) collective-permute-start(f32[2,8,32]{2,1,0:T(8,128)S(1)} %get-tuple-element.54), channel_id=1, source_target_pairs={{0,4},{4,12},{8,0},{12,8},{1,5},{5,13},{9,1},{13,9},{2,6},{6,14},{... | collective-permute-start | bytes 6152 | tf_op jit(solution)/shard_map/ppermute | solution.py:394
  52.9 2.5 %collective-permute-start.15 = (f32[2,8,32]{2,1,0:T(8,128)S(1)}, f32[2,8,32]{2,1,0:T(8,128)S(1)}, u32[]{:S(2)}, u32[]{:S(2)}) collective-permute-start(f32[2,8,32]{2,1,0:T(8,128)S(1)} %get-tuple-element.55), channel_id=1, source_target_pairs={{0,12},{4,8},{8,4},{12,0},{1,13},{5,9},{9,5},{13,1},{2,14},{6,10},... | collective-permute-start | bytes 6152 | tf_op jit(solution)/shard_map/ppermute | solution.py:394
  55.5 1.6 %collective-permute-start.16 = (f32[2,8,32]{2,1,0:T(8,128)S(1)}, f32[2,8,32]{2,1,0:T(8,128)S(1)}, u32[]{:S(2)}, u32[]{:S(2)}) collective-permute-start(f32[2,8,32]{2,1,0:T(8,128)S(1)} %get-tuple-element.56), channel_id=1, source_target_pairs={{0,8},{4,0},{8,12},{12,4},{1,9},{5,1},{9,13},{13,5},{2,10},{6,2},{... | collective-permute-start | bytes 6152 | tf_op jit(solution)/shard_map/ppermute | solution.py:394
  57.0 1.4 %collective-permute-done.15 = f32[2,8,32]{2,1,0:T(8,128)S(1)} collective-permute-done((f32[2,8,32]{2,1,0:T(8,128)S(1)}, f32[2,8,32]{2,1,0:T(8,128)S(1)}, u32[]{:S(2)}, u32[]{:S(2)}) %collective-permute-start.15) | collective-permute-done | bytes 2080 | tf_op jit(solution)/shard_map/ppermute | solution.py:394
  58.4 0.7 %collective-permute-done.16 = f32[2,8,32]{2,1,0:T(8,128)S(1)} collective-permute-done((f32[2,8,32]{2,1,0:T(8,128)S(1)}, f32[2,8,32]{2,1,0:T(8,128)S(1)}, u32[]{:S(2)}, u32[]{:S(2)}) %collective-permute-start.16) | collective-permute-done | bytes 2080 | tf_op jit(solution)/shard_map/ppermute | solution.py:394
  59.1 0.6 %add_add_fusion = f32[2,8,32]{2,1,0:T(8,128)} fusion(f32[2,8,32]{2,1,0:T(8,128)S(1)} %collective-permute-done.16, f32[2,8,32]{2,1,0:T(8,128)S(1)} %collective-permute-done.15, f32[2,8,32]{2,1,0:T(8,128)S(1)} %get-tuple-element.53, f32[2,8,32]{2,1,0:T(8,128)S(1)} %collective-permute-done.14), kind=kLoop, calls=%fused_computation | loop fusion | flops 1536 | bytes 10240 | tf_op jit(solution)/shard_map/add | solution.py:394
  (10 shorter events, 0.0 us)
Async XLA Ops:
  1.1 9.1 %collective-permute-start = (bf16[4,32,8,128]{3,2,1,0:T(8,128)(2,1)S(1)}, bf16[4,32,8,128]{3,2,1,0:T(8,128)(2,1)S(1)}, u32[]{:S(2)}, u32[]{:S(2)}) collective-permute-start(bf16[4,32,8,128]{3,2,1,0:T(8,128)(2,1)S(1)} %get-tuple-element.31), channel_id=1, source_target_pairs={{0,3},{1,2},{2,1},{3,0},{4,7},{5,6},{6,5},{7,4},{8,11},{9,10},{10,... | collective-permute-start | bytes 786440 | tf_op jit(solution)/shard_map/ppermute | solution.py:357
  3.5 13.3 %collective-permute-start.1 = (bf16[4,32,8,128]{3,2,1,0:T(8,128)(2,1)S(1)}, bf16[4,32,8,128]{3,2,1,0:T(8,128)(2,1)S(1)}, u32[]{:S(2)}, u32[]{:S(2)}) collective-permute-start(bf16[4,32,8,128]{3,2,1,0:T(8,128)(2,1)S(1)} %get-tuple-element.32), channel_id=1, source_target_pairs={{0,2},{1,3},{2,0},{3,1},{4,6},{5,7},{6,4},{7,5},{8,10},{9,11},{10,... | collective-permute-start | bytes 786440 | tf_op jit(solution)/shard_map/ppermute | solution.py:357
  5.7 18.6 %collective-permute-start.4 = (bf16[4,3,128,128]{3,2,1,0:T(8,128)(2,1)S(1)}, bf16[4,3,128,128]{3,2,1,0:T(8,128)(2,1)S(1)}, u32[]{:S(2)}, u32[]{:S(2)}) collective-permute-start(bf16[4,3,128,128]{3,2,1,0:T(8,128)(2,1)S(1)} %get-tuple-element.39), channel_id=1, source_target_pairs={{0,3},{1,2},{2,1},{3,0},{4,7},{5,6},{6,5},{7,4},{8,11},{9,10},{10,... | collective-permute-start | bytes 1179656 | tf_op jit(solution)/shard_map/ppermute | solution.py:357
  7.2 26.5 %collective-permute-start.5 = (bf16[4,3,128,128]{3,2,1,0:T(8,128)(2,1)S(1)}, bf16[4,3,128,128]{3,2,1,0:T(8,128)(2,1)S(1)}, u32[]{:S(2)}, u32[]{:S(2)}) collective-permute-start(bf16[4,3,128,128]{3,2,1,0:T(8,128)(2,1)S(1)} %get-tuple-element.40), channel_id=1, source_target_pairs={{0,2},{1,3},{2,0},{3,1},{4,6},{5,7},{6,4},{7,5},{8,10},{9,11},{10,... | collective-permute-start | bytes 1179656 | tf_op jit(solution)/shard_map/ppermute | solution.py:357
  20.6 13.1 %collective-permute-start.6 = (bf16[4,2,128,128]{3,2,1,0:T(8,128)(2,1)}, bf16[4,2,128,128]{3,2,1,0:T(8,128)(2,1)S(1)}, u32[]{:S(2)}, u32[]{:S(2)}) collective-permute-start(bf16[4,2,128,128]{3,2,1,0:T(8,128)(2,1)} %get-tuple-element.41), channel_id=1, source_target_pairs={{0,1},{1,0},{2,3},{3,2},{4,5},{5,4},{6,7},{7,6},{8,9},{9,8},{10,11... | collective-permute-start | bytes 786440 | tf_op jit(solution)/shard_map/ppermute | solution.py:357
  20.7 13.5 %collective-permute-start.7 = (bf16[4,2,128,128]{3,2,1,0:T(8,128)(2,1)}, bf16[4,2,128,128]{3,2,1,0:T(8,128)(2,1)S(1)}, u32[]{:S(2)}, u32[]{:S(2)}) collective-permute-start(bf16[4,2,128,128]{3,2,1,0:T(8,128)(2,1)} %get-tuple-element.42), channel_id=1, source_target_pairs={{0,1},{1,0},{2,3},{3,2},{4,5},{5,4},{6,7},{7,6},{8,9},{9,8},{10,11... | collective-permute-start | bytes 786440 | tf_op jit(solution)/shard_map/ppermute | solution.py:357
  21.2 1.5 %collective-permute-start.2 = (bf16[1,2,128,128]{3,2,1,0:T(8,128)(2,1)S(1)}, bf16[1,2,128,128]{3,2,1,0:T(8,128)(2,1)S(1)}, u32[]{:S(2)}, u32[]{:S(2)}) collective-permute-start(bf16[1,2,128,128]{3,2,1,0:T(8,128)(2,1)S(1)} %get-tuple-element.35), channel_id=1, source_target_pairs={{0,1},{1,0},{2,3},{3,2},{4,5},{5,4},{6,7},{7,6},{8,9},{9,8},{10,11... | collective-permute-start | bytes 196616 | tf_op jit(solution)/shard_map/ppermute | solution.py:357
  22.7 21.5 %collective-permute-start.12 = (bf16[3,3,128,128]{3,2,1,0:T(8,128)(2,1)}, bf16[3,3,128,128]{3,2,1,0:T(8,128)(2,1)S(1)}, u32[]{:S(2)}, u32[]{:S(2)}) collective-permute-start(bf16[3,3,128,128]{3,2,1,0:T(8,128)(2,1)} %get-tuple-element.51), channel_id=1, source_target_pairs={{0,3},{1,2},{2,1},{3,0},{4,7},{5,6},{6,5},{7,4},{8,11},{9,10},{10,... | collective-permute-start | bytes 884744 | tf_op jit(solution)/shard_map/ppermute | solution.py:357
  24.2 22.1 %collective-permute-start.13 = (bf16[3,3,128,128]{3,2,1,0:T(8,128)(2,1)}, bf16[3,3,128,128]{3,2,1,0:T(8,128)(2,1)S(1)}, u32[]{:S(2)}, u32[]{:S(2)}) collective-permute-start(bf16[3,3,128,128]{3,2,1,0:T(8,128)(2,1)} %get-tuple-element.52), channel_id=1, source_target_pairs={{0,2},{1,3},{2,0},{3,1},{4,6},{5,7},{6,4},{7,5},{8,10},{9,11},{10,... | collective-permute-start | bytes 884744 | tf_op jit(solution)/shard_map/ppermute | solution.py:357
  33.7 8.7 %collective-permute-start.10 = (bf16[3,2,128,128]{3,2,1,0:T(8,128)(2,1)S(1)}, bf16[3,2,128,128]{3,2,1,0:T(8,128)(2,1)S(1)}, u32[]{:S(2)}, u32[]{:S(2)}) collective-permute-start(bf16[3,2,128,128]{3,2,1,0:T(8,128)(2,1)S(1)} %get-tuple-element.47), channel_id=1, source_target_pairs={{0,1},{1,0},{2,3},{3,2},{4,5},{5,4},{6,7},{7,6},{8,9},{9,8},{10,11... | collective-permute-start | bytes 589832 | tf_op jit(solution)/shard_map/ppermute | solution.py:357
  33.7 9.4 %collective-permute-start.11 = (bf16[3,2,128,128]{3,2,1,0:T(8,128)(2,1)S(1)}, bf16[3,2,128,128]{3,2,1,0:T(8,128)(2,1)S(1)}, u32[]{:S(2)}, u32[]{:S(2)}) collective-permute-start(bf16[3,2,128,128]{3,2,1,0:T(8,128)(2,1)S(1)} %get-tuple-element.48), channel_id=1, source_target_pairs={{0,1},{1,0},{2,3},{3,2},{4,5},{5,4},{6,7},{7,6},{8,9},{9,8},{10,11... | collective-permute-start | bytes 589832 | tf_op jit(solution)/shard_map/ppermute | solution.py:357
  34.2 6.6 %collective-permute-start.3 = (bf16[1,2,128,128]{3,2,1,0:T(8,128)(2,1)S(1)}, bf16[1,2,128,128]{3,2,1,0:T(8,128)(2,1)S(1)}, u32[]{:S(2)}, u32[]{:S(2)}) collective-permute-start(bf16[1,2,128,128]{3,2,1,0:T(8,128)(2,1)S(1)} %get-tuple-element.36), channel_id=1, source_target_pairs={{0,1},{1,0},{2,3},{3,2},{4,5},{5,4},{6,7},{7,6},{8,9},{9,8},{10,11... | collective-permute-start | bytes 196616 | tf_op jit(solution)/shard_map/ppermute | solution.py:357
  34.5 0.7 %copy-start = (f32[2,8,128]{2,1,0:T(8,128)S(1)}, f32[2,8,128]{2,1,0:T(8,128)}, u32[]{:S(2)}) copy-start(f32[2,8,128]{2,1,0:T(8,128)} %gains.11) | copy-start | bytes 24580
  34.5 1.0 %copy-start.1 = (bf16[4,2,128,128]{3,2,1,0:T(8,128)(2,1)S(1)}, bf16[4,2,128,128]{3,2,1,0:T(8,128)(2,1)}, u32[]{:S(2)}) copy-start(bf16[4,2,128,128]{3,2,1,0:T(8,128)(2,1)} %get-tuple-element.43.refs_3_) | copy-start | bytes 786436
  34.5 1.0 %copy-start.2 = (bf16[4,2,128,128]{3,2,1,0:T(8,128)(2,1)S(1)}, bf16[4,2,128,128]{3,2,1,0:T(8,128)(2,1)}, u32[]{:S(2)}) copy-start(bf16[4,2,128,128]{3,2,1,0:T(8,128)(2,1)} %get-tuple-element.44.refs_4_) | copy-start | bytes 786436
  35.5 0.7 %copy-start.4 = (s32[4,4]{1,0:T(4,128)S(1)}, s32[4,4]{1,0:T(4,128)}, u32[]{:S(2)}) copy-start(s32[4,4]{1,0:T(4,128)} %units.5) | copy-start | bytes 196
  40.8 7.3 %collective-permute-start.8 = (bf16[1,3,128,128]{3,2,1,0:T(8,128)(2,1)S(1)}, bf16[1,3,128,128]{3,2,1,0:T(8,128)(2,1)S(1)}, u32[]{:S(2)}, u32[]{:S(2)}) collective-permute-start(bf16[1,3,128,128]{3,2,1,0:T(8,128)(2,1)S(1)} %get-tuple-element.45), channel_id=1, source_target_pairs={{0,3},{1,2},{2,1},{3,0},{4,7},{5,6},{6,5},{7,4},{8,11},{9,10},{10,... | collective-permute-start | bytes 294920 | tf_op jit(solution)/shard_map/ppermute | solution.py:357
  42.4 7.3 %collective-permute-start.9 = (bf16[1,3,128,128]{3,2,1,0:T(8,128)(2,1)S(1)}, bf16[1,3,128,128]{3,2,1,0:T(8,128)(2,1)S(1)}, u32[]{:S(2)}, u32[]{:S(2)}) collective-permute-start(bf16[1,3,128,128]{3,2,1,0:T(8,128)(2,1)S(1)} %get-tuple-element.46), channel_id=1, source_target_pairs={{0,2},{1,3},{2,0},{3,1},{4,6},{5,7},{6,4},{7,5},{8,10},{9,11},{10,... | collective-permute-start | bytes 294920 | tf_op jit(solution)/shard_map/ppermute | solution.py:357
  42.9 0.9 %copy-start.3 = (bf16[3,2,128,128]{3,2,1,0:T(8,128)(2,1)S(1)}, bf16[3,2,128,128]{3,2,1,0:T(8,128)(2,1)}, u32[]{:S(2)}) copy-start(bf16[3,2,128,128]{3,2,1,0:T(8,128)(2,1)} %get-tuple-element.50.refs_3_) | copy-start | bytes 589828
  50.6 6.4 %collective-permute-start.14 = (f32[2,8,32]{2,1,0:T(8,128)S(1)}, f32[2,8,32]{2,1,0:T(8,128)S(1)}, u32[]{:S(2)}, u32[]{:S(2)}) collective-permute-start(f32[2,8,32]{2,1,0:T(8,128)S(1)} %get-tuple-element.54), channel_id=1, source_target_pairs={{0,4},{4,12},{8,0},{12,8},{1,5},{5,13},{9,1},{13,9},{2,6},{6,14},{... | collective-permute-start | bytes 6152 | tf_op jit(solution)/shard_map/ppermute | solution.py:394
  52.9 5.5 %collective-permute-start.15 = (f32[2,8,32]{2,1,0:T(8,128)S(1)}, f32[2,8,32]{2,1,0:T(8,128)S(1)}, u32[]{:S(2)}, u32[]{:S(2)}) collective-permute-start(f32[2,8,32]{2,1,0:T(8,128)S(1)} %get-tuple-element.55), channel_id=1, source_target_pairs={{0,12},{4,8},{8,4},{12,0},{1,13},{5,9},{9,5},{13,1},{2,14},{6,10},... | collective-permute-start | bytes 6152 | tf_op jit(solution)/shard_map/ppermute | solution.py:394
  55.5 3.7 %collective-permute-start.16 = (f32[2,8,32]{2,1,0:T(8,128)S(1)}, f32[2,8,32]{2,1,0:T(8,128)S(1)}, u32[]{:S(2)}, u32[]{:S(2)}) collective-permute-start(f32[2,8,32]{2,1,0:T(8,128)S(1)} %get-tuple-element.56), channel_id=1, source_target_pairs={{0,8},{4,0},{8,12},{12,4},{1,9},{5,1},{9,13},{13,5},{2,10},{6,2},{... | collective-permute-start | bytes 6152 | tf_op jit(solution)/shard_map/ppermute | solution.py:394

commit v13 on v11

--- a/solution.py
+++ b/solution.py
@@ -66,7 +66,7 @@
     heads, slots = out.shape[:2]
     rows, held = pieces[0].shape[1:3]
     _, offset = tile_start(heads, 0)
-    for source, piece in enumerate(pieces):
+    for source, piece in enumerate(pieces[::-1]):
         for slot in range(slots):
             for span in range(held // TILE):
                 place = (source * slots + slot) % wide.shape[0]
@@ -368,8 +368,8 @@
     def far_plan(number):
         return [(flip, OTHERS, chunks[number : number + 1]) for flip in far]
 
-    *tiles, token = cut(arrays[VALUES], far, heads)
-    tiles = [send(block, flip) for flip, block in zip(far, tiles)]
+    *tiles, token = cut(arrays[VALUES], far[::-1], heads)
+    tiles = [send(block, flip) for flip, block in zip(far[::-1], tiles)]
     received, token = pack_and_send(far_plan(0), [token])
     later = far_plan(1) if len(chunks) > 1 else []
     whole = [(flip, pair, chunks) for flip in close for pair in ((0, 1), (2, 3))]

time: 58.3 us -> 59.9 us (1.027)
  starting transfers between devices: 16.2 us -> 17.7 us
    ppermute x3, starting transfers between devices: 5.64 us -> 6.56 us  [body(): result = result + lax.ppermute(part, 'dp', list(enumerate(targets)))]
    ppermute x14, starting transfers between devices: 10.5 us -> 11.1 us  [send(): return lax.ppermute(block, 'seq', [(s, s ^ flip) for s in range(sequence)])]
where the time goes in v13:
time: 59.9 us; the launch traced here: 59.7 us
  waiting for transfers between devices  24.5 us (41%)
  starting transfers between devices  17.7 us (30%)
  Pallas kernels  14.7 us (25%)
  local copies, waits for them, and re-layouts  2.08 us (3%)
  other arithmetic  0.6 us (1%)
    ppermute x14, waiting for transfers between devices, send(): return lax.ppermute(block, 'seq', [(s, s ^ flip) for s in range(sequence)])  22.4 us
    ppermute x14, starting transfers between devices, send(): return lax.ppermute(block, 'seq', [(s, s ^ flip) for s in range(sequence)])  11.1 us
    pallas_call x3, Pallas kernels, pack(): pl.pallas_call(functools.partial(pack_kernel, plan, heads, len(after)), o...  7.37 us
    ppermute x3, starting transfers between devices, body(): result = result + lax.ppermute(part, 'dp', list(enumerate(targets)))  6.56 us
    pallas_call x3, Pallas kernels, attend(): pl.pallas_call(kernel, out_shape=shapes, in_specs=[pl.BlockSpec(memory_sp...  5.19 us
    ppermute x3, waiting for transfers between devices, body(): result = result + lax.ppermute(part, 'dp', list(enumerate(targets)))  2.08 us
    unnamed x10, local copies, waits for them, and re-layouts  2.08 us
  transfers between devices with their start and end apart: 17, of which 10 were waited for; matrix products, arithmetic and copies ran while one was open for 0% of the time, Pallas kernels for 21%

profile of v13, /device:TPU:0, one launch (start us, length us, event | category | flops | bytes accessed | tf_op | source)
XLA Modules:
  0.0 59.7 jit_solution(4884511144819636156)
XLA Ops:
  0.0 1.1 %cut.1 = (bf16[4,32,8,128]{3,2,1,0:T(8,128)(2,1)S(1)}, bf16[4,32,8,128]{3,2,1,0:T(8,128)(2,1)S(1)}, f32[8,128]{1,0:T(8,128)S(1)}) custom-call(bf16[1,4,32,32,128]{4,3,2,1,0:T(8,128)(2,1)} %refs_2_.5), custom_call_target="tpu_custom_call" | custom-call | tf_op jit(solution)/shard_map/cut/pallas_call | solution.py:53
  1.1 2.4 %collective-permute-start = (bf16[4,32,8,128]{3,2,1,0:T(8,128)(2,1)S(1)}, bf16[4,32,8,128]{3,2,1,0:T(8,128)(2,1)S(1)}, u32[]{:S(2)}, u32[]{:S(2)}) collective-permute-start(bf16[4,32,8,128]{3,2,1,0:T(8,128)(2,1)S(1)} %get-tuple-element.31), channel_id=1, source_target_pairs={{0,3},{1,2},{2,1},{3,0},{4,7},{5,6},{6,5},{7,4},{8,11},{9,10},{10,... | collective-permute-start | bytes 786440 | tf_op jit(solution)/shard_map/ppermute | solution.py:357
  3.5 0.6 %collective-permute-start.1 = (bf16[4,32,8,128]{3,2,1,0:T(8,128)(2,1)S(1)}, bf16[4,32,8,128]{3,2,1,0:T(8,128)(2,1)S(1)}, u32[]{:S(2)}, u32[]{:S(2)}) collective-permute-start(bf16[4,32,8,128]{3,2,1,0:T(8,128)(2,1)S(1)} %get-tuple-element.32), channel_id=1, source_target_pairs={{0,2},{1,3},{2,0},{3,1},{4,6},{5,7},{6,4},{7,5},{8,10},{9,11},{10,... | collective-permute-start | bytes 786440 | tf_op jit(solution)/shard_map/ppermute | solution.py:357
  4.1 1.5 %pack.3 = (bf16[4,3,128,128]{3,2,1,0:T(8,128)(2,1)S(1)}, bf16[4,3,128,128]{3,2,1,0:T(8,128)(2,1)S(1)}, f32[8,128]{1,0:T(8,128)S(1)}) custom-call(bf16[1,4,32,32,128]{4,3,2,1,0:T(8,128)(2,1)} %refs_0_.5, bf16[1,4,32,32,128]{4,3,2,1,0:T(8,128)(2,1)} %refs_1_.5, bf16[1,4,32,32,128]{4,3,2,1,0:T(8,128)(2,1)} %refs_2_.5, bf16[1,4,32,32,128]{4,3,2,1,0:T(8,128)(2,1)} %refs_3_.5, ...), custom_call_target="tpu_custom_call" | custom-call | flops 2097152 | bytes 4194304 | tf_op jit(solution)/shard_map/pack/pallas_call | solution.py:145
  5.7 1.5 %collective-permute-start.4 = (bf16[4,3,128,128]{3,2,1,0:T(8,128)(2,1)S(1)}, bf16[4,3,128,128]{3,2,1,0:T(8,128)(2,1)S(1)}, u32[]{:S(2)}, u32[]{:S(2)}) collective-permute-start(bf16[4,3,128,128]{3,2,1,0:T(8,128)(2,1)S(1)} %get-tuple-element.39), channel_id=1, source_target_pairs={{0,2},{1,3},{2,0},{3,1},{4,6},{5,7},{6,4},{7,5},{8,10},{9,11},{10,... | collective-permute-start | bytes 1179656 | tf_op jit(solution)/shard_map/ppermute | solution.py:357
  7.1 0.1 collective-permute-start.5
  7.2 3.0 %collective-permute-done.refs_0_ = bf16[4,32,8,128]{3,2,1,0:T(8,128)(2,1)S(1)} collective-permute-done((bf16[4,32,8,128]{3,2,1,0:T(8,128)(2,1)S(1)}, bf16[4,32,8,128]{3,2,1,0:T(8,128)(2,1)S(1)}, u32[]{:S(2)}, u32[]{:S(2)}) %collective-permute-start) | collective-permute-done | bytes 262176 | tf_op jit(solution)/shard_map/ppermute | solution.py:357
  10.2 6.6 %collective-permute-done.1.refs_1_ = bf16[4,32,8,128]{3,2,1,0:T(8,128)(2,1)S(1)} collective-permute-done((bf16[4,32,8,128]{3,2,1,0:T(8,128)(2,1)S(1)}, bf16[4,32,8,128]{3,2,1,0:T(8,128)(2,1)S(1)}, u32[]{:S(2)}, u32[]{:S(2)}) %collective-permute-start.1) | collective-permute-done | bytes 262176 | tf_op jit(solution)/shard_map/ppermute | solution.py:357
  16.8 3.8 %pack.4 = (bf16[3,3,128,128]{3,2,1,0:T(8,128)(2,1)}, bf16[3,3,128,128]{3,2,1,0:T(8,128)(2,1)}, bf16[4,2,128,128]{3,2,1,0:T(8,128)(2,1)}, bf16[3,2,128,128]{3,2,1...) custom-call(bf16[1,4,32,32,128]{4,3,2,1,0:T(8,128)(2,1)} %refs_0_.5,, ...), custom_call_target="tpu_custom_call" | custom-call | flops 6291456 | bytes 12582912 | tf_op jit(solution)/shard_map/pack/pallas_call | solution.py:145
  20.6 0.1 collective-permute-start.6
  20.7 0.5 collective-permute-start.7
  21.2 0.1 collective-permute-start.2
  21.3 1.4 %collective-permute-done.2.refs_0_ = bf16[1,2,128,128]{3,2,1,0:T(8,128)(2,1)S(1)} collective-permute-done((bf16[1,2,128,128]{3,2,1,0:T(8,128)(2,1)S(1)}, bf16[1,2,128,128]{3,2,1,0:T(8,128)(2,1)S(1)}, u32[]{:S(2)}, u32[]{:S(2)}) %collective-permute-start.2) | collective-permute-done | bytes 65568 | tf_op jit(solution)/shard_map/ppermute | solution.py:357
  22.7 1.5 %collective-permute-start.12 = (bf16[3,3,128,128]{3,2,1,0:T(8,128)(2,1)}, bf16[3,3,128,128]{3,2,1,0:T(8,128)(2,1)S(1)}, u32[]{:S(2)}, u32[]{:S(2)}) collective-permute-start(bf16[3,3,128,128]{3,2,1,0:T(8,128)(2,1)} %get-tuple-element.51), channel_id=1, source_target_pairs={{0,2},{1,3},{2,0},{3,1},{4,6},{5,7},{6,4},{7,5},{8,10},{9,11},{10,... | collective-permute-start | bytes 884744 | tf_op jit(solution)/shard_map/ppermute | solution.py:357
  24.2 1.1 %collective-permute-done.4.refs_0_ = bf16[4,3,128,128]{3,2,1,0:T(8,128)(2,1)S(1)} collective-permute-done((bf16[4,3,128,128]{3,2,1,0:T(8,128)(2,1)S(1)}, bf16[4,3,128,128]{3,2,1,0:T(8,128)(2,1)S(1)}, u32[]{:S(2)}, u32[]{:S(2)}) %collective-permute-start.4) | collective-permute-done | bytes 393248 | tf_op jit(solution)/shard_map/ppermute | solution.py:357
  25.2 1.2 %collective-permute-start.13 = (bf16[3,3,128,128]{3,2,1,0:T(8,128)(2,1)}, bf16[3,3,128,128]{3,2,1,0:T(8,128)(2,1)S(1)}, u32[]{:S(2)}, u32[]{:S(2)}) collective-permute-start(bf16[3,3,128,128]{3,2,1,0:T(8,128)(2,1)} %get-tuple-element.52), channel_id=1, source_target_pairs={{0,3},{1,2},{2,1},{3,0},{4,7},{5,6},{6,5},{7,4},{8,11},{9,10},{10,... | collective-permute-start | bytes 884744 | tf_op jit(solution)/shard_map/ppermute | solution.py:357
  26.4 6.3 %collective-permute-done.5.refs_1_ = bf16[4,3,128,128]{3,2,1,0:T(8,128)(2,1)S(1)} collective-permute-done((bf16[4,3,128,128]{3,2,1,0:T(8,128)(2,1)S(1)}, bf16[4,3,128,128]{3,2,1,0:T(8,128)(2,1)S(1)}, u32[]{:S(2)}, u32[]{:S(2)}) %collective-permute-start.5) | collective-permute-done | bytes 393248 | tf_op jit(solution)/shard_map/ppermute | solution.py:357
  32.7 0.8 %collective-permute-start.10 = (bf16[3,2,128,128]{3,2,1,0:T(8,128)(2,1)S(1)}, bf16[3,2,128,128]{3,2,1,0:T(8,128)(2,1)S(1)}, u32[]{:S(2)}, u32[]{:S(2)}) collective-permute-start(bf16[3,2,128,128]{3,2,1,0:T(8,128)(2,1)S(1)} %get-tuple-element.47), channel_id=1, source_target_pairs={{0,1},{1,0},{2,3},{3,2},{4,5},{5,4},{6,7},{7,6},{8,9},{9,8},{10,11... | collective-permute-start | bytes 589832 | tf_op jit(solution)/shard_map/ppermute | solution.py:357
  33.5 0.0 collective-permute-start.11
  33.5 0.0 collective-permute-done.7.refs_2_
  33.5 0.5 collective-permute-start.3
  34.0 0.2 arrange.1.values
  34.2 0.0 copy-start
  34.3 0.7 %copy-done = f32[2,8,128]{2,1,0:T(8,128)S(1)} copy-done((f32[2,8,128]{2,1,0:T(8,128)S(1)}, f32[2,8,128]{2,1,0:T(8,128)}, u32[]{:S(2)}) %copy-start) | copy-done | bytes 8216
  34.9 0.3 copy-done.1
  35.2 0.1 copy-done.2
  35.3 0.4 prepare.4.close
  35.7 0.3 copy-done.4
  36.0 2.5 %attend.3.refs_4_.refs_2_ = f32[4,128]{1,0:T(4,128)S(1)} custom-call(s32[4,4]{1,0:T(4,128)S(1)} %copy-done.4, f32[2,8,128]{2,1,0:T(8,128)S(1)} %copy-done, bf16[8,4,64,128]{3,2,1,0:T(8,128)(2,1)S(1)} %arrange.1.values, bf16[4,4,4,64,128]{4,3,2,1,0:T(8,128)(2,1)S(1)} %prepare.4.close, bf16[4,3,128,128]{3,2,1,0:T(8,128)(2,1)S(1)} %collective-permute-done.4.refs_0_, ...), custom_call_target="tpu_custom_call" | custom-call | flops 402653184 | bytes 1048576 | tf_op jit(solution)/shard_map/attend/pallas_call | solution.py:314
  38.5 2.1 %pack.5 = (bf16[1,3,128,128]{3,2,1,0:T(8,128)(2,1)S(1)}, bf16[1,3,128,128]{3,2,1,0:T(8,128)(2,1)S(1)}, f32[8,128]{1,0:T(8,128)}) custom-call(bf16[1,4,32,32,128]{4,3,2,1,0:T(8,128)(2,1)} %refs_0_.5, bf16[1,4,32,32,128]{4,3,2,1,0:T(8,128)(2,1)} %refs_1_.5, bf16[1,4,32,32,128]{4,3,2,1,0:T(8,128)(2,1)} %refs_2_.5, bf16[1,4,32,32,128]{4,3,2,1,0:T(8,128)(2,1)} %refs_3_.5, ...), custom_call_target="tpu_custom_call" | custom-call | flops 2097152 | bytes 4194304 | tf_op jit(solution)/shard_map/pack/pallas_call | solution.py:145
  40.6 1.8 %collective-permute-start.8 = (bf16[1,3,128,128]{3,2,1,0:T(8,128)(2,1)S(1)}, bf16[1,3,128,128]{3,2,1,0:T(8,128)(2,1)S(1)}, u32[]{:S(2)}, u32[]{:S(2)}) collective-permute-start(bf16[1,3,128,128]{3,2,1,0:T(8,128)(2,1)S(1)} %get-tuple-element.45), channel_id=1, source_target_pairs={{0,2},{1,3},{2,0},{3,1},{4,6},{5,7},{6,4},{7,5},{8,10},{9,11},{10,... | collective-permute-start | bytes 294920 | tf_op jit(solution)/shard_map/ppermute | solution.py:357
  42.4 0.1 collective-permute-start.9
  42.5 0.2 prepare.3.close
  42.6 0.0 collective-permute-done.11.refs_1_
  42.6 0.8 %copy-done.3 = bf16[3,2,128,128]{3,2,1,0:T(8,128)(2,1)S(1)} copy-done((bf16[3,2,128,128]{3,2,1,0:T(8,128)(2,1)S(1)}, bf16[3,2,128,128]{3,2,1,0:T(8,128)(2,1)}, u32[]{:S(2)}) %copy-start.3) | copy-done | bytes 196632
  43.4 0.3 prepare.5.close
  43.7 0.0 collective-permute-done.12.refs_0_
  43.7 1.7 %collective-permute-done.13.refs_1_ = bf16[3,3,128,128]{3,2,1,0:T(8,128)(2,1)S(1)} collective-permute-done((bf16[3,3,128,128]{3,2,1,0:T(8,128)(2,1)}, bf16[3,3,128,128]{3,2,1,0:T(8,128)(2,1)S(1)}, u32[]{:S(2)}, u32[]{:S(2)}) %collective-permute-start.13) | collective-permute-done | bytes 294944 | tf_op jit(solution)/shard_map/ppermute | solution.py:357
  45.4 1.8 %attend.4.refs_3_ = f32[3,128]{1,0:T(4,128)S(1)} custom-call(s32[4,4]{1,0:T(4,128)S(1)} %copy-done.4, f32[2,8,128]{2,1,0:T(8,128)S(1)} %copy-done, bf16[8,4,64,128]{3,2,1,0:T(8,128)(2,1)S(1)} %arrange.1.values, bf16[3,4,4,64,128]{4,3,2,1,0:T(8,128)(2,1)S(1)} %prepare.5.close, bf16[3,3,128,128]{3,2,1,0:T(8,128)(2,1)S(1)} %collective-permute-done.12.refs_0_, ...), custom_call_target="tpu_custom_call" | custom-call | flops 301989888 | bytes 786432 | tf_op jit(solution)/shard_map/attend/pallas_call | solution.py:314
  47.2 1.2 %collective-permute-done.8.refs_0_ = bf16[1,3,128,128]{3,2,1,0:T(8,128)(2,1)S(1)} collective-permute-done((bf16[1,3,128,128]{3,2,1,0:T(8,128)(2,1)S(1)}, bf16[1,3,128,128]{3,2,1,0:T(8,128)(2,1)S(1)}, u32[]{:S(2)}, u32[]{:S(2)}) %collective-permute-start.8) | collective-permute-done | bytes 98336 | tf_op jit(solution)/shard_map/ppermute | solution.py:357
  48.4 1.1 %collective-permute-done.9.refs_1_ = bf16[1,3,128,128]{3,2,1,0:T(8,128)(2,1)S(1)} collective-permute-done((bf16[1,3,128,128]{3,2,1,0:T(8,128)(2,1)S(1)}, bf16[1,3,128,128]{3,2,1,0:T(8,128)(2,1)S(1)}, u32[]{:S(2)}, u32[]{:S(2)}) %collective-permute-start.9) | collective-permute-done | bytes 98336 | tf_op jit(solution)/shard_map/ppermute | solution.py:357
  49.5 0.9 %attend.5 = (f32[2,8,32]{2,1,0:T(8,128)S(1)}, f32[2,8,32]{2,1,0:T(8,128)S(1)}, f32[2,8,32]{2,1,0:T(8,128)S(1)}, f32[2,8,32]{2,1,0:T(8,128)S(1)}) custom-call(s32[4,4]{1,0:T(4,128)S(1)} %copy-done.4, f32[2,8,128]{2,1,0:T(8,128)S(1)} %copy-done, bf16[8,4,64,128]{3,2,1,0:T(8,128)(2,1)S(1)} %arrange.1.values, bf16[1,4,4,64,128]{4,3,2,1,0:T(8,128)(2,1)S(1)} %prepare.3.close, ...), custom_call_target="tpu_custom_call" | custom-call | flops 100663296 | bytes 262144 | tf_op jit(solution)/shard_map/attend/pallas_call | solution.py:314
  50.4 2.4 %collective-permute-start.14 = (f32[2,8,32]{2,1,0:T(8,128)S(1)}, f32[2,8,32]{2,1,0:T(8,128)S(1)}, u32[]{:S(2)}, u32[]{:S(2)}) collective-permute-start(f32[2,8,32]{2,1,0:T(8,128)S(1)} %get-tuple-element.54), channel_id=1, source_target_pairs={{0,4},{4,12},{8,0},{12,8},{1,5},{5,13},{9,1},{13,9},{2,6},{6,14},{... | collective-permute-start | bytes 6152 | tf_op jit(solution)/shard_map/ppermute | solution.py:394
  52.8 2.6 %collective-permute-start.15 = (f32[2,8,32]{2,1,0:T(8,128)S(1)}, f32[2,8,32]{2,1,0:T(8,128)S(1)}, u32[]{:S(2)}, u32[]{:S(2)}) collective-permute-start(f32[2,8,32]{2,1,0:T(8,128)S(1)} %get-tuple-element.55), channel_id=1, source_target_pairs={{0,12},{4,8},{8,4},{12,0},{1,13},{5,9},{9,5},{13,1},{2,14},{6,10},... | collective-permute-start | bytes 6152 | tf_op jit(solution)/shard_map/ppermute | solution.py:394
  55.4 1.6 %collective-permute-start.16 = (f32[2,8,32]{2,1,0:T(8,128)S(1)}, f32[2,8,32]{2,1,0:T(8,128)S(1)}, u32[]{:S(2)}, u32[]{:S(2)}) collective-permute-start(f32[2,8,32]{2,1,0:T(8,128)S(1)} %get-tuple-element.56), channel_id=1, source_target_pairs={{0,8},{4,0},{8,12},{12,4},{1,9},{5,1},{9,13},{13,5},{2,10},{6,2},{... | collective-permute-start | bytes 6152 | tf_op jit(solution)/shard_map/ppermute | solution.py:394
  57.0 1.3 %collective-permute-done.15 = f32[2,8,32]{2,1,0:T(8,128)S(1)} collective-permute-done((f32[2,8,32]{2,1,0:T(8,128)S(1)}, f32[2,8,32]{2,1,0:T(8,128)S(1)}, u32[]{:S(2)}, u32[]{:S(2)}) %collective-permute-start.15) | collective-permute-done | bytes 2080 | tf_op jit(solution)/shard_map/ppermute | solution.py:394
  58.3 0.8 %collective-permute-done.16 = f32[2,8,32]{2,1,0:T(8,128)S(1)} collective-permute-done((f32[2,8,32]{2,1,0:T(8,128)S(1)}, f32[2,8,32]{2,1,0:T(8,128)S(1)}, u32[]{:S(2)}, u32[]{:S(2)}) %collective-permute-start.16) | collective-permute-done | bytes 2080 | tf_op jit(solution)/shard_map/ppermute | solution.py:394
  59.1 0.6 %add_add_fusion = f32[2,8,32]{2,1,0:T(8,128)} fusion(f32[2,8,32]{2,1,0:T(8,128)S(1)} %collective-permute-done.16, f32[2,8,32]{2,1,0:T(8,128)S(1)} %collective-permute-done.15, f32[2,8,32]{2,1,0:T(8,128)S(1)} %get-tuple-element.53, f32[2,8,32]{2,1,0:T(8,128)S(1)} %collective-permute-done.14), kind=kLoop, calls=%fused_computation | loop fusion | flops 1536 | bytes 10240 | tf_op jit(solution)/shard_map/add | solution.py:394
  (10 shorter events, 0.0 us)
Async XLA Ops:
  1.1 9.1 %collective-permute-start = (bf16[4,32,8,128]{3,2,1,0:T(8,128)(2,1)S(1)}, bf16[4,32,8,128]{3,2,1,0:T(8,128)(2,1)S(1)}, u32[]{:S(2)}, u32[]{:S(2)}) collective-permute-start(bf16[4,32,8,128]{3,2,1,0:T(8,128)(2,1)S(1)} %get-tuple-element.31), channel_id=1, source_target_pairs={{0,3},{1,2},{2,1},{3,0},{4,7},{5,6},{6,5},{7,4},{8,11},{9,10},{10,... | collective-permute-start | bytes 786440 | tf_op jit(solution)/shard_map/ppermute | solution.py:357
  3.5 13.3 %collective-permute-start.1 = (bf16[4,32,8,128]{3,2,1,0:T(8,128)(2,1)S(1)}, bf16[4,32,8,128]{3,2,1,0:T(8,128)(2,1)S(1)}, u32[]{:S(2)}, u32[]{:S(2)}) collective-permute-start(bf16[4,32,8,128]{3,2,1,0:T(8,128)(2,1)S(1)} %get-tuple-element.32), channel_id=1, source_target_pairs={{0,2},{1,3},{2,0},{3,1},{4,6},{5,7},{6,4},{7,5},{8,10},{9,11},{10,... | collective-permute-start | bytes 786440 | tf_op jit(solution)/shard_map/ppermute | solution.py:357
  5.7 19.6 %collective-permute-start.4 = (bf16[4,3,128,128]{3,2,1,0:T(8,128)(2,1)S(1)}, bf16[4,3,128,128]{3,2,1,0:T(8,128)(2,1)S(1)}, u32[]{:S(2)}, u32[]{:S(2)}) collective-permute-start(bf16[4,3,128,128]{3,2,1,0:T(8,128)(2,1)S(1)} %get-tuple-element.39), channel_id=1, source_target_pairs={{0,2},{1,3},{2,0},{3,1},{4,6},{5,7},{6,4},{7,5},{8,10},{9,11},{10,... | collective-permute-start | bytes 1179656 | tf_op jit(solution)/shard_map/ppermute | solution.py:357
  7.1 25.5 %collective-permute-start.5 = (bf16[4,3,128,128]{3,2,1,0:T(8,128)(2,1)S(1)}, bf16[4,3,128,128]{3,2,1,0:T(8,128)(2,1)S(1)}, u32[]{:S(2)}, u32[]{:S(2)}) collective-permute-start(bf16[4,3,128,128]{3,2,1,0:T(8,128)(2,1)S(1)} %get-tuple-element.40), channel_id=1, source_target_pairs={{0,3},{1,2},{2,1},{3,0},{4,7},{5,6},{6,5},{7,4},{8,11},{9,10},{10,... | collective-permute-start | bytes 1179656 | tf_op jit(solution)/shard_map/ppermute | solution.py:357
  20.6 12.9 %collective-permute-start.6 = (bf16[4,2,128,128]{3,2,1,0:T(8,128)(2,1)}, bf16[4,2,128,128]{3,2,1,0:T(8,128)(2,1)S(1)}, u32[]{:S(2)}, u32[]{:S(2)}) collective-permute-start(bf16[4,2,128,128]{3,2,1,0:T(8,128)(2,1)} %get-tuple-element.41), channel_id=1, source_target_pairs={{0,1},{1,0},{2,3},{3,2},{4,5},{5,4},{6,7},{7,6},{8,9},{9,8},{10,11... | collective-permute-start | bytes 786440 | tf_op jit(solution)/shard_map/ppermute | solution.py:357
  20.7 12.8 %collective-permute-start.7 = (bf16[4,2,128,128]{3,2,1,0:T(8,128)(2,1)}, bf16[4,2,128,128]{3,2,1,0:T(8,128)(2,1)S(1)}, u32[]{:S(2)}, u32[]{:S(2)}) collective-permute-start(bf16[4,2,128,128]{3,2,1,0:T(8,128)(2,1)} %get-tuple-element.42), channel_id=1, source_target_pairs={{0,1},{1,0},{2,3},{3,2},{4,5},{5,4},{6,7},{7,6},{8,9},{9,8},{10,11... | collective-permute-start | bytes 786440 | tf_op jit(solution)/shard_map/ppermute | solution.py:357
  21.2 1.5 %collective-permute-start.2 = (bf16[1,2,128,128]{3,2,1,0:T(8,128)(2,1)S(1)}, bf16[1,2,128,128]{3,2,1,0:T(8,128)(2,1)S(1)}, u32[]{:S(2)}, u32[]{:S(2)}) collective-permute-start(bf16[1,2,128,128]{3,2,1,0:T(8,128)(2,1)S(1)} %get-tuple-element.35), channel_id=1, source_target_pairs={{0,1},{1,0},{2,3},{3,2},{4,5},{5,4},{6,7},{7,6},{8,9},{9,8},{10,11... | collective-permute-start | bytes 196616 | tf_op jit(solution)/shard_map/ppermute | solution.py:357
  22.7 21.0 %collective-permute-start.12 = (bf16[3,3,128,128]{3,2,1,0:T(8,128)(2,1)}, bf16[3,3,128,128]{3,2,1,0:T(8,128)(2,1)S(1)}, u32[]{:S(2)}, u32[]{:S(2)}) collective-permute-start(bf16[3,3,128,128]{3,2,1,0:T(8,128)(2,1)} %get-tuple-element.51), channel_id=1, source_target_pairs={{0,2},{1,3},{2,0},{3,1},{4,6},{5,7},{6,4},{7,5},{8,10},{9,11},{10,... | collective-permute-start | bytes 884744 | tf_op jit(solution)/shard_map/ppermute | solution.py:357
  25.2 20.2 %collective-permute-start.13 = (bf16[3,3,128,128]{3,2,1,0:T(8,128)(2,1)}, bf16[3,3,128,128]{3,2,1,0:T(8,128)(2,1)S(1)}, u32[]{:S(2)}, u32[]{:S(2)}) collective-permute-start(bf16[3,3,128,128]{3,2,1,0:T(8,128)(2,1)} %get-tuple-element.52), channel_id=1, source_target_pairs={{0,3},{1,2},{2,1},{3,0},{4,7},{5,6},{6,5},{7,4},{8,11},{9,10},{10,... | collective-permute-start | bytes 884744 | tf_op jit(solution)/shard_map/ppermute | solution.py:357
  32.7 9.7 %collective-permute-start.10 = (bf16[3,2,128,128]{3,2,1,0:T(8,128)(2,1)S(1)}, bf16[3,2,128,128]{3,2,1,0:T(8,128)(2,1)S(1)}, u32[]{:S(2)}, u32[]{:S(2)}) collective-permute-start(bf16[3,2,128,128]{3,2,1,0:T(8,128)(2,1)S(1)} %get-tuple-element.47), channel_id=1, source_target_pairs={{0,1},{1,0},{2,3},{3,2},{4,5},{5,4},{6,7},{7,6},{8,9},{9,8},{10,11... | collective-permute-start | bytes 589832 | tf_op jit(solution)/shard_map/ppermute | solution.py:357
  33.5 9.1 %collective-permute-start.11 = (bf16[3,2,128,128]{3,2,1,0:T(8,128)(2,1)S(1)}, bf16[3,2,128,128]{3,2,1,0:T(8,128)(2,1)S(1)}, u32[]{:S(2)}, u32[]{:S(2)}) collective-permute-start(bf16[3,2,128,128]{3,2,1,0:T(8,128)(2,1)S(1)} %get-tuple-element.48), channel_id=1, source_target_pairs={{0,1},{1,0},{2,3},{3,2},{4,5},{5,4},{6,7},{7,6},{8,9},{9,8},{10,11... | collective-permute-start | bytes 589832 | tf_op jit(solution)/shard_map/ppermute | solution.py:357
  33.5 7.0 %collective-permute-start.3 = (bf16[1,2,128,128]{3,2,1,0:T(8,128)(2,1)S(1)}, bf16[1,2,128,128]{3,2,1,0:T(8,128)(2,1)S(1)}, u32[]{:S(2)}, u32[]{:S(2)}) collective-permute-start(bf16[1,2,128,128]{3,2,1,0:T(8,128)(2,1)S(1)} %get-tuple-element.36), channel_id=1, source_target_pairs={{0,1},{1,0},{2,3},{3,2},{4,5},{5,4},{6,7},{7,6},{8,9},{9,8},{10,11... | collective-permute-start | bytes 196616 | tf_op jit(solution)/shard_map/ppermute | solution.py:357
  34.2 0.7 %copy-start = (f32[2,8,128]{2,1,0:T(8,128)S(1)}, f32[2,8,128]{2,1,0:T(8,128)}, u32[]{:S(2)}) copy-start(f32[2,8,128]{2,1,0:T(8,128)} %gains.11) | copy-start | bytes 24580
  34.3 1.0 %copy-start.1 = (bf16[4,2,128,128]{3,2,1,0:T(8,128)(2,1)S(1)}, bf16[4,2,128,128]{3,2,1,0:T(8,128)(2,1)}, u32[]{:S(2)}) copy-start(bf16[4,2,128,128]{3,2,1,0:T(8,128)(2,1)} %get-tuple-element.43.refs_3_) | copy-start | bytes 786436
  34.3 1.0 %copy-start.2 = (bf16[4,2,128,128]{3,2,1,0:T(8,128)(2,1)S(1)}, bf16[4,2,128,128]{3,2,1,0:T(8,128)(2,1)}, u32[]{:S(2)}) copy-start(bf16[4,2,128,128]{3,2,1,0:T(8,128)(2,1)} %get-tuple-element.44.refs_4_) | copy-start | bytes 786436
  35.3 0.7 %copy-start.4 = (s32[4,4]{1,0:T(4,128)S(1)}, s32[4,4]{1,0:T(4,128)}, u32[]{:S(2)}) copy-start(s32[4,4]{1,0:T(4,128)} %units.5) | copy-start | bytes 196
  40.6 7.9 %collective-permute-start.8 = (bf16[1,3,128,128]{3,2,1,0:T(8,128)(2,1)S(1)}, bf16[1,3,128,128]{3,2,1,0:T(8,128)(2,1)S(1)}, u32[]{:S(2)}, u32[]{:S(2)}) collective-permute-start(bf16[1,3,128,128]{3,2,1,0:T(8,128)(2,1)S(1)} %get-tuple-element.45), channel_id=1, source_target_pairs={{0,2},{1,3},{2,0},{3,1},{4,6},{5,7},{6,4},{7,5},{8,10},{9,11},{10,... | collective-permute-start | bytes 294920 | tf_op jit(solution)/shard_map/ppermute | solution.py:357
  42.4 7.1 %collective-permute-start.9 = (bf16[1,3,128,128]{3,2,1,0:T(8,128)(2,1)S(1)}, bf16[1,3,128,128]{3,2,1,0:T(8,128)(2,1)S(1)}, u32[]{:S(2)}, u32[]{:S(2)}) collective-permute-start(bf16[1,3,128,128]{3,2,1,0:T(8,128)(2,1)S(1)} %get-tuple-element.46), channel_id=1, source_target_pairs={{0,3},{1,2},{2,1},{3,0},{4,7},{5,6},{6,5},{7,4},{8,11},{9,10},{10,... | collective-permute-start | bytes 294920 | tf_op jit(solution)/shard_map/ppermute | solution.py:357
  42.5 0.9 %copy-start.3 = (bf16[3,2,128,128]{3,2,1,0:T(8,128)(2,1)S(1)}, bf16[3,2,128,128]{3,2,1,0:T(8,128)(2,1)}, u32[]{:S(2)}) copy-start(bf16[3,2,128,128]{3,2,1,0:T(8,128)(2,1)} %get-tuple-element.50.refs_3_) | copy-start | bytes 589828
  50.4 6.6 %collective-permute-start.14 = (f32[2,8,32]{2,1,0:T(8,128)S(1)}, f32[2,8,32]{2,1,0:T(8,128)S(1)}, u32[]{:S(2)}, u32[]{:S(2)}) collective-permute-start(f32[2,8,32]{2,1,0:T(8,128)S(1)} %get-tuple-element.54), channel_id=1, source_target_pairs={{0,4},{4,12},{8,0},{12,8},{1,5},{5,13},{9,1},{13,9},{2,6},{6,14},{... | collective-permute-start | bytes 6152 | tf_op jit(solution)/shard_map/ppermute | solution.py:394
  52.8 5.4 %collective-permute-start.15 = (f32[2,8,32]{2,1,0:T(8,128)S(1)}, f32[2,8,32]{2,1,0:T(8,128)S(1)}, u32[]{:S(2)}, u32[]{:S(2)}) collective-permute-start(f32[2,8,32]{2,1,0:T(8,128)S(1)} %get-tuple-element.55), channel_id=1, source_target_pairs={{0,12},{4,8},{8,4},{12,0},{1,13},{5,9},{9,5},{13,1},{2,14},{6,10},... | collective-permute-start | bytes 6152 | tf_op jit(solution)/shard_map/ppermute | solution.py:394
  55.4 3.7 %collective-permute-start.16 = (f32[2,8,32]{2,1,0:T(8,128)S(1)}, f32[2,8,32]{2,1,0:T(8,128)S(1)}, u32[]{:S(2)}, u32[]{:S(2)}) collective-permute-start(f32[2,8,32]{2,1,0:T(8,128)S(1)} %get-tuple-element.56), channel_id=1, source_target_pairs={{0,8},{4,0},{8,12},{12,4},{1,9},{5,1},{9,13},{13,5},{2,10},{6,2},{... | collective-permute-start | bytes 6152 | tf_op jit(solution)/shard_map/ppermute | solution.py:394

commit v14 on v11

--- a/solution.py
+++ b/solution.py
@@ -342,7 +342,7 @@
 
 
 def ring_targets(groups):
-    ring = [0] + list(range(1, groups, 2)) + list(range(2, groups, 2))[::-1]
+    ring = list(range(0, groups, 2)) + list(range(1, groups, 2))
     return [[ring[(ring.index(place) + step) % groups] for place in range(groups)] for step in range(groups)]
 
 

time: 58.3 us -> 59.4 us (1.019)
  waiting for transfers between devices: 24.9 us -> 26.6 us
  starting transfers between devices: 16.2 us -> 15.1 us
    ppermute x3, waiting for transfers between devices: 2.07 us -> 4.18 us  [body(): result = result + lax.ppermute(part, 'dp', list(enumerate(targets)))]
    ppermute x3, starting transfers between devices: 5.64 us -> 4.51 us  [body(): result = result + lax.ppermute(part, 'dp', list(enumerate(targets)))]
  transfers between devices with their start and end apart: 17 -> 17, of which waited for: 10 -> 11; matrix products, arithmetic and copies ran while one was open for 0% -> 0% of each run, Pallas kernels for 21% -> 22%
where the time goes in v14:
time: 59.4 us; the launch traced here: 59.1 us
  waiting for transfers between devices  26.6 us (45%)
  starting transfers between devices  15.1 us (25%)
  Pallas kernels  14.7 us (25%)
  local copies, waits for them, and re-layouts  2.08 us (4%)
  other arithmetic  0.6 us (1%)
    ppermute x14, waiting for transfers between devices, send(): return lax.ppermute(block, 'seq', [(s, s ^ flip) for s in range(sequence)])  22.4 us
    ppermute x14, starting transfers between devices, send(): return lax.ppermute(block, 'seq', [(s, s ^ flip) for s in range(sequence)])  10.5 us
    pallas_call x3, Pallas kernels, pack(): pl.pallas_call(functools.partial(pack_kernel, plan, heads, len(after)), o...  7.37 us
    pallas_call x3, Pallas kernels, attend(): pl.pallas_call(kernel, out_shape=shapes, in_specs=[pl.BlockSpec(memory_sp...  5.19 us
    ppermute x3, starting transfers between devices, body(): result = result + lax.ppermute(part, 'dp', list(enumerate(targets)))  4.51 us
    ppermute x3, waiting for transfers between devices, body(): result = result + lax.ppermute(part, 'dp', list(enumerate(targets)))  4.18 us
    unnamed x10, local copies, waits for them, and re-layouts  2.08 us
  transfers between devices with their start and end apart: 17, of which 11 were waited for; matrix products, arithmetic and copies ran while one was open for 0% of the time, Pallas kernels for 22%

profile of v14, /device:TPU:0, one launch (start us, length us, event | category | flops | bytes accessed | tf_op | source)
XLA Modules:
  0.0 59.1 jit_solution(17887133301532184457)
XLA Ops:
  0.0 1.1 %cut.1 = (bf16[4,32,8,128]{3,2,1,0:T(8,128)(2,1)S(1)}, bf16[4,32,8,128]{3,2,1,0:T(8,128)(2,1)S(1)}, f32[8,128]{1,0:T(8,128)S(1)}) custom-call(bf16[1,4,32,32,128]{4,3,2,1,0:T(8,128)(2,1)} %refs_2_.5), custom_call_target="tpu_custom_call" | custom-call | tf_op jit(solution)/shard_map/cut/pallas_call | solution.py:53
  1.1 3.0 %collective-permute-start = (bf16[4,32,8,128]{3,2,1,0:T(8,128)(2,1)S(1)}, bf16[4,32,8,128]{3,2,1,0:T(8,128)(2,1)S(1)}, u32[]{:S(2)}, u32[]{:S(2)}) collective-permute-start(bf16[4,32,8,128]{3,2,1,0:T(8,128)(2,1)S(1)} %get-tuple-element.31), channel_id=1, source_target_pairs={{0,2},{1,3},{2,0},{3,1},{4,6},{5,7},{6,4},{7,5},{8,10},{9,11},{10,... | collective-permute-start | bytes 786440 | tf_op jit(solution)/shard_map/ppermute | solution.py:357
  4.1 0.0 collective-permute-start.1
  4.1 1.5 %pack.3 = (bf16[4,3,128,128]{3,2,1,0:T(8,128)(2,1)S(1)}, bf16[4,3,128,128]{3,2,1,0:T(8,128)(2,1)S(1)}, f32[8,128]{1,0:T(8,128)S(1)}) custom-call(bf16[1,4,32,32,128]{4,3,2,1,0:T(8,128)(2,1)} %refs_0_.5, bf16[1,4,32,32,128]{4,3,2,1,0:T(8,128)(2,1)} %refs_1_.5, bf16[1,4,32,32,128]{4,3,2,1,0:T(8,128)(2,1)} %refs_2_.5, bf16[1,4,32,32,128]{4,3,2,1,0:T(8,128)(2,1)} %refs_3_.5, ...), custom_call_target="tpu_custom_call" | custom-call | flops 2097152 | bytes 4194304 | tf_op jit(solution)/shard_map/pack/pallas_call | solution.py:145
  5.6 1.2 %collective-permute-start.4 = (bf16[4,3,128,128]{3,2,1,0:T(8,128)(2,1)S(1)}, bf16[4,3,128,128]{3,2,1,0:T(8,128)(2,1)S(1)}, u32[]{:S(2)}, u32[]{:S(2)}) collective-permute-start(bf16[4,3,128,128]{3,2,1,0:T(8,128)(2,1)S(1)} %get-tuple-element.39), channel_id=1, source_target_pairs={{0,2},{1,3},{2,0},{3,1},{4,6},{5,7},{6,4},{7,5},{8,10},{9,11},{10,... | collective-permute-start | bytes 1179656 | tf_op jit(solution)/shard_map/ppermute | solution.py:357
  6.9 0.6 %collective-permute-start.5 = (bf16[4,3,128,128]{3,2,1,0:T(8,128)(2,1)S(1)}, bf16[4,3,128,128]{3,2,1,0:T(8,128)(2,1)S(1)}, u32[]{:S(2)}, u32[]{:S(2)}) collective-permute-start(bf16[4,3,128,128]{3,2,1,0:T(8,128)(2,1)S(1)} %get-tuple-element.40), channel_id=1, source_target_pairs={{0,3},{1,2},{2,1},{3,0},{4,7},{5,6},{6,5},{7,4},{8,11},{9,10},{10,... | collective-permute-start | bytes 1179656 | tf_op jit(solution)/shard_map/ppermute | solution.py:357
  7.5 3.7 %collective-permute-done.refs_0_ = bf16[4,32,8,128]{3,2,1,0:T(8,128)(2,1)S(1)} collective-permute-done((bf16[4,32,8,128]{3,2,1,0:T(8,128)(2,1)S(1)}, bf16[4,32,8,128]{3,2,1,0:T(8,128)(2,1)S(1)}, u32[]{:S(2)}, u32[]{:S(2)}) %collective-permute-start) | collective-permute-done | bytes 262176 | tf_op jit(solution)/shard_map/ppermute | solution.py:357
  11.2 5.2 %collective-permute-done.1.refs_1_ = bf16[4,32,8,128]{3,2,1,0:T(8,128)(2,1)S(1)} collective-permute-done((bf16[4,32,8,128]{3,2,1,0:T(8,128)(2,1)S(1)}, bf16[4,32,8,128]{3,2,1,0:T(8,128)(2,1)S(1)}, u32[]{:S(2)}, u32[]{:S(2)}) %collective-permute-start.1) | collective-permute-done | bytes 262176 | tf_op jit(solution)/shard_map/ppermute | solution.py:357
  16.4 3.8 %pack.4 = (bf16[3,3,128,128]{3,2,1,0:T(8,128)(2,1)}, bf16[3,3,128,128]{3,2,1,0:T(8,128)(2,1)}, bf16[4,2,128,128]{3,2,1,0:T(8,128)(2,1)}, bf16[3,2,128,128]{3,2,1...) custom-call(bf16[1,4,32,32,128]{4,3,2,1,0:T(8,128)(2,1)} %refs_0_.5,, ...), custom_call_target="tpu_custom_call" | custom-call | flops 6291456 | bytes 12582912 | tf_op jit(solution)/shard_map/pack/pallas_call | solution.py:145
  20.2 0.3 collective-permute-start.6
  20.5 0.3 collective-permute-start.7
  20.8 0.2 collective-permute-start.2
  21.0 1.2 %collective-permute-done.2.refs_0_ = bf16[1,2,128,128]{3,2,1,0:T(8,128)(2,1)S(1)} collective-permute-done((bf16[1,2,128,128]{3,2,1,0:T(8,128)(2,1)S(1)}, bf16[1,2,128,128]{3,2,1,0:T(8,128)(2,1)S(1)}, u32[]{:S(2)}, u32[]{:S(2)}) %collective-permute-start.2) | collective-permute-done | bytes 65568 | tf_op jit(solution)/shard_map/ppermute | solution.py:357
  22.2 1.9 %collective-permute-start.12 = (bf16[3,3,128,128]{3,2,1,0:T(8,128)(2,1)}, bf16[3,3,128,128]{3,2,1,0:T(8,128)(2,1)S(1)}, u32[]{:S(2)}, u32[]{:S(2)}) collective-permute-start(bf16[3,3,128,128]{3,2,1,0:T(8,128)(2,1)} %get-tuple-element.51), channel_id=1, source_target_pairs={{0,2},{1,3},{2,0},{3,1},{4,6},{5,7},{6,4},{7,5},{8,10},{9,11},{10,... | collective-permute-start | bytes 884744 | tf_op jit(solution)/shard_map/ppermute | solution.py:357
  24.2 1.1 %collective-permute-done.4.refs_0_ = bf16[4,3,128,128]{3,2,1,0:T(8,128)(2,1)S(1)} collective-permute-done((bf16[4,3,128,128]{3,2,1,0:T(8,128)(2,1)S(1)}, bf16[4,3,128,128]{3,2,1,0:T(8,128)(2,1)S(1)}, u32[]{:S(2)}, u32[]{:S(2)}) %collective-permute-start.4) | collective-permute-done | bytes 393248 | tf_op jit(solution)/shard_map/ppermute | solution.py:357
  25.2 0.0 collective-permute-start.13
  25.2 8.0 %collective-permute-done.5.refs_1_ = bf16[4,3,128,128]{3,2,1,0:T(8,128)(2,1)S(1)} collective-permute-done((bf16[4,3,128,128]{3,2,1,0:T(8,128)(2,1)S(1)}, bf16[4,3,128,128]{3,2,1,0:T(8,128)(2,1)S(1)}, u32[]{:S(2)}, u32[]{:S(2)}) %collective-permute-start.5) | collective-permute-done | bytes 393248 | tf_op jit(solution)/shard_map/ppermute | solution.py:357
  33.2 0.2 collective-permute-start.10
  33.5 0.3 collective-permute-start.11
  33.8 0.0 collective-permute-done.7.refs_2_
  33.8 0.2 collective-permute-start.3
  34.0 0.2 arrange.1.values
  34.2 0.0 copy-start
  34.3 0.7 %copy-done = f32[2,8,128]{2,1,0:T(8,128)S(1)} copy-done((f32[2,8,128]{2,1,0:T(8,128)S(1)}, f32[2,8,128]{2,1,0:T(8,128)}, u32[]{:S(2)}) %copy-start) | copy-done | bytes 8216
  34.9 0.3 copy-done.1
  35.2 0.1 copy-done.2
  35.3 0.4 prepare.4.close
  35.7 0.3 copy-done.4
  36.0 2.5 %attend.3.refs_4_.refs_2_ = f32[4,128]{1,0:T(4,128)S(1)} custom-call(s32[4,4]{1,0:T(4,128)S(1)} %copy-done.4, f32[2,8,128]{2,1,0:T(8,128)S(1)} %copy-done, bf16[8,4,64,128]{3,2,1,0:T(8,128)(2,1)S(1)} %arrange.1.values, bf16[4,4,4,64,128]{4,3,2,1,0:T(8,128)(2,1)S(1)} %prepare.4.close, bf16[4,3,128,128]{3,2,1,0:T(8,128)(2,1)S(1)} %collective-permute-done.4.refs_0_, ...), custom_call_target="tpu_custom_call" | custom-call | flops 402653184 | bytes 1048576 | tf_op jit(solution)/shard_map/attend/pallas_call | solution.py:314
  38.5 2.1 %pack.5 = (bf16[1,3,128,128]{3,2,1,0:T(8,128)(2,1)S(1)}, bf16[1,3,128,128]{3,2,1,0:T(8,128)(2,1)S(1)}, f32[8,128]{1,0:T(8,128)}) custom-call(bf16[1,4,32,32,128]{4,3,2,1,0:T(8,128)(2,1)} %refs_0_.5, bf16[1,4,32,32,128]{4,3,2,1,0:T(8,128)(2,1)} %refs_1_.5, bf16[1,4,32,32,128]{4,3,2,1,0:T(8,128)(2,1)} %refs_2_.5, bf16[1,4,32,32,128]{4,3,2,1,0:T(8,128)(2,1)} %refs_3_.5, ...), custom_call_target="tpu_custom_call" | custom-call | flops 2097152 | bytes 4194304 | tf_op jit(solution)/shard_map/pack/pallas_call | solution.py:145
  40.6 2.1 %collective-permute-start.8 = (bf16[1,3,128,128]{3,2,1,0:T(8,128)(2,1)S(1)}, bf16[1,3,128,128]{3,2,1,0:T(8,128)(2,1)S(1)}, u32[]{:S(2)}, u32[]{:S(2)}) collective-permute-start(bf16[1,3,128,128]{3,2,1,0:T(8,128)(2,1)S(1)} %get-tuple-element.45), channel_id=1, source_target_pairs={{0,2},{1,3},{2,0},{3,1},{4,6},{5,7},{6,4},{7,5},{8,10},{9,11},{10,... | collective-permute-start | bytes 294920 | tf_op jit(solution)/shard_map/ppermute | solution.py:357
  42.7 0.0 collective-permute-start.9
  42.7 0.2 prepare.3.close
  42.9 0.8 %copy-done.3 = bf16[3,2,128,128]{3,2,1,0:T(8,128)(2,1)S(1)} copy-done((bf16[3,2,128,128]{3,2,1,0:T(8,128)(2,1)S(1)}, bf16[3,2,128,128]{3,2,1,0:T(8,128)(2,1)}, u32[]{:S(2)}) %copy-start.3) | copy-done | bytes 196632
  43.6 0.3 prepare.5.close
  43.9 0.0 collective-permute-done.12.refs_0_
  43.9 2.1 %collective-permute-done.13.refs_1_ = bf16[3,3,128,128]{3,2,1,0:T(8,128)(2,1)S(1)} collective-permute-done((bf16[3,3,128,128]{3,2,1,0:T(8,128)(2,1)}, bf16[3,3,128,128]{3,2,1,0:T(8,128)(2,1)S(1)}, u32[]{:S(2)}, u32[]{:S(2)}) %collective-permute-start.13) | collective-permute-done | bytes 294944 | tf_op jit(solution)/shard_map/ppermute | solution.py:357
  46.0 1.8 %attend.4.refs_3_ = f32[3,128]{1,0:T(4,128)S(1)} custom-call(s32[4,4]{1,0:T(4,128)S(1)} %copy-done.4, f32[2,8,128]{2,1,0:T(8,128)S(1)} %copy-done, bf16[8,4,64,128]{3,2,1,0:T(8,128)(2,1)S(1)} %arrange.1.values, bf16[3,4,4,64,128]{4,3,2,1,0:T(8,128)(2,1)S(1)} %prepare.5.close, bf16[3,3,128,128]{3,2,1,0:T(8,128)(2,1)S(1)} %collective-permute-done.12.refs_0_, ...), custom_call_target="tpu_custom_call" | custom-call | flops 301989888 | bytes 786432 | tf_op jit(solution)/shard_map/attend/pallas_call | solution.py:314
  47.8 0.6 %collective-permute-done.8.refs_0_ = bf16[1,3,128,128]{3,2,1,0:T(8,128)(2,1)S(1)} collective-permute-done((bf16[1,3,128,128]{3,2,1,0:T(8,128)(2,1)S(1)}, bf16[1,3,128,128]{3,2,1,0:T(8,128)(2,1)S(1)}, u32[]{:S(2)}, u32[]{:S(2)}) %collective-permute-start.8) | collective-permute-done | bytes 98336 | tf_op jit(solution)/shard_map/ppermute | solution.py:357
  48.4 0.5 collective-permute-done.9.refs_1_
  49.0 0.9 %attend.5 = (f32[2,8,32]{2,1,0:T(8,128)S(1)}, f32[2,8,32]{2,1,0:T(8,128)S(1)}, f32[2,8,32]{2,1,0:T(8,128)S(1)}, f32[2,8,32]{2,1,0:T(8,128)S(1)}) custom-call(s32[4,4]{1,0:T(4,128)S(1)} %copy-done.4, f32[2,8,128]{2,1,0:T(8,128)S(1)} %copy-done, bf16[8,4,64,128]{3,2,1,0:T(8,128)(2,1)S(1)} %arrange.1.values, bf16[1,4,4,64,128]{4,3,2,1,0:T(8,128)(2,1)S(1)} %prepare.3.close, ...), custom_call_target="tpu_custom_call" | custom-call | flops 100663296 | bytes 262144 | tf_op jit(solution)/shard_map/attend/pallas_call | solution.py:314
  49.8 2.6 %collective-permute-start.14 = (f32[2,8,32]{2,1,0:T(8,128)S(1)}, f32[2,8,32]{2,1,0:T(8,128)S(1)}, u32[]{:S(2)}, u32[]{:S(2)}) collective-permute-start(f32[2,8,32]{2,1,0:T(8,128)S(1)} %get-tuple-element.54), channel_id=1, source_target_pairs={{0,8},{4,12},{8,4},{12,0},{1,9},{5,13},{9,5},{13,1},{2,10},{6,14},... | collective-permute-start | bytes 6152 | tf_op jit(solution)/shard_map/ppermute | solution.py:394
  52.4 1.5 %collective-permute-start.15 = (f32[2,8,32]{2,1,0:T(8,128)S(1)}, f32[2,8,32]{2,1,0:T(8,128)S(1)}, u32[]{:S(2)}, u32[]{:S(2)}) collective-permute-start(f32[2,8,32]{2,1,0:T(8,128)S(1)} %get-tuple-element.55), channel_id=1, source_target_pairs={{0,4},{4,0},{8,12},{12,8},{1,5},{5,1},{9,13},{13,9},{2,6},{6,2},{1... | collective-permute-start | bytes 6152 | tf_op jit(solution)/shard_map/ppermute | solution.py:394
  53.9 0.5 collective-permute-start.16
  54.4 0.9 %collective-permute-done.14 = f32[2,8,32]{2,1,0:T(8,128)S(1)} collective-permute-done((f32[2,8,32]{2,1,0:T(8,128)S(1)}, f32[2,8,32]{2,1,0:T(8,128)S(1)}, u32[]{:S(2)}, u32[]{:S(2)}) %collective-permute-start.14) | collective-permute-done | bytes 2080 | tf_op jit(solution)/shard_map/ppermute | solution.py:394
  55.3 0.8 %collective-permute-done.15 = f32[2,8,32]{2,1,0:T(8,128)S(1)} collective-permute-done((f32[2,8,32]{2,1,0:T(8,128)S(1)}, f32[2,8,32]{2,1,0:T(8,128)S(1)}, u32[]{:S(2)}, u32[]{:S(2)}) %collective-permute-start.15) | collective-permute-done | bytes 2080 | tf_op jit(solution)/shard_map/ppermute | solution.py:394
  56.1 2.4 %collective-permute-done.16 = f32[2,8,32]{2,1,0:T(8,128)S(1)} collective-permute-done((f32[2,8,32]{2,1,0:T(8,128)S(1)}, f32[2,8,32]{2,1,0:T(8,128)S(1)}, u32[]{:S(2)}, u32[]{:S(2)}) %collective-permute-start.16) | collective-permute-done | bytes 2080 | tf_op jit(solution)/shard_map/ppermute | solution.py:394
  58.5 0.6 %add_add_fusion = f32[2,8,32]{2,1,0:T(8,128)} fusion(f32[2,8,32]{2,1,0:T(8,128)S(1)} %collective-permute-done.16, f32[2,8,32]{2,1,0:T(8,128)S(1)} %collective-permute-done.15, f32[2,8,32]{2,1,0:T(8,128)S(1)} %get-tuple-element.53, f32[2,8,32]{2,1,0:T(8,128)S(1)} %collective-permute-done.14), kind=kLoop, calls=%fused_computation | loop fusion | flops 1536 | bytes 10240 | tf_op jit(solution)/shard_map/add | solution.py:394
  (10 shorter events, 0.0 us)
Async XLA Ops:
  1.1 10.1 %collective-permute-start = (bf16[4,32,8,128]{3,2,1,0:T(8,128)(2,1)S(1)}, bf16[4,32,8,128]{3,2,1,0:T(8,128)(2,1)S(1)}, u32[]{:S(2)}, u32[]{:S(2)}) collective-permute-start(bf16[4,32,8,128]{3,2,1,0:T(8,128)(2,1)S(1)} %get-tuple-element.31), channel_id=1, source_target_pairs={{0,2},{1,3},{2,0},{3,1},{4,6},{5,7},{6,4},{7,5},{8,10},{9,11},{10,... | collective-permute-start | bytes 786440 | tf_op jit(solution)/shard_map/ppermute | solution.py:357
  4.1 12.3 %collective-permute-start.1 = (bf16[4,32,8,128]{3,2,1,0:T(8,128)(2,1)S(1)}, bf16[4,32,8,128]{3,2,1,0:T(8,128)(2,1)S(1)}, u32[]{:S(2)}, u32[]{:S(2)}) collective-permute-start(bf16[4,32,8,128]{3,2,1,0:T(8,128)(2,1)S(1)} %get-tuple-element.32), channel_id=1, source_target_pairs={{0,3},{1,2},{2,1},{3,0},{4,7},{5,6},{6,5},{7,4},{8,11},{9,10},{10,... | collective-permute-start | bytes 786440 | tf_op jit(solution)/shard_map/ppermute | solution.py:357
  5.6 19.6 %collective-permute-start.4 = (bf16[4,3,128,128]{3,2,1,0:T(8,128)(2,1)S(1)}, bf16[4,3,128,128]{3,2,1,0:T(8,128)(2,1)S(1)}, u32[]{:S(2)}, u32[]{:S(2)}) collective-permute-start(bf16[4,3,128,128]{3,2,1,0:T(8,128)(2,1)S(1)} %get-tuple-element.39), channel_id=1, source_target_pairs={{0,2},{1,3},{2,0},{3,1},{4,6},{5,7},{6,4},{7,5},{8,10},{9,11},{10,... | collective-permute-start | bytes 1179656 | tf_op jit(solution)/shard_map/ppermute | solution.py:357
  6.9 26.4 %collective-permute-start.5 = (bf16[4,3,128,128]{3,2,1,0:T(8,128)(2,1)S(1)}, bf16[4,3,128,128]{3,2,1,0:T(8,128)(2,1)S(1)}, u32[]{:S(2)}, u32[]{:S(2)}) collective-permute-start(bf16[4,3,128,128]{3,2,1,0:T(8,128)(2,1)S(1)} %get-tuple-element.40), channel_id=1, source_target_pairs={{0,3},{1,2},{2,1},{3,0},{4,7},{5,6},{6,5},{7,4},{8,11},{9,10},{10,... | collective-permute-start | bytes 1179656 | tf_op jit(solution)/shard_map/ppermute | solution.py:357
  20.2 13.3 %collective-permute-start.6 = (bf16[4,2,128,128]{3,2,1,0:T(8,128)(2,1)}, bf16[4,2,128,128]{3,2,1,0:T(8,128)(2,1)S(1)}, u32[]{:S(2)}, u32[]{:S(2)}) collective-permute-start(bf16[4,2,128,128]{3,2,1,0:T(8,128)(2,1)} %get-tuple-element.41), channel_id=1, source_target_pairs={{0,1},{1,0},{2,3},{3,2},{4,5},{5,4},{6,7},{7,6},{8,9},{9,8},{10,11... | collective-permute-start | bytes 786440 | tf_op jit(solution)/shard_map/ppermute | solution.py:357
  20.5 13.3 %collective-permute-start.7 = (bf16[4,2,128,128]{3,2,1,0:T(8,128)(2,1)}, bf16[4,2,128,128]{3,2,1,0:T(8,128)(2,1)S(1)}, u32[]{:S(2)}, u32[]{:S(2)}) collective-permute-start(bf16[4,2,128,128]{3,2,1,0:T(8,128)(2,1)} %get-tuple-element.42), channel_id=1, source_target_pairs={{0,1},{1,0},{2,3},{3,2},{4,5},{5,4},{6,7},{7,6},{8,9},{9,8},{10,11... | collective-permute-start | bytes 786440 | tf_op jit(solution)/shard_map/ppermute | solution.py:357
  20.8 1.5 %collective-permute-start.2 = (bf16[1,2,128,128]{3,2,1,0:T(8,128)(2,1)S(1)}, bf16[1,2,128,128]{3,2,1,0:T(8,128)(2,1)S(1)}, u32[]{:S(2)}, u32[]{:S(2)}) collective-permute-start(bf16[1,2,128,128]{3,2,1,0:T(8,128)(2,1)S(1)} %get-tuple-element.35), channel_id=1, source_target_pairs={{0,1},{1,0},{2,3},{3,2},{4,5},{5,4},{6,7},{7,6},{8,9},{9,8},{10,11... | collective-permute-start | bytes 196616 | tf_op jit(solution)/shard_map/ppermute | solution.py:357
  22.2 21.7 %collective-permute-start.12 = (bf16[3,3,128,128]{3,2,1,0:T(8,128)(2,1)}, bf16[3,3,128,128]{3,2,1,0:T(8,128)(2,1)S(1)}, u32[]{:S(2)}, u32[]{:S(2)}) collective-permute-start(bf16[3,3,128,128]{3,2,1,0:T(8,128)(2,1)} %get-tuple-element.51), channel_id=1, source_target_pairs={{0,2},{1,3},{2,0},{3,1},{4,6},{5,7},{6,4},{7,5},{8,10},{9,11},{10,... | collective-permute-start | bytes 884744 | tf_op jit(solution)/shard_map/ppermute | solution.py:357
  25.2 20.7 %collective-permute-start.13 = (bf16[3,3,128,128]{3,2,1,0:T(8,128)(2,1)}, bf16[3,3,128,128]{3,2,1,0:T(8,128)(2,1)S(1)}, u32[]{:S(2)}, u32[]{:S(2)}) collective-permute-start(bf16[3,3,128,128]{3,2,1,0:T(8,128)(2,1)} %get-tuple-element.52), channel_id=1, source_target_pairs={{0,3},{1,2},{2,1},{3,0},{4,7},{5,6},{6,5},{7,4},{8,11},{9,10},{10,... | collective-permute-start | bytes 884744 | tf_op jit(solution)/shard_map/ppermute | solution.py:357
  33.2 9.4 %collective-permute-start.10 = (bf16[3,2,128,128]{3,2,1,0:T(8,128)(2,1)S(1)}, bf16[3,2,128,128]{3,2,1,0:T(8,128)(2,1)S(1)}, u32[]{:S(2)}, u32[]{:S(2)}) collective-permute-start(bf16[3,2,128,128]{3,2,1,0:T(8,128)(2,1)S(1)} %get-tuple-element.47), channel_id=1, source_target_pairs={{0,1},{1,0},{2,3},{3,2},{4,5},{5,4},{6,7},{7,6},{8,9},{9,8},{10,11... | collective-permute-start | bytes 589832 | tf_op jit(solution)/shard_map/ppermute | solution.py:357
  33.5 9.4 %collective-permute-start.11 = (bf16[3,2,128,128]{3,2,1,0:T(8,128)(2,1)S(1)}, bf16[3,2,128,128]{3,2,1,0:T(8,128)(2,1)S(1)}, u32[]{:S(2)}, u32[]{:S(2)}) collective-permute-start(bf16[3,2,128,128]{3,2,1,0:T(8,128)(2,1)S(1)} %get-tuple-element.48), channel_id=1, source_target_pairs={{0,1},{1,0},{2,3},{3,2},{4,5},{5,4},{6,7},{7,6},{8,9},{9,8},{10,11... | collective-permute-start | bytes 589832 | tf_op jit(solution)/shard_map/ppermute | solution.py:357
  33.8 6.8 %collective-permute-start.3 = (bf16[1,2,128,128]{3,2,1,0:T(8,128)(2,1)S(1)}, bf16[1,2,128,128]{3,2,1,0:T(8,128)(2,1)S(1)}, u32[]{:S(2)}, u32[]{:S(2)}) collective-permute-start(bf16[1,2,128,128]{3,2,1,0:T(8,128)(2,1)S(1)} %get-tuple-element.36), channel_id=1, source_target_pairs={{0,1},{1,0},{2,3},{3,2},{4,5},{5,4},{6,7},{7,6},{8,9},{9,8},{10,11... | collective-permute-start | bytes 196616 | tf_op jit(solution)/shard_map/ppermute | solution.py:357
  34.2 0.7 %copy-start = (f32[2,8,128]{2,1,0:T(8,128)S(1)}, f32[2,8,128]{2,1,0:T(8,128)}, u32[]{:S(2)}) copy-start(f32[2,8,128]{2,1,0:T(8,128)} %gains.11) | copy-start | bytes 24580
  34.3 1.0 %copy-start.1 = (bf16[4,2,128,128]{3,2,1,0:T(8,128)(2,1)S(1)}, bf16[4,2,128,128]{3,2,1,0:T(8,128)(2,1)}, u32[]{:S(2)}) copy-start(bf16[4,2,128,128]{3,2,1,0:T(8,128)(2,1)} %get-tuple-element.43.refs_3_) | copy-start | bytes 786436
  34.3 1.0 %copy-start.2 = (bf16[4,2,128,128]{3,2,1,0:T(8,128)(2,1)S(1)}, bf16[4,2,128,128]{3,2,1,0:T(8,128)(2,1)}, u32[]{:S(2)}) copy-start(bf16[4,2,128,128]{3,2,1,0:T(8,128)(2,1)} %get-tuple-element.44.refs_4_) | copy-start | bytes 786436
  35.3 0.7 %copy-start.4 = (s32[4,4]{1,0:T(4,128)S(1)}, s32[4,4]{1,0:T(4,128)}, u32[]{:S(2)}) copy-start(s32[4,4]{1,0:T(4,128)} %units.5) | copy-start | bytes 196
  40.6 7.9 %collective-permute-start.8 = (bf16[1,3,128,128]{3,2,1,0:T(8,128)(2,1)S(1)}, bf16[1,3,128,128]{3,2,1,0:T(8,128)(2,1)S(1)}, u32[]{:S(2)}, u32[]{:S(2)}) collective-permute-start(bf16[1,3,128,128]{3,2,1,0:T(8,128)(2,1)S(1)} %get-tuple-element.45), channel_id=1, source_target_pairs={{0,2},{1,3},{2,0},{3,1},{4,6},{5,7},{6,4},{7,5},{8,10},{9,11},{10,... | collective-permute-start | bytes 294920 | tf_op jit(solution)/shard_map/ppermute | solution.py:357
  42.7 6.3 %collective-permute-start.9 = (bf16[1,3,128,128]{3,2,1,0:T(8,128)(2,1)S(1)}, bf16[1,3,128,128]{3,2,1,0:T(8,128)(2,1)S(1)}, u32[]{:S(2)}, u32[]{:S(2)}) collective-permute-start(bf16[1,3,128,128]{3,2,1,0:T(8,128)(2,1)S(1)} %get-tuple-element.46), channel_id=1, source_target_pairs={{0,3},{1,2},{2,1},{3,0},{4,7},{5,6},{6,5},{7,4},{8,11},{9,10},{10,... | collective-permute-start | bytes 294920 | tf_op jit(solution)/shard_map/ppermute | solution.py:357
  42.7 0.9 %copy-start.3 = (bf16[3,2,128,128]{3,2,1,0:T(8,128)(2,1)S(1)}, bf16[3,2,128,128]{3,2,1,0:T(8,128)(2,1)}, u32[]{:S(2)}) copy-start(bf16[3,2,128,128]{3,2,1,0:T(8,128)(2,1)} %get-tuple-element.50.refs_3_) | copy-start | bytes 589828
  49.8 5.5 %collective-permute-start.14 = (f32[2,8,32]{2,1,0:T(8,128)S(1)}, f32[2,8,32]{2,1,0:T(8,128)S(1)}, u32[]{:S(2)}, u32[]{:S(2)}) collective-permute-start(f32[2,8,32]{2,1,0:T(8,128)S(1)} %get-tuple-element.54), channel_id=1, source_target_pairs={{0,8},{4,12},{8,4},{12,0},{1,9},{5,13},{9,5},{13,1},{2,10},{6,14},... | collective-permute-start | bytes 6152 | tf_op jit(solution)/shard_map/ppermute | solution.py:394
  52.4 3.7 %collective-permute-start.15 = (f32[2,8,32]{2,1,0:T(8,128)S(1)}, f32[2,8,32]{2,1,0:T(8,128)S(1)}, u32[]{:S(2)}, u32[]{:S(2)}) collective-permute-start(f32[2,8,32]{2,1,0:T(8,128)S(1)} %get-tuple-element.55), channel_id=1, source_target_pairs={{0,4},{4,0},{8,12},{12,8},{1,5},{5,1},{9,13},{13,9},{2,6},{6,2},{1... | collective-permute-start | bytes 6152 | tf_op jit(solution)/shard_map/ppermute | solution.py:394
  53.9 4.6 %collective-permute-start.16 = (f32[2,8,32]{2,1,0:T(8,128)S(1)}, f32[2,8,32]{2,1,0:T(8,128)S(1)}, u32[]{:S(2)}, u32[]{:S(2)}) collective-permute-start(f32[2,8,32]{2,1,0:T(8,128)S(1)} %get-tuple-element.56), channel_id=1, source_target_pairs={{0,12},{4,8},{8,0},{12,4},{1,13},{5,9},{9,1},{13,5},{2,14},{6,10},... | collective-permute-start | bytes 6152 | tf_op jit(solution)/shard_map/ppermute | solution.py:394

commit v15 on v11

--- a/solution.py
+++ b/solution.py
@@ -34,8 +34,8 @@
     return pl.multiple_of((head // TILE) * TILE, TILE), offset
 
 
-def cut_kernel(flips, heads, array, *refs):
-    outs, token, sems = refs[:-2], refs[-2], refs[-1]
+def cut_kernel(flips, heads, after, array, *refs):
+    outs, token, sems = refs[after:-2], refs[-2], refs[-1]
     token[...] = jnp.zeros_like(token)
     copies = []
     for index, flip in enumerate(flips):
@@ -47,18 +47,18 @@
         copy.wait()
 
 
-def cut(array, flips, heads):
+def cut(array, flips, heads, after):
     _, slots, rows, _, size = array.shape
     shape = jax.ShapeDtypeStruct((slots, rows, max(heads, TILE), size), array.dtype)
     return pl.pallas_call(
-        functools.partial(cut_kernel, flips, heads),
+        functools.partial(cut_kernel, flips, heads, len(after)),
         out_shape=[shape] * len(flips) + [jax.ShapeDtypeStruct((TILE, size), jnp.float32)],
-        in_specs=[pl.BlockSpec(memory_space=pltpu.HBM)],
+        in_specs=[pl.BlockSpec(memory_space=pltpu.HBM)] + [pl.BlockSpec(memory_space=pl.ANY)] * len(after),
         out_specs=[pl.BlockSpec(memory_space=pltpu.VMEM)] * (len(flips) + 1),
         scratch_shapes=[pltpu.SemaphoreType.DMA((len(flips),))],
         compiler_params=pltpu.CompilerParams(vmem_limit_bytes=PACK_VMEM_LIMIT),
         name="cut",
-    )(array)
+    )(array, *after)
 
 
 def arrange_kernel(*refs):
@@ -368,12 +368,18 @@
     def far_plan(number):
         return [(flip, OTHERS, chunks[number : number + 1]) for flip in far]
 
-    *tiles, token = cut(arrays[VALUES], far, heads)
-    tiles = [send(block, flip) for flip, block in zip(far, tiles)]
-    received, token = pack_and_send(far_plan(0), [token])
+    tiles, tokens = [], []
+    for flip in far:
+        block, token = cut(arrays[VALUES], [flip], heads, tokens)
+        tiles.append(send(block, flip))
+        tokens = [token]
+    received, token = pack_and_send(far_plan(0), tokens)
     later = far_plan(1) if len(chunks) > 1 else []
     whole = [(flip, pair, chunks) for flip in close for pair in ((0, 1), (2, 3))]
-    blocks, _ = pack_and_send(later + whole, [token, seen(tiles)])
+    arrived = []
+    for tile in tiles:
+        arrived = [seen([tile] + arrived)]
+    blocks, _ = pack_and_send(later + whole, [token] + arrived)
     values = arrange(tiles, heads)
     prepared = [
         prepare(low, norm_gains, blocks[len(later) + number :: len(chunks)], slots, [] if number else [seen(received)])

time: 58.3 us -> 58.6 us (level)
  Pallas kernels: 14.2 us -> 15.2 us
  waiting for transfers between devices: 24.9 us -> 23.9 us
    ppermute x14, waiting for transfers between devices: 22.8 us -> 21.9 us  [send(): return lax.ppermute(block, 'seq', [(s, s ^ flip) for s in range(sequence)])]
    pallas_call x1 -> x2, Pallas kernels: 1.05 us -> 1.92 us  [cut(): pl.pallas_call(functools.partial(cut_kernel, flips, heads, len(after)), o...]
  transfers between devices with their start and end apart: 17 -> 17, of which waited for: 10 -> 10; matrix products, arithmetic and copies ran while one was open for 0% -> 0% of each run, Pallas kernels for 21% -> 23%
where the time goes in v15:
time: 58.6 us; the launch traced here: 58.2 us
  waiting for transfers between devices  23.9 us (41%)
  starting transfers between devices  16.3 us (28%)
  Pallas kernels  15.2 us (26%)
  local copies, waits for them, and re-layouts  2.08 us (4%)
  other arithmetic  0.6 us (1%)
    ppermute x14, waiting for transfers between devices, send(): return lax.ppermute(block, 'seq', [(s, s ^ flip) for s in range(sequence)])  21.9 us
    ppermute x14, starting transfers between devices, send(): return lax.ppermute(block, 'seq', [(s, s ^ flip) for s in range(sequence)])  10.6 us
    pallas_call x3, Pallas kernels, pack(): pl.pallas_call(functools.partial(pack_kernel, plan, heads, len(after)), o...  7.37 us
    ppermute x3, starting transfers between devices, body(): result = result + lax.ppermute(part, 'dp', list(enumerate(targets)))  5.73 us
    pallas_call x3, Pallas kernels, attend(): pl.pallas_call(kernel, out_shape=shapes, in_specs=[pl.BlockSpec(memory_sp...  4.85 us
    unnamed x10, local copies, waits for them, and re-layouts  2.08 us
    ppermute x3, waiting for transfers between devices, body(): result = result + lax.ppermute(part, 'dp', list(enumerate(targets)))  2 us
    pallas_call x2, Pallas kernels, cut(): pl.pallas_call(functools.partial(cut_kernel, flips, heads, len(after)), o...  1.92 us
  transfers between devices with their start and end apart: 17, of which 10 were waited for; matrix products, arithmetic and copies ran while one was open for 0% of the time, Pallas kernels for 23%

profile of v15, /device:TPU:0, one launch (start us, length us, event | category | flops | bytes accessed | tf_op | source)
XLA Modules:
  0.0 58.2 jit_solution(7093961532624235500)
XLA Ops:
  0.0 1.0 %cut.2 = (bf16[4,32,8,128]{3,2,1,0:T(8,128)(2,1)S(1)}, f32[8,128]{1,0:T(8,128)S(1)}) custom-call(bf16[1,4,32,32,128]{4,3,2,1,0:T(8,128)(2,1)} %refs_2_.5), custom_call_target="tpu_custom_call" | custom-call | tf_op jit(solution)/shard_map/cut/pallas_call | solution.py:53
  1.0 3.0 %collective-permute-start = (bf16[4,32,8,128]{3,2,1,0:T(8,128)(2,1)S(1)}, bf16[4,32,8,128]{3,2,1,0:T(8,128)(2,1)S(1)}, u32[]{:S(2)}, u32[]{:S(2)}) collective-permute-start(bf16[4,32,8,128]{3,2,1,0:T(8,128)(2,1)S(1)} %get-tuple-element.32), channel_id=1, source_target_pairs={{0,2},{1,3},{2,0},{3,1},{4,6},{5,7},{6,4},{7,5},{8,10},{9,11},{10,... | collective-permute-start | bytes 786440 | tf_op jit(solution)/shard_map/ppermute | solution.py:357
  4.0 1.0 %cut.3 = (bf16[4,32,8,128]{3,2,1,0:T(8,128)(2,1)S(1)}, f32[8,128]{1,0:T(8,128)S(1)}) custom-call(bf16[1,4,32,32,128]{4,3,2,1,0:T(8,128)(2,1)} %refs_2_.5, f32[8,128]{1,0:T(8,128)S(1)} %get-tuple-element.33.refs_0_), custom_call_target="tpu_custom_call" | custom-call | tf_op jit(solution)/shard_map/cut/pallas_call | solution.py:53
  4.9 0.1 collective-permute-start.1
  5.0 1.5 %pack.3 = (bf16[4,3,128,128]{3,2,1,0:T(8,128)(2,1)S(1)}, bf16[4,3,128,128]{3,2,1,0:T(8,128)(2,1)S(1)}, f32[8,128]{1,0:T(8,128)S(1)}) custom-call(bf16[1,4,32,32,128]{4,3,2,1,0:T(8,128)(2,1)} %refs_0_.5, bf16[1,4,32,32,128]{4,3,2,1,0:T(8,128)(2,1)} %refs_1_.5, bf16[1,4,32,32,128]{4,3,2,1,0:T(8,128)(2,1)} %refs_2_.5, bf16[1,4,32,32,128]{4,3,2,1,0:T(8,128)(2,1)} %refs_3_.5, ...), custom_call_target="tpu_custom_call" | custom-call | flops 2097152 | bytes 4194304 | tf_op jit(solution)/shard_map/pack/pallas_call | solution.py:145
  6.6 1.2 %collective-permute-start.4 = (bf16[4,3,128,128]{3,2,1,0:T(8,128)(2,1)S(1)}, bf16[4,3,128,128]{3,2,1,0:T(8,128)(2,1)S(1)}, u32[]{:S(2)}, u32[]{:S(2)}) collective-permute-start(bf16[4,3,128,128]{3,2,1,0:T(8,128)(2,1)S(1)} %get-tuple-element.41), channel_id=1, source_target_pairs={{0,2},{1,3},{2,0},{3,1},{4,6},{5,7},{6,4},{7,5},{8,10},{9,11},{10,... | collective-permute-start | bytes 1179656 | tf_op jit(solution)/shard_map/ppermute | solution.py:357
  7.8 0.6 %collective-permute-start.5 = (bf16[4,3,128,128]{3,2,1,0:T(8,128)(2,1)S(1)}, bf16[4,3,128,128]{3,2,1,0:T(8,128)(2,1)S(1)}, u32[]{:S(2)}, u32[]{:S(2)}) collective-permute-start(bf16[4,3,128,128]{3,2,1,0:T(8,128)(2,1)S(1)} %get-tuple-element.42), channel_id=1, source_target_pairs={{0,3},{1,2},{2,1},{3,0},{4,7},{5,6},{6,5},{7,4},{8,11},{9,10},{10,... | collective-permute-start | bytes 1179656 | tf_op jit(solution)/shard_map/ppermute | solution.py:357
  8.4 2.7 %collective-permute-done.refs_0_ = bf16[4,32,8,128]{3,2,1,0:T(8,128)(2,1)S(1)} collective-permute-done((bf16[4,32,8,128]{3,2,1,0:T(8,128)(2,1)S(1)}, bf16[4,32,8,128]{3,2,1,0:T(8,128)(2,1)S(1)}, u32[]{:S(2)}, u32[]{:S(2)}) %collective-permute-start) | collective-permute-done | bytes 262176 | tf_op jit(solution)/shard_map/ppermute | solution.py:357
  11.1 5.2 %collective-permute-done.1.refs_1_.refs_0_ = bf16[4,32,8,128]{3,2,1,0:T(8,128)(2,1)S(1)} collective-permute-done((bf16[4,32,8,128]{3,2,1,0:T(8,128)(2,1)S(1)}, bf16[4,32,8,128]{3,2,1,0:T(8,128)(2,1)S(1)}, u32[]{:S(2)}, u32[]{:S(2)}) %collective-permute-start.1) | collective-permute-done | bytes 262176 | tf_op jit(solution)/shard_map/ppermute | solution.py:357
  16.3 3.8 %pack.4 = (bf16[3,3,128,128]{3,2,1,0:T(8,128)(2,1)}, bf16[3,3,128,128]{3,2,1,0:T(8,128)(2,1)}, bf16[4,2,128,128]{3,2,1,0:T(8,128)(2,1)}, bf16[3,2,128,128]{3,2,1...) custom-call(bf16[1,4,32,32,128]{4,3,2,1,0:T(8,128)(2,1)} %refs_0_.5,, ...), custom_call_target="tpu_custom_call" | custom-call | flops 6291456 | bytes 12582912 | tf_op jit(solution)/shard_map/pack/pallas_call | solution.py:145
  20.1 0.3 collective-permute-start.6
  20.4 0.3 collective-permute-start.7
  20.6 0.2 collective-permute-start.2
  20.9 1.2 %collective-permute-done.2.refs_0_ = bf16[1,2,128,128]{3,2,1,0:T(8,128)(2,1)S(1)} collective-permute-done((bf16[1,2,128,128]{3,2,1,0:T(8,128)(2,1)S(1)}, bf16[1,2,128,128]{3,2,1,0:T(8,128)(2,1)S(1)}, u32[]{:S(2)}, u32[]{:S(2)}) %collective-permute-start.2) | collective-permute-done | bytes 65568 | tf_op jit(solution)/shard_map/ppermute | solution.py:357
  22.1 1.9 %collective-permute-start.12 = (bf16[3,3,128,128]{3,2,1,0:T(8,128)(2,1)}, bf16[3,3,128,128]{3,2,1,0:T(8,128)(2,1)S(1)}, u32[]{:S(2)}, u32[]{:S(2)}) collective-permute-start(bf16[3,3,128,128]{3,2,1,0:T(8,128)(2,1)} %get-tuple-element.53), channel_id=1, source_target_pairs={{0,2},{1,3},{2,0},{3,1},{4,6},{5,7},{6,4},{7,5},{8,10},{9,11},{10,... | collective-permute-start | bytes 884744 | tf_op jit(solution)/shard_map/ppermute | solution.py:357
  24.1 1.1 %collective-permute-done.4.refs_0_ = bf16[4,3,128,128]{3,2,1,0:T(8,128)(2,1)S(1)} collective-permute-done((bf16[4,3,128,128]{3,2,1,0:T(8,128)(2,1)S(1)}, bf16[4,3,128,128]{3,2,1,0:T(8,128)(2,1)S(1)}, u32[]{:S(2)}, u32[]{:S(2)}) %collective-permute-start.4) | collective-permute-done | bytes 393248 | tf_op jit(solution)/shard_map/ppermute | solution.py:357
  25.1 0.0 collective-permute-start.13
  25.2 8.0 %collective-permute-done.5.refs_1_ = bf16[4,3,128,128]{3,2,1,0:T(8,128)(2,1)S(1)} collective-permute-done((bf16[4,3,128,128]{3,2,1,0:T(8,128)(2,1)S(1)}, bf16[4,3,128,128]{3,2,1,0:T(8,128)(2,1)S(1)}, u32[]{:S(2)}, u32[]{:S(2)}) %collective-permute-start.5) | collective-permute-done | bytes 393248 | tf_op jit(solution)/shard_map/ppermute | solution.py:357
  33.2 0.2 collective-permute-start.10
  33.4 0.0 collective-permute-done.6.refs_1_
  33.4 0.3 collective-permute-start.11
  33.7 0.0 collective-permute-done.7.refs_2_
  33.7 0.2 collective-permute-start.3
  33.9 0.2 arrange.1.values
  34.2 0.0 copy-start
  34.2 0.7 %copy-done = f32[2,8,128]{2,1,0:T(8,128)S(1)} copy-done((f32[2,8,128]{2,1,0:T(8,128)S(1)}, f32[2,8,128]{2,1,0:T(8,128)}, u32[]{:S(2)}) %copy-start) | copy-done | bytes 8216
  34.9 0.3 copy-done.1
  35.1 0.1 copy-done.2
  35.2 0.4 prepare.4.close
  35.6 0.3 copy-done.4
  35.9 2.2 %attend.3.refs_4_.refs_2_ = f32[4,128]{1,0:T(4,128)S(1)} custom-call(s32[4,4]{1,0:T(4,128)S(1)} %copy-done.4, f32[2,8,128]{2,1,0:T(8,128)S(1)} %copy-done, bf16[8,4,64,128]{3,2,1,0:T(8,128)(2,1)S(1)} %arrange.1.values, bf16[4,4,4,64,128]{4,3,2,1,0:T(8,128)(2,1)S(1)} %prepare.4.close, bf16[4,3,128,128]{3,2,1,0:T(8,128)(2,1)S(1)} %collective-permute-done.4.refs_0_, ...), custom_call_target="tpu_custom_call" | custom-call | flops 402653184 | bytes 1048576 | tf_op jit(solution)/shard_map/attend/pallas_call | solution.py:314
  38.1 2.1 %pack.5 = (bf16[1,3,128,128]{3,2,1,0:T(8,128)(2,1)S(1)}, bf16[1,3,128,128]{3,2,1,0:T(8,128)(2,1)S(1)}, f32[8,128]{1,0:T(8,128)}) custom-call(bf16[1,4,32,32,128]{4,3,2,1,0:T(8,128)(2,1)} %refs_0_.5, bf16[1,4,32,32,128]{4,3,2,1,0:T(8,128)(2,1)} %refs_1_.5, bf16[1,4,32,32,128]{4,3,2,1,0:T(8,128)(2,1)} %refs_2_.5, bf16[1,4,32,32,128]{4,3,2,1,0:T(8,128)(2,1)} %refs_3_.5, ...), custom_call_target="tpu_custom_call" | custom-call | flops 2097152 | bytes 4194304 | tf_op jit(solution)/shard_map/pack/pallas_call | solution.py:145
  40.2 0.0 collective-permute-done.3.refs_1_
  40.2 2.1 %collective-permute-start.8 = (bf16[1,3,128,128]{3,2,1,0:T(8,128)(2,1)S(1)}, bf16[1,3,128,128]{3,2,1,0:T(8,128)(2,1)S(1)}, u32[]{:S(2)}, u32[]{:S(2)}) collective-permute-start(bf16[1,3,128,128]{3,2,1,0:T(8,128)(2,1)S(1)} %get-tuple-element.47), channel_id=1, source_target_pairs={{0,2},{1,3},{2,0},{3,1},{4,6},{5,7},{6,4},{7,5},{8,10},{9,11},{10,... | collective-permute-start | bytes 294920 | tf_op jit(solution)/shard_map/ppermute | solution.py:357
  42.3 0.2 prepare.3.close
  42.5 0.8 %copy-done.3 = bf16[3,2,128,128]{3,2,1,0:T(8,128)(2,1)S(1)} copy-done((bf16[3,2,128,128]{3,2,1,0:T(8,128)(2,1)S(1)}, bf16[3,2,128,128]{3,2,1,0:T(8,128)(2,1)}, u32[]{:S(2)}) %copy-start.3) | copy-done | bytes 196632
  43.3 0.3 prepare.5.close
  43.6 2.3 %collective-permute-done.13.refs_1_ = bf16[3,3,128,128]{3,2,1,0:T(8,128)(2,1)S(1)} collective-permute-done((bf16[3,3,128,128]{3,2,1,0:T(8,128)(2,1)}, bf16[3,3,128,128]{3,2,1,0:T(8,128)(2,1)S(1)}, u32[]{:S(2)}, u32[]{:S(2)}) %collective-permute-start.13) | collective-permute-done | bytes 294944 | tf_op jit(solution)/shard_map/ppermute | solution.py:357
  45.9 1.6 %attend.4.refs_3_ = f32[3,128]{1,0:T(4,128)S(1)} custom-call(s32[4,4]{1,0:T(4,128)S(1)} %copy-done.4, f32[2,8,128]{2,1,0:T(8,128)S(1)} %copy-done, bf16[8,4,64,128]{3,2,1,0:T(8,128)(2,1)S(1)} %arrange.1.values, bf16[3,4,4,64,128]{4,3,2,1,0:T(8,128)(2,1)S(1)} %prepare.5.close, bf16[3,3,128,128]{3,2,1,0:T(8,128)(2,1)S(1)} %collective-permute-done.12.refs_0_, ...), custom_call_target="tpu_custom_call" | custom-call | flops 301989888 | bytes 786432 | tf_op jit(solution)/shard_map/attend/pallas_call | solution.py:314
  47.5 0.8 %collective-permute-done.8.refs_0_ = bf16[1,3,128,128]{3,2,1,0:T(8,128)(2,1)S(1)} collective-permute-done((bf16[1,3,128,128]{3,2,1,0:T(8,128)(2,1)S(1)}, bf16[1,3,128,128]{3,2,1,0:T(8,128)(2,1)S(1)}, u32[]{:S(2)}, u32[]{:S(2)}) %collective-permute-start.8) | collective-permute-done | bytes 98336 | tf_op jit(solution)/shard_map/ppermute | solution.py:357
  48.3 0.5 collective-permute-done.9.refs_1_
  48.9 1.0 %attend.5 = (f32[2,8,32]{2,1,0:T(8,128)S(1)}, f32[2,8,32]{2,1,0:T(8,128)S(1)}, f32[2,8,32]{2,1,0:T(8,128)S(1)}, f32[2,8,32]{2,1,0:T(8,128)S(1)}) custom-call(s32[4,4]{1,0:T(4,128)S(1)} %copy-done.4, f32[2,8,128]{2,1,0:T(8,128)S(1)} %copy-done, bf16[8,4,64,128]{3,2,1,0:T(8,128)(2,1)S(1)} %arrange.1.values, bf16[1,4,4,64,128]{4,3,2,1,0:T(8,128)(2,1)S(1)} %prepare.3.close, ...), custom_call_target="tpu_custom_call" | custom-call | flops 100663296 | bytes 262144 | tf_op jit(solution)/shard_map/attend/pallas_call | solution.py:314
  49.9 1.7 %collective-permute-start.14 = (f32[2,8,32]{2,1,0:T(8,128)S(1)}, f32[2,8,32]{2,1,0:T(8,128)S(1)}, u32[]{:S(2)}, u32[]{:S(2)}) collective-permute-start(f32[2,8,32]{2,1,0:T(8,128)S(1)} %get-tuple-element.56), channel_id=1, source_target_pairs={{0,4},{4,12},{8,0},{12,8},{1,5},{5,13},{9,1},{13,9},{2,6},{6,14},{... | collective-permute-start | bytes 6152 | tf_op jit(solution)/shard_map/ppermute | solution.py:400
  51.5 2.4 %collective-permute-start.15 = (f32[2,8,32]{2,1,0:T(8,128)S(1)}, f32[2,8,32]{2,1,0:T(8,128)S(1)}, u32[]{:S(2)}, u32[]{:S(2)}) collective-permute-start(f32[2,8,32]{2,1,0:T(8,128)S(1)} %get-tuple-element.57), channel_id=1, source_target_pairs={{0,12},{4,8},{8,4},{12,0},{1,13},{5,9},{9,5},{13,1},{2,14},{6,10},... | collective-permute-start | bytes 6152 | tf_op jit(solution)/shard_map/ppermute | solution.py:400
  54.0 1.6 %collective-permute-start.16 = (f32[2,8,32]{2,1,0:T(8,128)S(1)}, f32[2,8,32]{2,1,0:T(8,128)S(1)}, u32[]{:S(2)}, u32[]{:S(2)}) collective-permute-start(f32[2,8,32]{2,1,0:T(8,128)S(1)} %get-tuple-element.58), channel_id=1, source_target_pairs={{0,8},{4,0},{8,12},{12,4},{1,9},{5,1},{9,13},{13,5},{2,10},{6,2},{... | collective-permute-start | bytes 6152 | tf_op jit(solution)/shard_map/ppermute | solution.py:400
  55.6 1.4 %collective-permute-done.15 = f32[2,8,32]{2,1,0:T(8,128)S(1)} collective-permute-done((f32[2,8,32]{2,1,0:T(8,128)S(1)}, f32[2,8,32]{2,1,0:T(8,128)S(1)}, u32[]{:S(2)}, u32[]{:S(2)}) %collective-permute-start.15) | collective-permute-done | bytes 2080 | tf_op jit(solution)/shard_map/ppermute | solution.py:400
  57.0 0.6 %collective-permute-done.16 = f32[2,8,32]{2,1,0:T(8,128)S(1)} collective-permute-done((f32[2,8,32]{2,1,0:T(8,128)S(1)}, f32[2,8,32]{2,1,0:T(8,128)S(1)}, u32[]{:S(2)}, u32[]{:S(2)}) %collective-permute-start.16) | collective-permute-done | bytes 2080 | tf_op jit(solution)/shard_map/ppermute | solution.py:400
  57.6 0.6 %add_add_fusion = f32[2,8,32]{2,1,0:T(8,128)} fusion(f32[2,8,32]{2,1,0:T(8,128)S(1)} %collective-permute-done.16, f32[2,8,32]{2,1,0:T(8,128)S(1)} %collective-permute-done.15, f32[2,8,32]{2,1,0:T(8,128)S(1)} %get-tuple-element.55, f32[2,8,32]{2,1,0:T(8,128)S(1)} %collective-permute-done.14), kind=kLoop, calls=%fused_computation | loop fusion | flops 1536 | bytes 10240 | tf_op jit(solution)/shard_map/add | solution.py:400
  (12 shorter events, 0.0 us)
Async XLA Ops:
  1.0 10.1 %collective-permute-start = (bf16[4,32,8,128]{3,2,1,0:T(8,128)(2,1)S(1)}, bf16[4,32,8,128]{3,2,1,0:T(8,128)(2,1)S(1)}, u32[]{:S(2)}, u32[]{:S(2)}) collective-permute-start(bf16[4,32,8,128]{3,2,1,0:T(8,128)(2,1)S(1)} %get-tuple-element.32), channel_id=1, source_target_pairs={{0,2},{1,3},{2,0},{3,1},{4,6},{5,7},{6,4},{7,5},{8,10},{9,11},{10,... | collective-permute-start | bytes 786440 | tf_op jit(solution)/shard_map/ppermute | solution.py:357
  4.9 11.4 %collective-permute-start.1 = (bf16[4,32,8,128]{3,2,1,0:T(8,128)(2,1)S(1)}, bf16[4,32,8,128]{3,2,1,0:T(8,128)(2,1)S(1)}, u32[]{:S(2)}, u32[]{:S(2)}) collective-permute-start(bf16[4,32,8,128]{3,2,1,0:T(8,128)(2,1)S(1)} %get-tuple-element.34), channel_id=1, source_target_pairs={{0,3},{1,2},{2,1},{3,0},{4,7},{5,6},{6,5},{7,4},{8,11},{9,10},{10,... | collective-permute-start | bytes 786440 | tf_op jit(solution)/shard_map/ppermute | solution.py:357
  6.6 18.6 %collective-permute-start.4 = (bf16[4,3,128,128]{3,2,1,0:T(8,128)(2,1)S(1)}, bf16[4,3,128,128]{3,2,1,0:T(8,128)(2,1)S(1)}, u32[]{:S(2)}, u32[]{:S(2)}) collective-permute-start(bf16[4,3,128,128]{3,2,1,0:T(8,128)(2,1)S(1)} %get-tuple-element.41), channel_id=1, source_target_pairs={{0,2},{1,3},{2,0},{3,1},{4,6},{5,7},{6,4},{7,5},{8,10},{9,11},{10,... | collective-permute-start | bytes 1179656 | tf_op jit(solution)/shard_map/ppermute | solution.py:357
  7.8 25.4 %collective-permute-start.5 = (bf16[4,3,128,128]{3,2,1,0:T(8,128)(2,1)S(1)}, bf16[4,3,128,128]{3,2,1,0:T(8,128)(2,1)S(1)}, u32[]{:S(2)}, u32[]{:S(2)}) collective-permute-start(bf16[4,3,128,128]{3,2,1,0:T(8,128)(2,1)S(1)} %get-tuple-element.42), channel_id=1, source_target_pairs={{0,3},{1,2},{2,1},{3,0},{4,7},{5,6},{6,5},{7,4},{8,11},{9,10},{10,... | collective-permute-start | bytes 1179656 | tf_op jit(solution)/shard_map/ppermute | solution.py:357
  20.1 13.3 %collective-permute-start.6 = (bf16[4,2,128,128]{3,2,1,0:T(8,128)(2,1)}, bf16[4,2,128,128]{3,2,1,0:T(8,128)(2,1)S(1)}, u32[]{:S(2)}, u32[]{:S(2)}) collective-permute-start(bf16[4,2,128,128]{3,2,1,0:T(8,128)(2,1)} %get-tuple-element.43), channel_id=1, source_target_pairs={{0,1},{1,0},{2,3},{3,2},{4,5},{5,4},{6,7},{7,6},{8,9},{9,8},{10,11... | collective-permute-start | bytes 786440 | tf_op jit(solution)/shard_map/ppermute | solution.py:357
  20.4 13.3 %collective-permute-start.7 = (bf16[4,2,128,128]{3,2,1,0:T(8,128)(2,1)}, bf16[4,2,128,128]{3,2,1,0:T(8,128)(2,1)S(1)}, u32[]{:S(2)}, u32[]{:S(2)}) collective-permute-start(bf16[4,2,128,128]{3,2,1,0:T(8,128)(2,1)} %get-tuple-element.44), channel_id=1, source_target_pairs={{0,1},{1,0},{2,3},{3,2},{4,5},{5,4},{6,7},{7,6},{8,9},{9,8},{10,11... | collective-permute-start | bytes 786440 | tf_op jit(solution)/shard_map/ppermute | solution.py:357
  20.6 1.5 %collective-permute-start.2 = (bf16[1,2,128,128]{3,2,1,0:T(8,128)(2,1)S(1)}, bf16[1,2,128,128]{3,2,1,0:T(8,128)(2,1)S(1)}, u32[]{:S(2)}, u32[]{:S(2)}) collective-permute-start(bf16[1,2,128,128]{3,2,1,0:T(8,128)(2,1)S(1)} %get-tuple-element.37), channel_id=1, source_target_pairs={{0,1},{1,0},{2,3},{3,2},{4,5},{5,4},{6,7},{7,6},{8,9},{9,8},{10,11... | collective-permute-start | bytes 196616 | tf_op jit(solution)/shard_map/ppermute | solution.py:357
  22.1 21.4 %collective-permute-start.12 = (bf16[3,3,128,128]{3,2,1,0:T(8,128)(2,1)}, bf16[3,3,128,128]{3,2,1,0:T(8,128)(2,1)S(1)}, u32[]{:S(2)}, u32[]{:S(2)}) collective-permute-start(bf16[3,3,128,128]{3,2,1,0:T(8,128)(2,1)} %get-tuple-element.53), channel_id=1, source_target_pairs={{0,2},{1,3},{2,0},{3,1},{4,6},{5,7},{6,4},{7,5},{8,10},{9,11},{10,... | collective-permute-start | bytes 884744 | tf_op jit(solution)/shard_map/ppermute | solution.py:357
  25.1 20.7 %collective-permute-start.13 = (bf16[3,3,128,128]{3,2,1,0:T(8,128)(2,1)}, bf16[3,3,128,128]{3,2,1,0:T(8,128)(2,1)S(1)}, u32[]{:S(2)}, u32[]{:S(2)}) collective-permute-start(bf16[3,3,128,128]{3,2,1,0:T(8,128)(2,1)} %get-tuple-element.54), channel_id=1, source_target_pairs={{0,3},{1,2},{2,1},{3,0},{4,7},{5,6},{6,5},{7,4},{8,11},{9,10},{10,... | collective-permute-start | bytes 884744 | tf_op jit(solution)/shard_map/ppermute | solution.py:357
  33.2 9.2 %collective-permute-start.10 = (bf16[3,2,128,128]{3,2,1,0:T(8,128)(2,1)S(1)}, bf16[3,2,128,128]{3,2,1,0:T(8,128)(2,1)S(1)}, u32[]{:S(2)}, u32[]{:S(2)}) collective-permute-start(bf16[3,2,128,128]{3,2,1,0:T(8,128)(2,1)S(1)} %get-tuple-element.49), channel_id=1, source_target_pairs={{0,1},{1,0},{2,3},{3,2},{4,5},{5,4},{6,7},{7,6},{8,9},{9,8},{10,11... | collective-permute-start | bytes 589832 | tf_op jit(solution)/shard_map/ppermute | solution.py:357
  33.4 9.1 %collective-permute-start.11 = (bf16[3,2,128,128]{3,2,1,0:T(8,128)(2,1)S(1)}, bf16[3,2,128,128]{3,2,1,0:T(8,128)(2,1)S(1)}, u32[]{:S(2)}, u32[]{:S(2)}) collective-permute-start(bf16[3,2,128,128]{3,2,1,0:T(8,128)(2,1)S(1)} %get-tuple-element.50), channel_id=1, source_target_pairs={{0,1},{1,0},{2,3},{3,2},{4,5},{5,4},{6,7},{7,6},{8,9},{9,8},{10,11... | collective-permute-start | bytes 589832 | tf_op jit(solution)/shard_map/ppermute | solution.py:357
  33.7 6.5 %collective-permute-start.3 = (bf16[1,2,128,128]{3,2,1,0:T(8,128)(2,1)S(1)}, bf16[1,2,128,128]{3,2,1,0:T(8,128)(2,1)S(1)}, u32[]{:S(2)}, u32[]{:S(2)}) collective-permute-start(bf16[1,2,128,128]{3,2,1,0:T(8,128)(2,1)S(1)} %get-tuple-element.38), channel_id=1, source_target_pairs={{0,1},{1,0},{2,3},{3,2},{4,5},{5,4},{6,7},{7,6},{8,9},{9,8},{10,11... | collective-permute-start | bytes 196616 | tf_op jit(solution)/shard_map/ppermute | solution.py:357
  34.2 0.7 %copy-start = (f32[2,8,128]{2,1,0:T(8,128)S(1)}, f32[2,8,128]{2,1,0:T(8,128)}, u32[]{:S(2)}) copy-start(f32[2,8,128]{2,1,0:T(8,128)} %gains.11) | copy-start | bytes 24580
  34.2 1.0 %copy-start.1 = (bf16[4,2,128,128]{3,2,1,0:T(8,128)(2,1)S(1)}, bf16[4,2,128,128]{3,2,1,0:T(8,128)(2,1)}, u32[]{:S(2)}) copy-start(bf16[4,2,128,128]{3,2,1,0:T(8,128)(2,1)} %get-tuple-element.45.refs_3_) | copy-start | bytes 786436
  34.2 1.0 %copy-start.2 = (bf16[4,2,128,128]{3,2,1,0:T(8,128)(2,1)S(1)}, bf16[4,2,128,128]{3,2,1,0:T(8,128)(2,1)}, u32[]{:S(2)}) copy-start(bf16[4,2,128,128]{3,2,1,0:T(8,128)(2,1)} %get-tuple-element.46.refs_4_) | copy-start | bytes 786436
  35.2 0.7 %copy-start.4 = (s32[4,4]{1,0:T(4,128)S(1)}, s32[4,4]{1,0:T(4,128)}, u32[]{:S(2)}) copy-start(s32[4,4]{1,0:T(4,128)} %units.5) | copy-start | bytes 196
  40.2 8.1 %collective-permute-start.8 = (bf16[1,3,128,128]{3,2,1,0:T(8,128)(2,1)S(1)}, bf16[1,3,128,128]{3,2,1,0:T(8,128)(2,1)S(1)}, u32[]{:S(2)}, u32[]{:S(2)}) collective-permute-start(bf16[1,3,128,128]{3,2,1,0:T(8,128)(2,1)S(1)} %get-tuple-element.47), channel_id=1, source_target_pairs={{0,2},{1,3},{2,0},{3,1},{4,6},{5,7},{6,4},{7,5},{8,10},{9,11},{10,... | collective-permute-start | bytes 294920 | tf_op jit(solution)/shard_map/ppermute | solution.py:357
  42.3 6.5 %collective-permute-start.9 = (bf16[1,3,128,128]{3,2,1,0:T(8,128)(2,1)S(1)}, bf16[1,3,128,128]{3,2,1,0:T(8,128)(2,1)S(1)}, u32[]{:S(2)}, u32[]{:S(2)}) collective-permute-start(bf16[1,3,128,128]{3,2,1,0:T(8,128)(2,1)S(1)} %get-tuple-element.48), channel_id=1, source_target_pairs={{0,3},{1,2},{2,1},{3,0},{4,7},{5,6},{6,5},{7,4},{8,11},{9,10},{10,... | collective-permute-start | bytes 294920 | tf_op jit(solution)/shard_map/ppermute | solution.py:357
  42.3 0.9 %copy-start.3 = (bf16[3,2,128,128]{3,2,1,0:T(8,128)(2,1)S(1)}, bf16[3,2,128,128]{3,2,1,0:T(8,128)(2,1)}, u32[]{:S(2)}) copy-start(bf16[3,2,128,128]{3,2,1,0:T(8,128)(2,1)} %get-tuple-element.52.refs_3_) | copy-start | bytes 589828
  49.9 5.7 %collective-permute-start.14 = (f32[2,8,32]{2,1,0:T(8,128)S(1)}, f32[2,8,32]{2,1,0:T(8,128)S(1)}, u32[]{:S(2)}, u32[]{:S(2)}) collective-permute-start(f32[2,8,32]{2,1,0:T(8,128)S(1)} %get-tuple-element.56), channel_id=1, source_target_pairs={{0,4},{4,12},{8,0},{12,8},{1,5},{5,13},{9,1},{13,9},{2,6},{6,14},{... | collective-permute-start | bytes 6152 | tf_op jit(solution)/shard_map/ppermute | solution.py:400
  51.5 5.4 %collective-permute-start.15 = (f32[2,8,32]{2,1,0:T(8,128)S(1)}, f32[2,8,32]{2,1,0:T(8,128)S(1)}, u32[]{:S(2)}, u32[]{:S(2)}) collective-permute-start(f32[2,8,32]{2,1,0:T(8,128)S(1)} %get-tuple-element.57), channel_id=1, source_target_pairs={{0,12},{4,8},{8,4},{12,0},{1,13},{5,9},{9,5},{13,1},{2,14},{6,10},... | collective-permute-start | bytes 6152 | tf_op jit(solution)/shard_map/ppermute | solution.py:400
  54.0 3.7 %collective-permute-start.16 = (f32[2,8,32]{2,1,0:T(8,128)S(1)}, f32[2,8,32]{2,1,0:T(8,128)S(1)}, u32[]{:S(2)}, u32[]{:S(2)}) collective-permute-start(f32[2,8,32]{2,1,0:T(8,128)S(1)} %get-tuple-element.58), channel_id=1, source_target_pairs={{0,8},{4,0},{8,12},{12,4},{1,9},{5,1},{9,13},{13,5},{2,10},{6,2},{... | collective-permute-start | bytes 6152 | tf_op jit(solution)/shard_map/ppermute | solution.py:400
